TPU v7x, 32 devices: a whole 2x2x4 slice. The times are simulated.
32 devices in a mesh: grp: 2 (over y), ep: 4 (over z), tp: 4 (over x, core).
Axes of the slice: x: 2, y: 2, z: 4, core: 2. Of those that a mesh axis runs over, the one named last changes fastest.
Arguments:
- question_q: bfloat16 [1024, 32, 128], P(('grp', 'ep'), 'tp'), parts along dimension 0, may hold values from -125 to 125
- question_kv: bfloat16 [1024, 4, 2, 128], P(('grp', 'ep')), parts along dimension 0, may hold values from -6 to 6
- doc_kv: bfloat16 [16, 128, 4, 2, 128], P(('grp', 'ep')), parts along dimension 0, may hold values from -6 to 6
- doc_lens: int32 [16], P('grp'), parts along dimension 0, may hold values from 1 to 128, as said below
- query_docs: int32 [8, 4], P('grp'), parts along dimension 0, may hold values from 0 to 7, as said below
- ctx_pos: int32 [8, 5], P('grp'), parts along dimension 0, may hold values from 0 to 827, as said below
- hidden: bfloat16 [1024, 4096], P(('grp', 'ep'), 'tp'), parts along dimension 0, may hold values from -1.5 to 1.5
- out_proj: bfloat16 [4096, 4096], P('ep', 'tp'), may hold values from -0.0234375 to 0.0234375
- norm_gain: bfloat16 [4096], P('tp'), may hold values from 0.5 to 1.5
- router_weight: bfloat16 [4096, 16], P('tp'), may hold values from -0.046875 to 0.046875
- w_gate_up: bfloat16 [16, 4096, 2, 1024], P('ep', 'tp'), may hold values from -0.09375 to 0.09375
- w_down: bfloat16 [16, 1024, 4096], P('ep', None, 'tp'), may hold values from -0.1875 to 0.1875
- expert_ids: int32 [1024, 8], P(('grp', 'ep')), parts along dimension 0, may hold values from 0 to 15, all different within a row; in each aligned block of 128 rows (0 to 127, 128 to 255, ...) at most 64 rows name the same one
Outputs:
- layer_out: bfloat16 [1024, 4096], P(('grp', 'ep'), 'tp'), parts along dimension 0
There are 2 independent parts, one for each index of `grp`. A program takes and returns all parts, laid end to end along the dimension named above; an argument that names none is the same for every part. Nothing has to cross between parts.
Inputs may be any that keep to these rules, and one draw needn't show every extreme that they name: `doc_lens`: document d is held at row d of doc_kv; some document of some query's list has exactly 128 tokens. `query_docs`: the 4 documents of a query lie in 4 different blocks of 2 consecutive documents. `ctx_pos`: in each row, every entry is at least the one before it plus the length of the document before it. `expert_ids`: each query's 128 tokens name every expert exactly 64 times.
All inputs are finite; a program needn't handle non-finite values.
Results may differ from a plain program's by a relative error of at most 0.017.
Values may be sent and summed in bfloat16 or wider, within the bound.
No kernel may reach another device: no remote copies, remote signals or barrier semaphores. Data moves between devices by JAX's collectives and lax.ppermute only.
A program may use at most 128 MiB of HBM per device.

v0:
```python
import math

import jax
import jax.numpy as jnp
from jax import lax
from jax.sharding import PartitionSpec as P

D = 4096
HID = 1024


rope_theta = 1000000.0
norm_eps = 1e-06


def narrow(values):
    return lax.optimization_barrier(values.astype(jnp.bfloat16))


def rotate(values, positions):
    half = values.shape[-1] // 2
    freq = jnp.exp(
        jnp.arange(half, dtype=jnp.float32) * (-2.0 * math.log(rope_theta) / values.shape[-1])
    )
    angle = positions.astype(jnp.float32)[:, None] * freq[None, :]
    shape = (values.shape[0],) + (1,) * (values.ndim - 2) + (half,)
    cosine = jnp.cos(angle).reshape(shape)
    sine = jnp.sin(angle).reshape(shape)
    floats = values.astype(jnp.float32)
    first = floats[..., :half]
    second = floats[..., half:]
    return jnp.concatenate(
        [first * cosine - second * sine, second * cosine + first * sine], axis=-1
    )


def fetch_context(doc_kv, doc_lens, query_docs, row_pos, device, kv_pick):
    pool_dev, doc_max, kv_heads, pair, head_dim = doc_kv.shape
    docs_per = query_docs.shape[1]
    pool_head = lax.dynamic_index_in_dim(doc_kv, kv_pick, 2, keepdims=False).reshape(
        pool_dev, doc_max, pair * head_dim
    )
    held = device * pool_dev + jnp.arange(pool_dev, dtype=jnp.int32)
    wanted = jnp.sum((query_docs[:, :, None] == held[None, None, :]).astype(jnp.float32), axis=1)
    sending = jnp.einsum(
        "rl,lkc->rkc", wanted.astype(jnp.bfloat16), pool_head, preferred_element_type=jnp.float32
    ).astype(jnp.bfloat16)
    received = lax.all_to_all(sending, "ep", split_axis=0, concat_axis=0, tiled=True)
    my_docs = lax.dynamic_index_in_dim(query_docs, device, 0, keepdims=False)
    context = jnp.take(received, my_docs // pool_dev, axis=0)
    lengths = jnp.take(doc_lens, my_docs)
    positions = jnp.repeat(row_pos[:docs_per], doc_max, total_repeat_length=docs_per * doc_max)
    keys = rotate(context[:, :, :head_dim].reshape(docs_per * doc_max, head_dim), positions).astype(
        jnp.bfloat16
    )
    values = context[:, :, head_dim:].reshape(docs_per * doc_max, head_dim)
    valid = (jnp.arange(doc_max, dtype=jnp.int32)[None, :] < lengths[:, None]).reshape(
        docs_per * doc_max
    )
    return (keys, values, valid)


def per_device(
    question_q,
    question_kv,
    doc_kv,
    doc_lens,
    query_docs,
    ctx_pos,
    hidden,
    out_proj,
    norm_gain,
    router_weight,
    w_gate_up,
    w_down,
    expert_ids,
):
    lanes = lax.axis_size("tp")
    groups = lax.axis_size("ep")
    lane = lax.axis_index("tp")
    device = lax.axis_index("ep")
    length, heads_here, head_dim = question_q.shape
    kv_heads = question_kv.shape[1]
    kv_pick = lane * kv_heads // lanes
    scale = head_dim ** (-0.5)
    docs_per = query_docs.shape[1]
    row_pos = lax.dynamic_index_in_dim(ctx_pos, device, 0, keepdims=False)
    question_pos = row_pos[docs_per] + jnp.arange(length, dtype=jnp.int32)
    queries = rotate(question_q, question_pos).astype(jnp.bfloat16)
    own_kv = lax.dynamic_index_in_dim(question_kv, kv_pick, 1, keepdims=False)
    own_keys = rotate(own_kv[:, 0], question_pos).astype(jnp.bfloat16)
    own_values = own_kv[:, 1]
    causal = jnp.arange(length)[:, None] >= jnp.arange(length)[None, :]
    doc_keys, doc_values, valid = fetch_context(
        doc_kv, doc_lens, query_docs, row_pos, device, kv_pick
    )
    keys = jnp.concatenate([doc_keys, own_keys], axis=0)
    values = jnp.concatenate([doc_values, own_values], axis=0)
    allowed = jnp.concatenate(
        [jnp.broadcast_to(valid[None, :], (length, valid.shape[0])), causal], axis=1
    )
    scores = jnp.einsum("ihd,jd->hij", queries, keys, preferred_element_type=jnp.float32) * scale
    scores = jnp.where(allowed[None], scores, -jnp.inf)
    ceiling = jnp.max(scores, axis=-1, keepdims=True)
    probs = jnp.exp(scores - ceiling)
    denominator = jnp.sum(probs, axis=-1, keepdims=True)
    mixed = jnp.einsum(
        "hij,jd->hid", probs.astype(jnp.bfloat16), values, preferred_element_type=jnp.float32
    )
    attended = (
        jnp.transpose(mixed / denominator, (1, 0, 2))
        .reshape(length, heads_here * head_dim)
        .astype(jnp.bfloat16)
    )
    all_heads = lax.all_gather(attended, "tp", axis=1, tiled=True)
    width_here = hidden.shape[1]
    projected = jnp.dot(
        all_heads,
        lax.all_gather(out_proj, "ep", axis=0, tiled=True),
        preferred_element_type=jnp.float32,
    )
    residual_wide = narrow(hidden.astype(jnp.float32) + projected).astype(jnp.float32)
    gain = norm_gain.astype(jnp.float32)
    squares, logit_part = lax.psum(
        (
            jnp.sum(residual_wide * residual_wide, axis=1),
            jnp.dot(
                residual_wide * gain[None, :],
                router_weight.astype(jnp.float32),
                precision=lax.Precision.HIGHEST,
            ),
        ),
        "tp",
    )
    inv_rms = lax.rsqrt(squares / D + norm_eps)
    normed = (residual_wide * inv_rms[:, None] * gain[None, :]).astype(jnp.bfloat16)
    logits = logit_part * inv_rms[:, None]
    mix = jax.nn.softmax(jnp.take_along_axis(logits, expert_ids, axis=1), axis=1)
    local_experts = w_gate_up.shape[0]
    experts = local_experts * groups
    choose = expert_ids.shape[1]
    slots = length * choose
    capacity = slots // experts
    flat_ids = expert_ids.reshape(slots)
    onehot = (flat_ids[:, None] == jnp.arange(experts, dtype=jnp.int32)[None, :]).astype(jnp.int32)
    rank = jnp.sum(jnp.cumsum(onehot, axis=0) * onehot, axis=1) - 1
    position = flat_ids * capacity + rank
    source_row = (
        jnp.zeros((slots,), jnp.int32)
        .at[position]
        .set(jnp.arange(slots, dtype=jnp.int32) // choose)
    )
    sending = jnp.take(normed, source_row, axis=0)
    arrived = lax.all_to_all(sending, "ep", split_axis=0, concat_axis=0, tiled=True).reshape(
        groups, local_experts, capacity, width_here
    )
    hidden_here = HID // lanes
    piece = w_gate_up
    term = jnp.einsum("secd,edgh->hegsc", arrived, piece, preferred_element_type=jnp.float32)
    summed = lax.psum_scatter(
        term.reshape(lax.axis_size("tp") * hidden_here, local_experts, 2, groups * capacity).astype(
            jnp.bfloat16
        ),
        "tp",
        scatter_dimension=0,
        tiled=True,
    ).astype(jnp.float32)
    activated = (jax.nn.silu(summed[:, :, 0]) * summed[:, :, 1]).astype(jnp.bfloat16)
    piece = lax.all_gather(activated, "tp", axis=0, tiled=True)
    count = piece.shape[0]
    expert_out = jnp.einsum(
        "hesc,ehd->secd",
        piece.reshape(count, local_experts, groups, capacity),
        w_down,
        preferred_element_type=jnp.float32,
    )
    returned = lax.all_to_all(
        expert_out.astype(jnp.bfloat16), "ep", split_axis=0, concat_axis=0, tiled=True
    ).reshape(slots, width_here)
    gathered = jnp.take(returned, position, axis=0).reshape(length, choose, width_here)
    combined = jnp.einsum("tk,tkd->td", mix, gathered.astype(jnp.float32))
    return (residual_wide + combined).astype(jnp.bfloat16)


def solution(mesh):
    placed = (
        P(("grp", "ep"), "tp", None),
        P(("grp", "ep"), None, None, None),
        P(("grp", "ep"), None, None, None, None),
        P("grp"),
        P("grp", None),
        P("grp", None),
        P(("grp", "ep"), "tp"),
        P("ep", "tp"),
        P("tp"),
        P("tp", None),
        P("ep", "tp", None, None),
        P("ep", None, "tp"),
        P(("grp", "ep"), None),
    )
    return jax.shard_map(
        per_device, mesh=mesh, in_specs=placed, out_specs=P(("grp", "ep"), "tp"), check_vma=False
    )
```

profile of v0, /device:TPU:0, one launch (start us, length us, event | category | flops | bytes accessed | tf_op | source)
XLA Modules:
  0.0 429.2 jit_solution(6567068346125474226)
XLA Ops:
  6.5 1.0 copy-done
  7.8 0.8 convert_reduce_fusion
  9.0 0.7 copy.90
  9.7 6.3 %all-to-all-start = ((bf16[4,128,256]{2,1,0:T(8,128)(2,1)}), bf16[4,128,256]{2,1,0:T(8,128)(2,1)S(1)}, u32[]{:S(2)}, u32[]{:S(2)}) async-start(bf16[4,128,256]{2,1,0:T(8,128)(2,1)} %copy.90), calls=%async_computation | async-start | bytes 524288 | tf_op jit(solution)/shard_map/all_to_all | solution.py:48
  16.1 0.7 fusion.71
  18.2 2.5 compare_select_fusion.5
  20.7 0.9 constant_dynamic-slice_fusion
  24.0 0.9 all-to-all-done
  28.0 1.5 fusion.24
  29.6 0.7 all-gather.6.cloned.1.call-update
  30.7 4.5 %reduce-window.14 = s32[16,8,128]{2,1,0:T(8,128)S(1)} reduce-window(s32[16,8,128]{2,1,0:T(8,128)S(1)} %fusion.59, s32[]{:T(128)} %constant.209.clone.1), window={size=1x1x128 pad=0_0x0_0x127_0}, to_apply=%region_8.9 | reduce-window | flops 2080768 | bytes 131076 | tf_op jit(solution)/shard_map/reduce-window.3
  35.9 4.3 %scatter_custom_fusion = s32[1024]{0:T(1024)S(1)} fusion(s32[1024]{0:T(1024)S(1)} %bitcast.163, s32[1024]{0:T(1024)S(1)} %add_select_fusion, s32[]{:T(128)} %constant.209.clone.1), kind=kCustom, calls=%fused_computation.122 | custom fusion | bytes 4100 | tf_op jit(solution)/shard_map/scatter | solution.py:151
  40.2 6.8 %all-gather.4.cloned.1.call-done = bf16[128,4096]{0,1:T(8,128)(2,1)} async-done(((bf16[128,1024]{0,1:T(8,128)(2,1)}), bf16[128,4096]{0,1:T(8,128)(2,1)}) %all-gather.4.cloned.1.call-update) | async-done | bytes 1048592 | tf_op jit(solution)/shard_map/all_gather | solution.py:115
  47.0 151.2 %all-gather.6.cloned.1.call-done = bf16[4096,1024]{1,0:T(8,128)(2,1)} async-done(((bf16[1024,1024]{1,0:T(8,128)(2,1)}), bf16[4096,1024]{1,0:T(8,128)(2,1)}) %all-gather.6.cloned.1.call-update) | async-done | bytes 8388624 | tf_op jit(solution)/shard_map/all_gather | solution.py:119
  198.2 5.0 %fusion.20 = bf16[128,1024]{1,0:T(8,128)(2,1)S(1)} fusion(bf16[128,4096]{0,1:T(8,128)(2,1)} %all-gather.4.cloned.1.call-done, bf16[4096,1024]{1,0:T(8,128)(2,1)} %all-gather.6.cloned.1.call-done, bf16[128,1024]{1,0:T(8,128)(2,1)S(1)} %copy-done.3), kind=kOutput, calls=%fused_computation.26 | convolution fusion | flops 1074135040 | bytes 9961472 | tf_op jit(solution)/shard_map/dot_general | solution.py:117
  203.8 7.1 %all-reduce = (f32[128,16]{0,1:T(8,128)S(1)}, f32[128]{0:T(128)S(1)}) all-reduce(f32[128,16]{0,1:T(8,128)S(1)} %fusion.30, f32[128]{0:T(128)S(1)} %fusion.31), channel_id=1, replica_groups=mesh['grp'=2,'ep'=4,'tp'=4] {'tp'}, use_global_device_ids=true, to_apply=%region_3.4 | all-reduce | flops 2176 | bytes 17408 | tf_op jit(solution)/shard_map/psum | solution.py:124
  211.0 4.1 gather_fusion.2
  215.4 49.7 %all_to_all.16 = bf16[4,256,1024]{2,1,0:T(8,128)(2,1)S(1)} all-to-all(bf16[4,256,1024]{2,1,0:T(8,128)(2,1)S(1)} %broadcast_select_fusion), channel_id=1, replica_groups=mesh['grp'=2,'ep'=4,'tp'=4] {'ep'}, dimensions={0} | all-to-all | bytes 4194304 | tf_op jit(solution)/shard_map/all_to_all | solution.py:154
  265.1 13.6 %convert_bitcast_fusion = bf16[1024,4,2,4,64]{0,4,2,3,1:T(8,128)(2,1)} fusion(bf16[4,1024,2,1024,1]{3,2,1,0,4:T(2,128)(2,1)} %bitcast.169, bf16[4,4,64,1024,1]{3,2,1,0,4:T(8,128)(2,1)S(1)} %bitcast.156), kind=kOutput, calls=%fused_computation.10 | convolution fusion | flops 4297064448 | bytes 23068672 | tf_op jit(solution)/shard_map/secd,edgh->hegsc/dot_general | solution.py:159
  278.6 4.8 %copy.111 = bf16[1024,4,2,4,64]{0,4,3,2,1:T(8,128)(2,1)} copy(bf16[1024,4,2,4,64]{0,4,2,3,1:T(8,128)(2,1)} %convert_bitcast_fusion) | data formatting | bytes 8388608 | tf_op jit(solution)/shard_map/convert_element_type | solution.py:161
  283.5 43.9 %reduce-scatter.2.cloned.1.call-done = bf16[256,4,2,256]{0,3,2,1:T(8,128)(2,1)} async-done(((bf16[1024,4,2,256]{0,3,2,1:T(8,128)(2,1)}), bf16[256,4,2,256]{0,3,2,1:T(8,128)(2,1)}) %reduce-scatter.2.cloned.1.call-update) | async-done | bytes 1048592 | tf_op jit(solution)/shard_map/reduce_scatter | solution.py:160
  327.4 1.4 convert_element_type.119
  328.8 1.1 fusion.28
  329.9 23.0 %all-gather.8.cloned.1.call-done = bf16[1024,4,256]{0,2,1:T(8,128)(2,1)} async-done(((bf16[256,4,256]{0,2,1:T(8,128)(2,1)}), bf16[1024,4,256]{0,2,1:T(8,128)(2,1)}) %all-gather.8.cloned.1.call-update) | async-done | bytes 2097168 | tf_op jit(solution)/shard_map/all_gather | solution.py:169
  353.0 6.4 %convert_bitcast_fusion.1 = bf16[4,4,64,1024]{3,2,0,1:T(8,128)(2,1)S(1)} fusion(bf16[1024,4,4,64]{0,3,2,1:T(8,128)(2,1)} %bitcast.170, bf16[4,1024,1024]{2,1,0:T(8,128)(2,1)} %param.26), kind=kOutput, calls=%fused_computation.18 | convolution fusion | flops 2148532224 | bytes 12582912 | tf_op jit(solution)/shard_map/hesc,ehd->secd/dot_general | solution.py:171
  359.3 1.6 copy.113
  360.9 4.6 %all-to-all-start.2 = ((bf16[4,4,64,1024]{3,2,1,0:T(8,128)(2,1)}), bf16[4,4,64,1024]{3,2,1,0:T(8,128)(2,1)S(1)}, u32[]{:S(2)}, u32[]{:S(2)}) async-start(bf16[4,4,64,1024]{3,2,1,0:T(8,128)(2,1)} %copy.113), calls=%async_computation.3 | async-start | bytes 4194304 | tf_op jit(solution)/shard_map/all_to_all | solution.py:177
  366.0 7.0 %gather_fusion.4 = f32[1024]{0:T(1024)S(1)} fusion(f32[128,16]{0,1:T(8,128)S(1)} %broadcast_multiply_fusion, s32[1024]{0:T(1024)S(1)} %reshape.475), kind=kCustom, calls=%fused_computation.4 | custom fusion | bytes 16384 | tf_op jit(solution)/shard_map/jit(take_along_axis)/gather | solution.py:138
  373.4 40.7 %all-to-all-done.2 = bf16[4,4,64,1024]{3,2,1,0:T(8,128)(2,1)S(1)} async-done(((bf16[4,4,64,1024]{3,2,1,0:T(8,128)(2,1)}), bf16[4,4,64,1024]{3,2,1,0:T(8,128)(2,1)S(1)}, u32[]{:S(2)}, u32[]{:S(2)}) %all-to-all-start.2) | async-done | bytes 2097184 | tf_op jit(solution)/shard_map/all_to_all | solution.py:177
  414.1 5.4 %gather_fusion.3 = bf16[1024,1024]{1,0:T(8,128)(2,1)} fusion(bf16[1024,1024]{1,0:T(8,128)(2,1)S(1)} %bitcast.153, s32[1024]{0:T(1024)S(1)} %broadcast_clamp_fusion), kind=kCustom, calls=%fused_computation.3 | custom fusion | bytes 4198400 | tf_op jit(solution)/shard_map/jit(_take)/gather | solution.py:180
  419.5 2.4 fusion.8
  421.8 0.8 fusion.34
  (102 shorter events, 10.1 us)
Async XLA Ops:
  6.5 1.0 copy-start
  6.5 15.8 %copy-start.4 = (bf16[128,8,128]{2,1,0:T(8,128)(2,1)S(1)}, bf16[128,8,128]{2,1,0:T(8,128)(2,1)}, u32[]{:S(2)}) copy-start(bf16[128,8,128]{2,1,0:T(8,128)(2,1)} %param.15) | copy-start | bytes 786436
  6.5 15.9 %copy-start.2 = (s32[8]{0:T(128)S(1)}, s32[8]{0:T(128)}, u32[]{:S(2)}) copy-start(s32[8]{0:T(128)} %param.18) | copy-start | bytes 100
  9.7 15.2 %all-to-all-start = ((bf16[4,128,256]{2,1,0:T(8,128)(2,1)}), bf16[4,128,256]{2,1,0:T(8,128)(2,1)S(1)}, u32[]{:S(2)}, u32[]{:S(2)}) async-start(bf16[4,128,256]{2,1,0:T(8,128)(2,1)} %copy.90), calls=%async_computation | async-start | bytes 524288 | tf_op jit(solution)/shard_map/all_to_all | solution.py:48
  16.0 31.0 %all-gather.4.cloned.1.call-start = ((), (), s32[]{:S(2)}) async-start(), calls=%async_computation.4 | async-start | bytes 1310720 | tf_op jit(solution)/shard_map/all_gather | solution.py:115
  28.0 2.4 copy-start.5
  28.0 2.6 copy-start.7
  29.5 168.7 %copy-start.3 = (bf16[128,1024]{1,0:T(8,128)(2,1)S(1)}, bf16[128,1024]{1,0:T(8,128)(2,1)}, u32[]{:S(2)}) copy-start(bf16[128,1024]{1,0:T(8,128)(2,1)} %param.21) | copy-start | bytes 786436
  29.5 168.7 %all-gather.6.cloned.1.call-start = ((), (), s32[]{:S(2)}) async-start(), calls=%async_computation.5 | async-start | bytes 10485760 | tf_op jit(solution)/shard_map/all_gather | solution.py:119
  30.3 297.1 %reduce-scatter.2.cloned.1.call-start = ((), (), s32[]{:S(2)}) async-start(), calls=%async_computation.6 | async-start | bytes 5242880 | tf_op jit(solution)/shard_map/reduce_scatter | solution.py:160
  40.2 163.2 %copy-start.6 = (bf16[1024,16]{0,1:T(8,128)(2,1)S(1)}, bf16[1024,16]{0,1:T(8,128)(2,1)}, u32[]{:S(2)}) copy-start(bf16[1024,16]{0,1:T(8,128)(2,1)} %param.24) | copy-start | bytes 98308
  283.5 69.5 %all-gather.8.cloned.1.call-start = ((), (), s32[]{:S(2)}) async-start(), calls=%async_computation.7 | async-start | bytes 2621440 | tf_op jit(solution)/shard_map/all_gather | solution.py:169
  360.9 53.2 %all-to-all-start.2 = ((bf16[4,4,64,1024]{3,2,1,0:T(8,128)(2,1)}), bf16[4,4,64,1024]{3,2,1,0:T(8,128)(2,1)S(1)}, u32[]{:S(2)}, u32[]{:S(2)}) async-start(bf16[4,4,64,1024]{3,2,1,0:T(8,128)(2,1)} %copy.113), calls=%async_computation.3 | async-start | bytes 4194304 | tf_op jit(solution)/shard_map/all_to_all | solution.py:177
  414.1 8.6 %copy-start.1 = (bf16[2,128,4,2,128]{4,3,2,1,0:T(2,128)(2,1)S(1)}, bf16[2,128,4,2,128]{4,3,2,1,0:T(2,128)(2,1)}, u32[]{:S(2)}) copy-start(bf16[2,128,4,2,128]{4,3,2,1,0:T(2,128)(2,1)} %param.17) | copy-start | bytes 1572868
Sparse Core Ops, SparseCore 0:
  29.6 17.3 all-gather.3
  48.6 149.6 all-gather.5
  283.6 43.7 reduce-scatter.1
  330.1 22.8 all-gather.7
where the time goes:
time: 430 us; the launch traced here: 429 us
  waiting for transfers between devices  267 us (62%)
  blocking collectives  56.8 us (13%)
  local copies, waits for them, and re-layouts  34.9 us (8%)
  matrix products  30.2 us (7%)
  other arithmetic  15.4 us (4%)
  between operations  13.7 us (3%)
  starting transfers between devices  11 us (3%)
    all_gather x1, waiting for transfers between devices, per_device(): lax.all_gather(out_proj, 'ep', axis=0, tiled=True)  151 us
    all_to_all x1, blocking collectives, per_device(): lax.all_to_all(sending, 'ep', split_axis=0, concat_axis=0, tiled=True)  49.7 us
    reduce_scatter x1, waiting for transfers between devices, per_device(): lax.psum_scatter(term.reshape(lax.axis_size('tp') * hidden_here, local_ex...  43.9 us
    all_to_all x1, waiting for transfers between devices, per_device(): lax.all_to_all(expert_out.astype(jnp.bfloat16), 'ep', split_axis=0, conca...  40.7 us
    all_gather x1, waiting for transfers between devices, per_device(): piece = lax.all_gather(activated, 'tp', axis=0, tiled=True)  23 us
    dot_general x1, matrix products, per_device(): jnp.einsum('secd,edgh->hegsc', arrived, piece, preferred_element_type=jnp...  13.6 us
  transfers between devices with their start and end apart: 6, of which 6 were waited for; matrix products, arithmetic and copies ran while one was open for 6% of the time, Pallas kernels for 0%

commit v1 on v0

v1 whole, which is shorter than its diff:
```python
import math

import jax
import jax.numpy as jnp
from jax import lax
from jax.sharding import PartitionSpec as P

rope_theta = 1000000.0
norm_eps = 1e-06


def tables(positions, head_dim):
    half = head_dim // 2
    freq = jnp.exp(jnp.arange(half, dtype=jnp.float32) * (-2.0 * math.log(rope_theta) / head_dim))
    angle = positions.astype(jnp.float32)[:, None] * freq[None, :]
    return (jnp.cos(angle), jnp.sin(angle))


def rotate(values, positions):
    half = values.shape[-1] // 2
    cosine, sine = tables(positions, values.shape[-1])
    shape = (values.shape[0],) + (1,) * (values.ndim - 2) + (half,)
    cosine, sine = (cosine.reshape(shape), sine.reshape(shape))
    floats = values.astype(jnp.float32)
    first = floats[..., :half]
    second = floats[..., half:]
    return jnp.concatenate(
        [first * cosine - second * sine, second * cosine + first * sine], axis=-1
    )


def attend(q_rows, own_kv, context, starts, lengths, question_start):
    length, heads_here, head_dim = q_rows.shape
    docs_per, doc_max, _ = context.shape
    question_pos = question_start + jnp.arange(length, dtype=jnp.int32)
    queries = rotate(q_rows, question_pos).astype(jnp.bfloat16)
    own_keys = rotate(own_kv[:, :head_dim], question_pos).astype(jnp.bfloat16)
    positions = jnp.repeat(starts, doc_max, total_repeat_length=docs_per * doc_max)
    doc_keys = rotate(context[:, :, :head_dim].reshape(docs_per * doc_max, head_dim), positions)
    keys = jnp.concatenate([doc_keys.astype(jnp.bfloat16), own_keys], axis=0)
    values = jnp.concatenate(
        [context[:, :, head_dim:].reshape(docs_per * doc_max, head_dim), own_kv[:, head_dim:]],
        axis=0,
    )
    valid = (jnp.arange(doc_max, dtype=jnp.int32)[None, :] < lengths[:, None]).reshape(-1)
    causal = jnp.arange(length)[:, None] >= jnp.arange(length)[None, :]
    allowed = jnp.concatenate(
        [jnp.broadcast_to(valid[None, :], (length, valid.shape[0])), causal], axis=1
    )
    scores = jnp.einsum("ihd,jd->hij", queries, keys, preferred_element_type=jnp.float32)
    scores = jnp.where(allowed[None], scores * head_dim ** (-0.5), -jnp.inf)
    ceiling = jnp.max(scores, axis=-1, keepdims=True)
    probs = jnp.exp(scores - ceiling)
    denominator = jnp.sum(probs, axis=-1, keepdims=True)
    mixed = jnp.einsum(
        "hij,jd->hid", probs.astype(jnp.bfloat16), values, preferred_element_type=jnp.float32
    )
    return (
        jnp.transpose(mixed / denominator, (1, 0, 2))
        .reshape(length, heads_here * head_dim)
        .astype(jnp.bfloat16)
    )


def context_by_row(doc_kv, doc_lens, query_docs, ctx_pos, device, kv_pick):
    pool_dev, doc_max, _, pair, head_dim = doc_kv.shape
    docs_per = query_docs.shape[1]
    pool_head = lax.dynamic_index_in_dim(doc_kv, kv_pick, 2, keepdims=False).reshape(
        pool_dev, doc_max, pair * head_dim
    )
    held = device * pool_dev + jnp.arange(pool_dev, dtype=jnp.int32)
    wanted = jnp.sum((query_docs[:, :, None] == held[None, None, :]).astype(jnp.float32), axis=1)
    sending = jnp.einsum(
        "rl,lkc->rkc", wanted.astype(jnp.bfloat16), pool_head, preferred_element_type=jnp.float32
    ).astype(jnp.bfloat16)
    received = lax.all_to_all(sending, "ep", split_axis=0, concat_axis=0, tiled=True)
    my_docs = lax.dynamic_index_in_dim(query_docs, device, 0, keepdims=False)
    starts = lax.dynamic_index_in_dim(ctx_pos, device, 0, keepdims=False)
    return (jnp.take(received, my_docs // pool_dev, axis=0), starts[:docs_per], jnp.take(doc_lens, my_docs))


def context_by_column(doc_kv, doc_lens, query_docs, ctx_pos, device, query):
    pool_dev, doc_max, kv_heads, pair, head_dim = doc_kv.shape
    docs_per = query_docs.shape[1]
    my_docs = lax.dynamic_index_in_dim(query_docs, query, 0, keepdims=False)
    starts = lax.dynamic_index_in_dim(ctx_pos, query, 0, keepdims=False)
    held = device * pool_dev + jnp.arange(pool_dev, dtype=jnp.int32)
    local = jnp.sum(
        jnp.where(my_docs[:, None] == held[None, :], jnp.arange(pool_dev, dtype=jnp.int32)[None, :], 0)
    )
    block = lax.dynamic_index_in_dim(doc_kv, local, 0, keepdims=False)
    sending = jnp.transpose(block, (1, 0, 2, 3)).reshape(kv_heads, doc_max, pair * head_dim)
    received = lax.all_to_all(sending, "ep", split_axis=0, concat_axis=0, tiled=True)
    owner = my_docs // pool_dev
    here = owner[None, :] == jnp.arange(docs_per, dtype=jnp.int32)[:, None]
    lengths = jnp.sum(jnp.where(here, jnp.take(doc_lens, my_docs)[None, :], 0), axis=1)
    return (received, jnp.sum(jnp.where(here, starts[None, :docs_per], 0), axis=1), lengths)


def pairs(lanes, flip):
    return [(i, i ^ flip) for i in range(lanes)]


def gather_lanes(mine, lanes):
    across = jnp.stack([mine, lax.ppermute(mine, "tp", pairs(lanes, 2))])
    return jnp.concatenate([across, lax.ppermute(across, "tp", pairs(lanes, 1))])


def scatter_lanes(parts, lanes):
    chip = parts[:2].astype(jnp.float32) + lax.ppermute(parts[2:], "tp", pairs(lanes, 1)).astype(
        jnp.float32
    )
    away = lax.ppermute(chip[1].astype(jnp.bfloat16), "tp", pairs(lanes, 2))
    return chip[0] + away.astype(jnp.float32)


def per_device(
    question_q,
    question_kv,
    doc_kv,
    doc_lens,
    query_docs,
    ctx_pos,
    hidden,
    out_proj,
    norm_gain,
    router_weight,
    w_gate_up,
    w_down,
    expert_ids,
):
    lanes = lax.axis_size("tp")
    groups = lax.axis_size("ep")
    lane = lax.axis_index("tp")
    device = lax.axis_index("ep")
    length, heads_here, head_dim = question_q.shape
    kv_heads = question_kv.shape[1]
    docs_per = query_docs.shape[1]
    width_here = hidden.shape[1]
    square = lanes == 4 and groups == 4 and kv_heads == 4 and docs_per == groups
    ids = lax.all_gather(expert_ids, "ep", axis=0, tiled=False)
    order = lane ^ jnp.array([0, 2, 1, 3], jnp.int32) if square else None

    if square:
        kv_head = lax.dynamic_index_in_dim(question_kv, lane, 1, keepdims=False).reshape(
            length, 2 * head_dim
        )
        outgoing = jnp.concatenate(
            [question_q.reshape(length, heads_here * head_dim), kv_head], axis=1
        )
        turned = lax.ppermute(
            outgoing,
            ("ep", "tp"),
            [(e * lanes + t, t * lanes + e) for e in range(groups) for t in range(lanes)],
        )
        context, starts, lengths = context_by_column(
            doc_kv, doc_lens, query_docs, ctx_pos, device, lane
        )
        question_start = lax.dynamic_index_in_dim(ctx_pos, lane, 0, keepdims=False)[docs_per]
        q_rows = turned[:, : heads_here * head_dim].reshape(length, heads_here, head_dim)
        attended = attend(
            q_rows, turned[:, heads_here * head_dim :], context, starts, lengths, question_start
        )
        all_queries = gather_lanes(attended, lanes).reshape(lanes * length, -1)
        partial = jnp.dot(all_queries, out_proj, preferred_element_type=jnp.float32)
        partial = partial.astype(jnp.bfloat16).reshape(lanes, length, width_here)
        slot_of = jnp.array([0, 2, 1, 3], jnp.int32)[lane ^ jnp.arange(lanes, dtype=jnp.int32)]
        partial = jnp.take(partial, slot_of, axis=0)
        projected = lax.psum_scatter(partial, "ep", scatter_dimension=0, tiled=True)[0]
    else:
        kv_pick = lane * kv_heads // lanes
        kv_head = lax.dynamic_index_in_dim(question_kv, kv_pick, 1, keepdims=False).reshape(
            length, 2 * head_dim
        )
        context, starts, lengths = context_by_row(
            doc_kv, doc_lens, query_docs, ctx_pos, device, kv_pick
        )
        question_start = lax.dynamic_index_in_dim(ctx_pos, device, 0, keepdims=False)[docs_per]
        attended = attend(question_q, kv_head, context, starts, lengths, question_start)
        projected = jnp.dot(
            lax.all_gather(attended, "tp", axis=1, tiled=True),
            lax.all_gather(out_proj, "ep", axis=0, tiled=True),
            preferred_element_type=jnp.float32,
        )
    residual = (hidden.astype(jnp.float32) + projected.astype(jnp.float32)).astype(jnp.bfloat16)

    tokens = lax.all_gather(residual, "ep", axis=0, tiled=False)
    wide = tokens.astype(jnp.float32)
    gain = norm_gain.astype(jnp.float32)
    scaled = wide * gain
    logit_part = jnp.einsum(
        "snd,de->sne", scaled, router_weight.astype(jnp.float32), precision=lax.Precision.HIGHEST
    )
    square_part = jnp.sum(wide * wide, axis=2, keepdims=True)
    stats = jnp.sum(
        lax.all_gather(jnp.concatenate([logit_part, square_part], axis=2), "tp", axis=0), axis=0
    )
    experts = router_weight.shape[1]
    inv_rms = lax.rsqrt(stats[:, :, experts] / (width_here * lanes) + norm_eps)
    logits = stats[:, :, :experts] * inv_rms[:, :, None]

    local_experts = w_gate_up.shape[0]
    capacity = length * expert_ids.shape[1] // experts
    hid = w_gate_up.shape[3]
    chosen_all = jnp.any(
        ids[:, :, :, None] == jnp.arange(experts, dtype=jnp.int32), axis=2
    )
    top = jnp.max(jnp.where(chosen_all, logits, -jnp.inf), axis=2, keepdims=True)
    weight = jnp.where(chosen_all, jnp.exp(logits - top), 0.0)
    mix = weight / jnp.sum(weight, axis=2, keepdims=True)

    if square:
        shuffled = jnp.take(chosen_all, order, axis=0)
        scaled_rows = jnp.take(scaled.astype(jnp.bfloat16), order, axis=0)
        inv_rms = jnp.take(inv_rms, order, axis=0)
        mix = jnp.take(mix, order, axis=0)
    else:
        shuffled, scaled_rows = (chosen_all, scaled.astype(jnp.bfloat16))
    first = device * local_experts
    chosen = lax.dynamic_slice_in_dim(shuffled, first, local_experts, 2)
    mix_here = lax.dynamic_slice_in_dim(mix, first, local_experts, 2)
    before = (jnp.arange(length)[:, None] > jnp.arange(length)[None, :]).astype(jnp.bfloat16)
    rank = jnp.einsum(
        "mn,sne->sem", before, chosen.astype(jnp.bfloat16), preferred_element_type=jnp.float32
    ).astype(jnp.int32)
    pick = jnp.logical_and(
        jnp.transpose(chosen, (0, 2, 1))[:, :, None, :],
        rank[:, :, None, :] == jnp.arange(capacity, dtype=jnp.int32)[None, None, :, None],
    )
    onehot = pick.astype(jnp.bfloat16)
    inv_row = jnp.sum(jnp.where(pick, inv_rms[:, None, None, :], 0.0), axis=3)
    mix_row = jnp.sum(jnp.where(pick, jnp.transpose(mix_here, (0, 2, 1))[:, :, None, :], 0.0), axis=3)

    rows = jnp.einsum(
        "sern,snd->serd", onehot, scaled_rows, preferred_element_type=jnp.float32
    ).astype(jnp.bfloat16)
    term = jnp.einsum(
        "serd,edgh->sergh", rows, w_gate_up, preferred_element_type=jnp.float32
    ).astype(jnp.bfloat16)
    per_lane = groups * local_experts * capacity // lanes
    term = term.reshape(lanes, per_lane, 2 * hid)
    inv_row = inv_row.reshape(lanes, per_lane, 1)
    if square:
        summed = scatter_lanes(term, lanes)
        inv_mine = inv_row[0]
    else:
        summed = lax.psum_scatter(term, "tp", scatter_dimension=0, tiled=True)[0].astype(jnp.float32)
        inv_mine = lax.dynamic_index_in_dim(inv_row, lane, 0, keepdims=False)
    summed = summed * inv_mine
    act = (jax.nn.silu(summed[:, :hid]) * summed[:, hid:]).astype(jnp.bfloat16)
    if square:
        acts = gather_lanes(act, lanes)
    else:
        acts = lax.all_gather(act, "tp", axis=0, tiled=False)
    acts = acts.reshape(groups, local_experts, capacity, hid)
    expert_out = jnp.einsum("serh,ehd->serd", acts, w_down, preferred_element_type=jnp.float32)
    expert_out = (expert_out * mix_row[:, :, :, None]).astype(jnp.bfloat16)
    combined = jnp.einsum(
        "sern,serd->snd", onehot, expert_out, preferred_element_type=jnp.float32
    ).astype(jnp.bfloat16)
    if square:
        combined = jnp.take(combined, slot_of, axis=0)
    returned = lax.psum_scatter(combined, "ep", scatter_dimension=0, tiled=True)[0]
    return (residual.astype(jnp.float32) + returned.astype(jnp.float32)).astype(jnp.bfloat16)


def solution(mesh):
    placed = (
        P(("grp", "ep"), "tp", None),
        P(("grp", "ep"), None, None, None),
        P(("grp", "ep"), None, None, None, None),
        P("grp"),
        P("grp", None),
        P("grp", None),
        P(("grp", "ep"), "tp"),
        P("ep", "tp"),
        P("tp"),
        P("tp", None),
        P("ep", "tp", None, None),
        P("ep", None, "tp"),
        P(("grp", "ep"), None),
    )
    return jax.shard_map(
        per_device, mesh=mesh, in_specs=placed, out_specs=P(("grp", "ep"), "tp"), check_vma=False
    )
```

time: 430 us -> 268 us (0.62)
  waiting for transfers between devices: 267 us -> 86.5 us
  blocking collectives: 56.8 us -> 39.4 us
  other arithmetic: 15.4 us -> 31.9 us
  starting transfers between devices: 11 us -> 24.9 us
  local copies, waits for them, and re-layouts: 34.9 us -> 39.4 us
    all_gather x3 -> x1, waiting for transfers between devices: 181 us -> 12.5 us  [per_device(): tokens = lax.all_gather(residual, 'ep', axis=0, tiled=False)]
    all_to_all x1 -> x0, blocking collectives: 49.7 us -> none  [per_device(): lax.all_to_all(sending, 'ep', split_axis=0, concat_axis=0, tiled=True)]
    all_to_all x2 -> x1, waiting for transfers between devices: 41.6 us -> 0.01 us  [context_by_column(): lax.all_to_all(sending, 'ep', split_axis=0, concat_axis=0, tiled=True)]
    all_gather x0 -> x2, blocking collectives: none -> 39.4 us  [the longest x1 26 us: per_device(): lax.all_gather(jnp.concatenate([logit_part, square_part], axis=2), 'tp',...]
    ppermute x0 -> x7, waiting for transfers between devices: none -> 20.4 us  [the longest x2 15.9 us: gather_lanes(): across = jnp.stack([mine, lax.ppermute(mine, 'tp', pairs(lanes, 2))])]
    ppermute x0 -> x7, starting transfers between devices: none -> 18.5 us  [the longest x2 16.1 us: gather_lanes(): across = jnp.stack([mine, lax.ppermute(mine, 'tp', pairs(lanes, 2))])]
    gather x10 -> x9, local copies, waits for them, and re-layouts: 18.6 us -> 6.41 us  [the longest x1 1.58 us: per_device(): combined = jnp.take(combined, slot_of, axis=0)]
    reduce_scatter x1 -> x2, waiting for transfers between devices: 43.9 us -> 53.5 us  [the longest x1 26.8 us: per_device(): lax.psum_scatter(partial, 'ep', scatter_dimension=0, tiled=True)[0]]
  transfers between devices with their start and end apart: 6 -> 11, of which waited for: 6 -> 7; matrix products, arithmetic and copies ran while one was open for 6% -> 13% of each run, Pallas kernels for 0% -> 0%
where the time goes in v1:
time: 268 us; the launch traced here: 267 us
  waiting for transfers between devices  86.5 us (32%)
  local copies, waits for them, and re-layouts  39.4 us (15%)
  blocking collectives  39.4 us (15%)
  other arithmetic  31.9 us (12%)
  matrix products  29.3 us (11%)
  starting transfers between devices  24.9 us (9%)
  between operations  15.6 us (6%)
    reduce_scatter x1, waiting for transfers between devices, per_device(): lax.psum_scatter(partial, 'ep', scatter_dimension=0, tiled=True)[0]  26.8 us
    reduce_scatter x1, waiting for transfers between devices, per_device(): lax.psum_scatter(combined, 'ep', scatter_dimension=0, tiled=True)[0]  26.8 us
    all_gather x1, blocking collectives, per_device(): lax.all_gather(jnp.concatenate([logit_part, square_part], axis=2), 'tp',...  26 us
    dot_general x1, matrix products, per_device(): jnp.einsum('serd,edgh->sergh', rows, w_gate_up, preferred_element_type=jn...  18 us
    ppermute x2, starting transfers between devices, gather_lanes(): across = jnp.stack([mine, lax.ppermute(mine, 'tp', pairs(lanes, 2))])  16.1 us
    ppermute x2, waiting for transfers between devices, gather_lanes(): across = jnp.stack([mine, lax.ppermute(mine, 'tp', pairs(lanes, 2))])  15.9 us
    convert_element_type x2, local copies, waits for them, and re-layouts, scatter_lanes(): parts[:2].astype(jnp.float32)  14.1 us
    all_gather x1, blocking collectives, per_device(): ids = lax.all_gather(expert_ids, 'ep', axis=0, tiled=False)  13.4 us
  transfers between devices with their start and end apart: 11, of which 7 were waited for; matrix products, arithmetic and copies ran while one was open for 13% of the time, Pallas kernels for 0%

profile of v1, /device:TPU:0, one launch (start us, length us, event | category | flops | bytes accessed | tf_op | source)
XLA Modules:
  0.0 267.0 jit_solution(1071656195490627313)
XLA Ops:
  12.0 6.3 %all-to-all-start = ((bf16[4,128,256]{1,2,0:T(8,128)(2,1)}), bf16[4,128,256]{1,2,0:T(8,128)(2,1)S(1)}, u32[]{:S(2)}, u32[]{:S(2)}) async-start(bf16[4,128,256]{1,2,0:T(8,128)(2,1)} %bitcast.10), calls=%async_computation | async-start | bytes 524288 | tf_op jit(solution)/shard_map/all_to_all | solution.py:93
  24.7 2.4 compare_select_fusion.1
  33.0 1.8 subtract_convert_fusion
  36.1 1.7 fusion.25
  39.3 14.6 %collective-permute-start.1 = (bf16[128,1024]{1,0:T(8,128)(2,1)S(1)}, bf16[128,1024]{1,0:T(8,128)(2,1)S(1)}, u32[]{:S(2)}, u32[]{:S(2)}) collective-permute-start(bf16[128,1024]{1,0:T(8,128)(2,1)S(1)} %copy.117), channel_id=1, source_target_pairs={{0,2},{1,3},{2,0},{3,1},{4,6},{5,7},{6,4},{7,5},{8,10},{9,11},{10,... | collective-permute-start | bytes 786440 | tf_op jit(solution)/shard_map/ppermute | solution.py:105
  54.8 3.5 %collective-permute-done.1 = bf16[128,1024]{1,0:T(8,128)(2,1)S(1)} collective-permute-done((bf16[128,1024]{1,0:T(8,128)(2,1)S(1)}, bf16[128,1024]{1,0:T(8,128)(2,1)S(1)}, u32[]{:S(2)}, u32[]{:S(2)}) %collective-permute-start.1) | collective-permute-done | bytes 262176 | tf_op jit(solution)/shard_map/ppermute | solution.py:105
  58.5 1.9 collective-permute-done.2
  60.4 1.3 convolution_convert_fusion
  63.6 26.8 %reduce-scatter.3.cloned.1.call-done = bf16[1,128,1024]{2,1,0:T(8,128)(2,1)} async-done(((bf16[4,128,1024]{2,1,0:T(8,128)(2,1)}), bf16[1,128,1024]{2,1,0:T(8,128)(2,1)}) %reduce-scatter.3.cloned.1.call-update) | async-done | bytes 262160 | tf_op jit(solution)/shard_map/reduce_scatter | solution.py:169
  90.4 1.7 fusion.54
  92.2 13.4 %all-gather = s32[512,8]{0,1:T(8,128)S(1)} all-gather(s32[128,8]{0,1:T(8,128)S(1)} %copy-done.10), channel_id=2, replica_groups=mesh['grp'=2,'ep'=4,'tp'=4] {'ep'}, dimensions={0}, use_global_device_ids=true | all-gather | bytes 20480 | tf_op jit(solution)/shard_map/all_gather | solution.py:141
  106.4 12.5 %all-gather.5.cloned.1.call-done = bf16[512,1024]{1,0:T(8,128)(2,1)} async-done(((bf16[128,1024]{1,0:T(8,128)(2,1)}), bf16[512,1024]{1,0:T(8,128)(2,1)}) %all-gather.5.cloned.1.call-update) | async-done | bytes 1048592 | tf_op jit(solution)/shard_map/all_gather | solution.py:187
  118.9 1.5 fusion.10
  121.0 18.0 %convert_bitcast_fusion = bf16[4,4,64,2,1024]{4,2,3,0,1:T(8,128)(2,1)} fusion(bf16[4,1024,2,1024,1]{3,2,1,0,4:T(2,128)(2,1)} %bitcast.181, bf16[4,128,1024]{2,1,0:T(8,128)(2,1)S(1)} %gather_fusion.6, pred[4]{0:T(512)(128)(4,1)S(1)} %get-tuple-element.22, s32[4,4,128]{2,1,0:T(4,128)S(1)} %convolution_convert_fusion.1, pred[4,4,128]{2,1,0:T(4,128)(4,1)S(1)} %fusion.109), kind=kOutput, calls=%fused_computation.17 | convolution fusion | flops 4567334912 | bytes 22030340 | tf_op jit(solution)/shard_map/serd,edgh->sergh/dot_general | solution.py:237
  139.0 5.0 %fusion.111 = (bf16[2,4,64,2,1024]{4,2,3,0,1:T(8,128)(2,1)S(1)}, f32[2,4,64,2,1024]{4,2,3,0,1:T(8,128)}) fusion(bf16[4,4,64,2,1024]{4,2,3,0,1:T(8,128)(2,1)} %convert_bitcast_fusion), kind=kLoop, calls=%fused_computation.183 | loop fusion | flops 1048576 | bytes 10485760 | tf_op jit(solution)/shard_map/slice | solution.py:110
  144.0 3.5 %copy.123 = bf16[2,4,64,2,1024]{4,3,2,1,0:T(2,128)(2,1)} copy(bf16[2,4,64,2,1024]{4,2,3,0,1:T(8,128)(2,1)S(1)} %get-tuple-element.26) | data formatting | bytes 4194304 | tf_op jit(solution)/shard_map/slice | solution.py:110
  147.5 4.5 %slice.108 = bf16[2,256,2048]{2,1,0:T(8,128)(2,1)} reshape(bf16[2,4,64,2,1024]{4,3,2,1,0:T(2,128)(2,1)} %copy.123) | data formatting | bytes 4194304 | tf_op jit(solution)/shard_map/slice | solution.py:110
  152.0 7.4 %copy.122 = f32[2,4,64,2,1024]{4,3,2,1,0:T(2,128)} copy(f32[2,4,64,2,1024]{4,2,3,0,1:T(8,128)} %get-tuple-element.27) | data formatting | bytes 8388608 | tf_op jit(solution)/shard_map/convert_element_type | solution.py:110
  159.4 6.7 %reshape.331 = f32[2,256,2048]{2,1,0:T(8,128)} reshape(f32[2,4,64,2,1024]{4,3,2,1,0:T(2,128)} %copy.122) | data formatting | bytes 8388608 | tf_op jit(solution)/shard_map/convert_element_type | solution.py:110
  167.6 3.5 %convert_add_fusion = f32[2,256,2048]{2,1,0:T(8,128)S(1)} fusion(f32[2,256,2048]{2,1,0:T(8,128)} %reshape.331, bf16[2,256,2048]{2,1,0:T(8,128)(2,1)} %collective-permute-done.3), kind=kLoop, calls=%fused_computation.16 | loop fusion | flops 2097152 | bytes 10485760 | tf_op jit(solution)/shard_map/add | solution.py:110
  171.1 1.9 copy-done.4
  173.1 1.5 collective-permute-start.4
  174.7 26.0 %all-gather.2 = f32[16,128,17]{1,2,0:T(8,128)S(1)} all-gather(f32[4,128,17]{1,2,0:T(8,128)S(1)} %pad_maximum_fusion.4), channel_id=4, replica_groups=mesh['grp'=2,'ep'=4,'tp'=4] {'tp'}, dimensions={0}, use_global_device_ids=true | all-gather | bytes 174080 | tf_op jit(solution)/shard_map/all_gather | solution.py:196
  202.5 1.8 fusion.17
  204.7 1.5 collective-permute-start.5
  206.5 12.4 %collective-permute-done.5 = bf16[256,1024]{1,0:T(8,128)(2,1)S(1)} collective-permute-done((bf16[256,1024]{1,0:T(8,128)(2,1)S(1)}, bf16[256,1024]{1,0:T(8,128)(2,1)S(1)}, u32[]{:S(2)}, u32[]{:S(2)}) %collective-permute-start.5) | collective-permute-done | bytes 524320 | tf_op jit(solution)/shard_map/ppermute | solution.py:105
  219.1 2.6 collective-permute-done.6
  221.7 5.7 %fusion.6 = bf16[4,4,64,1024]{3,2,1,0:T(8,128)(2,1)S(1)} fusion(bf16[4,1024,1024]{2,1,0:T(8,128)(2,1)} %param.30, bf16[2,4,64,1024]{3,2,1,0:T(8,128)(2,1)S(1)} %bitcast.182, bf16[1,4,64,1024]{3,2,1,0:T(8,128)(2,1)S(1)} %bitcast.170, bf16[1,4,64,1024]{3,2,1,0:T(8,128)(2,1)S(1)} %bitcast.168, f32[4,4,64]{2,1,0:T(4,128)S(1)} %get-tuple-element.18), kind=kOutput, calls=%fused_computation.15 | convolution fusion | flops 2151677952 | bytes 12587008 | tf_op jit(solution)/shard_map/serh,ehd->serd/dot_general | solution.py:256
  228.0 1.6 gather_fusion.7
  229.6 2.4 broadcast_select_fusion
  232.0 26.8 %reduce-scatter.5.cloned.1.call-done = bf16[1,128,1024]{2,1,0:T(8,128)(2,1)} async-done(((bf16[4,128,1024]{2,1,0:T(8,128)(2,1)}), bf16[1,128,1024]{2,1,0:T(8,128)(2,1)}) %reduce-scatter.5.cloned.1.call-update) | async-done | bytes 262160 | tf_op jit(solution)/shard_map/reduce_scatter | solution.py:263
  258.7 1.7 fusion.53
  (120 shorter events, 27.5 us)
Async XLA Ops:
  6.5 53.9 %copy-start = (bf16[1024,1024]{1,0:T(8,128)(2,1)S(1)}, bf16[1024,1024]{1,0:T(8,128)(2,1)}, u32[]{:S(2)}) copy-start(bf16[1024,1024]{1,0:T(8,128)(2,1)} %param.26) | copy-start | bytes 6291460
  6.5 16.7 %copy-start.3 = (s32[8]{0:T(128)S(1)}, s32[8]{0:T(128)}, u32[]{:S(2)}) copy-start(s32[8]{0:T(128)} %param.22) | copy-start | bytes 100
  12.0 22.7 %all-to-all-start = ((bf16[4,128,256]{1,2,0:T(8,128)(2,1)}), bf16[4,128,256]{1,2,0:T(8,128)(2,1)S(1)}, u32[]{:S(2)}, u32[]{:S(2)}) async-start(bf16[4,128,256]{1,2,0:T(8,128)(2,1)} %bitcast.10), calls=%async_computation | async-start | bytes 524288 | tf_op jit(solution)/shard_map/all_to_all | solution.py:93
  18.4 72.0 %reduce-scatter.3.cloned.1.call-start = ((), (), s32[]{:S(2)}) async-start(), calls=%async_computation.3 | async-start | bytes 1310720 | tf_op jit(solution)/shard_map/reduce_scatter | solution.py:169
  20.6 8.0 %collective-permute-start = (bf16[128,1280]{0,1:T(8,128)(2,1)S(1)}, bf16[128,1280]{0,1:T(8,128)(2,1)S(1)}, u32[]{:S(2)}, u32[]{:S(2)}) collective-permute-start(bf16[128,1280]{0,1:T(8,128)(2,1)S(1)} %pad_maximum_fusion.3), channel_id=1, source_target_pairs={{0,0},{1,4},{2,8},{3,12},{4,1},{5,5},{6,9},{7,13},{8,2},{9,6},{10,... | collective-permute-start | bytes 983048 | tf_op jit(solution)/shard_map/ppermute | solution.py:151
  22.6 8.3 %copy-start.11 = (f32[64]{0:T(128)}, f32[64]{0:T(128)S(1)}, u32[]{:S(2)}) copy-start(f32[64]{0:T(128)S(1)} %multiply_exponential_fusion) | copy-start | bytes 772
  36.1 2.2 copy-start.9
  38.4 15.6 %copy-start.13 = (s32[4]{0:T(128)S(1)}, s32[4]{0:T(128)}, u32[]{:S(2)}) copy-start(s32[4]{0:T(128)} %get-tuple-element.49) | copy-start | bytes 52
  38.4 15.6 %copy-start.2 = (s32[4]{0:T(128)S(1)}, s32[4]{0:T(128)}, u32[]{:S(2)}) copy-start(s32[4]{0:T(128)} %constant.201.clone) | copy-start | bytes 52
  39.3 19.0 %collective-permute-start.1 = (bf16[128,1024]{1,0:T(8,128)(2,1)S(1)}, bf16[128,1024]{1,0:T(8,128)(2,1)S(1)}, u32[]{:S(2)}, u32[]{:S(2)}) collective-permute-start(bf16[128,1024]{1,0:T(8,128)(2,1)S(1)} %copy.117), channel_id=1, source_target_pairs={{0,2},{1,3},{2,0},{3,1},{4,6},{5,7},{6,4},{7,5},{8,10},{9,11},{10,... | collective-permute-start | bytes 786440 | tf_op jit(solution)/shard_map/ppermute | solution.py:105
  58.4 2.0 collective-permute-start.2
  61.7 28.6 %copy-start.7 = (bf16[128,1024]{1,0:T(8,128)(2,1)S(1)}, bf16[128,1024]{1,0:T(8,128)(2,1)}, u32[]{:S(2)}) copy-start(bf16[128,1024]{1,0:T(8,128)(2,1)} %param.25) | copy-start | bytes 786436
  62.4 29.8 %copy-start.12 = (bf16[1024]{0:T(1024)(128)(2,1)S(1)}, bf16[1024]{0:T(1024)(128)(2,1)}, u32[]{:S(2)}) copy-start(bf16[1024]{0:T(1024)(128)(2,1)} %param.27) | copy-start | bytes 6148
  62.4 29.8 %copy-start.10 = (s32[128,8]{0,1:T(8,128)S(1)}, s32[128,8]{0,1:T(8,128)}, u32[]{:S(2)}) copy-start(s32[128,8]{0,1:T(8,128)} %param.31) | copy-start | bytes 12292
  63.5 55.4 %all-gather.5.cloned.1.call-start = ((), (), s32[]{:S(2)}) async-start(), calls=%async_computation.5 | async-start | bytes 1310720 | tf_op jit(solution)/shard_map/all_gather | solution.py:187
  92.1 166.6 %reduce-scatter.5.cloned.1.call-start = ((), (), s32[]{:S(2)}) async-start(), calls=%async_computation.4 | async-start | bytes 1310720 | tf_op jit(solution)/shard_map/reduce_scatter | solution.py:263
  152.0 15.6 %collective-permute-start.3 = (bf16[2,256,2048]{2,1,0:T(8,128)(2,1)}, bf16[2,256,2048]{2,1,0:T(8,128)(2,1)}, u32[]{:S(2)}, u32[]{:S(2)}) collective-permute-start(bf16[2,256,2048]{2,1,0:T(8,128)(2,1)} %slice.108), channel_id=1, source_target_pairs={{0,1},{1,0},{2,3},{3,2},{4,5},{5,4},{6,7},{7,6},{8,9},{9,8},{10,11... | collective-permute-start | bytes 6291464 | tf_op jit(solution)/shard_map/ppermute | solution.py:110
  159.4 6.7 %copy-start.5 = (bf16[512,1024]{1,0:T(8,128)(2,1)S(1)}, bf16[512,1024]{1,0:T(8,128)(2,1)}, u32[]{:S(2)}) copy-start(bf16[512,1024]{1,0:T(8,128)(2,1)} %all-gather.5.cloned.1.call-done) | copy-start | bytes 3145732
  159.4 7.0 %copy-start.8 = (bf16[1024,16]{0,1:T(8,128)(2,1)S(1)}, bf16[1024,16]{0,1:T(8,128)(2,1)}, u32[]{:S(2)}) copy-start(bf16[1024,16]{0,1:T(8,128)(2,1)} %param.28) | copy-start | bytes 98308
  171.1 1.9 copy-start.4
  173.1 29.3 %collective-permute-start.4 = (bf16[256,2048]{1,0:T(8,128)(2,1)S(1)}, bf16[256,2048]{1,0:T(8,128)(2,1)S(1)}, u32[]{:S(2)}, u32[]{:S(2)}) collective-permute-start(bf16[256,2048]{1,0:T(8,128)(2,1)S(1)} %fusion.44), channel_id=1, source_target_pairs={{0,2},{1,3},{2,0},{3,1},{4,6},{5,7},{6,4},{7,5},{8,10},{9,11},{10,... | collective-permute-start | bytes 3145736 | tf_op jit(solution)/shard_map/ppermute | solution.py:113
  204.7 14.2 %collective-permute-start.5 = (bf16[256,1024]{1,0:T(8,128)(2,1)S(1)}, bf16[256,1024]{1,0:T(8,128)(2,1)S(1)}, u32[]{:S(2)}, u32[]{:S(2)}) collective-permute-start(bf16[256,1024]{1,0:T(8,128)(2,1)S(1)} %fusion.45), channel_id=1, source_target_pairs={{0,2},{1,3},{2,0},{3,1},{4,6},{5,7},{6,4},{7,5},{8,10},{9,11},{10,... | collective-permute-start | bytes 1572872 | tf_op jit(solution)/shard_map/ppermute | solution.py:105
  219.0 2.7 %collective-permute-start.6 = (bf16[2,256,1024]{2,1,0:T(8,128)(2,1)S(1)}, bf16[2,256,1024]{2,1,0:T(8,128)(2,1)S(1)}, u32[]{:S(2)}, u32[]{:S(2)}) collective-permute-start(bf16[2,256,1024]{2,1,0:T(8,128)(2,1)S(1)} %pad_maximum_fusion.1), channel_id=1, source_target_pairs={{0,1},{1,0},{2,3},{3,2},{4,5},{5,4},{6,7},{7,6},{8,9},{9,8},{10,11... | collective-permute-start | bytes 3145736 | tf_op jit(solution)/shard_map/ppermute | solution.py:106
  227.5 33.0 %copy-start.1 = (bf16[1024,1024]{1,0:T(8,128)(2,1)S(1)}, bf16[1024,1024]{1,0:T(8,128)(2,1)}, u32[]{:S(2)}) copy-start(bf16[1024,1024]{1,0:T(8,128)(2,1)} %param.26) | copy-start | bytes 6291460
  228.0 30.7 %copy-start.6 = (bf16[128,1024]{1,0:T(8,128)(2,1)S(1)}, bf16[128,1024]{1,0:T(8,128)(2,1)}, u32[]{:S(2)}) copy-start(bf16[128,1024]{1,0:T(8,128)(2,1)} %fusion.54) | copy-start | bytes 786436
Sparse Core Ops, SparseCore 0:
  63.7 26.6 reduce-scatter.2
  92.2 26.6 all-gather.4
  232.1 26.5 reduce-scatter.4

commit v2 on v1

--- a/solution.py
+++ b/solution.py
@@ -3,6 +3,8 @@
 import jax
 import jax.numpy as jnp
 from jax import lax
+from jax.experimental import pallas as pl
+from jax.experimental.pallas import tpu as pltpu
 from jax.sharding import PartitionSpec as P
 
 rope_theta = 1000000.0
@@ -79,42 +81,7 @@
     return (jnp.take(received, my_docs // pool_dev, axis=0), starts[:docs_per], jnp.take(doc_lens, my_docs))
 
 
-def context_by_column(doc_kv, doc_lens, query_docs, ctx_pos, device, query):
-    pool_dev, doc_max, kv_heads, pair, head_dim = doc_kv.shape
-    docs_per = query_docs.shape[1]
-    my_docs = lax.dynamic_index_in_dim(query_docs, query, 0, keepdims=False)
-    starts = lax.dynamic_index_in_dim(ctx_pos, query, 0, keepdims=False)
-    held = device * pool_dev + jnp.arange(pool_dev, dtype=jnp.int32)
-    local = jnp.sum(
-        jnp.where(my_docs[:, None] == held[None, :], jnp.arange(pool_dev, dtype=jnp.int32)[None, :], 0)
-    )
-    block = lax.dynamic_index_in_dim(doc_kv, local, 0, keepdims=False)
-    sending = jnp.transpose(block, (1, 0, 2, 3)).reshape(kv_heads, doc_max, pair * head_dim)
-    received = lax.all_to_all(sending, "ep", split_axis=0, concat_axis=0, tiled=True)
-    owner = my_docs // pool_dev
-    here = owner[None, :] == jnp.arange(docs_per, dtype=jnp.int32)[:, None]
-    lengths = jnp.sum(jnp.where(here, jnp.take(doc_lens, my_docs)[None, :], 0), axis=1)
-    return (received, jnp.sum(jnp.where(here, starts[None, :docs_per], 0), axis=1), lengths)
-
-
-def pairs(lanes, flip):
-    return [(i, i ^ flip) for i in range(lanes)]
-
-
-def gather_lanes(mine, lanes):
-    across = jnp.stack([mine, lax.ppermute(mine, "tp", pairs(lanes, 2))])
-    return jnp.concatenate([across, lax.ppermute(across, "tp", pairs(lanes, 1))])
-
-
-def scatter_lanes(parts, lanes):
-    chip = parts[:2].astype(jnp.float32) + lax.ppermute(parts[2:], "tp", pairs(lanes, 1)).astype(
-        jnp.float32
-    )
-    away = lax.ppermute(chip[1].astype(jnp.bfloat16), "tp", pairs(lanes, 2))
-    return chip[0] + away.astype(jnp.float32)
-
-
-def per_device(
+def per_device_general(
     question_q,
     question_kv,
     doc_kv,
@@ -137,51 +104,21 @@
     kv_heads = question_kv.shape[1]
     docs_per = query_docs.shape[1]
     width_here = hidden.shape[1]
-    square = lanes == 4 and groups == 4 and kv_heads == 4 and docs_per == groups
     ids = lax.all_gather(expert_ids, "ep", axis=0, tiled=False)
-    order = lane ^ jnp.array([0, 2, 1, 3], jnp.int32) if square else None
-
-    if square:
-        kv_head = lax.dynamic_index_in_dim(question_kv, lane, 1, keepdims=False).reshape(
-            length, 2 * head_dim
-        )
-        outgoing = jnp.concatenate(
-            [question_q.reshape(length, heads_here * head_dim), kv_head], axis=1
-        )
-        turned = lax.ppermute(
-            outgoing,
-            ("ep", "tp"),
-            [(e * lanes + t, t * lanes + e) for e in range(groups) for t in range(lanes)],
-        )
-        context, starts, lengths = context_by_column(
-            doc_kv, doc_lens, query_docs, ctx_pos, device, lane
-        )
-        question_start = lax.dynamic_index_in_dim(ctx_pos, lane, 0, keepdims=False)[docs_per]
-        q_rows = turned[:, : heads_here * head_dim].reshape(length, heads_here, head_dim)
-        attended = attend(
-            q_rows, turned[:, heads_here * head_dim :], context, starts, lengths, question_start
-        )
-        all_queries = gather_lanes(attended, lanes).reshape(lanes * length, -1)
-        partial = jnp.dot(all_queries, out_proj, preferred_element_type=jnp.float32)
-        partial = partial.astype(jnp.bfloat16).reshape(lanes, length, width_here)
-        slot_of = jnp.array([0, 2, 1, 3], jnp.int32)[lane ^ jnp.arange(lanes, dtype=jnp.int32)]
-        partial = jnp.take(partial, slot_of, axis=0)
-        projected = lax.psum_scatter(partial, "ep", scatter_dimension=0, tiled=True)[0]
-    else:
-        kv_pick = lane * kv_heads // lanes
-        kv_head = lax.dynamic_index_in_dim(question_kv, kv_pick, 1, keepdims=False).reshape(
-            length, 2 * head_dim
-        )
-        context, starts, lengths = context_by_row(
-            doc_kv, doc_lens, query_docs, ctx_pos, device, kv_pick
-        )
-        question_start = lax.dynamic_index_in_dim(ctx_pos, device, 0, keepdims=False)[docs_per]
-        attended = attend(question_q, kv_head, context, starts, lengths, question_start)
-        projected = jnp.dot(
-            lax.all_gather(attended, "tp", axis=1, tiled=True),
-            lax.all_gather(out_proj, "ep", axis=0, tiled=True),
-            preferred_element_type=jnp.float32,
-        )
+    kv_pick = lane * kv_heads // lanes
+    kv_head = lax.dynamic_index_in_dim(question_kv, kv_pick, 1, keepdims=False).reshape(
+        length, 2 * head_dim
+    )
+    context, starts, lengths = context_by_row(
+        doc_kv, doc_lens, query_docs, ctx_pos, device, kv_pick
+    )
+    question_start = lax.dynamic_index_in_dim(ctx_pos, device, 0, keepdims=False)[docs_per]
+    attended = attend(question_q, kv_head, context, starts, lengths, question_start)
+    projected = jnp.dot(
+        lax.all_gather(attended, "tp", axis=1, tiled=True),
+        lax.all_gather(out_proj, "ep", axis=0, tiled=True),
+        preferred_element_type=jnp.float32,
+    )
     residual = (hidden.astype(jnp.float32) + projected.astype(jnp.float32)).astype(jnp.bfloat16)
 
     tokens = lax.all_gather(residual, "ep", axis=0, tiled=False)
@@ -209,13 +146,7 @@
     weight = jnp.where(chosen_all, jnp.exp(logits - top), 0.0)
     mix = weight / jnp.sum(weight, axis=2, keepdims=True)
 
-    if square:
-        shuffled = jnp.take(chosen_all, order, axis=0)
-        scaled_rows = jnp.take(scaled.astype(jnp.bfloat16), order, axis=0)
-        inv_rms = jnp.take(inv_rms, order, axis=0)
-        mix = jnp.take(mix, order, axis=0)
-    else:
-        shuffled, scaled_rows = (chosen_all, scaled.astype(jnp.bfloat16))
+    shuffled, scaled_rows = (chosen_all, scaled.astype(jnp.bfloat16))
     first = device * local_experts
     chosen = lax.dynamic_slice_in_dim(shuffled, first, local_experts, 2)
     mix_here = lax.dynamic_slice_in_dim(mix, first, local_experts, 2)
@@ -240,28 +171,419 @@
     per_lane = groups * local_experts * capacity // lanes
     term = term.reshape(lanes, per_lane, 2 * hid)
     inv_row = inv_row.reshape(lanes, per_lane, 1)
-    if square:
-        summed = scatter_lanes(term, lanes)
-        inv_mine = inv_row[0]
-    else:
-        summed = lax.psum_scatter(term, "tp", scatter_dimension=0, tiled=True)[0].astype(jnp.float32)
-        inv_mine = lax.dynamic_index_in_dim(inv_row, lane, 0, keepdims=False)
+    summed = lax.psum_scatter(term, "tp", scatter_dimension=0, tiled=True)[0].astype(jnp.float32)
+    inv_mine = lax.dynamic_index_in_dim(inv_row, lane, 0, keepdims=False)
     summed = summed * inv_mine
     act = (jax.nn.silu(summed[:, :hid]) * summed[:, hid:]).astype(jnp.bfloat16)
-    if square:
-        acts = gather_lanes(act, lanes)
-    else:
-        acts = lax.all_gather(act, "tp", axis=0, tiled=False)
+    acts = lax.all_gather(act, "tp", axis=0, tiled=False)
     acts = acts.reshape(groups, local_experts, capacity, hid)
     expert_out = jnp.einsum("serh,ehd->serd", acts, w_down, preferred_element_type=jnp.float32)
     expert_out = (expert_out * mix_row[:, :, :, None]).astype(jnp.bfloat16)
     combined = jnp.einsum(
         "sern,serd->snd", onehot, expert_out, preferred_element_type=jnp.float32
     ).astype(jnp.bfloat16)
-    if square:
-        combined = jnp.take(combined, slot_of, axis=0)
     returned = lax.psum_scatter(combined, "ep", scatter_dimension=0, tiled=True)[0]
     return (residual.astype(jnp.float32) + returned.astype(jnp.float32)).astype(jnp.bfloat16)
+
+
+def pairs(lanes, flip):
+    return [(i, i ^ flip) for i in range(lanes)]
+
+
+def chain_scatter(parts, axis):
+    n = len(parts)
+    right = left = None
+    for k in range(n - 1):
+        send_right, send_left = (parts[n - 1 - k], parts[k + 1])
+        if k:
+            send_right = send_right + right
+            send_left = send_left + left
+        right = lax.ppermute(send_right, axis, [(i, i + 1) for i in range(k + 1)])
+        left = lax.ppermute(send_left, axis, [(i, i - 1) for i in range(n - 1 - k, n)])
+    return (parts[0], right, left)
+
+
+def chain_gather(mine, axis, n):
+    right, left = ([], [])
+    for k in range(n - 1):
+        right.append(
+            lax.ppermute(right[-1] if k else mine, axis, [(i, i + 1) for i in range(k, n - 1)])
+        )
+        left.append(
+            lax.ppermute(left[-1] if k else mine, axis, [(i, i - 1) for i in range(1, n - k)])
+        )
+    return (right, left)
+
+
+def query_of(device, lane):
+    return 2 * (lane & 1) + ((lane >> 1) ^ (device & 1))
+
+
+def turn(values, groups, lanes):
+    moves = [
+        (e * lanes + t, t * lanes + 2 * ((e ^ t) & 1) + (e >> 1))
+        for e in range(groups)
+        for t in range(lanes)
+    ]
+    return lax.ppermute(values, ("ep", "tp"), moves)
+
+
+def call(body, outs, scratch, flops, moved, **kwargs):
+    return pl.pallas_call(
+        body,
+        out_shape=outs,
+        scratch_shapes=scratch,
+        compiler_params=pltpu.CompilerParams(vmem_limit_bytes=40 * 1024 * 1024),
+        cost_estimate=pl.CostEstimate(flops=flops, bytes_accessed=moved, transcendentals=0),
+        **kwargs,
+    )
+
+
+VMEM = pl.BlockSpec(memory_space=pltpu.VMEM)
+SMEM = pl.BlockSpec(memory_space=pltpu.SMEM)
+NT = (((1,), (1,)), ((), ()))
+
+
+def dot(a, b):
+    return jnp.dot(a, b, preferred_element_type=jnp.float32)
+
+
+def attention_body(lens, q, own, ctx, cos_q, sin_q, cos_d, sin_d, out, wide, keys, vals):
+    length, head_dim = cos_q.shape
+    heads = out.shape[1] // head_dim
+    docs, doc_max, _ = ctx.shape
+    half = head_dim // 2
+
+    def turned(x, cosine, sine):
+        return x * cosine + pltpu.roll(x, half, 1) * sine
+
+    cosine, sine = (cos_q[...], sin_q[...])
+    for j in range(docs):
+        key = turned(
+            ctx[j, :, :head_dim].astype(jnp.float32), cos_d[j : j + 1, :], sin_d[j : j + 1, :]
+        )
+        keys[j * doc_max : (j + 1) * doc_max, :] = key.astype(jnp.bfloat16)
+        vals[j * doc_max : (j + 1) * doc_max, :] = ctx[j, :, head_dim:]
+    base = docs * doc_max
+    keys[base:, :] = turned(own[:, :head_dim].astype(jnp.float32), cosine, sine).astype(
+        jnp.bfloat16
+    )
+    vals[base:, :] = own[:, head_dim:]
+    wide[...] = q[...].astype(jnp.float32)
+    column = lax.broadcasted_iota(jnp.int32, (1, doc_max), 1)
+    allowed = [column < lens[j] for j in range(docs)]
+    causal = lax.broadcasted_iota(jnp.int32, (length, length), 0) >= lax.broadcasted_iota(
+        jnp.int32, (length, length), 1
+    )
+    for h in range(heads):
+        query = turned(wide[pl.ds(h, length, stride=heads), :], cosine, sine).astype(jnp.bfloat16)
+        scores = lax.dot_general(query, keys[...], NT, preferred_element_type=jnp.float32)
+        scores = scores * head_dim ** (-0.5)
+        parts = [
+            jnp.where(allowed[j], scores[:, j * doc_max : (j + 1) * doc_max], -jnp.inf)
+            for j in range(docs)
+        ] + [jnp.where(causal, scores[:, base:], -jnp.inf)]
+        scores = jnp.concatenate(parts, axis=1)
+        ceiling = jnp.max(scores, axis=1, keepdims=True)
+        probs = jnp.exp(scores - ceiling)
+        denominator = jnp.sum(probs, axis=1, keepdims=True)
+        mixed = dot(probs.astype(jnp.bfloat16), vals[...])
+        out[:, h * head_dim : (h + 1) * head_dim] = (mixed / denominator).astype(jnp.bfloat16)
+
+
+def attention(lens, q, own, ctx, tables_q, tables_d):
+    length, head_dim = tables_q[0].shape
+    heads = q.shape[0] // length
+    rows = ctx.shape[0] * ctx.shape[1] + length
+    return call(
+        attention_body,
+        jax.ShapeDtypeStruct((length, heads * head_dim), jnp.bfloat16),
+        [
+            pltpu.VMEM(q.shape, jnp.float32),
+            pltpu.VMEM((rows, head_dim), jnp.bfloat16),
+            pltpu.VMEM((rows, head_dim), jnp.bfloat16),
+        ],
+        4 * heads * length * rows * head_dim * 4,
+        4 * 1024 * 1024,
+        in_specs=[SMEM] + [VMEM] * 7,
+        out_specs=VMEM,
+        name="attention",
+    )(lens, q, own, ctx, *tables_q, *tables_d)
+
+
+def project_body(place, a, b, c, d, weight, *rest):
+    outs, rows = (rest[:-1], rest[-1])
+    for j, ref in enumerate((a, b, c, d)):
+        rows[place[j]] = ref[...]
+    for m, out in enumerate(outs):
+        out[...] = dot(rows[m], weight[...]).astype(jnp.bfloat16)
+
+
+def project(place, parts, weight):
+    length, depth = parts[0].shape
+    shape = jax.ShapeDtypeStruct((length, weight.shape[1]), jnp.bfloat16)
+    return call(
+        project_body,
+        [shape] * 4,
+        [pltpu.VMEM((4, length, depth), jnp.bfloat16)],
+        2 * 4 * length * depth * weight.shape[1],
+        4 * 1024 * 1024,
+        in_specs=[SMEM] + [VMEM] * 5,
+        out_specs=[VMEM] * 4,
+        name="project",
+    )(place, *parts, weight)
+
+
+def assemble_body(mine, a0, a1, a2, b0, b1, b2, gain, router, scaled, stats):
+    length = mine.shape[0]
+    experts = router.shape[0]
+    blocks = (mine[...], a2[...] + b0[...], a1[...] + b1[...], a0[...] + b2[...])
+    ones = jnp.ones((8, mine.shape[1]), jnp.float32)
+    for m, block in enumerate(blocks):
+        wide = block.astype(jnp.float32)
+        grown = wide * gain[...]
+        scaled[m] = grown.astype(jnp.bfloat16)
+        here = slice(m * length, (m + 1) * length)
+        stats[:experts, here] = lax.dot_general(
+            router[...], grown, NT, preferred_element_type=jnp.float32,
+            precision=lax.Precision.HIGHEST,
+        )
+        stats[experts:, here] = lax.dot_general(
+            ones, wide * wide, NT, preferred_element_type=jnp.float32,
+            precision=lax.Precision.HIGHEST,
+        )
+
+
+def assemble(mine, right, left, gain, router):
+    length, width = mine.shape
+    return call(
+        assemble_body,
+        [
+            jax.ShapeDtypeStruct((4, length, width), jnp.bfloat16),
+            jax.ShapeDtypeStruct((router.shape[0] + 8, 4 * length), jnp.float32),
+        ],
+        [],
+        2 * 4 * length * width * 256,
+        3 * 1024 * 1024,
+        in_specs=[VMEM] * 9,
+        out_specs=[VMEM] * 2,
+        name="assemble",
+    )(mine, *right, *left, gain, router)
+
+
+def gate_up_body(order, tokens, pick, weight, *rest):
+    outs, rows = (rest[:-1], rest[-1])
+    local = rows.shape[0]
+    capacity = pick.shape[1] // local
+    hid = weight.shape[3]
+
+    @pl.when(pl.program_id(0) == 0)
+    def _():
+        for j in range(4):
+            m = order[j]
+            chosen = dot(pick[m], tokens[m]).astype(jnp.bfloat16)
+            for e in range(local):
+                rows[e, j * capacity : (j + 1) * capacity, :] = chosen[
+                    e * capacity : (e + 1) * capacity, :
+                ]
+
+    mine = rows[pl.program_id(0)]
+    for g in range(2):
+        term = dot(mine, weight[0, g]).astype(jnp.bfloat16)
+        for j, out in enumerate(outs):
+            out[0, :, g * hid : (g + 1) * hid] = term[j * capacity : (j + 1) * capacity, :]
+
+
+def gate_up(order, tokens, pick, weight):
+    local, _, width, hid = weight.shape
+    capacity = pick.shape[1] // local
+    shape = jax.ShapeDtypeStruct((local, capacity, 2 * hid), jnp.bfloat16)
+    return call(
+        gate_up_body,
+        [shape] * 4,
+        [pltpu.VMEM((local, 4 * capacity, width), jnp.bfloat16)],
+        2 * local * 4 * capacity * width * 2 * hid,
+        22 * 1024 * 1024,
+        grid=(local,),
+        in_specs=[SMEM, VMEM, VMEM, pl.BlockSpec((1, 2, width, hid), lambda i: (i, 0, 0, 0))],
+        out_specs=[pl.BlockSpec((1, capacity, 2 * hid), lambda i: (i, 0, 0))] * 4,
+        name="gate_up",
+    )(order, tokens, pick, weight)
+
+
+def down_body(order, a, b, c, d, spread, weight, *rest):
+    outs, results = (rest[:-1], rest[-1])
+    e = pl.program_id(0)
+    capacity = a.shape[1]
+    acts = jnp.concatenate([a[0], b[0], c[0], d[0]], axis=0)
+    result = dot(acts, weight[0]).astype(jnp.bfloat16)
+    start = pl.multiple_of(e * capacity, capacity)
+    for j in range(4):
+        results[order[j], pl.ds(start, capacity), :] = result[j * capacity : (j + 1) * capacity, :]
+
+    @pl.when(e == pl.num_programs(0) - 1)
+    def _():
+        for m, out in enumerate(outs):
+            out[...] = dot(spread[m], results[m]).astype(jnp.bfloat16)
+
+
+def down(order, acts, spread, weight):
+    local, hid, width = weight.shape
+    capacity = acts[0].shape[1]
+    length = spread.shape[1]
+    shape = jax.ShapeDtypeStruct((length, width), jnp.bfloat16)
+    block = pl.BlockSpec((1, capacity, hid), lambda i: (i, 0, 0))
+    return call(
+        down_body,
+        [shape] * 4,
+        [pltpu.VMEM((4, local * capacity, width), jnp.bfloat16)],
+        2 * local * 4 * capacity * width * hid,
+        10 * 1024 * 1024,
+        grid=(local,),
+        in_specs=[SMEM] + [block] * 4 + [VMEM, pl.BlockSpec((1, hid, width), lambda i: (i, 0, 0))],
+        out_specs=[VMEM] * 4,
+        name="down",
+    )(order, *acts, spread, weight)
+
+
+def signed_tables(positions, head_dim):
+    cosine, sine = tables(positions, head_dim)
+    return (
+        jnp.concatenate([cosine, cosine], axis=1),
+        jnp.concatenate([-sine, sine], axis=1),
+    )
+
+
+def per_device_square(
+    question_q,
+    question_kv,
+    doc_kv,
+    doc_lens,
+    query_docs,
+    ctx_pos,
+    hidden,
+    out_proj,
+    norm_gain,
+    router_weight,
+    w_gate_up,
+    w_down,
+    expert_ids,
+):
+    n = 4
+    lane = lax.axis_index("tp")
+    device = lax.axis_index("ep")
+    length, heads_here, head_dim = question_q.shape
+    pool_dev, doc_max, kv_heads, _, _ = doc_kv.shape
+    docs_per = query_docs.shape[1]
+    width_here = hidden.shape[1]
+    experts = router_weight.shape[1]
+    local = w_gate_up.shape[0]
+    capacity = length * expert_ids.shape[1] // experts
+    hid = w_gate_up.shape[3]
+    seats = jnp.arange(n, dtype=jnp.int32)
+
+    q_rows = turn(question_q.reshape(length * heads_here, head_dim), n, n)
+    kv_head = lax.dynamic_index_in_dim(question_kv, lane, 1, keepdims=False)
+    own = turn(kv_head.reshape(length, 2 * head_dim), n, n)
+
+    for_query = query_of(seats, lane)
+    docs_of = jnp.take(query_docs, for_query, axis=0)
+    held = device * pool_dev + jnp.arange(pool_dev, dtype=jnp.int32)
+    choice = jnp.any(docs_of[:, :, None] == held[None, None, :], axis=1)
+    sending = doc_kv[0]
+    for p in range(1, pool_dev):
+        sending = jnp.where(choice[None, :, p, None, None], doc_kv[p], sending)
+    sending = jnp.transpose(sending, (1, 0, 2, 3)).reshape(kv_heads, doc_max, 2 * head_dim)
+    context = lax.all_to_all(sending, "ep", split_axis=0, concat_axis=0, tiled=True)
+    ids = lax.all_gather(expert_ids, "ep", axis=0, tiled=False)
+
+    query = query_of(device, lane)
+    my_docs = lax.dynamic_index_in_dim(query_docs, query, 0, keepdims=False)
+    starts = lax.dynamic_index_in_dim(ctx_pos, query, 0, keepdims=False)
+    here = (my_docs // pool_dev)[None, :] == seats[:, None]
+    lengths = jnp.sum(jnp.where(here, jnp.take(doc_lens, my_docs)[None, :], 0), axis=1)
+    doc_starts = jnp.sum(jnp.where(here, starts[None, :docs_per], 0), axis=1)
+    tables_q = signed_tables(starts[docs_per] + jnp.arange(length, dtype=jnp.int32), head_dim)
+    tables_d = signed_tables(doc_starts, head_dim)
+
+    ids = jnp.take(ids, (device + seats) % n, axis=0)
+    named = device * local + jnp.arange(local, dtype=jnp.int32)
+    chosen = jnp.any(ids[:, None, :, :] == named[None, :, None, None], axis=3)
+    before = (jnp.arange(length)[:, None] < jnp.arange(length)[None, :]).astype(jnp.bfloat16)
+    rank = jnp.einsum(
+        "men,nk->mek", chosen.astype(jnp.bfloat16), before, preferred_element_type=jnp.float32
+    ).astype(jnp.int32)
+    picked = jnp.logical_and(
+        chosen[:, :, None, :],
+        rank[:, :, None, :] == jnp.arange(capacity, dtype=jnp.int32)[None, None, :, None],
+    ).reshape(n, local * capacity, length)
+    pick = picked.astype(jnp.bfloat16)
+    spread = jnp.transpose(pick, (0, 2, 1))
+    named_all = jnp.any(
+        ids[:, None, :, :] == jnp.arange(experts, dtype=jnp.int32)[None, :, None, None], axis=3
+    )
+    weight = jnp.transpose(w_gate_up, (0, 2, 1, 3))
+
+    attended = attention(lengths, q_rows, own, context, tables_q, tables_d)
+    far = lax.ppermute(attended, "tp", pairs(n, 2))
+    near = lax.ppermute(attended, "tp", pairs(n, 1))
+    farther = lax.ppermute(far, "tp", pairs(n, 1))
+    order = lane ^ jnp.array([0, 2, 1, 3], jnp.int32)
+    place = (query_of(device, order) - device) % n
+    parts = project(place, (attended, far, near, farther), out_proj)
+    mine, right, left = chain_scatter(parts, "ep")
+    residual = (
+        hidden.astype(jnp.float32)
+        + mine.astype(jnp.float32)
+        + (right.astype(jnp.float32) + left.astype(jnp.float32))
+    ).astype(jnp.bfloat16)
+
+    right, left = chain_gather(residual, "ep", n)
+    tokens, stats = assemble(
+        residual,
+        right,
+        left,
+        norm_gain.astype(jnp.float32)[None, :],
+        router_weight.T.astype(jnp.float32),
+    )
+    stats = stats + lax.ppermute(stats, "tp", pairs(n, 2))
+    stats = stats + lax.ppermute(stats, "tp", pairs(n, 1))
+
+    terms = gate_up(order, tokens, pick, weight)
+    for_far = lax.ppermute(terms[3], "tp", pairs(n, 1))
+    for_me = lax.ppermute(terms[2], "tp", pairs(n, 1))
+    chip_far = (terms[1].astype(jnp.float32) + for_far.astype(jnp.float32)).astype(jnp.bfloat16)
+    across = lax.ppermute(chip_far, "tp", pairs(n, 2))
+
+    stats = lax.dynamic_index_in_dim(stats.reshape(experts + 8, n, length), lane, 1, keepdims=False)
+    inv_rms = lax.rsqrt(stats[experts] / (width_here * n) + norm_eps)
+    logits = stats[:experts] * inv_rms[None, :]
+    named_mine = lax.dynamic_index_in_dim(named_all, lane, 0, keepdims=False)
+    top = jnp.max(jnp.where(named_mine, logits, -jnp.inf), axis=0, keepdims=True)
+    grown = jnp.where(named_mine, jnp.exp(logits - top), 0.0)
+    mix = grown / jnp.sum(grown, axis=0, keepdims=True)
+    mix = lax.dynamic_slice_in_dim(mix, device * local, local, 0)
+    picked_mine = lax.dynamic_index_in_dim(picked, lane, 0, keepdims=False).reshape(
+        local, capacity, length
+    )
+    inv_row = jnp.sum(jnp.where(picked_mine, inv_rms[None, None, :], 0.0), axis=2)[:, :, None]
+    mix_row = jnp.sum(jnp.where(picked_mine, mix[:, None, :], 0.0), axis=2)[:, :, None]
+
+    summed = (
+        terms[0].astype(jnp.float32) + for_me.astype(jnp.float32) + across.astype(jnp.float32)
+    ) * inv_row
+    act = jax.nn.silu(summed[:, :, :hid]) * summed[:, :, hid:] * mix_row
+    act = act.astype(jnp.bfloat16)
+    far = lax.ppermute(act, "tp", pairs(n, 2))
+    near = lax.ppermute(act, "tp", pairs(n, 1))
+    farther = lax.ppermute(far, "tp", pairs(n, 1))
+    parts = down(order, (act, far, near, farther), spread, w_down)
+    mine, right, left = chain_scatter(parts, "ep")
+    return (
+        residual.astype(jnp.float32)
+        + mine.astype(jnp.float32)
+        + (right.astype(jnp.float32) + left.astype(jnp.float32))
+    ).astype(jnp.bfloat16)
 
 
 def solution(mesh):
@@ -280,6 +602,15 @@
         P("ep", None, "tp"),
         P(("grp", "ep"), None),
     )
+    def per_device(*args):
+        square = (
+            lax.axis_size("tp") == 4
+            and lax.axis_size("ep") == 4
+            and args[1].shape[1] == 4
+            and args[4].shape == (4, 4)
+        )
+        return (per_device_square if square else per_device_general)(*args)
+
     return jax.shard_map(
         per_device, mesh=mesh, in_specs=placed, out_specs=P(("grp", "ep"), "tp"), check_vma=False
     )

time: 268 us -> 229 us (0.85)
  starting transfers between devices: 24.9 us -> 63.1 us
  matrix products: 29.3 us -> 0.14 us
  blocking collectives: 39.4 us -> 14.2 us
  Pallas kernels: 0 us -> 21.7 us
  other arithmetic: 31.9 us -> 10.5 us
  between operations: 15.6 us -> 0.63 us
  local copies, waits for them, and re-layouts: 39.4 us -> 25.8 us
  waiting for transfers between devices: 86.5 us -> 92.4 us
    ppermute x7 -> x31, waiting for transfers between devices: 20.4 us -> 81.1 us  [the longest x6 24.3 us: chain_scatter(): right = lax.ppermute(send_right, axis, [(i, i + 1) for i in range(k + 1)])]
    reduce_scatter x2 -> x0, waiting for transfers between devices: 53.5 us -> none  [the longest x1 26.8 us: per_device(): lax.psum_scatter(partial, 'ep', scatter_dimension=0, tiled=True)[0]]
    ppermute x7 -> x31, starting transfers between devices: 18.5 us -> 56.8 us  [the longest x6 26.9 us: chain_scatter(): right = lax.ppermute(send_right, axis, [(i, i + 1) for i in range(k + 1)])]
    dot_general x8 -> x1, matrix products: 29.3 us -> 0.14 us  [per_device_square(): jnp.einsum('men,nk->mek', chosen.astype(jnp.bfloat16), before, preferred_...]
    all_gather x2 -> x1, blocking collectives: 39.4 us -> 14.2 us  [per_device_square(): ids = lax.all_gather(expert_ids, 'ep', axis=0, tiled=False)]
    pallas_call x0 -> x5, Pallas kernels: none -> 21.7 us  [the longest x1 9.16 us: gate_up(): call(gate_up_body, [shape] * 4, [pltpu.VMEM((local, 4 * capacity, width),...]
    unnamed x31 -> x24, local copies, waits for them, and re-layouts: 4.51 us -> 20 us
    convert_element_type x6 -> x1, local copies, waits for them, and re-layouts: 14.5 us -> 0.17 us  [per_device_square(): pick = picked.astype(jnp.bfloat16)]
  transfers between devices with their start and end apart: 11 -> 32, of which waited for: 7 -> 17; matrix products, arithmetic and copies ran while one was open for 13% -> 11% of each run, Pallas kernels for 0% -> 0%
where the time goes in v2:
time: 229 us; the launch traced here: 228 us
  waiting for transfers between devices  92.4 us (40%)
  starting transfers between devices  63.1 us (28%)
  local copies, waits for them, and re-layouts  25.8 us (11%)
  Pallas kernels  21.7 us (9%)
  blocking collectives  14.2 us (6%)
  other arithmetic  10.5 us (5%)
    ppermute x6, starting transfers between devices, chain_scatter(): right = lax.ppermute(send_right, axis, [(i, i + 1) for i in range(k + 1)])  26.9 us
    ppermute x6, waiting for transfers between devices, chain_scatter(): right = lax.ppermute(send_right, axis, [(i, i + 1) for i in range(k + 1)])  24.3 us
    ppermute x1, waiting for transfers between devices, per_device_square(): across = lax.ppermute(chip_far, 'tp', pairs(n, 2))  22.1 us
    unnamed x24, local copies, waits for them, and re-layouts  20 us
    all_gather x1, blocking collectives, per_device_square(): ids = lax.all_gather(expert_ids, 'ep', axis=0, tiled=False)  14.2 us
    ppermute x1, waiting for transfers between devices, per_device_square(): far = lax.ppermute(act, 'tp', pairs(n, 2))  11.6 us
    all_to_all x1, waiting for transfers between devices, per_device_square(): lax.all_to_all(sending, 'ep', split_axis=0, concat_axis=0, tiled=True)  11.3 us
    pallas_call x1, Pallas kernels, gate_up(): call(gate_up_body, [shape] * 4, [pltpu.VMEM((local, 4 * capacity, width),...  9.16 us
  transfers between devices with their start and end apart: 32, of which 17 were waited for; matrix products, arithmetic and copies ran while one was open for 11% of the time, Pallas kernels for 0%

profile of v2, /device:TPU:0, one launch (start us, length us, event | category | flops | bytes accessed | tf_op | source)
XLA Modules:
  0.0 228.4 jit_solution(2772240060026200375)
XLA Ops:
  4.6 6.3 %all-to-all-start = ((bf16[4,128,256]{2,1,0:T(8,128)(2,1)}), bf16[4,128,256]{2,1,0:T(8,128)(2,1)S(1)}, u32[]{:S(2)}, u32[]{:S(2)}) async-start(bf16[4,128,256]{2,1,0:T(8,128)(2,1)} %copy.37), calls=%async_computation | async-start | bytes 524288 | tf_op jit(solution)/shard_map/all_to_all | solution.py:497
  16.6 11.3 %all-to-all-done.ctx = bf16[4,128,256]{2,1,0:T(8,128)(2,1)S(1)} async-done(((bf16[4,128,256]{2,1,0:T(8,128)(2,1)}), bf16[4,128,256]{2,1,0:T(8,128)(2,1)S(1)}, u32[]{:S(2)}, u32[]{:S(2)}) %all-to-all-start) | async-done | bytes 262176 | tf_op jit(solution)/shard_map/all_to_all | solution.py:497
  28.0 3.4 %attention.1.a = bf16[128,1024]{1,0:T(8,128)(2,1)S(1)} custom-call(s32[4]{0:T(128)S(1)} %get-tuple-element.36.lens, bf16[1024,128]{1,0:T(8,128)(2,1)S(1)} %collective-permute-done.q, bf16[128,256]{1,0:T(8,128)(2,1)S(1)} %collective-permute-done.1.own, bf16[4,128,256]{2,1,0:T(8,128)(2,1)S(1)} %all-to-all-done.ctx, f32[128,128]{1,0:T(8,128)S(1)} %get-tuple-element.57.cos_q, ...), custom_call_target="tpu_custom_call" | custom-call | flops 1342177280 | bytes 4194304 | tf_op jit(solution)/shard_map/attention/pallas_call | solution.py:298
  31.4 2.7 %collective-permute-start.2 = (bf16[128,1024]{1,0:T(8,128)(2,1)S(1)}, bf16[128,1024]{1,0:T(8,128)(2,1)S(1)}, u32[]{:S(2)}, u32[]{:S(2)}) collective-permute-start(bf16[128,1024]{1,0:T(8,128)(2,1)S(1)} %attention.1.a), channel_id=1, source_target_pairs={{0,2},{1,3},{2,0},{3,1},{4,6},{5,7},{6,4},{7,5},{8,10},{9,11},{10,... | collective-permute-start | bytes 786440 | tf_op jit(solution)/shard_map/ppermute | solution.py:528
  34.1 3.2 %collective-permute-start.3 = (bf16[128,1024]{1,0:T(8,128)(2,1)S(1)}, bf16[128,1024]{1,0:T(8,128)(2,1)S(1)}, u32[]{:S(2)}, u32[]{:S(2)}) collective-permute-start(bf16[128,1024]{1,0:T(8,128)(2,1)S(1)} %attention.1.a), channel_id=1, source_target_pairs={{0,1},{1,0},{2,3},{3,2},{4,5},{5,4},{6,7},{7,6},{8,9},{9,8},{10,11... | collective-permute-start | bytes 786440 | tf_op jit(solution)/shard_map/ppermute | solution.py:529
  38.4 4.0 %collective-permute-start.4 = (bf16[128,1024]{1,0:T(8,128)(2,1)S(1)}, bf16[128,1024]{1,0:T(8,128)(2,1)S(1)}, u32[]{:S(2)}, u32[]{:S(2)}) collective-permute-start(bf16[128,1024]{1,0:T(8,128)(2,1)S(1)} %collective-permute-done.2.b), channel_id=1, source_target_pairs={{0,1},{1,0},{2,3},{3,2},{4,5},{5,4},{6,7},{7,6},{8,9},{9,8},{10,11... | collective-permute-start | bytes 786440 | tf_op jit(solution)/shard_map/ppermute | solution.py:530
  45.5 4.6 %collective-permute-start.5 = (bf16[128,1024]{1,0:T(8,128)(2,1)S(1)}, bf16[128,1024]{1,0:T(8,128)(2,1)S(1)}, u32[]{:S(2)}, u32[]{:S(2)}) collective-permute-start(bf16[128,1024]{1,0:T(8,128)(2,1)S(1)} %get-tuple-element.22), channel_id=1, source_target_pairs={{0,4},{1,5},{2,6},{3,7},{16,20},{17,21},{18,22},{19,23}} | collective-permute-start | bytes 786440 | tf_op jit(solution)/shard_map/ppermute | solution.py:201
  50.8 5.1 %collective-permute-done.5 = bf16[128,1024]{1,0:T(8,128)(2,1)S(1)} collective-permute-done((bf16[128,1024]{1,0:T(8,128)(2,1)S(1)}, bf16[128,1024]{1,0:T(8,128)(2,1)S(1)}, u32[]{:S(2)}, u32[]{:S(2)}) %collective-permute-start.5) | collective-permute-done | bytes 262176 | tf_op jit(solution)/shard_map/ppermute | solution.py:201
  56.0 4.4 %collective-permute-start.6 = (bf16[128,1024]{1,0:T(8,128)(2,1)S(1)}, bf16[128,1024]{1,0:T(8,128)(2,1)S(1)}, u32[]{:S(2)}, u32[]{:S(2)}) collective-permute-start(bf16[128,1024]{1,0:T(8,128)(2,1)S(1)} %get-tuple-element.43), channel_id=1, source_target_pairs={{0,4},{4,8},{1,5},{5,9},{2,6},{6,10},{3,7},{7,11},{16,20},{20,24},... | collective-permute-start | bytes 786440 | tf_op jit(solution)/shard_map/ppermute | solution.py:201
  61.1 4.3 %collective-permute-done.6 = bf16[128,1024]{1,0:T(8,128)(2,1)S(1)} collective-permute-done((bf16[128,1024]{1,0:T(8,128)(2,1)S(1)}, bf16[128,1024]{1,0:T(8,128)(2,1)S(1)}, u32[]{:S(2)}, u32[]{:S(2)}) %collective-permute-start.6) | collective-permute-done | bytes 262176 | tf_op jit(solution)/shard_map/ppermute | solution.py:201
  65.5 4.4 %collective-permute-start.7 = (bf16[128,1024]{1,0:T(8,128)(2,1)S(1)}, bf16[128,1024]{1,0:T(8,128)(2,1)S(1)}, u32[]{:S(2)}, u32[]{:S(2)}) collective-permute-start(bf16[128,1024]{1,0:T(8,128)(2,1)S(1)} %add.250), channel_id=1, source_target_pairs={{0,4},{4,8},{8,12},{1,5},{5,9},{9,13},{2,6},{6,10},{10,14},{3,7},{... | collective-permute-start | bytes 786440 | tf_op jit(solution)/shard_map/ppermute | solution.py:201
  71.3 2.6 %collective-permute-done.7 = bf16[128,1024]{1,0:T(8,128)(2,1)S(1)} collective-permute-done((bf16[128,1024]{1,0:T(8,128)(2,1)S(1)}, bf16[128,1024]{1,0:T(8,128)(2,1)S(1)}, u32[]{:S(2)}, u32[]{:S(2)}) %collective-permute-start.7) | collective-permute-done | bytes 262176 | tf_op jit(solution)/shard_map/ppermute | solution.py:201
  74.0 4.3 %collective-permute-done.10 = bf16[128,1024]{1,0:T(8,128)(2,1)S(1)} collective-permute-done((bf16[128,1024]{1,0:T(8,128)(2,1)S(1)}, bf16[128,1024]{1,0:T(8,128)(2,1)S(1)}, u32[]{:S(2)}, u32[]{:S(2)}) %collective-permute-start.10) | collective-permute-done | bytes 262176 | tf_op jit(solution)/shard_map/ppermute | solution.py:202
  78.4 2.7 %collective-permute-start.11 = (bf16[128,1024]{1,0:T(8,128)(2,1)S(1)}, bf16[128,1024]{1,0:T(8,128)(2,1)S(1)}, u32[]{:S(2)}, u32[]{:S(2)}) collective-permute-start(bf16[128,1024]{1,0:T(8,128)(2,1)S(1)} %add_convert_fusion.2.mine), channel_id=1, source_target_pairs={{0,4},{4,8},{8,12},{1,5},{5,9},{9,13},{2,6},{6,10},{10,14},{3,7},{... | collective-permute-start | bytes 786440 | tf_op jit(solution)/shard_map/ppermute | solution.py:210
  82.5 14.2 %all-gather = s32[512,8]{0,1:T(8,128)S(1)} all-gather(s32[128,8]{0,1:T(8,128)S(1)} %copy-done.7), channel_id=2, replica_groups=mesh['grp'=2,'ep'=4,'tp'=4] {'ep'}, dimensions={0}, use_global_device_ids=true | all-gather | bytes 20480 | tf_op jit(solution)/shard_map/all_gather | solution.py:498
  100.8 8.4 %collective-permute-done.15.b1 = bf16[128,1024]{1,0:T(8,128)(2,1)S(1)} collective-permute-done((bf16[128,1024]{1,0:T(8,128)(2,1)S(1)}, bf16[128,1024]{1,0:T(8,128)(2,1)S(1)}, u32[]{:S(2)}, u32[]{:S(2)}) %collective-permute-start.15) | collective-permute-done | bytes 262176 | tf_op jit(solution)/shard_map/ppermute | solution.py:213
  111.1 16.5 %copy.41 = bf16[4,1024,2,1024]{3,1,2,0:T(8,128)(2,1)} copy(bf16[4,1024,2,1024]{3,2,1,0:T(2,128)(2,1)} %param.24) | data formatting | bytes 33554432 | tf_op args[10]
  127.7 3.5 %assemble.1 = (bf16[4,128,1024]{2,1,0:T(8,128)(2,1)S(1)}, f32[24,512]{1,0:T(8,128)S(1)}) custom-call(bf16[128,1024]{1,0:T(8,128)(2,1)S(1)} %add_convert_fusion.2.mine, bf16[128,1024]{1,0:T(8,128)(2,1)S(1)} %collective-permute-done.11.a0, bf16[128,1024]{1,0:T(8,128)(2,1)S(1)} %collective-permute-done.12.a1, bf16[128,1024]{1,0:T(8,128)(2,1)S(1)} %collective-permute-done.13.a2, ...), custom_call_target="tpu_custom_call" | custom-call | flops 268435456 | bytes 3145728 | tf_op jit(solution)/shard_map/assemble/pallas_call | solution.py:359
  131.1 9.2 %gate_up.1 = (bf16[4,64,2048]{2,1,0:T(8,128)(2,1)S(1)}, bf16[4,64,2048]{2,1,0:T(8,128)(2,1)S(1)}, bf16[4,64,2048]{2,1,0:T(8,128)(2,1)S(1)}, bf16[4,64,2048]{2,1,0:T(8,128)(2,1)S(1)}) custom-call(s32[4]{0:T(128)S(1)} %get-tuple-element.54.order, bf16[4,128,1024]{2,1,0:T(8,128)(2,1)S(1)} %get-tuple-element.23.tokens, bf16[4,256,128]{2,1,0:T(8,128)(2,1)S(1)} %copy.35.pick, ...), custom_call_target="tpu_custom_call" | custom-call | flops 4294967296 | bytes 23068672 | tf_op jit(solution)/shard_map/gate_up/pallas_call | solution.py:401
  147.8 22.1 %collective-permute-done.19 = bf16[4,64,2048]{2,1,0:T(8,128)(2,1)} collective-permute-done((bf16[4,64,2048]{2,1,0:T(8,128)(2,1)}, bf16[4,64,2048]{2,1,0:T(8,128)(2,1)}, u32[]{:S(2)}, u32[]{:S(2)}) %collective-permute-start.19) | collective-permute-done | bytes 1048608 | tf_op jit(solution)/shard_map/ppermute | solution.py:556
  169.9 2.1 add_multiply_fusion
  173.9 11.6 %collective-permute-done.22.b = bf16[4,64,1024]{2,1,0:T(8,128)(2,1)S(1)} collective-permute-done((bf16[4,64,1024]{2,1,0:T(8,128)(2,1)S(1)}, bf16[4,64,1024]{2,1,0:T(8,128)(2,1)S(1)}, u32[]{:S(2)}, u32[]{:S(2)}) %collective-permute-start.22) | collective-permute-done | bytes 524320 | tf_op jit(solution)/shard_map/ppermute | solution.py:577
  185.5 1.9 collective-permute-done.24.d
  187.4 3.4 %copy-done.2 = bf16[4,1024,1024]{2,1,0:T(8,128)(2,1)S(1)} copy-done((bf16[4,1024,1024]{2,1,0:T(8,128)(2,1)S(1)}, bf16[4,1024,1024]{2,1,0:T(8,128)(2,1)}, u32[]{:S(2)}) %copy-start.2) | copy-done | bytes 8388632
  190.8 3.9 %down.1 = (bf16[128,1024]{1,0:T(8,128)(2,1)S(1)}, bf16[128,1024]{1,0:T(8,128)(2,1)S(1)}, bf16[128,1024]{1,0:T(8,128)(2,1)S(1)}, bf16[128,1024]{1,0:T(8,128)(2,1)S(1)}) custom-call(s32[4]{0:T(128)S(1)} %get-tuple-element.54.order, bf16[4,64,1024]{2,1,0:T(8,128)(2,1)S(1)} %fusion.1.a, bf16[4,64,1024]{2,1,0:T(8,128)(2,1)S(1)} %collective-permute-done.22.b, ...), custom_call_target="tpu_custom_call" | custom-call | flops 2147483648 | bytes 10485760 | tf_op jit(solution)/shard_map/down/pallas_call | solution.py:436
  194.7 4.6 %collective-permute-start.25 = (bf16[128,1024]{1,0:T(8,128)(2,1)S(1)}, bf16[128,1024]{1,0:T(8,128)(2,1)S(1)}, u32[]{:S(2)}, u32[]{:S(2)}) collective-permute-start(bf16[128,1024]{1,0:T(8,128)(2,1)S(1)} %get-tuple-element.32), channel_id=1, source_target_pairs={{0,4},{1,5},{2,6},{3,7},{16,20},{17,21},{18,22},{19,23}} | collective-permute-start | bytes 786440 | tf_op jit(solution)/shard_map/ppermute | solution.py:201
  200.0 5.2 %collective-permute-done.25 = bf16[128,1024]{1,0:T(8,128)(2,1)S(1)} collective-permute-done((bf16[128,1024]{1,0:T(8,128)(2,1)S(1)}, bf16[128,1024]{1,0:T(8,128)(2,1)S(1)}, u32[]{:S(2)}, u32[]{:S(2)}) %collective-permute-start.25) | collective-permute-done | bytes 262176 | tf_op jit(solution)/shard_map/ppermute | solution.py:201
  205.2 4.5 %collective-permute-start.26 = (bf16[128,1024]{1,0:T(8,128)(2,1)S(1)}, bf16[128,1024]{1,0:T(8,128)(2,1)S(1)}, u32[]{:S(2)}, u32[]{:S(2)}) collective-permute-start(bf16[128,1024]{1,0:T(8,128)(2,1)S(1)} %get-tuple-element.41), channel_id=1, source_target_pairs={{0,4},{4,8},{1,5},{5,9},{2,6},{6,10},{3,7},{7,11},{16,20},{20,24},... | collective-permute-start | bytes 786440 | tf_op jit(solution)/shard_map/ppermute | solution.py:201
  210.4 4.3 %collective-permute-done.26 = bf16[128,1024]{1,0:T(8,128)(2,1)S(1)} collective-permute-done((bf16[128,1024]{1,0:T(8,128)(2,1)S(1)}, bf16[128,1024]{1,0:T(8,128)(2,1)S(1)}, u32[]{:S(2)}, u32[]{:S(2)}) %collective-permute-start.26) | collective-permute-done | bytes 262176 | tf_op jit(solution)/shard_map/ppermute | solution.py:201
  214.8 4.4 %collective-permute-start.27 = (bf16[128,1024]{1,0:T(8,128)(2,1)S(1)}, bf16[128,1024]{1,0:T(8,128)(2,1)S(1)}, u32[]{:S(2)}, u32[]{:S(2)}) collective-permute-start(bf16[128,1024]{1,0:T(8,128)(2,1)S(1)} %add.274), channel_id=1, source_target_pairs={{0,4},{4,8},{8,12},{1,5},{5,9},{9,13},{2,6},{6,10},{10,14},{3,7},{... | collective-permute-start | bytes 786440 | tf_op jit(solution)/shard_map/ppermute | solution.py:201
  220.6 2.7 %collective-permute-done.27 = bf16[128,1024]{1,0:T(8,128)(2,1)S(1)} collective-permute-done((bf16[128,1024]{1,0:T(8,128)(2,1)S(1)}, bf16[128,1024]{1,0:T(8,128)(2,1)S(1)}, u32[]{:S(2)}, u32[]{:S(2)}) %collective-permute-start.27) | collective-permute-done | bytes 262176 | tf_op jit(solution)/shard_map/ppermute | solution.py:201
  223.3 4.3 %collective-permute-done.30 = bf16[128,1024]{1,0:T(8,128)(2,1)S(1)} collective-permute-done((bf16[128,1024]{1,0:T(8,128)(2,1)S(1)}, bf16[128,1024]{1,0:T(8,128)(2,1)S(1)}, u32[]{:S(2)}, u32[]{:S(2)}) %collective-permute-start.30) | collective-permute-done | bytes 262176 | tf_op jit(solution)/shard_map/ppermute | solution.py:202
  (134 shorter events, 37.8 us)
Async XLA Ops:
  4.6 23.3 %all-to-all-start = ((bf16[4,128,256]{2,1,0:T(8,128)(2,1)}), bf16[4,128,256]{2,1,0:T(8,128)(2,1)S(1)}, u32[]{:S(2)}, u32[]{:S(2)}) async-start(bf16[4,128,256]{2,1,0:T(8,128)(2,1)} %copy.37), calls=%async_computation | async-start | bytes 524288 | tf_op jit(solution)/shard_map/all_to_all | solution.py:497
  11.1 5.6 %collective-permute-start.1 = (bf16[128,256]{1,0:T(8,128)(2,1)S(1)}, bf16[128,256]{1,0:T(8,128)(2,1)S(1)}, u32[]{:S(2)}, u32[]{:S(2)}) collective-permute-start(bf16[128,256]{1,0:T(8,128)(2,1)S(1)} %bitcast.71), channel_id=1, source_target_pairs={{0,0},{1,6},{2,8},{3,14},{4,2},{5,4},{6,10},{7,12},{8,1},{9,7},{10... | collective-permute-start | bytes 196616 | tf_op jit(solution)/shard_map/ppermute | solution.py:228
  11.7 4.9 %collective-permute-start = (bf16[1024,128]{1,0:T(8,128)(2,1)S(1)}, bf16[1024,128]{1,0:T(8,128)(2,1)S(1)}, u32[]{:S(2)}, u32[]{:S(2)}) collective-permute-start(bf16[1024,128]{1,0:T(8,128)(2,1)S(1)} %bitcast.72), channel_id=1, source_target_pairs={{0,0},{1,6},{2,8},{3,14},{4,2},{5,4},{6,10},{7,12},{8,1},{9,7},{10... | collective-permute-start | bytes 786440 | tf_op jit(solution)/shard_map/ppermute | solution.py:228
  31.4 7.1 %collective-permute-start.2 = (bf16[128,1024]{1,0:T(8,128)(2,1)S(1)}, bf16[128,1024]{1,0:T(8,128)(2,1)S(1)}, u32[]{:S(2)}, u32[]{:S(2)}) collective-permute-start(bf16[128,1024]{1,0:T(8,128)(2,1)S(1)} %attention.1.a), channel_id=1, source_target_pairs={{0,2},{1,3},{2,0},{3,1},{4,6},{5,7},{6,4},{7,5},{8,10},{9,11},{10,... | collective-permute-start | bytes 786440 | tf_op jit(solution)/shard_map/ppermute | solution.py:528
  34.1 8.4 %collective-permute-start.3 = (bf16[128,1024]{1,0:T(8,128)(2,1)S(1)}, bf16[128,1024]{1,0:T(8,128)(2,1)S(1)}, u32[]{:S(2)}, u32[]{:S(2)}) collective-permute-start(bf16[128,1024]{1,0:T(8,128)(2,1)S(1)} %attention.1.a), channel_id=1, source_target_pairs={{0,1},{1,0},{2,3},{3,2},{4,5},{5,4},{6,7},{7,6},{8,9},{9,8},{10,11... | collective-permute-start | bytes 786440 | tf_op jit(solution)/shard_map/ppermute | solution.py:529
  38.4 5.2 %collective-permute-start.4 = (bf16[128,1024]{1,0:T(8,128)(2,1)S(1)}, bf16[128,1024]{1,0:T(8,128)(2,1)S(1)}, u32[]{:S(2)}, u32[]{:S(2)}) collective-permute-start(bf16[128,1024]{1,0:T(8,128)(2,1)S(1)} %collective-permute-done.2.b), channel_id=1, source_target_pairs={{0,1},{1,0},{2,3},{3,2},{4,5},{5,4},{6,7},{7,6},{8,9},{9,8},{10,11... | collective-permute-start | bytes 786440 | tf_op jit(solution)/shard_map/ppermute | solution.py:530
  45.5 10.5 %collective-permute-start.5 = (bf16[128,1024]{1,0:T(8,128)(2,1)S(1)}, bf16[128,1024]{1,0:T(8,128)(2,1)S(1)}, u32[]{:S(2)}, u32[]{:S(2)}) collective-permute-start(bf16[128,1024]{1,0:T(8,128)(2,1)S(1)} %get-tuple-element.22), channel_id=1, source_target_pairs={{0,4},{1,5},{2,6},{3,7},{16,20},{17,21},{18,22},{19,23}} | collective-permute-start | bytes 786440 | tf_op jit(solution)/shard_map/ppermute | solution.py:201
  50.1 5.8 %collective-permute-start.8 = (bf16[128,1024]{1,0:T(8,128)(2,1)S(1)}, bf16[128,1024]{1,0:T(8,128)(2,1)S(1)}, u32[]{:S(2)}, u32[]{:S(2)}) collective-permute-start(bf16[128,1024]{1,0:T(8,128)(2,1)S(1)} %get-tuple-element.20), channel_id=1, source_target_pairs={{12,8},{13,9},{14,10},{15,11},{28,24},{29,25},{30,26},{31,27}} | collective-permute-start | bytes 786440 | tf_op jit(solution)/shard_map/ppermute | solution.py:202
  56.0 9.4 %collective-permute-start.6 = (bf16[128,1024]{1,0:T(8,128)(2,1)S(1)}, bf16[128,1024]{1,0:T(8,128)(2,1)S(1)}, u32[]{:S(2)}, u32[]{:S(2)}) collective-permute-start(bf16[128,1024]{1,0:T(8,128)(2,1)S(1)} %get-tuple-element.43), channel_id=1, source_target_pairs={{0,4},{4,8},{1,5},{5,9},{2,6},{6,10},{3,7},{7,11},{16,20},{20,24},... | collective-permute-start | bytes 786440 | tf_op jit(solution)/shard_map/ppermute | solution.py:201
  60.4 9.5 %collective-permute-start.9 = (bf16[128,1024]{1,0:T(8,128)(2,1)S(1)}, bf16[128,1024]{1,0:T(8,128)(2,1)S(1)}, u32[]{:S(2)}, u32[]{:S(2)}) collective-permute-start(bf16[128,1024]{1,0:T(8,128)(2,1)S(1)} %get-tuple-element.44), channel_id=1, source_target_pairs={{8,4},{12,8},{9,5},{13,9},{10,6},{14,10},{11,7},{15,11},{24,20},{2... | collective-permute-start | bytes 786440 | tf_op jit(solution)/shard_map/ppermute | solution.py:202
  65.5 8.5 %collective-permute-start.7 = (bf16[128,1024]{1,0:T(8,128)(2,1)S(1)}, bf16[128,1024]{1,0:T(8,128)(2,1)S(1)}, u32[]{:S(2)}, u32[]{:S(2)}) collective-permute-start(bf16[128,1024]{1,0:T(8,128)(2,1)S(1)} %add.250), channel_id=1, source_target_pairs={{0,4},{4,8},{8,12},{1,5},{5,9},{9,13},{2,6},{6,10},{10,14},{3,7},{... | collective-permute-start | bytes 786440 | tf_op jit(solution)/shard_map/ppermute | solution.py:201
  70.0 8.3 %collective-permute-start.10 = (bf16[128,1024]{1,0:T(8,128)(2,1)S(1)}, bf16[128,1024]{1,0:T(8,128)(2,1)S(1)}, u32[]{:S(2)}, u32[]{:S(2)}) collective-permute-start(bf16[128,1024]{1,0:T(8,128)(2,1)S(1)} %add.252), channel_id=1, source_target_pairs={{4,0},{8,4},{12,8},{5,1},{9,5},{13,9},{6,2},{10,6},{14,10},{7,3},{... | collective-permute-start | bytes 786440 | tf_op jit(solution)/shard_map/ppermute | solution.py:202
  78.4 18.9 %collective-permute-start.11 = (bf16[128,1024]{1,0:T(8,128)(2,1)S(1)}, bf16[128,1024]{1,0:T(8,128)(2,1)S(1)}, u32[]{:S(2)}, u32[]{:S(2)}) collective-permute-start(bf16[128,1024]{1,0:T(8,128)(2,1)S(1)} %add_convert_fusion.2.mine), channel_id=1, source_target_pairs={{0,4},{4,8},{8,12},{1,5},{5,9},{9,13},{2,6},{6,10},{10,14},{3,7},{... | collective-permute-start | bytes 786440 | tf_op jit(solution)/shard_map/ppermute | solution.py:210
  81.2 16.8 %collective-permute-start.14 = (bf16[128,1024]{1,0:T(8,128)(2,1)S(1)}, bf16[128,1024]{1,0:T(8,128)(2,1)S(1)}, u32[]{:S(2)}, u32[]{:S(2)}) collective-permute-start(bf16[128,1024]{1,0:T(8,128)(2,1)S(1)} %add_convert_fusion.2.mine), channel_id=1, source_target_pairs={{4,0},{8,4},{12,8},{5,1},{9,5},{13,9},{6,2},{10,6},{14,10},{7,3},{... | collective-permute-start | bytes 786440 | tf_op jit(solution)/shard_map/ppermute | solution.py:213
  97.3 2.9 %collective-permute-start.12 = (bf16[128,1024]{1,0:T(8,128)(2,1)S(1)}, bf16[128,1024]{1,0:T(8,128)(2,1)S(1)}, u32[]{:S(2)}, u32[]{:S(2)}) collective-permute-start(bf16[128,1024]{1,0:T(8,128)(2,1)S(1)} %collective-permute-done.11.a0), channel_id=1, source_target_pairs={{4,8},{8,12},{5,9},{9,13},{6,10},{10,14},{7,11},{11,15},{20,24},{2... | collective-permute-start | bytes 786440 | tf_op jit(solution)/shard_map/ppermute | solution.py:210
  98.0 11.3 %collective-permute-start.15 = (bf16[128,1024]{1,0:T(8,128)(2,1)S(1)}, bf16[128,1024]{1,0:T(8,128)(2,1)S(1)}, u32[]{:S(2)}, u32[]{:S(2)}) collective-permute-start(bf16[128,1024]{1,0:T(8,128)(2,1)S(1)} %collective-permute-done.14.b0), channel_id=1, source_target_pairs={{4,0},{8,4},{5,1},{9,5},{6,2},{10,6},{7,3},{11,7},{20,16},{24,20},... | collective-permute-start | bytes 786440 | tf_op jit(solution)/shard_map/ppermute | solution.py:213
  100.2 27.5 %collective-permute-start.13 = (bf16[128,1024]{1,0:T(8,128)(2,1)S(1)}, bf16[128,1024]{1,0:T(8,128)(2,1)S(1)}, u32[]{:S(2)}, u32[]{:S(2)}) collective-permute-start(bf16[128,1024]{1,0:T(8,128)(2,1)S(1)} %collective-permute-done.12.a1), channel_id=1, source_target_pairs={{8,12},{9,13},{10,14},{11,15},{24,28},{25,29},{26,30},{27,31}} | collective-permute-start | bytes 786440 | tf_op jit(solution)/shard_map/ppermute | solution.py:210
  109.2 18.4 %collective-permute-start.16 = (bf16[128,1024]{1,0:T(8,128)(2,1)S(1)}, bf16[128,1024]{1,0:T(8,128)(2,1)S(1)}, u32[]{:S(2)}, u32[]{:S(2)}) collective-permute-start(bf16[128,1024]{1,0:T(8,128)(2,1)S(1)} %collective-permute-done.15.b1), channel_id=1, source_target_pairs={{4,0},{5,1},{6,2},{7,3},{20,16},{21,17},{22,18},{23,19}} | collective-permute-start | bytes 786440 | tf_op jit(solution)/shard_map/ppermute | solution.py:213
  140.3 2.7 %collective-permute-start.18 = (bf16[4,64,2048]{2,1,0:T(8,128)(2,1)S(1)}, bf16[4,64,2048]{2,1,0:T(8,128)(2,1)S(1)}, u32[]{:S(2)}, u32[]{:S(2)}) collective-permute-start(bf16[4,64,2048]{2,1,0:T(8,128)(2,1)S(1)} %get-tuple-element.27), channel_id=1, source_target_pairs={{0,1},{1,0},{2,3},{3,2},{4,5},{5,4},{6,7},{7,6},{8,9},{9,8},{10,11... | collective-permute-start | bytes 3145736 | tf_op jit(solution)/shard_map/ppermute | solution.py:553
  140.4 5.6 %collective-permute-start.20 = (f32[24,512]{1,0:T(8,128)S(1)}, f32[24,512]{1,0:T(8,128)S(1)}, u32[]{:S(2)}, u32[]{:S(2)}) collective-permute-start(f32[24,512]{1,0:T(8,128)S(1)} %get-tuple-element.28), channel_id=1, source_target_pairs={{0,2},{1,3},{2,0},{3,1},{4,6},{5,7},{6,4},{7,5},{8,10},{9,11},{10,... | collective-permute-start | bytes 147464 | tf_op jit(solution)/shard_map/ppermute | solution.py:549
  142.0 5.8 %collective-permute-start.17 = (bf16[4,64,2048]{2,1,0:T(8,128)(2,1)S(1)}, bf16[4,64,2048]{2,1,0:T(8,128)(2,1)}, u32[]{:S(2)}, u32[]{:S(2)}) collective-permute-start(bf16[4,64,2048]{2,1,0:T(8,128)(2,1)S(1)} %get-tuple-element.25), channel_id=1, source_target_pairs={{0,1},{1,0},{2,3},{3,2},{4,5},{5,4},{6,7},{7,6},{8,9},{9,8},{10,11... | collective-permute-start | bytes 3145736 | tf_op jit(solution)/shard_map/ppermute | solution.py:554
  144.4 25.5 %collective-permute-start.19 = (bf16[4,64,2048]{2,1,0:T(8,128)(2,1)}, bf16[4,64,2048]{2,1,0:T(8,128)(2,1)}, u32[]{:S(2)}, u32[]{:S(2)}) collective-permute-start(bf16[4,64,2048]{2,1,0:T(8,128)(2,1)} %add_convert_fusion), channel_id=1, source_target_pairs={{0,2},{1,3},{2,0},{3,1},{4,6},{5,7},{6,4},{7,5},{8,10},{9,11},{10,... | collective-permute-start | bytes 3145736 | tf_op jit(solution)/shard_map/ppermute | solution.py:556
  146.0 1.3 collective-permute-start.21
  172.3 13.2 %collective-permute-start.22 = (bf16[4,64,1024]{2,1,0:T(8,128)(2,1)S(1)}, bf16[4,64,1024]{2,1,0:T(8,128)(2,1)S(1)}, u32[]{:S(2)}, u32[]{:S(2)}) collective-permute-start(bf16[4,64,1024]{2,1,0:T(8,128)(2,1)S(1)} %fusion.1.a), channel_id=1, source_target_pairs={{0,2},{1,3},{2,0},{3,1},{4,6},{5,7},{6,4},{7,5},{8,10},{9,11},{10,... | collective-permute-start | bytes 1572872 | tf_op jit(solution)/shard_map/ppermute | solution.py:577
  173.9 11.6 %collective-permute-start.23 = (bf16[4,64,1024]{2,1,0:T(8,128)(2,1)S(1)}, bf16[4,64,1024]{2,1,0:T(8,128)(2,1)S(1)}, u32[]{:S(2)}, u32[]{:S(2)}) collective-permute-start(bf16[4,64,1024]{2,1,0:T(8,128)(2,1)S(1)} %fusion.1.a), channel_id=1, source_target_pairs={{0,1},{1,0},{2,3},{3,2},{4,5},{5,4},{6,7},{7,6},{8,9},{9,8},{10,11... | collective-permute-start | bytes 1572872 | tf_op jit(solution)/shard_map/ppermute | solution.py:578
  185.5 1.9 collective-permute-start.24
  194.7 10.4 %collective-permute-start.25 = (bf16[128,1024]{1,0:T(8,128)(2,1)S(1)}, bf16[128,1024]{1,0:T(8,128)(2,1)S(1)}, u32[]{:S(2)}, u32[]{:S(2)}) collective-permute-start(bf16[128,1024]{1,0:T(8,128)(2,1)S(1)} %get-tuple-element.32), channel_id=1, source_target_pairs={{0,4},{1,5},{2,6},{3,7},{16,20},{17,21},{18,22},{19,23}} | collective-permute-start | bytes 786440 | tf_op jit(solution)/shard_map/ppermute | solution.py:201
  199.3 5.8 %collective-permute-start.28 = (bf16[128,1024]{1,0:T(8,128)(2,1)S(1)}, bf16[128,1024]{1,0:T(8,128)(2,1)S(1)}, u32[]{:S(2)}, u32[]{:S(2)}) collective-permute-start(bf16[128,1024]{1,0:T(8,128)(2,1)S(1)} %get-tuple-element.30), channel_id=1, source_target_pairs={{12,8},{13,9},{14,10},{15,11},{28,24},{29,25},{30,26},{31,27}} | collective-permute-start | bytes 786440 | tf_op jit(solution)/shard_map/ppermute | solution.py:202
  205.2 9.6 %collective-permute-start.26 = (bf16[128,1024]{1,0:T(8,128)(2,1)S(1)}, bf16[128,1024]{1,0:T(8,128)(2,1)S(1)}, u32[]{:S(2)}, u32[]{:S(2)}) collective-permute-start(bf16[128,1024]{1,0:T(8,128)(2,1)S(1)} %get-tuple-element.41), channel_id=1, source_target_pairs={{0,4},{4,8},{1,5},{5,9},{2,6},{6,10},{3,7},{7,11},{16,20},{20,24},... | collective-permute-start | bytes 786440 | tf_op jit(solution)/shard_map/ppermute | solution.py:201
  209.7 9.5 %collective-permute-start.29 = (bf16[128,1024]{1,0:T(8,128)(2,1)S(1)}, bf16[128,1024]{1,0:T(8,128)(2,1)S(1)}, u32[]{:S(2)}, u32[]{:S(2)}) collective-permute-start(bf16[128,1024]{1,0:T(8,128)(2,1)S(1)} %get-tuple-element.42), channel_id=1, source_target_pairs={{8,4},{12,8},{9,5},{13,9},{10,6},{14,10},{11,7},{15,11},{24,20},{2... | collective-permute-start | bytes 786440 | tf_op jit(solution)/shard_map/ppermute | solution.py:202
  214.8 8.5 %collective-permute-start.27 = (bf16[128,1024]{1,0:T(8,128)(2,1)S(1)}, bf16[128,1024]{1,0:T(8,128)(2,1)S(1)}, u32[]{:S(2)}, u32[]{:S(2)}) collective-permute-start(bf16[128,1024]{1,0:T(8,128)(2,1)S(1)} %add.274), channel_id=1, source_target_pairs={{0,4},{4,8},{8,12},{1,5},{5,9},{9,13},{2,6},{6,10},{10,14},{3,7},{... | collective-permute-start | bytes 786440 | tf_op jit(solution)/shard_map/ppermute | solution.py:201
  219.3 8.3 %collective-permute-start.30 = (bf16[128,1024]{1,0:T(8,128)(2,1)S(1)}, bf16[128,1024]{1,0:T(8,128)(2,1)S(1)}, u32[]{:S(2)}, u32[]{:S(2)}) collective-permute-start(bf16[128,1024]{1,0:T(8,128)(2,1)S(1)} %add.276), channel_id=1, source_target_pairs={{4,0},{8,4},{12,8},{5,1},{9,5},{13,9},{6,2},{10,6},{14,10},{7,3},{... | collective-permute-start | bytes 786440 | tf_op jit(solution)/shard_map/ppermute | solution.py:202
  (11 other events, 202.3 us)

commit v3 on v2

--- a/solution.py
+++ b/solution.py
@@ -1,3 +1,4 @@
+import functools
 import math
 
 import jax
@@ -190,31 +191,6 @@
     return [(i, i ^ flip) for i in range(lanes)]
 
 
-def chain_scatter(parts, axis):
-    n = len(parts)
-    right = left = None
-    for k in range(n - 1):
-        send_right, send_left = (parts[n - 1 - k], parts[k + 1])
-        if k:
-            send_right = send_right + right
-            send_left = send_left + left
-        right = lax.ppermute(send_right, axis, [(i, i + 1) for i in range(k + 1)])
-        left = lax.ppermute(send_left, axis, [(i, i - 1) for i in range(n - 1 - k, n)])
-    return (parts[0], right, left)
-
-
-def chain_gather(mine, axis, n):
-    right, left = ([], [])
-    for k in range(n - 1):
-        right.append(
-            lax.ppermute(right[-1] if k else mine, axis, [(i, i + 1) for i in range(k, n - 1)])
-        )
-        left.append(
-            lax.ppermute(left[-1] if k else mine, axis, [(i, i - 1) for i in range(1, n - k)])
-        )
-    return (right, left)
-
-
 def query_of(device, lane):
     return 2 * (lane & 1) + ((lane >> 1) ^ (device & 1))
 
@@ -232,7 +208,7 @@
     return pl.pallas_call(
         body,
         out_shape=outs,
-        scratch_shapes=scratch,
+        **({} if scratch is None else {"scratch_shapes": scratch}),
         compiler_params=pltpu.CompilerParams(vmem_limit_bytes=40 * 1024 * 1024),
         cost_estimate=pl.CostEstimate(flops=flops, bytes_accessed=moved, transcendentals=0),
         **kwargs,
@@ -248,28 +224,61 @@
     return jnp.dot(a, b, preferred_element_type=jnp.float32)
 
 
-def attention_body(lens, q, own, ctx, cos_q, sin_q, cos_d, sin_d, out, wide, keys, vals):
+def prepare_body(here, query_docs, pool, ids, *outs):
+    pool_dev = pool.shape[0]
+    docs_per = query_docs.shape[1]
+    rows = pool.shape[2] * pool.shape[3]
+    device, lane = (here[0], here[1])
+    for d, out in enumerate(outs):
+        target = device ^ d
+        query = query_of(target, lane)
+        local = jnp.int32(0)
+        for j in range(docs_per):
+            offset = query_docs[query, j] - device * pool_dev
+            inside = jnp.logical_and(offset >= 0, offset < pool_dev)
+            local = jnp.where(inside, offset, local)
+        out[:rows, :] = pool[local, target].reshape(rows, pool.shape[4])
+        out[rows:, :] = ids[...]
+
+
+def prepare(here, query_docs, pool, ids):
+    _, _, pair, doc_max, head_dim = pool.shape
+    shape = jax.ShapeDtypeStruct((pair * doc_max + ids.shape[0], head_dim), jnp.bfloat16)
+    return call(
+        prepare_body,
+        [shape] * 4,
+        [],
+        1024,
+        1024 * 1024,
+        in_specs=[SMEM, SMEM, VMEM, VMEM],
+        out_specs=[VMEM] * 4,
+        name="prepare",
+    )(here, query_docs, pool, ids)
+
+
+def attention_body(lens, q, c0, c1, c2, c3, cos_q, sin_q, cos_d, sin_d, out, wide, keys, vals):
     length, head_dim = cos_q.shape
     heads = out.shape[1] // head_dim
-    docs, doc_max, _ = ctx.shape
+    pieces = (c0, c1, c2, c3)
+    docs = len(pieces)
+    doc_max = (keys.shape[0] - length) // docs
     half = head_dim // 2
 
     def turned(x, cosine, sine):
         return x * cosine + pltpu.roll(x, half, 1) * sine
 
     cosine, sine = (cos_q[...], sin_q[...])
-    for j in range(docs):
-        key = turned(
-            ctx[j, :, :head_dim].astype(jnp.float32), cos_d[j : j + 1, :], sin_d[j : j + 1, :]
-        )
+    for j, piece in enumerate(pieces):
+        key = turned(piece[:doc_max, :].astype(jnp.float32), cos_d[j : j + 1, :], sin_d[j : j + 1, :])
         keys[j * doc_max : (j + 1) * doc_max, :] = key.astype(jnp.bfloat16)
-        vals[j * doc_max : (j + 1) * doc_max, :] = ctx[j, :, head_dim:]
+        vals[j * doc_max : (j + 1) * doc_max, :] = piece[doc_max : 2 * doc_max, :]
     base = docs * doc_max
-    keys[base:, :] = turned(own[:, :head_dim].astype(jnp.float32), cosine, sine).astype(
+    first = heads * length
+    keys[base:, :] = turned(q[first : first + length, :].astype(jnp.float32), cosine, sine).astype(
         jnp.bfloat16
     )
-    vals[base:, :] = own[:, head_dim:]
-    wide[...] = q[...].astype(jnp.float32)
+    vals[base:, :] = q[first + length : first + 2 * length, :]
+    wide[...] = q[:first, :].astype(jnp.float32)
     column = lax.broadcasted_iota(jnp.int32, (1, doc_max), 1)
     allowed = [column < lens[j] for j in range(docs)]
     causal = lax.broadcasted_iota(jnp.int32, (length, length), 0) >= lax.broadcasted_iota(
@@ -291,157 +300,170 @@
         out[:, h * head_dim : (h + 1) * head_dim] = (mixed / denominator).astype(jnp.bfloat16)
 
 
-def attention(lens, q, own, ctx, tables_q, tables_d):
+def attention(lens, q, pieces, heads, tables_q, tables_d):
     length, head_dim = tables_q[0].shape
-    heads = q.shape[0] // length
-    rows = ctx.shape[0] * ctx.shape[1] + length
+    rows = 5 * length
     return call(
         attention_body,
         jax.ShapeDtypeStruct((length, heads * head_dim), jnp.bfloat16),
         [
-            pltpu.VMEM(q.shape, jnp.float32),
+            pltpu.VMEM((heads * length, head_dim), jnp.float32),
             pltpu.VMEM((rows, head_dim), jnp.bfloat16),
             pltpu.VMEM((rows, head_dim), jnp.bfloat16),
         ],
         4 * heads * length * rows * head_dim * 4,
         4 * 1024 * 1024,
-        in_specs=[SMEM] + [VMEM] * 7,
+        in_specs=[SMEM] + [VMEM] * 9,
         out_specs=VMEM,
         name="attention",
-    )(lens, q, own, ctx, *tables_q, *tables_d)
-
-
-def project_body(place, a, b, c, d, weight, *rest):
-    outs, rows = (rest[:-1], rest[-1])
-    for j, ref in enumerate((a, b, c, d)):
-        rows[place[j]] = ref[...]
-    for m, out in enumerate(outs):
-        out[...] = dot(rows[m], weight[...]).astype(jnp.bfloat16)
-
-
-def project(place, parts, weight):
+    )(lens, q, *pieces, *tables_q, *tables_d)
+
+
+def project_body(here, a, b, c, d, weight, hidden, out, rows):
+    device, lane = (here[0], here[1])
+    for flip, ref in zip((0, 2, 1, 3), (a, b, c, d)):
+        rows[query_of(device, lane ^ flip)] = ref[...]
+    for s in range(4):
+        base = jnp.where(device == s, hidden[...].astype(jnp.float32), 0.0)
+        out[s] = (base + dot(rows[s], weight[...])).astype(jnp.bfloat16)
+
+
+def project(here, parts, weight, hidden):
     length, depth = parts[0].shape
-    shape = jax.ShapeDtypeStruct((length, weight.shape[1]), jnp.bfloat16)
     return call(
         project_body,
-        [shape] * 4,
+        jax.ShapeDtypeStruct((4, length, weight.shape[1]), jnp.bfloat16),
         [pltpu.VMEM((4, length, depth), jnp.bfloat16)],
         2 * 4 * length * depth * weight.shape[1],
         4 * 1024 * 1024,
-        in_specs=[SMEM] + [VMEM] * 5,
-        out_specs=[VMEM] * 4,
+        in_specs=[SMEM] + [VMEM] * 6,
+        out_specs=VMEM,
         name="project",
-    )(place, *parts, weight)
-
-
-def assemble_body(mine, a0, a1, a2, b0, b1, b2, gain, router, scaled, stats):
-    length = mine.shape[0]
+    )(here, *parts, weight, hidden)
+
+
+def assemble_body(here, tokens, gain, router, scaled, stats, residual):
+    length = tokens.shape[1]
     experts = router.shape[0]
-    blocks = (mine[...], a2[...] + b0[...], a1[...] + b1[...], a0[...] + b2[...])
-    ones = jnp.ones((8, mine.shape[1]), jnp.float32)
-    for m, block in enumerate(blocks):
-        wide = block.astype(jnp.float32)
+    device = here[0]
+    ones = jnp.ones((8, tokens.shape[2]), jnp.float32)
+    residual[...] = tokens[device]
+    for d in range(4):
+        wide = tokens[device ^ d].astype(jnp.float32)
         grown = wide * gain[...]
-        scaled[m] = grown.astype(jnp.bfloat16)
-        here = slice(m * length, (m + 1) * length)
-        stats[:experts, here] = lax.dot_general(
+        scaled[d] = grown.astype(jnp.bfloat16)
+        block = slice(d * length, (d + 1) * length)
+        stats[:experts, block] = lax.dot_general(
             router[...], grown, NT, preferred_element_type=jnp.float32,
             precision=lax.Precision.HIGHEST,
         )
-        stats[experts:, here] = lax.dot_general(
+        stats[experts:, block] = lax.dot_general(
             ones, wide * wide, NT, preferred_element_type=jnp.float32,
             precision=lax.Precision.HIGHEST,
         )
 
 
-def assemble(mine, right, left, gain, router):
-    length, width = mine.shape
+def assemble(here, tokens, gain, router):
+    n, length, width = tokens.shape
     return call(
         assemble_body,
         [
-            jax.ShapeDtypeStruct((4, length, width), jnp.bfloat16),
-            jax.ShapeDtypeStruct((router.shape[0] + 8, 4 * length), jnp.float32),
+            jax.ShapeDtypeStruct((n, length, width), jnp.bfloat16),
+            jax.ShapeDtypeStruct((router.shape[0] + 8, n * length), jnp.float32),
+            jax.ShapeDtypeStruct((length, width), jnp.bfloat16),
         ],
         [],
-        2 * 4 * length * width * 256,
+        2 * n * length * width * 256,
         3 * 1024 * 1024,
-        in_specs=[VMEM] * 9,
-        out_specs=[VMEM] * 2,
+        in_specs=[SMEM] + [VMEM] * 3,
+        out_specs=[VMEM] * 3,
         name="assemble",
-    )(mine, *right, *left, gain, router)
-
-
-def gate_up_body(order, tokens, pick, weight, *rest):
-    outs, rows = (rest[:-1], rest[-1])
-    local = rows.shape[0]
-    capacity = pick.shape[1] // local
+    )(here, tokens, gain, router)
+
+
+def gate_up_body(first, order, tokens, pick, weight, *outs):
     hid = weight.shape[3]
-
-    @pl.when(pl.program_id(0) == 0)
-    def _():
-        for j in range(4):
-            m = order[j]
-            chosen = dot(pick[m], tokens[m]).astype(jnp.bfloat16)
-            for e in range(local):
-                rows[e, j * capacity : (j + 1) * capacity, :] = chosen[
-                    e * capacity : (e + 1) * capacity, :
-                ]
-
-    mine = rows[pl.program_id(0)]
+    capacity = pick.shape[2]
+    expert = order[pl.program_id(0)]
+    rows = jnp.concatenate(
+        [dot(pick[d, expert], tokens[d]).astype(jnp.bfloat16) for d in (first, first + 1)], axis=0
+    )
     for g in range(2):
-        term = dot(mine, weight[0, g]).astype(jnp.bfloat16)
+        term = dot(rows, weight[0, g]).astype(jnp.bfloat16)
         for j, out in enumerate(outs):
-            out[0, :, g * hid : (g + 1) * hid] = term[j * capacity : (j + 1) * capacity, :]
-
-
-def gate_up(order, tokens, pick, weight):
+
+            @pl.when(pl.program_id(0) == j)
+            def _():
+                out[:, g * hid : (g + 1) * hid] = term
+
+
+def gate_up(first, order, tokens, pick, weight):
     local, _, width, hid = weight.shape
-    capacity = pick.shape[1] // local
-    shape = jax.ShapeDtypeStruct((local, capacity, 2 * hid), jnp.bfloat16)
+    capacity = pick.shape[2]
+    shape = jax.ShapeDtypeStruct((2 * capacity, 2 * hid), jnp.bfloat16)
+    whole = lambda rank: lambda i, order: (0,) * rank
     return call(
-        gate_up_body,
+        functools.partial(gate_up_body, first),
         [shape] * 4,
-        [pltpu.VMEM((local, 4 * capacity, width), jnp.bfloat16)],
-        2 * local * 4 * capacity * width * 2 * hid,
-        22 * 1024 * 1024,
-        grid=(local,),
-        in_specs=[SMEM, VMEM, VMEM, pl.BlockSpec((1, 2, width, hid), lambda i: (i, 0, 0, 0))],
-        out_specs=[pl.BlockSpec((1, capacity, 2 * hid), lambda i: (i, 0, 0))] * 4,
+        None,
+        2 * local * 2 * capacity * width * 2 * hid,
+        20 * 1024 * 1024,
+        grid_spec=pltpu.PrefetchScalarGridSpec(
+            num_scalar_prefetch=1,
+            grid=(local,),
+            in_specs=[
+                pl.BlockSpec(tokens.shape, whole(3)),
+                pl.BlockSpec(pick.shape, whole(4)),
+                pl.BlockSpec((1, 2, width, hid), lambda i, order: (order[i], 0, 0, 0)),
+            ],
+            out_specs=[pl.BlockSpec(shape.shape, whole(2))] * 4,
+        ),
         name="gate_up",
     )(order, tokens, pick, weight)
 
 
 def down_body(order, a, b, c, d, spread, weight, *rest):
     outs, results = (rest[:-1], rest[-1])
-    e = pl.program_id(0)
-    capacity = a.shape[1]
-    acts = jnp.concatenate([a[0], b[0], c[0], d[0]], axis=0)
-    result = dot(acts, weight[0]).astype(jnp.bfloat16)
-    start = pl.multiple_of(e * capacity, capacity)
-    for j in range(4):
-        results[order[j], pl.ds(start, capacity), :] = result[j * capacity : (j + 1) * capacity, :]
-
-    @pl.when(e == pl.num_programs(0) - 1)
+    i = pl.program_id(0)
+    capacity = results.shape[2]
+    expert = order[i]
+    for j, ref in enumerate((a, b, c, d)):
+
+        @pl.when(i == j)
+        def _():
+            result = dot(ref[...], weight[0]).astype(jnp.bfloat16)
+            for k in range(2):
+                results[k, expert] = result[k * capacity : (k + 1) * capacity, :]
+
+    @pl.when(i == pl.num_programs(0) - 1)
     def _():
-        for m, out in enumerate(outs):
-            out[...] = dot(spread[m], results[m]).astype(jnp.bfloat16)
+        for k, out in enumerate(outs):
+            out[...] = dot(spread[k], results[k].reshape(-1, results.shape[3])).astype(jnp.bfloat16)
 
 
 def down(order, acts, spread, weight):
     local, hid, width = weight.shape
-    capacity = acts[0].shape[1]
+    capacity = acts[0].shape[0] // 2
     length = spread.shape[1]
     shape = jax.ShapeDtypeStruct((length, width), jnp.bfloat16)
-    block = pl.BlockSpec((1, capacity, hid), lambda i: (i, 0, 0))
+    whole = lambda rank: lambda i, order: (0,) * rank
     return call(
         down_body,
-        [shape] * 4,
-        [pltpu.VMEM((4, local * capacity, width), jnp.bfloat16)],
-        2 * local * 4 * capacity * width * hid,
+        [shape] * 2,
+        None,
+        2 * local * 2 * capacity * width * hid,
         10 * 1024 * 1024,
-        grid=(local,),
-        in_specs=[SMEM] + [block] * 4 + [VMEM, pl.BlockSpec((1, hid, width), lambda i: (i, 0, 0))],
-        out_specs=[VMEM] * 4,
+        grid_spec=pltpu.PrefetchScalarGridSpec(
+            num_scalar_prefetch=1,
+            grid=(local,),
+            in_specs=[pl.BlockSpec(acts[0].shape, whole(2))] * 4
+            + [
+                pl.BlockSpec(spread.shape, whole(3)),
+                pl.BlockSpec((1, hid, width), lambda i, order: (order[i], 0, 0)),
+            ],
+            out_specs=[pl.BlockSpec(shape.shape, whole(2))] * 2,
+            scratch_shapes=[pltpu.VMEM((2, local, capacity, width), jnp.bfloat16)],
+        ),
         name="down",
     )(order, *acts, spread, weight)
 
@@ -481,34 +503,41 @@
     capacity = length * expert_ids.shape[1] // experts
     hid = w_gate_up.shape[3]
     seats = jnp.arange(n, dtype=jnp.int32)
-
-    q_rows = turn(question_q.reshape(length * heads_here, head_dim), n, n)
+    here = jnp.stack([device, lane]).astype(jnp.int32)
+    order = (lane ^ jnp.array([0, 2, 1, 3], jnp.int32)).astype(jnp.int32)
+    reach = device ^ seats
+
     kv_head = lax.dynamic_index_in_dim(question_kv, lane, 1, keepdims=False)
-    own = turn(kv_head.reshape(length, 2 * head_dim), n, n)
-
-    for_query = query_of(seats, lane)
-    docs_of = jnp.take(query_docs, for_query, axis=0)
-    held = device * pool_dev + jnp.arange(pool_dev, dtype=jnp.int32)
-    choice = jnp.any(docs_of[:, :, None] == held[None, None, :], axis=1)
-    sending = doc_kv[0]
-    for p in range(1, pool_dev):
-        sending = jnp.where(choice[None, :, p, None, None], doc_kv[p], sending)
-    sending = jnp.transpose(sending, (1, 0, 2, 3)).reshape(kv_heads, doc_max, 2 * head_dim)
-    context = lax.all_to_all(sending, "ep", split_axis=0, concat_axis=0, tiled=True)
-    ids = lax.all_gather(expert_ids, "ep", axis=0, tiled=False)
+    kv_rows = jnp.transpose(kv_head, (1, 0, 2)).reshape(2 * length, head_dim)
+    q_rows = turn(
+        jnp.concatenate([question_q.reshape(length * heads_here, head_dim), kv_rows], axis=0), n, n
+    )
+
+    pool = jnp.transpose(doc_kv, (0, 2, 3, 1, 4))
+    ids_rows = jnp.pad(expert_ids.T.astype(jnp.bfloat16), ((0, 8), (0, 0)))
+    pieces = prepare(here, query_docs, pool, ids_rows)
+    pieces = [pieces[0]] + [lax.ppermute(pieces[d], "ep", pairs(n, d)) for d in range(1, n)]
 
     query = query_of(device, lane)
     my_docs = lax.dynamic_index_in_dim(query_docs, query, 0, keepdims=False)
     starts = lax.dynamic_index_in_dim(ctx_pos, query, 0, keepdims=False)
-    here = (my_docs // pool_dev)[None, :] == seats[:, None]
-    lengths = jnp.sum(jnp.where(here, jnp.take(doc_lens, my_docs)[None, :], 0), axis=1)
-    doc_starts = jnp.sum(jnp.where(here, starts[None, :docs_per], 0), axis=1)
+    owned = (my_docs // pool_dev)[None, :] == reach[:, None]
+    lengths = jnp.sum(jnp.where(owned, jnp.take(doc_lens, my_docs)[None, :], 0), axis=1)
+    doc_starts = jnp.sum(jnp.where(owned, starts[None, :docs_per], 0), axis=1)
     tables_q = signed_tables(starts[docs_per] + jnp.arange(length, dtype=jnp.int32), head_dim)
     tables_d = signed_tables(doc_starts, head_dim)
 
-    ids = jnp.take(ids, (device + seats) % n, axis=0)
+    attended = attention(lengths, q_rows, pieces, heads_here, tables_q, tables_d)
+    far = lax.ppermute(attended, "tp", pairs(n, 2))
+    near = lax.ppermute(attended, "tp", pairs(n, 1))
+    farther = lax.ppermute(far, "tp", pairs(n, 1))
+    partial = project(here, (attended, far, near, farther), out_proj, hidden)
+    tokens = lax.psum(partial, "ep")
+
+    ids = jnp.stack([p[2 * doc_max : 2 * doc_max + expert_ids.shape[1]] for p in pieces])
+    ids = ids.astype(jnp.int32)
     named = device * local + jnp.arange(local, dtype=jnp.int32)
-    chosen = jnp.any(ids[:, None, :, :] == named[None, :, None, None], axis=3)
+    chosen = jnp.any(ids[:, None, :, :] == named[None, :, None, None], axis=2)
     before = (jnp.arange(length)[:, None] < jnp.arange(length)[None, :]).astype(jnp.bfloat16)
     rank = jnp.einsum(
         "men,nk->mek", chosen.astype(jnp.bfloat16), before, preferred_element_type=jnp.float32
@@ -516,74 +545,52 @@
     picked = jnp.logical_and(
         chosen[:, :, None, :],
         rank[:, :, None, :] == jnp.arange(capacity, dtype=jnp.int32)[None, None, :, None],
-    ).reshape(n, local * capacity, length)
+    )
     pick = picked.astype(jnp.bfloat16)
-    spread = jnp.transpose(pick, (0, 2, 1))
+    spread = jnp.transpose(pick.reshape(n, local * capacity, length), (0, 2, 1))
     named_all = jnp.any(
-        ids[:, None, :, :] == jnp.arange(experts, dtype=jnp.int32)[None, :, None, None], axis=3
+        ids[:, None, :, :] == jnp.arange(experts, dtype=jnp.int32)[None, :, None, None], axis=2
     )
     weight = jnp.transpose(w_gate_up, (0, 2, 1, 3))
 
-    attended = attention(lengths, q_rows, own, context, tables_q, tables_d)
-    far = lax.ppermute(attended, "tp", pairs(n, 2))
-    near = lax.ppermute(attended, "tp", pairs(n, 1))
-    farther = lax.ppermute(far, "tp", pairs(n, 1))
-    order = lane ^ jnp.array([0, 2, 1, 3], jnp.int32)
-    place = (query_of(device, order) - device) % n
-    parts = project(place, (attended, far, near, farther), out_proj)
-    mine, right, left = chain_scatter(parts, "ep")
-    residual = (
-        hidden.astype(jnp.float32)
-        + mine.astype(jnp.float32)
-        + (right.astype(jnp.float32) + left.astype(jnp.float32))
-    ).astype(jnp.bfloat16)
-
-    right, left = chain_gather(residual, "ep", n)
-    tokens, stats = assemble(
-        residual,
-        right,
-        left,
-        norm_gain.astype(jnp.float32)[None, :],
-        router_weight.T.astype(jnp.float32),
+    scaled, stats, residual = assemble(
+        here, tokens, norm_gain.astype(jnp.float32)[None, :], router_weight.T.astype(jnp.float32)
     )
     stats = stats + lax.ppermute(stats, "tp", pairs(n, 2))
     stats = stats + lax.ppermute(stats, "tp", pairs(n, 1))
-
-    terms = gate_up(order, tokens, pick, weight)
-    for_far = lax.ppermute(terms[3], "tp", pairs(n, 1))
-    for_me = lax.ppermute(terms[2], "tp", pairs(n, 1))
-    chip_far = (terms[1].astype(jnp.float32) + for_far.astype(jnp.float32)).astype(jnp.bfloat16)
-    across = lax.ppermute(chip_far, "tp", pairs(n, 2))
-
-    stats = lax.dynamic_index_in_dim(stats.reshape(experts + 8, n, length), lane, 1, keepdims=False)
+    stats = stats.reshape(experts + 8, n, length)
     inv_rms = lax.rsqrt(stats[experts] / (width_here * n) + norm_eps)
-    logits = stats[:experts] * inv_rms[None, :]
-    named_mine = lax.dynamic_index_in_dim(named_all, lane, 0, keepdims=False)
-    top = jnp.max(jnp.where(named_mine, logits, -jnp.inf), axis=0, keepdims=True)
-    grown = jnp.where(named_mine, jnp.exp(logits - top), 0.0)
-    mix = grown / jnp.sum(grown, axis=0, keepdims=True)
-    mix = lax.dynamic_slice_in_dim(mix, device * local, local, 0)
-    picked_mine = lax.dynamic_index_in_dim(picked, lane, 0, keepdims=False).reshape(
-        local, capacity, length
-    )
-    inv_row = jnp.sum(jnp.where(picked_mine, inv_rms[None, None, :], 0.0), axis=2)[:, :, None]
-    mix_row = jnp.sum(jnp.where(picked_mine, mix[:, None, :], 0.0), axis=2)[:, :, None]
-
-    summed = (
-        terms[0].astype(jnp.float32) + for_me.astype(jnp.float32) + across.astype(jnp.float32)
-    ) * inv_row
-    act = jax.nn.silu(summed[:, :, :hid]) * summed[:, :, hid:] * mix_row
-    act = act.astype(jnp.bfloat16)
-    far = lax.ppermute(act, "tp", pairs(n, 2))
-    near = lax.ppermute(act, "tp", pairs(n, 1))
-    farther = lax.ppermute(far, "tp", pairs(n, 1))
-    parts = down(order, (act, far, near, farther), spread, w_down)
-    mine, right, left = chain_scatter(parts, "ep")
-    return (
-        residual.astype(jnp.float32)
-        + mine.astype(jnp.float32)
-        + (right.astype(jnp.float32) + left.astype(jnp.float32))
-    ).astype(jnp.bfloat16)
+    logits = jnp.transpose(stats[:experts], (1, 0, 2)) * inv_rms[:, None, :]
+    top = jnp.max(jnp.where(named_all, logits, -jnp.inf), axis=1, keepdims=True)
+    grown = jnp.where(named_all, jnp.exp(logits - top), 0.0)
+    mine = device * local + lane
+    mix = lax.dynamic_index_in_dim(grown, mine, 1, keepdims=False) / jnp.sum(grown, axis=1)
+    picked_mine = lax.dynamic_index_in_dim(picked, lane, 1, keepdims=False)
+    inv_row = jnp.sum(jnp.where(picked_mine, inv_rms[:, None, :], 0.0), axis=2)
+    mix_row = jnp.sum(jnp.where(picked_mine, mix[:, None, :], 0.0), axis=2)
+
+    total = None
+    for first in (2, 0):
+        rows = slice(first, first + 2)
+        terms = gate_up(first, order, scaled, pick, weight)
+        for_far = lax.ppermute(terms[3], "tp", pairs(n, 1))
+        for_me = lax.ppermute(terms[2], "tp", pairs(n, 1))
+        chip_far = (terms[1].astype(jnp.float32) + for_far.astype(jnp.float32)).astype(jnp.bfloat16)
+        across = lax.ppermute(chip_far, "tp", pairs(n, 2))
+        summed = (
+            terms[0].astype(jnp.float32) + for_me.astype(jnp.float32) + across.astype(jnp.float32)
+        ) * inv_row[rows].reshape(-1, 1)
+        act = jax.nn.silu(summed[:, :hid]) * summed[:, hid:] * mix_row[rows].reshape(-1, 1)
+        act = act.astype(jnp.bfloat16)
+        far = lax.ppermute(act, "tp", pairs(n, 2))
+        near = lax.ppermute(act, "tp", pairs(n, 1))
+        farther = lax.ppermute(far, "tp", pairs(n, 1))
+        parts = down(order, (act, far, near, farther), spread[rows], w_down)
+        for d, part in zip((first, first + 1), parts):
+            back = lax.ppermute(part, "ep", pairs(n, d)) if d else part
+            back = back.astype(jnp.float32)
+            total = back if total is None else total + back
+    return (residual.astype(jnp.float32) + total).astype(jnp.bfloat16)
 
 
 def solution(mesh):

time: 229 us -> 229 us (level)
  starting transfers between devices: 63.1 us -> 19.6 us
  waiting for transfers between devices: 92.4 us -> 110 us
  blocking collectives: 14.2 us -> 0 us
  Pallas kernels: 21.7 us -> 34.9 us
  between operations: 0.63 us -> 13.7 us
  local copies, waits for them, and re-layouts: 25.8 us -> 34.2 us
  other arithmetic: 10.5 us -> 15.5 us
    psum x0 -> x1, waiting for transfers between devices: none -> 50.5 us  [per_device_square(): tokens = lax.psum(partial, 'ep')]
    ppermute x18 -> x6, starting transfers between devices: 40.3 us -> 12 us  [the longest x3 8.13 us: per_device_square(): lax.ppermute(pieces[d], 'ep', pairs(n, d))]
    ppermute x18 -> x6, waiting for transfers between devices: 41.2 us -> 24.2 us  [the longest x3 16.5 us: per_device_square(): back = lax.ppermute(part, 'ep', pairs(n, d)) if d else part]
    all_gather x1 -> x0, blocking collectives: 14.2 us -> none  [per_device_square(): ids = lax.all_gather(expert_ids, 'ep', axis=0, tiled=False)]
    pallas_call x4 -> x7, Pallas kernels: 18.4 us -> 31.6 us  [the longest x2 18.1 us: gate_up(): call(functools.partial(gate_up_body, first), [shape] * 4, None, 2 * local...]
    all_to_all x1 -> x0, waiting for transfers between devices: 11.3 us -> none  [per_device_square(): lax.all_to_all(sending, 'ep', split_axis=0, concat_axis=0, tiled=True)]
    unnamed x24 -> x23, local copies, waits for them, and re-layouts: 20 us -> 28.1 us
    all_to_all x1 -> x0, starting transfers between devices: 6.34 us -> none  [per_device_square(): lax.all_to_all(sending, 'ep', split_axis=0, concat_axis=0, tiled=True)]
  transfers between devices with their start and end apart: 32 -> 25, of which waited for: 17 -> 10; matrix products, arithmetic and copies ran while one was open for 11% -> 16% of each run, Pallas kernels for 0% -> 11%
where the time goes in v3:
time: 229 us; the launch traced here: 228 us
  waiting for transfers between devices  110 us (48%)
  Pallas kernels  34.9 us (15%)
  local copies, waits for them, and re-layouts  34.2 us (15%)
  starting transfers between devices  19.6 us (9%)
  other arithmetic  15.5 us (7%)
  between operations  13.7 us (6%)
    psum x1, waiting for transfers between devices, per_device_square(): tokens = lax.psum(partial, 'ep')  50.5 us
    unnamed x23, local copies, waits for them, and re-layouts  28.1 us
    ppermute x2, waiting for transfers between devices, per_device_square(): across = lax.ppermute(chip_far, 'tp', pairs(n, 2))  20.3 us
    pallas_call x2, Pallas kernels, gate_up(): call(functools.partial(gate_up_body, first), [shape] * 4, None, 2 * local...  18.1 us
    ppermute x3, waiting for transfers between devices, per_device_square(): back = lax.ppermute(part, 'ep', pairs(n, d)) if d else part  16.5 us
    ppermute x3, starting transfers between devices, per_device_square(): lax.ppermute(pieces[d], 'ep', pairs(n, d))  8.13 us
    ppermute x3, waiting for transfers between devices, per_device_square(): lax.ppermute(pieces[d], 'ep', pairs(n, d))  7.71 us
    ppermute x2, waiting for transfers between devices, per_device_square(): far = lax.ppermute(act, 'tp', pairs(n, 2))  7.18 us
  transfers between devices with their start and end apart: 25, of which 10 were waited for; matrix products, arithmetic and copies ran while one was open for 16% of the time, Pallas kernels for 11%

profile of v3, /device:TPU:0, one launch (start us, length us, event | category | flops | bytes accessed | tf_op | source)
XLA Modules:
  0.0 228.3 jit_solution(6603936642585435912)
XLA Ops:
  12.5 5.7 %collective-permute-start.1 = (bf16[272,128]{1,0:T(8,128)(2,1)S(1)}, bf16[272,128]{1,0:T(8,128)(2,1)S(1)}, u32[]{:S(2)}, u32[]{:S(2)}) collective-permute-start(bf16[272,128]{1,0:T(8,128)(2,1)S(1)} %get-tuple-element.25), channel_id=1, source_target_pairs={{0,4},{4,0},{8,12},{12,8},{1,5},{5,1},{9,13},{13,9},{2,6},{6,2},{1... | collective-permute-start | bytes 208904 | tf_op jit(solution)/shard_map/ppermute | solution.py:519
  18.2 1.8 collective-permute-start.2
  22.6 1.3 gather_fusion
  26.6 7.7 %collective-permute-done.2.c2 = bf16[272,128]{1,0:T(8,128)(2,1)S(1)} collective-permute-done((bf16[272,128]{1,0:T(8,128)(2,1)S(1)}, bf16[272,128]{1,0:T(8,128)(2,1)S(1)}, u32[]{:S(2)}, u32[]{:S(2)}) %collective-permute-start.2) | collective-permute-done | bytes 69664 | tf_op jit(solution)/shard_map/ppermute | solution.py:519
  35.0 3.4 %attention.1.a = bf16[128,1024]{1,0:T(8,128)(2,1)S(1)} custom-call(s32[4]{0:T(128)S(1)} %get-tuple-element.46.lens, bf16[1280,128]{1,0:T(8,128)(2,1)S(1)} %collective-permute-done.q, bf16[272,128]{1,0:T(8,128)(2,1)S(1)} %get-tuple-element.24.c0, bf16[272,128]{1,0:T(8,128)(2,1)S(1)} %collective-permute-done.1.c1, ...), custom_call_target="tpu_custom_call" | custom-call | flops 1342177280 | bytes 4194304 | tf_op jit(solution)/shard_map/attention/pallas_call | solution.py:306
  40.1 6.8 %collective-permute-done.4.b = bf16[128,1024]{1,0:T(8,128)(2,1)S(1)} collective-permute-done((bf16[128,1024]{1,0:T(8,128)(2,1)S(1)}, bf16[128,1024]{1,0:T(8,128)(2,1)S(1)}, u32[]{:S(2)}, u32[]{:S(2)}) %collective-permute-start.4) | collective-permute-done | bytes 262176 | tf_op jit(solution)/shard_map/ppermute | solution.py:531
  48.2 16.7 %copy.45 = bf16[4,1024,2,1024]{3,1,2,0:T(8,128)(2,1)} copy(bf16[4,1024,2,1024]{3,2,1,0:T(2,128)(2,1)} %param.24) | data formatting | bytes 33554432 | tf_op args[10]
  64.8 1.3 slice_bitcast_fusion.1
  66.1 2.8 %project.1 = bf16[4,128,1024]{2,1,0:T(8,128)(2,1)} custom-call(s32[2]{0:T(128)S(1)} %pad_add_fusion.here, bf16[128,1024]{1,0:T(8,128)(2,1)S(1)} %attention.1.a, bf16[128,1024]{1,0:T(8,128)(2,1)S(1)} %collective-permute-done.4.b, bf16[128,1024]{1,0:T(8,128)(2,1)S(1)} %collective-permute-done.5.c, bf16[128,1024]{1,0:T(8,128)(2,1)S(1)} %collective-permute-done.6.d, ...), custom_call_target="tpu_custom_call" | custom-call | flops 1073741824 | bytes 4194304 | tf_op jit(solution)/shard_map/project/pallas_call | solution.py:333
  71.5 50.5 %all-reduce.3.cloned.1.call-done.tokens = bf16[4,128,1024]{2,1,0:T(8,128)(2,1)} async-done(((bf16[4,128,1024]{2,1,0:T(8,128)(2,1)}), bf16[4,128,1024]{2,1,0:T(8,128)(2,1)}) %all-reduce.3.cloned.1.call-update) | async-done | bytes 1048592 | tf_op jit(solution)/shard_map/psum | solution.py:535
  122.0 1.2 copy-done.5
  123.2 4.1 %assemble.1 = (bf16[4,128,1024]{2,1,0:T(8,128)(2,1)S(1)}, f32[24,512]{1,0:T(8,128)S(1)}, bf16[128,1024]{1,0:T(8,128)(2,1)S(1)}) custom-call(s32[2]{0:T(128)S(1)} %pad_add_fusion.here, bf16[4,128,1024]{2,1,0:T(8,128)(2,1)S(1)} %copy-done.5, f32[1,1024]{1,0:T(1,128)S(1)} %bitcast.87, f32[16,1024]{1,0:T(8,128)S(1)} %convert_bitcast_fusion.router), custom_call_target="tpu_custom_call" | custom-call | flops 268435456 | bytes 3145728 | tf_op jit(solution)/shard_map/assemble/pallas_call | solution.py:368
  127.4 1.5 collective-permute-start.10
  128.8 8.7 %gate_up.2 = (bf16[128,2048]{1,0:T(8,128)(2,1)S(1)}, bf16[128,2048]{1,0:T(8,128)(2,1)S(1)}, bf16[128,2048]{1,0:T(8,128)(2,1)S(1)}, bf16[128,2048]{1,0:T(8,128)(2,1)S(1)}) custom-call(s32[4]{0:T(128)S(1)} %broadcast_xor_fusion.order, bf16[4,128,1024]{2,1,0:T(8,128)(2,1)S(1)} %get-tuple-element.29.tokens, bf16[4,4,64,128]{3,2,1,0:T(8,128)(2,1)S(1)} %get-tuple-element.50.pick, ...), custom_call_target="tpu_custom_call" | custom-call | flops 2147483648 | bytes 20971520 | tf_op jit(solution)/shard_map/gate_up/pallas_call | solution.py:405
  137.6 9.5 %gate_up.3 = (bf16[128,2048]{1,0:T(8,128)(2,1)S(1)}, bf16[128,2048]{1,0:T(8,128)(2,1)S(1)}, bf16[128,2048]{1,0:T(8,128)(2,1)S(1)}, bf16[128,2048]{1,0:T(8,128)(2,1)}) custom-call(s32[4]{0:T(128)S(1)} %broadcast_xor_fusion.order, bf16[4,128,1024]{2,1,0:T(8,128)(2,1)S(1)} %get-tuple-element.29.tokens, bf16[4,4,64,128]{3,2,1,0:T(8,128)(2,1)S(1)} %get-tuple-element.50.pick, ...), custom_call_target="tpu_custom_call" | custom-call | flops 2147483648 | bytes 20971520 | tf_op jit(solution)/shard_map/gate_up/pallas_call | solution.py:405
  148.5 1.2 collective-permute-done.8
  151.5 1.2 add_convert_fusion
  152.7 1.5 collective-permute-start.19
  154.3 11.4 %collective-permute-done.9 = bf16[128,2048]{1,0:T(8,128)(2,1)} collective-permute-done((bf16[128,2048]{1,0:T(8,128)(2,1)}, bf16[128,2048]{1,0:T(8,128)(2,1)}, u32[]{:S(2)}, u32[]{:S(2)}) %collective-permute-start.9) | collective-permute-done | bytes 524320 | tf_op jit(solution)/shard_map/ppermute | solution.py:579
  165.7 1.4 add_multiply_fusion.1
  168.0 8.9 %collective-permute-done.19 = bf16[128,2048]{1,0:T(8,128)(2,1)S(1)} collective-permute-done((bf16[128,2048]{1,0:T(8,128)(2,1)S(1)}, bf16[128,2048]{1,0:T(8,128)(2,1)S(1)}, u32[]{:S(2)}, u32[]{:S(2)}) %collective-permute-start.19) | collective-permute-done | bytes 524320 | tf_op jit(solution)/shard_map/ppermute | solution.py:579
  176.8 1.3 add_multiply_fusion
  179.6 2.8 %collective-permute-done.12.b = bf16[128,1024]{1,0:T(8,128)(2,1)S(1)} collective-permute-done((bf16[128,1024]{1,0:T(8,128)(2,1)S(1)}, bf16[128,1024]{1,0:T(8,128)(2,1)S(1)}, u32[]{:S(2)}, u32[]{:S(2)}) %collective-permute-start.12) | collective-permute-done | bytes 262176 | tf_op jit(solution)/shard_map/ppermute | solution.py:585
  183.1 4.4 %collective-permute-done.20.b = bf16[128,1024]{1,0:T(8,128)(2,1)S(1)} collective-permute-done((bf16[128,1024]{1,0:T(8,128)(2,1)S(1)}, bf16[128,1024]{1,0:T(8,128)(2,1)S(1)}, u32[]{:S(2)}, u32[]{:S(2)}) %collective-permute-start.20) | collective-permute-done | bytes 262176 | tf_op jit(solution)/shard_map/ppermute | solution.py:585
  187.6 3.4 %copy-done.2 = bf16[4,1024,1024]{2,1,0:T(8,128)(2,1)S(1)} copy-done((bf16[4,1024,1024]{2,1,0:T(8,128)(2,1)S(1)}, bf16[4,1024,1024]{2,1,0:T(8,128)(2,1)}, u32[]{:S(2)}) %copy-start.2) | copy-done | bytes 8388632
  190.9 3.0 %down.2 = (bf16[128,1024]{1,0:T(8,128)(2,1)S(1)}, bf16[128,1024]{1,0:T(8,128)(2,1)S(1)}) custom-call(s32[4]{0:T(128)S(1)} %broadcast_xor_fusion.order, bf16[128,1024]{1,0:T(8,128)(2,1)S(1)} %fusion.7.a, bf16[128,1024]{1,0:T(8,128)(2,1)S(1)} %collective-permute-done.12.b, bf16[128,1024]{1,0:T(8,128)(2,1)S(1)} %collective-permute-done.13.c, ...), custom_call_target="tpu_custom_call" | custom-call | flops 1073741824 | bytes 10485760 | tf_op jit(solution)/shard_map/down/pallas_call | solution.py:450
  194.0 1.9 collective-permute-start.15
  195.8 1.9 collective-permute-start.16
  197.7 3.4 %copy-done.3 = bf16[4,1024,1024]{2,1,0:T(8,128)(2,1)S(1)} copy-done((bf16[4,1024,1024]{2,1,0:T(8,128)(2,1)S(1)}, bf16[4,1024,1024]{2,1,0:T(8,128)(2,1)}, u32[]{:S(2)}) %copy-start.3) | copy-done | bytes 8388632
  201.1 2.8 %down.3 = (bf16[128,1024]{1,0:T(8,128)(2,1)S(1)}, bf16[128,1024]{1,0:T(8,128)(2,1)S(1)}) custom-call(s32[4]{0:T(128)S(1)} %broadcast_xor_fusion.order, bf16[128,1024]{1,0:T(8,128)(2,1)S(1)} %fusion.5.a, bf16[128,1024]{1,0:T(8,128)(2,1)S(1)} %collective-permute-done.20.b, bf16[128,1024]{1,0:T(8,128)(2,1)S(1)} %collective-permute-done.21.c, ...), custom_call_target="tpu_custom_call" | custom-call | flops 1073741824 | bytes 10485760 | tf_op jit(solution)/shard_map/down/pallas_call | solution.py:450
  204.0 11.3 %collective-permute-done.15 = bf16[128,1024]{1,0:T(8,128)(2,1)S(1)} collective-permute-done((bf16[128,1024]{1,0:T(8,128)(2,1)S(1)}, bf16[128,1024]{1,0:T(8,128)(2,1)S(1)}, u32[]{:S(2)}, u32[]{:S(2)}) %collective-permute-start.15) | collective-permute-done | bytes 262176 | tf_op jit(solution)/shard_map/ppermute | solution.py:590
  215.3 5.2 %collective-permute-done.23 = bf16[128,1024]{1,0:T(8,128)(2,1)S(1)} collective-permute-done((bf16[128,1024]{1,0:T(8,128)(2,1)S(1)}, bf16[128,1024]{1,0:T(8,128)(2,1)S(1)}, u32[]{:S(2)}, u32[]{:S(2)}) %collective-permute-start.23) | collective-permute-done | bytes 262176 | tf_op jit(solution)/shard_map/ppermute | solution.py:590
  (111 shorter events, 24.7 us)
Async XLA Ops:
  6.5 1.0 copy-start
  6.5 115.5 %all-reduce.3.cloned.1.call-start = ((), (), s32[]{:S(2)}) async-start(), calls=%async_computation | async-start | bytes 2097152 | tf_op jit(solution)/shard_map/psum | solution.py:535
  8.5 25.8 %collective-permute-start = (bf16[1280,128]{1,0:T(8,128)(2,1)S(1)}, bf16[1280,128]{1,0:T(8,128)(2,1)S(1)}, u32[]{:S(2)}, u32[]{:S(2)}) collective-permute-start(bf16[1280,128]{1,0:T(8,128)(2,1)S(1)} %pad_maximum_fusion), channel_id=1, source_target_pairs={{0,0},{1,6},{2,8},{3,14},{4,2},{5,4},{6,10},{7,12},{8,1},{9,7},{10... | collective-permute-start | bytes 983048 | tf_op jit(solution)/shard_map/ppermute | solution.py:204
  12.5 14.2 %collective-permute-start.1 = (bf16[272,128]{1,0:T(8,128)(2,1)S(1)}, bf16[272,128]{1,0:T(8,128)(2,1)S(1)}, u32[]{:S(2)}, u32[]{:S(2)}) collective-permute-start(bf16[272,128]{1,0:T(8,128)(2,1)S(1)} %get-tuple-element.25), channel_id=1, source_target_pairs={{0,4},{4,0},{8,12},{12,8},{1,5},{5,1},{9,13},{13,9},{2,6},{6,2},{1... | collective-permute-start | bytes 208904 | tf_op jit(solution)/shard_map/ppermute | solution.py:519
  18.2 16.2 %collective-permute-start.2 = (bf16[272,128]{1,0:T(8,128)(2,1)S(1)}, bf16[272,128]{1,0:T(8,128)(2,1)S(1)}, u32[]{:S(2)}, u32[]{:S(2)}) collective-permute-start(bf16[272,128]{1,0:T(8,128)(2,1)S(1)} %get-tuple-element.26), channel_id=1, source_target_pairs={{0,8},{4,12},{8,0},{12,4},{1,9},{5,13},{9,1},{13,5},{2,10},{6,14},... | collective-permute-start | bytes 208904 | tf_op jit(solution)/shard_map/ppermute | solution.py:519
  20.0 14.4 %collective-permute-start.3 = (bf16[272,128]{1,0:T(8,128)(2,1)S(1)}, bf16[272,128]{1,0:T(8,128)(2,1)S(1)}, u32[]{:S(2)}, u32[]{:S(2)}) collective-permute-start(bf16[272,128]{1,0:T(8,128)(2,1)S(1)} %get-tuple-element.27), channel_id=1, source_target_pairs={{0,12},{4,8},{8,4},{12,0},{1,13},{5,9},{9,5},{13,1},{2,14},{6,10},... | collective-permute-start | bytes 208904 | tf_op jit(solution)/shard_map/ppermute | solution.py:519
  38.4 8.5 %collective-permute-start.4 = (bf16[128,1024]{1,0:T(8,128)(2,1)S(1)}, bf16[128,1024]{1,0:T(8,128)(2,1)S(1)}, u32[]{:S(2)}, u32[]{:S(2)}) collective-permute-start(bf16[128,1024]{1,0:T(8,128)(2,1)S(1)} %attention.1.a), channel_id=1, source_target_pairs={{0,2},{1,3},{2,0},{3,1},{4,6},{5,7},{6,4},{7,5},{8,10},{9,11},{10,... | collective-permute-start | bytes 786440 | tf_op jit(solution)/shard_map/ppermute | solution.py:531
  39.9 26.2 %collective-permute-start.5 = (bf16[128,1024]{1,0:T(8,128)(2,1)S(1)}, bf16[128,1024]{1,0:T(8,128)(2,1)S(1)}, u32[]{:S(2)}, u32[]{:S(2)}) collective-permute-start(bf16[128,1024]{1,0:T(8,128)(2,1)S(1)} %attention.1.a), channel_id=1, source_target_pairs={{0,1},{1,0},{2,3},{3,2},{4,5},{5,4},{6,7},{7,6},{8,9},{9,8},{10,11... | collective-permute-start | bytes 786440 | tf_op jit(solution)/shard_map/ppermute | solution.py:532
  46.9 19.2 %collective-permute-start.6 = (bf16[128,1024]{1,0:T(8,128)(2,1)S(1)}, bf16[128,1024]{1,0:T(8,128)(2,1)S(1)}, u32[]{:S(2)}, u32[]{:S(2)}) collective-permute-start(bf16[128,1024]{1,0:T(8,128)(2,1)S(1)} %collective-permute-done.4.b), channel_id=1, source_target_pairs={{0,1},{1,0},{2,3},{3,2},{4,5},{5,4},{6,7},{7,6},{8,9},{9,8},{10,11... | collective-permute-start | bytes 786440 | tf_op jit(solution)/shard_map/ppermute | solution.py:533
  48.2 17.9 %copy-start.4 = (bf16[1024,1024]{1,0:T(8,128)(2,1)S(1)}, bf16[1024,1024]{1,0:T(8,128)(2,1)}, u32[]{:S(2)}) copy-start(bf16[1024,1024]{1,0:T(8,128)(2,1)} %weight.3) | copy-start | bytes 6291460
  48.2 17.9 %copy-start.6 = (bf16[128,1024]{1,0:T(8,128)(2,1)S(1)}, bf16[128,1024]{1,0:T(8,128)(2,1)}, u32[]{:S(2)}) copy-start(bf16[128,1024]{1,0:T(8,128)(2,1)} %hidden.1) | copy-start | bytes 786436
  122.0 1.2 copy-start.5
  127.4 10.2 %collective-permute-start.10 = (f32[24,512]{1,0:T(8,128)S(1)}, f32[24,512]{1,0:T(8,128)S(1)}, u32[]{:S(2)}, u32[]{:S(2)}) collective-permute-start(f32[24,512]{1,0:T(8,128)S(1)} %get-tuple-element.34), channel_id=1, source_target_pairs={{0,2},{1,3},{2,0},{3,1},{4,6},{5,7},{6,4},{7,5},{8,10},{9,11},{10,... | collective-permute-start | bytes 147464 | tf_op jit(solution)/shard_map/ppermute | solution.py:559
  137.5 10.6 %collective-permute-start.11 = (f32[24,512]{1,0:T(8,128)S(1)}, f32[24,512]{1,0:T(8,128)S(1)}, u32[]{:S(2)}, u32[]{:S(2)}) collective-permute-start(f32[24,512]{1,0:T(8,128)S(1)} %add.130), channel_id=1, source_target_pairs={{0,1},{1,0},{2,3},{3,2},{4,5},{5,4},{6,7},{7,6},{8,9},{9,8},{10,11... | collective-permute-start | bytes 147464 | tf_op jit(solution)/shard_map/ppermute | solution.py:560
  147.1 2.6 %collective-permute-start.8 = (bf16[128,2048]{1,0:T(8,128)(2,1)S(1)}, bf16[128,2048]{1,0:T(8,128)(2,1)S(1)}, u32[]{:S(2)}, u32[]{:S(2)}) collective-permute-start(bf16[128,2048]{1,0:T(8,128)(2,1)S(1)} %get-tuple-element.33), channel_id=1, source_target_pairs={{0,1},{1,0},{2,3},{3,2},{4,5},{5,4},{6,7},{7,6},{8,9},{9,8},{10,11... | collective-permute-start | bytes 1572872 | tf_op jit(solution)/shard_map/ppermute | solution.py:576
  147.6 6.7 %collective-permute-start.7 = (bf16[128,2048]{1,0:T(8,128)(2,1)S(1)}, bf16[128,2048]{1,0:T(8,128)(2,1)}, u32[]{:S(2)}, u32[]{:S(2)}) collective-permute-start(bf16[128,2048]{1,0:T(8,128)(2,1)S(1)} %get-tuple-element.31), channel_id=1, source_target_pairs={{0,1},{1,0},{2,3},{3,2},{4,5},{5,4},{6,7},{7,6},{8,9},{9,8},{10,11... | collective-permute-start | bytes 1572872 | tf_op jit(solution)/shard_map/ppermute | solution.py:577
  147.6 3.9 %collective-permute-start.18 = (bf16[128,2048]{1,0:T(8,128)(2,1)}, bf16[128,2048]{1,0:T(8,128)(2,1)}, u32[]{:S(2)}, u32[]{:S(2)}) collective-permute-start(bf16[128,2048]{1,0:T(8,128)(2,1)} %get-tuple-element.40), channel_id=1, source_target_pairs={{0,1},{1,0},{2,3},{3,2},{4,5},{5,4},{6,7},{7,6},{8,9},{9,8},{10,11... | collective-permute-start | bytes 1572872 | tf_op jit(solution)/shard_map/ppermute | solution.py:576
  148.1 19.9 %collective-permute-start.17 = (bf16[128,2048]{1,0:T(8,128)(2,1)S(1)}, bf16[128,2048]{1,0:T(8,128)(2,1)}, u32[]{:S(2)}, u32[]{:S(2)}) collective-permute-start(bf16[128,2048]{1,0:T(8,128)(2,1)S(1)} %get-tuple-element.38), channel_id=1, source_target_pairs={{0,1},{1,0},{2,3},{3,2},{4,5},{5,4},{6,7},{7,6},{8,9},{9,8},{10,11... | collective-permute-start | bytes 1572872 | tf_op jit(solution)/shard_map/ppermute | solution.py:577
  150.6 15.1 %collective-permute-start.9 = (bf16[128,2048]{1,0:T(8,128)(2,1)}, bf16[128,2048]{1,0:T(8,128)(2,1)}, u32[]{:S(2)}, u32[]{:S(2)}) collective-permute-start(bf16[128,2048]{1,0:T(8,128)(2,1)} %add_convert_fusion.1), channel_id=1, source_target_pairs={{0,2},{1,3},{2,0},{3,1},{4,6},{5,7},{6,4},{7,5},{8,10},{9,11},{10,... | collective-permute-start | bytes 1572872 | tf_op jit(solution)/shard_map/ppermute | solution.py:579
  151.5 69.9 %copy-start.1 = (bf16[128,4,2,128]{3,2,1,0:T(2,128)(2,1)S(1)}, bf16[128,4,2,128]{3,2,1,0:T(2,128)(2,1)}, u32[]{:S(2)}) copy-start(bf16[128,4,2,128]{3,2,1,0:T(2,128)(2,1)} %param.15) | copy-start | bytes 786436
  152.7 24.1 %collective-permute-start.19 = (bf16[128,2048]{1,0:T(8,128)(2,1)S(1)}, bf16[128,2048]{1,0:T(8,128)(2,1)S(1)}, u32[]{:S(2)}, u32[]{:S(2)}) collective-permute-start(bf16[128,2048]{1,0:T(8,128)(2,1)S(1)} %add_convert_fusion), channel_id=1, source_target_pairs={{0,2},{1,3},{2,0},{3,1},{4,6},{5,7},{6,4},{7,5},{8,10},{9,11},{10,... | collective-permute-start | bytes 1572872 | tf_op jit(solution)/shard_map/ppermute | solution.py:579
  167.3 15.1 %collective-permute-start.12 = (bf16[128,1024]{1,0:T(8,128)(2,1)S(1)}, bf16[128,1024]{1,0:T(8,128)(2,1)S(1)}, u32[]{:S(2)}, u32[]{:S(2)}) collective-permute-start(bf16[128,1024]{1,0:T(8,128)(2,1)S(1)} %fusion.7.a), channel_id=1, source_target_pairs={{0,2},{1,3},{2,0},{3,1},{4,6},{5,7},{6,4},{7,5},{8,10},{9,11},{10,... | collective-permute-start | bytes 786440 | tf_op jit(solution)/shard_map/ppermute | solution.py:585
  178.3 9.2 %collective-permute-start.20 = (bf16[128,1024]{1,0:T(8,128)(2,1)S(1)}, bf16[128,1024]{1,0:T(8,128)(2,1)S(1)}, u32[]{:S(2)}, u32[]{:S(2)}) collective-permute-start(bf16[128,1024]{1,0:T(8,128)(2,1)S(1)} %fusion.5.a), channel_id=1, source_target_pairs={{0,2},{1,3},{2,0},{3,1},{4,6},{5,7},{6,4},{7,5},{8,10},{9,11},{10,... | collective-permute-start | bytes 786440 | tf_op jit(solution)/shard_map/ppermute | solution.py:585
  179.6 8.0 %collective-permute-start.13 = (bf16[128,1024]{1,0:T(8,128)(2,1)S(1)}, bf16[128,1024]{1,0:T(8,128)(2,1)S(1)}, u32[]{:S(2)}, u32[]{:S(2)}) collective-permute-start(bf16[128,1024]{1,0:T(8,128)(2,1)S(1)} %fusion.7.a), channel_id=1, source_target_pairs={{0,1},{1,0},{2,3},{3,2},{4,5},{5,4},{6,7},{7,6},{8,9},{9,8},{10,11... | collective-permute-start | bytes 786440 | tf_op jit(solution)/shard_map/ppermute | solution.py:586
  182.4 5.1 %collective-permute-start.14 = (bf16[128,1024]{1,0:T(8,128)(2,1)S(1)}, bf16[128,1024]{1,0:T(8,128)(2,1)S(1)}, u32[]{:S(2)}, u32[]{:S(2)}) collective-permute-start(bf16[128,1024]{1,0:T(8,128)(2,1)S(1)} %collective-permute-done.12.b), channel_id=1, source_target_pairs={{0,1},{1,0},{2,3},{3,2},{4,5},{5,4},{6,7},{7,6},{8,9},{9,8},{10,11... | collective-permute-start | bytes 786440 | tf_op jit(solution)/shard_map/ppermute | solution.py:587
  182.5 15.2 %collective-permute-start.21 = (bf16[128,1024]{1,0:T(8,128)(2,1)S(1)}, bf16[128,1024]{1,0:T(8,128)(2,1)S(1)}, u32[]{:S(2)}, u32[]{:S(2)}) collective-permute-start(bf16[128,1024]{1,0:T(8,128)(2,1)S(1)} %fusion.5.a), channel_id=1, source_target_pairs={{0,1},{1,0},{2,3},{3,2},{4,5},{5,4},{6,7},{7,6},{8,9},{9,8},{10,11... | collective-permute-start | bytes 786440 | tf_op jit(solution)/shard_map/ppermute | solution.py:586
  187.5 10.2 %collective-permute-start.22 = (bf16[128,1024]{1,0:T(8,128)(2,1)S(1)}, bf16[128,1024]{1,0:T(8,128)(2,1)S(1)}, u32[]{:S(2)}, u32[]{:S(2)}) collective-permute-start(bf16[128,1024]{1,0:T(8,128)(2,1)S(1)} %collective-permute-done.20.b), channel_id=1, source_target_pairs={{0,1},{1,0},{2,3},{3,2},{4,5},{5,4},{6,7},{7,6},{8,9},{9,8},{10,11... | collective-permute-start | bytes 786440 | tf_op jit(solution)/shard_map/ppermute | solution.py:587
  187.6 3.4 %copy-start.2 = (bf16[4,1024,1024]{2,1,0:T(8,128)(2,1)S(1)}, bf16[4,1024,1024]{2,1,0:T(8,128)(2,1)}, u32[]{:S(2)}) copy-start(bf16[4,1024,1024]{2,1,0:T(8,128)(2,1)} %weight.5) | copy-start | bytes 25165828
  194.0 21.3 %collective-permute-start.15 = (bf16[128,1024]{1,0:T(8,128)(2,1)S(1)}, bf16[128,1024]{1,0:T(8,128)(2,1)S(1)}, u32[]{:S(2)}, u32[]{:S(2)}) collective-permute-start(bf16[128,1024]{1,0:T(8,128)(2,1)S(1)} %get-tuple-element.35), channel_id=1, source_target_pairs={{0,8},{4,12},{8,0},{12,4},{1,9},{5,13},{9,1},{13,5},{2,10},{6,14},... | collective-permute-start | bytes 786440 | tf_op jit(solution)/shard_map/ppermute | solution.py:590
  195.8 19.5 %collective-permute-start.16 = (bf16[128,1024]{1,0:T(8,128)(2,1)S(1)}, bf16[128,1024]{1,0:T(8,128)(2,1)S(1)}, u32[]{:S(2)}, u32[]{:S(2)}) collective-permute-start(bf16[128,1024]{1,0:T(8,128)(2,1)S(1)} %get-tuple-element.36), channel_id=1, source_target_pairs={{0,12},{4,8},{8,4},{12,0},{1,13},{5,9},{9,5},{13,1},{2,14},{6,10},... | collective-permute-start | bytes 786440 | tf_op jit(solution)/shard_map/ppermute | solution.py:590
  197.7 3.4 %copy-start.3 = (bf16[4,1024,1024]{2,1,0:T(8,128)(2,1)S(1)}, bf16[4,1024,1024]{2,1,0:T(8,128)(2,1)}, u32[]{:S(2)}) copy-start(bf16[4,1024,1024]{2,1,0:T(8,128)(2,1)} %weight.5) | copy-start | bytes 25165828
  204.0 16.6 %collective-permute-start.23 = (bf16[128,1024]{1,0:T(8,128)(2,1)S(1)}, bf16[128,1024]{1,0:T(8,128)(2,1)S(1)}, u32[]{:S(2)}, u32[]{:S(2)}) collective-permute-start(bf16[128,1024]{1,0:T(8,128)(2,1)S(1)} %get-tuple-element.42), channel_id=1, source_target_pairs={{0,4},{4,0},{8,12},{12,8},{1,5},{5,1},{9,13},{13,9},{2,6},{6,2},{1... | collective-permute-start | bytes 786440 | tf_op jit(solution)/shard_map/ppermute | solution.py:590
  (3 other events, 2.0 us)
Sparse Core Ops, SparseCore 0:
  69.1 52.8 all-reduce.2

commit v4 on v3

--- a/solution.py
+++ b/solution.py
@@ -195,21 +195,28 @@
     return 2 * (lane & 1) + ((lane >> 1) ^ (device & 1))
 
 
-def turn(values, groups, lanes):
-    moves = [
-        (e * lanes + t, t * lanes + 2 * ((e ^ t) & 1) + (e >> 1))
-        for e in range(groups)
-        for t in range(lanes)
-    ]
-    return lax.ppermute(values, ("ep", "tp"), moves)
-
-
-def call(body, outs, scratch, flops, moved, **kwargs):
+def turn(question, keys_values, device, lane, n):
+    crosses = lambda e, t: ((e ^ t) & 1) != (t >> 1)
+    devices = [(e, t) for e in range(n) for t in range(n)]
+    swap = [(e * n + t, e * n + (t ^ 3)) for e, t in devices if crosses(e, t)]
+    crossed = lax.ppermute(question, ("ep", "tp"), swap)
+    heads = jnp.where(crosses(device, lane), lane ^ 3, lane)
+    picked = lax.dynamic_index_in_dim(keys_values, heads, 1, keepdims=False)
+    picked = jnp.transpose(picked, (1, 0, 2)).reshape(-1, question.shape[1])
+    held = jnp.where(crosses(device, lane), crossed, question)
+    moves = []
+    for e, t in devices:
+        h = t ^ 3 if crosses(e, t) else t
+        moves.append((e * n + t, h * n + 2 * ((e ^ h) & 1) + (e >> 1)))
+    return lax.ppermute(jnp.concatenate([held, picked], axis=0), ("ep", "tp"), moves)
+
+
+def call(body, outs, scratch, flops, moved, mib=40, **kwargs):
     return pl.pallas_call(
         body,
         out_shape=outs,
         **({} if scratch is None else {"scratch_shapes": scratch}),
-        compiler_params=pltpu.CompilerParams(vmem_limit_bytes=40 * 1024 * 1024),
+        compiler_params=pltpu.CompilerParams(vmem_limit_bytes=mib * 1024 * 1024),
         cost_estimate=pl.CostEstimate(flops=flops, bytes_accessed=moved, transcendentals=0),
         **kwargs,
     )
@@ -277,7 +284,7 @@
     keys[base:, :] = turned(q[first : first + length, :].astype(jnp.float32), cosine, sine).astype(
         jnp.bfloat16
     )
-    vals[base:, :] = q[first + length : first + 2 * length, :]
+    vals[base:, :] = q[first + length :, :]
     wide[...] = q[:first, :].astype(jnp.float32)
     column = lax.broadcasted_iota(jnp.int32, (1, doc_max), 1)
     allowed = [column < lens[j] for j in range(docs)]
@@ -300,8 +307,9 @@
         out[:, h * head_dim : (h + 1) * head_dim] = (mixed / denominator).astype(jnp.bfloat16)
 
 
-def attention(lens, q, pieces, heads, tables_q, tables_d):
+def attention(lens, q, pieces, tables_q, tables_d):
     length, head_dim = tables_q[0].shape
+    heads = q.shape[0] // length - 2
     rows = 5 * length
     return call(
         attention_body,
@@ -321,8 +329,12 @@
 
 def project_body(here, a, b, c, d, weight, hidden, out, rows):
     device, lane = (here[0], here[1])
-    for flip, ref in zip((0, 2, 1, 3), (a, b, c, d)):
-        rows[query_of(device, lane ^ flip)] = ref[...]
+
+    @pl.when(pl.program_id(0) == 0)
+    def _():
+        for flip, ref in zip((0, 2, 1, 3), (a, b, c, d)):
+            rows[query_of(device, lane ^ flip)] = ref[...]
+
     for s in range(4):
         base = jnp.where(device == s, hidden[...].astype(jnp.float32), 0.0)
         out[s] = (base + dot(rows[s], weight[...])).astype(jnp.bfloat16)
@@ -330,78 +342,90 @@
 
 def project(here, parts, weight, hidden):
     length, depth = parts[0].shape
+    width = weight.shape[1]
+    step = width // 4
+    whole = pl.BlockSpec((length, depth), lambda i: (0, 0))
+    column = lambda rows: pl.BlockSpec((rows, step), lambda i: (0, i))
     return call(
         project_body,
-        jax.ShapeDtypeStruct((4, length, weight.shape[1]), jnp.bfloat16),
+        jax.ShapeDtypeStruct((4, length, width), jnp.bfloat16),
         [pltpu.VMEM((4, length, depth), jnp.bfloat16)],
-        2 * 4 * length * depth * weight.shape[1],
+        2 * 4 * length * depth * width,
         4 * 1024 * 1024,
-        in_specs=[SMEM] + [VMEM] * 6,
-        out_specs=VMEM,
+        grid=(4,),
+        in_specs=[SMEM] + [whole] * 4 + [column(depth), column(length)],
+        out_specs=pl.BlockSpec((4, length, step), lambda i: (0, 0, i)),
+        mib=58,
         name="project",
     )(here, *parts, weight, hidden)
 
 
-def assemble_body(here, tokens, gain, router, scaled, stats, residual):
+def assemble_body(here, tokens, gain, router, after, scaled, stats, residual):
     length = tokens.shape[1]
-    experts = router.shape[0]
+    rows = stats.shape[0]
     device = here[0]
-    ones = jnp.ones((8, tokens.shape[2]), jnp.float32)
     residual[...] = tokens[device]
+    column = lax.broadcasted_iota(jnp.int32, (length, router.shape[1]), 1)
     for d in range(4):
         wide = tokens[device ^ d].astype(jnp.float32)
         grown = wide * gain[...]
-        scaled[d] = grown.astype(jnp.bfloat16)
-        block = slice(d * length, (d + 1) * length)
-        stats[:experts, block] = lax.dot_general(
-            router[...], grown, NT, preferred_element_type=jnp.float32,
-            precision=lax.Precision.HIGHEST,
-        )
-        stats[experts:, block] = lax.dot_general(
-            ones, wide * wide, NT, preferred_element_type=jnp.float32,
-            precision=lax.Precision.HIGHEST,
-        )
-
-
-def assemble(here, tokens, gain, router):
+        high = grown.astype(jnp.bfloat16)
+        rest = grown - high.astype(jnp.float32)
+        middle = rest.astype(jnp.bfloat16)
+        low = (rest - middle.astype(jnp.float32)).astype(jnp.bfloat16)
+        scaled[d] = high
+        logits = dot(high, router[...]) + (dot(middle, router[...]) + dot(low, router[...]))
+        squares = jnp.sum(wide * wide, axis=1, keepdims=True)
+        both = jnp.where(column == rows - 8, squares, logits)
+        stats[:, d * length : (d + 1) * length] = jnp.transpose(both)[:rows, :]
+
+
+def assemble(here, tokens, gain, router, experts, after):
     n, length, width = tokens.shape
     return call(
         assemble_body,
         [
             jax.ShapeDtypeStruct((n, length, width), jnp.bfloat16),
-            jax.ShapeDtypeStruct((router.shape[0] + 8, n * length), jnp.float32),
+            jax.ShapeDtypeStruct((experts + 8, n * length), jnp.float32),
             jax.ShapeDtypeStruct((length, width), jnp.bfloat16),
         ],
         [],
-        2 * n * length * width * 256,
+        2 * n * length * width * 384,
         3 * 1024 * 1024,
-        in_specs=[SMEM] + [VMEM] * 3,
+        in_specs=[SMEM] + [VMEM] * 3 + [pl.BlockSpec(memory_space=pl.ANY)],
         out_specs=[VMEM] * 3,
+        mib=58,
         name="assemble",
-    )(here, tokens, gain, router)
-
-
-def gate_up_body(first, order, tokens, pick, weight, *outs):
+    )(here, tokens, gain, router, after)
+
+
+def gate_up_body(first, order, tokens, pick, weight, *rest):
+    outs, rows = (rest[:-1], rest[-1])
     hid = weight.shape[3]
     capacity = pick.shape[2]
-    expert = order[pl.program_id(0)]
-    rows = jnp.concatenate(
-        [dot(pick[d, expert], tokens[d]).astype(jnp.bfloat16) for d in (first, first + 1)], axis=0
-    )
-    for g in range(2):
-        term = dot(rows, weight[0, g]).astype(jnp.bfloat16)
-        for j, out in enumerate(outs):
-
-            @pl.when(pl.program_id(0) == j)
-            def _():
-                out[:, g * hid : (g + 1) * hid] = term
+    i, g = (pl.program_id(0), pl.program_id(1))
+    expert = order[i]
+
+    @pl.when(g == 0)
+    def _():
+        for k in range(2):
+            chosen = dot(pick[first + k, expert], tokens[first + k])
+            rows[k * capacity : (k + 1) * capacity, :] = chosen.astype(jnp.bfloat16)
+
+    term = dot(rows[...], weight[0, 0]).astype(jnp.bfloat16)
+    column = pl.multiple_of(g * hid, hid)
+    for j, out in enumerate(outs):
+
+        @pl.when(i == j)
+        def _():
+            out[:, pl.ds(column, hid)] = term
 
 
 def gate_up(first, order, tokens, pick, weight):
     local, _, width, hid = weight.shape
     capacity = pick.shape[2]
     shape = jax.ShapeDtypeStruct((2 * capacity, 2 * hid), jnp.bfloat16)
-    whole = lambda rank: lambda i, order: (0,) * rank
+    whole = lambda rank: lambda i, g, order: (0,) * rank
     return call(
         functools.partial(gate_up_body, first),
         [shape] * 4,
@@ -410,14 +434,16 @@
         20 * 1024 * 1024,
         grid_spec=pltpu.PrefetchScalarGridSpec(
             num_scalar_prefetch=1,
-            grid=(local,),
+            grid=(local, 2),
             in_specs=[
                 pl.BlockSpec(tokens.shape, whole(3)),
                 pl.BlockSpec(pick.shape, whole(4)),
-                pl.BlockSpec((1, 2, width, hid), lambda i, order: (order[i], 0, 0, 0)),
+                pl.BlockSpec((1, 1, width, hid), lambda i, g, order: (order[i], g, 0, 0)),
             ],
             out_specs=[pl.BlockSpec(shape.shape, whole(2))] * 4,
+            scratch_shapes=[pltpu.VMEM((2 * capacity, width), jnp.bfloat16)],
         ),
+        mib=48,
         name="gate_up",
     )(order, tokens, pick, weight)
 
@@ -464,6 +490,7 @@
             out_specs=[pl.BlockSpec(shape.shape, whole(2))] * 2,
             scratch_shapes=[pltpu.VMEM((2, local, capacity, width), jnp.bfloat16)],
         ),
+        mib=54,
         name="down",
     )(order, *acts, spread, weight)
 
@@ -507,10 +534,8 @@
     order = (lane ^ jnp.array([0, 2, 1, 3], jnp.int32)).astype(jnp.int32)
     reach = device ^ seats
 
-    kv_head = lax.dynamic_index_in_dim(question_kv, lane, 1, keepdims=False)
-    kv_rows = jnp.transpose(kv_head, (1, 0, 2)).reshape(2 * length, head_dim)
     q_rows = turn(
-        jnp.concatenate([question_q.reshape(length * heads_here, head_dim), kv_rows], axis=0), n, n
+        question_q.reshape(length * heads_here, head_dim), question_kv, device, lane, n
     )
 
     pool = jnp.transpose(doc_kv, (0, 2, 3, 1, 4))
@@ -527,11 +552,14 @@
     tables_q = signed_tables(starts[docs_per] + jnp.arange(length, dtype=jnp.int32), head_dim)
     tables_d = signed_tables(doc_starts, head_dim)
 
-    attended = attention(lengths, q_rows, pieces, heads_here, tables_q, tables_d)
+    attended = attention(lengths, q_rows, pieces, tables_q, tables_d)
     far = lax.ppermute(attended, "tp", pairs(n, 2))
     near = lax.ppermute(attended, "tp", pairs(n, 1))
     farther = lax.ppermute(far, "tp", pairs(n, 1))
+    gain = norm_gain.astype(jnp.float32)[None, :]
+    router = jnp.pad(router_weight, ((0, 0), (0, 128 - experts)))
     partial = project(here, (attended, far, near, farther), out_proj, hidden)
+    partial, w_gate_up = lax.optimization_barrier((partial, w_gate_up))
     tokens = lax.psum(partial, "ep")
 
     ids = jnp.stack([p[2 * doc_max : 2 * doc_max + expert_ids.shape[1]] for p in pieces])
@@ -553,9 +581,7 @@
     )
     weight = jnp.transpose(w_gate_up, (0, 2, 1, 3))
 
-    scaled, stats, residual = assemble(
-        here, tokens, norm_gain.astype(jnp.float32)[None, :], router_weight.T.astype(jnp.float32)
-    )
+    scaled, stats, residual = assemble(here, tokens, gain, router, experts, weight)
     stats = stats + lax.ppermute(stats, "tp", pairs(n, 2))
     stats = stats + lax.ppermute(stats, "tp", pairs(n, 1))
     stats = stats.reshape(experts + 8, n, length)
@@ -569,28 +595,38 @@
     inv_row = jnp.sum(jnp.where(picked_mine, inv_rms[:, None, :], 0.0), axis=2)
     mix_row = jnp.sum(jnp.where(picked_mine, mix[:, None, :], 0.0), axis=2)
 
-    total = None
-    for first in (2, 0):
-        rows = slice(first, first + 2)
+    def exchange(first, order):
         terms = gate_up(first, order, scaled, pick, weight)
         for_far = lax.ppermute(terms[3], "tp", pairs(n, 1))
         for_me = lax.ppermute(terms[2], "tp", pairs(n, 1))
         chip_far = (terms[1].astype(jnp.float32) + for_far.astype(jnp.float32)).astype(jnp.bfloat16)
-        across = lax.ppermute(chip_far, "tp", pairs(n, 2))
+        return (chip_far, terms[0], for_me, lax.ppermute(chip_far, "tp", pairs(n, 2)))
+
+    def finish(first, order, mine, for_me, across):
+        rows = slice(first, first + 2)
         summed = (
-            terms[0].astype(jnp.float32) + for_me.astype(jnp.float32) + across.astype(jnp.float32)
+            mine.astype(jnp.float32) + for_me.astype(jnp.float32) + across.astype(jnp.float32)
         ) * inv_row[rows].reshape(-1, 1)
         act = jax.nn.silu(summed[:, :hid]) * summed[:, hid:] * mix_row[rows].reshape(-1, 1)
         act = act.astype(jnp.bfloat16)
         far = lax.ppermute(act, "tp", pairs(n, 2))
         near = lax.ppermute(act, "tp", pairs(n, 1))
         farther = lax.ppermute(far, "tp", pairs(n, 1))
-        parts = down(order, (act, far, near, farther), spread[rows], w_down)
-        for d, part in zip((first, first + 1), parts):
-            back = lax.ppermute(part, "ep", pairs(n, d)) if d else part
-            back = back.astype(jnp.float32)
-            total = back if total is None else total + back
-    return (residual.astype(jnp.float32) + total).astype(jnp.bfloat16)
+        return down(order, (act, far, near, farther), spread[rows], w_down)
+
+    chip_far, *ahead = exchange(2, order)
+    order, _ = lax.optimization_barrier((order, chip_far))
+    _, *behind = exchange(0, order)
+    away_2, away_3 = finish(2, order, *ahead)
+    behind[0], away_2, away_3 = lax.optimization_barrier((behind[0], away_2, away_3))
+    away_2 = lax.ppermute(away_2, "ep", pairs(n, 2))
+    away_3 = lax.ppermute(away_3, "ep", pairs(n, 3))
+    mine, away_1 = finish(0, order, *behind)
+    away_1 = lax.ppermute(away_1, "ep", pairs(n, 1))
+    total = residual.astype(jnp.float32)
+    for part in (mine, away_2, away_3, away_1):
+        total = total + part.astype(jnp.float32)
+    return total.astype(jnp.bfloat16)
 
 
 def solution(mesh):

time: 229 us -> 218 us (0.952)
  waiting for transfers between devices: 110 us -> 72.4 us
  starting transfers between devices: 19.6 us -> 34.8 us
  Pallas kernels: 34.9 us -> 47.9 us
    unnamed x23 -> x41, local copies, waits for them, and re-layouts: 28.1 us -> 6.16 us
    optimization_barrier x0 -> x1, local copies, waits for them, and re-layouts: none -> 16.5 us  [per_device_square(): partial, w_gate_up = lax.optimization_barrier((partial, w_gate_up))]
    ppermute x14 -> x17, waiting for transfers between devices: 45.2 us -> 31.2 us  [the longest x2 14 us: finish(): far = lax.ppermute(act, 'tp', pairs(n, 2))]
    psum x1, waiting for transfers between devices: 50.5 us -> 36.8 us  [per_device_square(): tokens = lax.psum(partial, 'ep')]
    ppermute x1, starting transfers between devices: 0.07 us -> 10.6 us  [per_device_square(): far = lax.ppermute(attended, 'tp', pairs(n, 2))]
    pallas_call x2, Pallas kernels: 5.86 us -> 14.1 us  [down(): call(down_body, [shape] * 2, None, 2 * local * 2 * capacity * width * hid...]
    ppermute x3, waiting for transfers between devices: 7.71 us -> 0.01 us  [per_device_square(): lax.ppermute(pieces[d], 'ep', pairs(n, d))]
    ppermute x1, waiting for transfers between devices: 6.77 us -> 3.03 us  [per_device_square(): far = lax.ppermute(attended, 'tp', pairs(n, 2))]
  transfers between devices with their start and end apart: 25 -> 26, of which waited for: 10 -> 9; matrix products, arithmetic and copies ran while one was open for 16% -> 18% of each run, Pallas kernels for 11% -> 17%
where the time goes in v4:
time: 218 us; the launch traced here: 216 us
  waiting for transfers between devices  72.4 us (33%)
  Pallas kernels  47.9 us (22%)
  starting transfers between devices  34.8 us (16%)
  local copies, waits for them, and re-layouts  32 us (15%)
  other arithmetic  15.3 us (7%)
  between operations  13.8 us (6%)
    psum x1, waiting for transfers between devices, per_device_square(): tokens = lax.psum(partial, 'ep')  36.8 us
    pallas_call x2, Pallas kernels, gate_up(): call(functools.partial(gate_up_body, first), [shape] * 4, None, 2 * local...  21.5 us
    optimization_barrier x1, local copies, waits for them, and re-layouts, per_device_square(): partial, w_gate_up = lax.optimization_barrier((partial, w_gate_up))  16.5 us
    pallas_call x2, Pallas kernels, down(): call(down_body, [shape] * 2, None, 2 * local * 2 * capacity * width * hid...  14.1 us
    ppermute x2, waiting for transfers between devices, finish(): far = lax.ppermute(act, 'tp', pairs(n, 2))  14 us
    ppermute x1, starting transfers between devices, per_device_square(): far = lax.ppermute(attended, 'tp', pairs(n, 2))  10.6 us
    ppermute x1, waiting for transfers between devices, per_device_square(): away_2 = lax.ppermute(away_2, 'ep', pairs(n, 2))  9.92 us
    ppermute x3, starting transfers between devices, per_device_square(): lax.ppermute(pieces[d], 'ep', pairs(n, d))  7.84 us
  transfers between devices with their start and end apart: 26, of which 9 were waited for; matrix products, arithmetic and copies ran while one was open for 18% of the time, Pallas kernels for 17%

profile of v4, /device:TPU:0, one launch (start us, length us, event | category | flops | bytes accessed | tf_op | source)
XLA Modules:
  0.0 216.4 jit_solution(5236638537230787887)
XLA Ops:
  10.6 5.3 %collective-permute-start.2 = (bf16[272,128]{1,0:T(8,128)(2,1)S(1)}, bf16[272,128]{1,0:T(8,128)(2,1)S(1)}, u32[]{:S(2)}, u32[]{:S(2)}) collective-permute-start(bf16[272,128]{1,0:T(8,128)(2,1)S(1)} %get-tuple-element.31), channel_id=1, source_target_pairs={{0,4},{4,0},{8,12},{12,8},{1,5},{5,1},{9,13},{13,9},{2,6},{6,2},{1... | collective-permute-start | bytes 208904 | tf_op jit(solution)/shard_map/ppermute | solution.py:544
  15.8 2.6 %collective-permute-start.3 = (bf16[272,128]{1,0:T(8,128)(2,1)S(1)}, bf16[272,128]{1,0:T(8,128)(2,1)S(1)}, u32[]{:S(2)}, u32[]{:S(2)}) collective-permute-start(bf16[272,128]{1,0:T(8,128)(2,1)S(1)} %get-tuple-element.32), channel_id=1, source_target_pairs={{0,8},{4,12},{8,0},{12,4},{1,9},{5,13},{9,1},{13,5},{2,10},{6,14},... | collective-permute-start | bytes 208904 | tf_op jit(solution)/shard_map/ppermute | solution.py:544
  21.1 1.3 gather_fusion
  25.7 3.4 %attention.1.a = bf16[128,1024]{1,0:T(8,128)(2,1)S(1)} custom-call(s32[4]{0:T(128)S(1)} %get-tuple-element.58.lens, bf16[1280,128]{1,0:T(8,128)(2,1)S(1)} %collective-permute-done.1.q, bf16[272,128]{1,0:T(8,128)(2,1)S(1)} %get-tuple-element.30.c0, bf16[272,128]{1,0:T(8,128)(2,1)S(1)} %collective-permute-done.2.c1, ...), custom_call_target="tpu_custom_call" | custom-call | flops 1342177280 | bytes 4194304 | tf_op jit(solution)/shard_map/attention/pallas_call | solution.py:314
  29.1 10.6 %collective-permute-start.5 = (bf16[128,1024]{1,0:T(8,128)(2,1)S(1)}, bf16[128,1024]{1,0:T(8,128)(2,1)S(1)}, u32[]{:S(2)}, u32[]{:S(2)}) collective-permute-start(bf16[128,1024]{1,0:T(8,128)(2,1)S(1)} %attention.1.a), channel_id=1, source_target_pairs={{0,2},{1,3},{2,0},{3,1},{4,6},{5,7},{6,4},{7,5},{8,10},{9,11},{10,... | collective-permute-start | bytes 786440 | tf_op jit(solution)/shard_map/ppermute | solution.py:556
  40.3 1.8 collective-permute-start.6
  42.2 3.0 %collective-permute-done.5.b = bf16[128,1024]{1,0:T(8,128)(2,1)S(1)} collective-permute-done((bf16[128,1024]{1,0:T(8,128)(2,1)S(1)}, bf16[128,1024]{1,0:T(8,128)(2,1)S(1)}, u32[]{:S(2)}, u32[]{:S(2)}) %collective-permute-start.5) | collective-permute-done | bytes 262176 | tf_op jit(solution)/shard_map/ppermute | solution.py:556
  45.2 1.4 collective-permute-start.7
  48.4 1.3 broadcast_in_dim.90
  51.7 4.9 %project.1 = bf16[4,128,1024]{2,1,0:T(8,128)(2,1)} custom-call(s32[2]{0:T(128)} %copy-done.6, bf16[128,1024]{1,0:T(8,128)(2,1)} %copy-done.4, bf16[128,1024]{1,0:T(8,128)(2,1)} %copy-done.10, bf16[128,1024]{1,0:T(8,128)(2,1)} %copy-done.12, bf16[128,1024]{1,0:T(8,128)(2,1)} %copy-done.13, bf16[1024,1024]{1,0:T(8,128)(2,1)} %weight.3, bf16[128,1024]{1,0:T(8,128)(2,1)} %hidden.1), custom_call_target="tpu_custom_call" | custom-call | flops 1073741824 | bytes 4194304 | tf_op jit(solution)/shard_map/project/pallas_call | solution.py:349
  57.0 16.5 %copy.48 = bf16[4,1024,2,1024]{3,1,2,0:T(8,128)(2,1)} copy(bf16[4,1024,2,1024]{3,2,1,0:T(2,128)(2,1)} %param.24) | data formatting | bytes 33554432 | tf_op jit(solution)/shard_map/optimization_barrier | solution.py:562
  73.6 36.8 %all-reduce.4.cloned.1.call-done.tokens = bf16[4,128,1024]{2,1,0:T(8,128)(2,1)} async-done(((bf16[4,128,1024]{2,1,0:T(8,128)(2,1)}), bf16[4,128,1024]{2,1,0:T(8,128)(2,1)}) %all-reduce.4.cloned.1.call-update) | async-done | bytes 1048592 | tf_op jit(solution)/shard_map/psum | solution.py:563
  110.4 3.4 %assemble.1 = (bf16[4,128,1024]{2,1,0:T(8,128)(2,1)}, f32[24,512]{1,0:T(8,128)}, bf16[128,1024]{1,0:T(8,128)(2,1)}) custom-call(s32[2]{0:T(128)} %copy-done.6, bf16[4,128,1024]{2,1,0:T(8,128)(2,1)} %all-reduce.4.cloned.1.call-done.tokens, f32[1,1024]{1,0:T(1,128)} %bitcast.93, bf16[1024,128]{1,0:T(8,128)(2,1)} %pad.9.router, bf16[4,2,1024,1024]{3,2,1,0:T(8,128)(2,1)} %bitcast.86), custom_call_target="tpu_custom_call" | custom-call | flops 402653184 | bytes 3145728 | tf_op jit(solution)/shard_map/assemble/pallas_call | solution.py:385
  113.7 1.5 collective-permute-start.11
  116.6 1.4 collective-permute-done.11
  120.1 11.1 %gate_up.2 = (bf16[128,2048]{1,0:T(8,128)(2,1)S(1)}, bf16[128,2048]{1,0:T(8,128)(2,1)S(1)}, bf16[128,2048]{1,0:T(8,128)(2,1)}, bf16[128,2048]{1,0:T(8,128)(2,1)S(1)}) custom-call(s32[4]{0:T(128)S(1)} %broadcast_xor_fusion.order, bf16[4,128,1024]{2,1,0:T(8,128)(2,1)S(1)} %copy-done.2, bf16[4,4,64,128]{3,2,1,0:T(8,128)(2,1)S(1)} %get-tuple-element.62.pick, ...), custom_call_target="tpu_custom_call" | custom-call | flops 2147483648 | bytes 20971520 | tf_op jit(solution)/shard_map/gate_up/pallas_call | solution.py:429
  132.0 1.8 collective-permute-done.8
  134.8 1.5 collective-permute-start.10
  138.1 10.4 %gate_up.3 = (bf16[128,2048]{1,0:T(8,128)(2,1)S(1)}, bf16[128,2048]{1,0:T(8,128)(2,1)S(1)}, bf16[128,2048]{1,0:T(8,128)(2,1)S(1)}, bf16[128,2048]{1,0:T(8,128)(2,1)S(1)}) custom-call(s32[4]{0:T(128)S(1)} %broadcast_xor_fusion.order, bf16[4,128,1024]{2,1,0:T(8,128)(2,1)S(1)} %copy-done.3, bf16[4,4,64,128]{3,2,1,0:T(8,128)(2,1)S(1)} %get-tuple-element.62.pick, ...), custom_call_target="tpu_custom_call" | custom-call | flops 2147483648 | bytes 20971520 | tf_op jit(solution)/shard_map/gate_up/pallas_call | solution.py:429
  149.3 1.4 add_multiply_fusion.1
  151.0 1.5 collective-permute-start.13
  153.3 7.0 %collective-permute-done.13.b = bf16[128,1024]{1,0:T(8,128)(2,1)S(1)} collective-permute-done((bf16[128,1024]{1,0:T(8,128)(2,1)S(1)}, bf16[128,1024]{1,0:T(8,128)(2,1)S(1)}, u32[]{:S(2)}, u32[]{:S(2)}) %collective-permute-start.13) | collective-permute-done | bytes 262176 | tf_op jit(solution)/shard_map/ppermute | solution.py:612
  163.7 7.1 %down.2 = (bf16[128,1024]{1,0:T(8,128)(2,1)}, bf16[128,1024]{1,0:T(8,128)(2,1)}) custom-call(s32[4]{0:T(128)} %copy-done.5, bf16[128,1024]{1,0:T(8,128)(2,1)} %copy-done.8, bf16[128,1024]{1,0:T(8,128)(2,1)} %copy-done.11, bf16[128,1024]{1,0:T(8,128)(2,1)} %collective-permute-done.14.c, bf16[128,1024]{1,0:T(8,128)(2,1)} %collective-permute-done.15.d, ...), custom_call_target="tpu_custom_call" | custom-call | flops 1073741824 | bytes 10485760 | tf_op jit(solution)/shard_map/down/pallas_call | solution.py:476
  170.8 1.3 add_multiply_fusion
  172.3 1.6 collective-permute-start.19
  174.0 7.0 %collective-permute-done.19.b = bf16[128,1024]{1,0:T(8,128)(2,1)S(1)} collective-permute-done((bf16[128,1024]{1,0:T(8,128)(2,1)S(1)}, bf16[128,1024]{1,0:T(8,128)(2,1)S(1)}, u32[]{:S(2)}, u32[]{:S(2)}) %collective-permute-start.19) | collective-permute-done | bytes 262176 | tf_op jit(solution)/shard_map/ppermute | solution.py:612
  181.0 1.8 collective-permute-start.22
  182.8 1.9 collective-permute-start.23
  185.5 7.1 %down.3 = (bf16[128,1024]{1,0:T(8,128)(2,1)}, bf16[128,1024]{1,0:T(8,128)(2,1)}) custom-call(s32[4]{0:T(128)} %copy-done.5, bf16[128,1024]{1,0:T(8,128)(2,1)} %copy-done.9, bf16[128,1024]{1,0:T(8,128)(2,1)} %copy-done.14, bf16[128,1024]{1,0:T(8,128)(2,1)} %copy-done.15, bf16[128,1024]{1,0:T(8,128)(2,1)} %copy-done.16, ...), custom_call_target="tpu_custom_call" | custom-call | flops 1073741824 | bytes 10485760 | tf_op jit(solution)/shard_map/down/pallas_call | solution.py:476
  192.5 9.9 %collective-permute-done.22 = bf16[128,1024]{1,0:T(8,128)(2,1)S(1)} collective-permute-done((bf16[128,1024]{1,0:T(8,128)(2,1)}, bf16[128,1024]{1,0:T(8,128)(2,1)S(1)}, u32[]{:S(2)}, u32[]{:S(2)}) %collective-permute-start.22) | collective-permute-done | bytes 262176 | tf_op jit(solution)/shard_map/ppermute | solution.py:622
  202.5 5.2 %collective-permute-done.24 = bf16[128,1024]{1,0:T(8,128)(2,1)S(1)} collective-permute-done((bf16[128,1024]{1,0:T(8,128)(2,1)}, bf16[128,1024]{1,0:T(8,128)(2,1)S(1)}, u32[]{:S(2)}, u32[]{:S(2)}) %collective-permute-start.24) | collective-permute-done | bytes 262176 | tf_op jit(solution)/shard_map/ppermute | solution.py:625
  207.7 1.9 add_convert_fusion.2
  (133 shorter events, 28.0 us)
Async XLA Ops:
  6.5 103.8 %all-reduce.4.cloned.1.call-start = ((), (), s32[]{:S(2)}) async-start(), calls=%async_computation | async-start | bytes 2097152 | tf_op jit(solution)/shard_map/psum | solution.py:563
  6.5 17.2 %collective-permute-start = (bf16[1024,128]{1,0:T(8,128)(2,1)}, bf16[1024,128]{1,0:T(8,128)(2,1)S(1)}, u32[]{:S(2)}, u32[]{:S(2)}) collective-permute-start(bf16[1024,128]{1,0:T(8,128)(2,1)} %bitcast.92), channel_id=1, source_target_pairs={{1,2},{2,1},{4,7},{7,4},{9,10},{10,9},{12,15},{15,12},{17,18},{18,... | collective-permute-start | bytes 786440 | tf_op jit(solution)/shard_map/ppermute | solution.py:202
  9.3 41.0 %copy-start.6 = (s32[2]{0:T(128)}, s32[2]{0:T(128)S(1)}, u32[]{:S(2)}) copy-start(s32[2]{0:T(128)S(1)} %pad_add_fusion.here) | copy-start | bytes 28
  10.6 15.1 %collective-permute-start.2 = (bf16[272,128]{1,0:T(8,128)(2,1)S(1)}, bf16[272,128]{1,0:T(8,128)(2,1)S(1)}, u32[]{:S(2)}, u32[]{:S(2)}) collective-permute-start(bf16[272,128]{1,0:T(8,128)(2,1)S(1)} %get-tuple-element.31), channel_id=1, source_target_pairs={{0,4},{4,0},{8,12},{12,8},{1,5},{5,1},{9,13},{13,9},{2,6},{6,2},{1... | collective-permute-start | bytes 208904 | tf_op jit(solution)/shard_map/ppermute | solution.py:544
  15.8 9.9 %collective-permute-start.3 = (bf16[272,128]{1,0:T(8,128)(2,1)S(1)}, bf16[272,128]{1,0:T(8,128)(2,1)S(1)}, u32[]{:S(2)}, u32[]{:S(2)}) collective-permute-start(bf16[272,128]{1,0:T(8,128)(2,1)S(1)} %get-tuple-element.32), channel_id=1, source_target_pairs={{0,8},{4,12},{8,0},{12,4},{1,9},{5,13},{9,1},{13,5},{2,10},{6,14},... | collective-permute-start | bytes 208904 | tf_op jit(solution)/shard_map/ppermute | solution.py:544
  18.4 7.3 %collective-permute-start.4 = (bf16[272,128]{1,0:T(8,128)(2,1)S(1)}, bf16[272,128]{1,0:T(8,128)(2,1)S(1)}, u32[]{:S(2)}, u32[]{:S(2)}) collective-permute-start(bf16[272,128]{1,0:T(8,128)(2,1)S(1)} %get-tuple-element.33), channel_id=1, source_target_pairs={{0,12},{4,8},{8,4},{12,0},{1,13},{5,9},{9,5},{13,1},{2,14},{6,10},... | collective-permute-start | bytes 208904 | tf_op jit(solution)/shard_map/ppermute | solution.py:544
  24.8 0.9 collective-permute-start.1
  29.1 21.2 %copy-start.4 = (bf16[128,1024]{1,0:T(8,128)(2,1)}, bf16[128,1024]{1,0:T(8,128)(2,1)S(1)}, u32[]{:S(2)}) copy-start(bf16[128,1024]{1,0:T(8,128)(2,1)S(1)} %attention.1.a) | copy-start | bytes 786436
  29.1 16.1 %collective-permute-start.5 = (bf16[128,1024]{1,0:T(8,128)(2,1)S(1)}, bf16[128,1024]{1,0:T(8,128)(2,1)S(1)}, u32[]{:S(2)}, u32[]{:S(2)}) collective-permute-start(bf16[128,1024]{1,0:T(8,128)(2,1)S(1)} %attention.1.a), channel_id=1, source_target_pairs={{0,2},{1,3},{2,0},{3,1},{4,6},{5,7},{6,4},{7,5},{8,10},{9,11},{10,... | collective-permute-start | bytes 786440 | tf_op jit(solution)/shard_map/ppermute | solution.py:556
  40.3 97.7 %copy-start.5 = (s32[4]{0:T(128)}, s32[4]{0:T(128)S(1)}, u32[]{:S(2)}) copy-start(s32[4]{0:T(128)S(1)} %broadcast_xor_fusion.order) | copy-start | bytes 52
  40.3 9.9 %collective-permute-start.6 = (bf16[128,1024]{1,0:T(8,128)(2,1)S(1)}, bf16[128,1024]{1,0:T(8,128)(2,1)S(1)}, u32[]{:S(2)}, u32[]{:S(2)}) collective-permute-start(bf16[128,1024]{1,0:T(8,128)(2,1)S(1)} %attention.1.a), channel_id=1, source_target_pairs={{0,1},{1,0},{2,3},{3,2},{4,5},{5,4},{6,7},{7,6},{8,9},{9,8},{10,11... | collective-permute-start | bytes 786440 | tf_op jit(solution)/shard_map/ppermute | solution.py:557
  45.2 5.1 %collective-permute-start.7 = (bf16[128,1024]{1,0:T(8,128)(2,1)S(1)}, bf16[128,1024]{1,0:T(8,128)(2,1)S(1)}, u32[]{:S(2)}, u32[]{:S(2)}) collective-permute-start(bf16[128,1024]{1,0:T(8,128)(2,1)S(1)} %collective-permute-done.5.b), channel_id=1, source_target_pairs={{0,1},{1,0},{2,3},{3,2},{4,5},{5,4},{6,7},{7,6},{8,9},{9,8},{10,11... | collective-permute-start | bytes 786440 | tf_op jit(solution)/shard_map/ppermute | solution.py:558
  113.7 24.4 %copy-start.3 = (bf16[4,128,1024]{2,1,0:T(8,128)(2,1)S(1)}, bf16[4,128,1024]{2,1,0:T(8,128)(2,1)}, u32[]{:S(2)}) copy-start(bf16[4,128,1024]{2,1,0:T(8,128)(2,1)} %get-tuple-element.37.tokens) | copy-start | bytes 3145732
  113.7 4.3 %collective-permute-start.11 = (f32[24,512]{1,0:T(8,128)}, f32[24,512]{1,0:T(8,128)S(1)}, u32[]{:S(2)}, u32[]{:S(2)}) collective-permute-start(f32[24,512]{1,0:T(8,128)} %get-tuple-element.44), channel_id=1, source_target_pairs={{0,2},{1,3},{2,0},{3,1},{4,6},{5,7},{6,4},{7,5},{8,10},{9,11},{10,... | collective-permute-start | bytes 147464 | tf_op jit(solution)/shard_map/ppermute | solution.py:585
  118.8 12.9 %collective-permute-start.12 = (f32[24,512]{1,0:T(8,128)S(1)}, f32[24,512]{1,0:T(8,128)S(1)}, u32[]{:S(2)}, u32[]{:S(2)}) collective-permute-start(f32[24,512]{1,0:T(8,128)S(1)} %add.135), channel_id=1, source_target_pairs={{0,1},{1,0},{2,3},{3,2},{4,5},{5,4},{6,7},{7,6},{8,9},{9,8},{10,11... | collective-permute-start | bytes 147464 | tf_op jit(solution)/shard_map/ppermute | solution.py:586
  131.2 2.7 %collective-permute-start.8 = (bf16[128,2048]{1,0:T(8,128)(2,1)S(1)}, bf16[128,2048]{1,0:T(8,128)(2,1)S(1)}, u32[]{:S(2)}, u32[]{:S(2)}) collective-permute-start(bf16[128,2048]{1,0:T(8,128)(2,1)S(1)} %get-tuple-element.39), channel_id=1, source_target_pairs={{0,1},{1,0},{2,3},{3,2},{4,5},{5,4},{6,7},{7,6},{8,9},{9,8},{10,11... | collective-permute-start | bytes 1572872 | tf_op jit(solution)/shard_map/ppermute | solution.py:600
  131.7 17.4 %collective-permute-start.9 = (bf16[128,2048]{1,0:T(8,128)(2,1)}, bf16[128,2048]{1,0:T(8,128)(2,1)}, u32[]{:S(2)}, u32[]{:S(2)}) collective-permute-start(bf16[128,2048]{1,0:T(8,128)(2,1)} %get-tuple-element.43), channel_id=1, source_target_pairs={{0,1},{1,0},{2,3},{3,2},{4,5},{5,4},{6,7},{7,6},{8,9},{9,8},{10,11... | collective-permute-start | bytes 1572872 | tf_op jit(solution)/shard_map/ppermute | solution.py:601
  134.8 14.5 %collective-permute-start.10 = (bf16[128,2048]{1,0:T(8,128)(2,1)}, bf16[128,2048]{1,0:T(8,128)(2,1)}, u32[]{:S(2)}, u32[]{:S(2)}) collective-permute-start(bf16[128,2048]{1,0:T(8,128)(2,1)} %add_convert_fusion.1), channel_id=1, source_target_pairs={{0,2},{1,3},{2,0},{3,1},{4,6},{5,7},{6,4},{7,5},{8,10},{9,11},{10,... | collective-permute-start | bytes 1572872 | tf_op jit(solution)/shard_map/ppermute | solution.py:603
  138.1 71.4 %copy-start.1 = (bf16[128,4,2,128]{3,2,1,0:T(2,128)(2,1)S(1)}, bf16[128,4,2,128]{3,2,1,0:T(2,128)(2,1)}, u32[]{:S(2)}) copy-start(bf16[128,4,2,128]{3,2,1,0:T(2,128)(2,1)} %param.15) | copy-start | bytes 786436
  148.4 59.2 %copy-start.17 = (bf16[128,1024]{1,0:T(8,128)(2,1)S(1)}, bf16[128,1024]{1,0:T(8,128)(2,1)}, u32[]{:S(2)}) copy-start(bf16[128,1024]{1,0:T(8,128)(2,1)} %get-tuple-element.36) | copy-start | bytes 786436
  148.5 4.1 %collective-permute-start.17 = (bf16[128,2048]{1,0:T(8,128)(2,1)S(1)}, bf16[128,2048]{1,0:T(8,128)(2,1)S(1)}, u32[]{:S(2)}, u32[]{:S(2)}) collective-permute-start(bf16[128,2048]{1,0:T(8,128)(2,1)S(1)} %get-tuple-element.50), channel_id=1, source_target_pairs={{0,1},{1,0},{2,3},{3,2},{4,5},{5,4},{6,7},{7,6},{8,9},{9,8},{10,11... | collective-permute-start | bytes 1572872 | tf_op jit(solution)/shard_map/ppermute | solution.py:600
  148.6 22.2 %collective-permute-start.16 = (bf16[128,2048]{1,0:T(8,128)(2,1)S(1)}, bf16[128,2048]{1,0:T(8,128)(2,1)}, u32[]{:S(2)}, u32[]{:S(2)}) collective-permute-start(bf16[128,2048]{1,0:T(8,128)(2,1)S(1)} %get-tuple-element.48), channel_id=1, source_target_pairs={{0,1},{1,0},{2,3},{3,2},{4,5},{5,4},{6,7},{7,6},{8,9},{9,8},{10,11... | collective-permute-start | bytes 1572872 | tf_op jit(solution)/shard_map/ppermute | solution.py:601
  151.0 9.3 %collective-permute-start.13 = (bf16[128,1024]{1,0:T(8,128)(2,1)S(1)}, bf16[128,1024]{1,0:T(8,128)(2,1)S(1)}, u32[]{:S(2)}, u32[]{:S(2)}) collective-permute-start(bf16[128,1024]{1,0:T(8,128)(2,1)S(1)} %fusion.7.a), channel_id=1, source_target_pairs={{0,2},{1,3},{2,0},{3,1},{4,6},{5,7},{6,4},{7,5},{8,10},{9,11},{10,... | collective-permute-start | bytes 786440 | tf_op jit(solution)/shard_map/ppermute | solution.py:612
  152.5 11.2 %collective-permute-start.14 = (bf16[128,1024]{1,0:T(8,128)(2,1)S(1)}, bf16[128,1024]{1,0:T(8,128)(2,1)}, u32[]{:S(2)}, u32[]{:S(2)}) collective-permute-start(bf16[128,1024]{1,0:T(8,128)(2,1)S(1)} %fusion.7.a), channel_id=1, source_target_pairs={{0,1},{1,0},{2,3},{3,2},{4,5},{5,4},{6,7},{7,6},{8,9},{9,8},{10,11... | collective-permute-start | bytes 786440 | tf_op jit(solution)/shard_map/ppermute | solution.py:613
  152.6 18.1 %collective-permute-start.18 = (bf16[128,2048]{1,0:T(8,128)(2,1)S(1)}, bf16[128,2048]{1,0:T(8,128)(2,1)S(1)}, u32[]{:S(2)}, u32[]{:S(2)}) collective-permute-start(bf16[128,2048]{1,0:T(8,128)(2,1)S(1)} %add_convert_fusion), channel_id=1, source_target_pairs={{0,2},{1,3},{2,0},{3,1},{4,6},{5,7},{6,4},{7,5},{8,10},{9,11},{10,... | collective-permute-start | bytes 1572872 | tf_op jit(solution)/shard_map/ppermute | solution.py:603
  160.2 3.5 %collective-permute-start.15 = (bf16[128,1024]{1,0:T(8,128)(2,1)S(1)}, bf16[128,1024]{1,0:T(8,128)(2,1)}, u32[]{:S(2)}, u32[]{:S(2)}) collective-permute-start(bf16[128,1024]{1,0:T(8,128)(2,1)S(1)} %collective-permute-done.13.b), channel_id=1, source_target_pairs={{0,1},{1,0},{2,3},{3,2},{4,5},{5,4},{6,7},{7,6},{8,9},{9,8},{10,11... | collective-permute-start | bytes 786440 | tf_op jit(solution)/shard_map/ppermute | solution.py:614
  172.3 8.7 %collective-permute-start.19 = (bf16[128,1024]{1,0:T(8,128)(2,1)S(1)}, bf16[128,1024]{1,0:T(8,128)(2,1)S(1)}, u32[]{:S(2)}, u32[]{:S(2)}) collective-permute-start(bf16[128,1024]{1,0:T(8,128)(2,1)S(1)} %fusion.5.a), channel_id=1, source_target_pairs={{0,2},{1,3},{2,0},{3,1},{4,6},{5,7},{6,4},{7,5},{8,10},{9,11},{10,... | collective-permute-start | bytes 786440 | tf_op jit(solution)/shard_map/ppermute | solution.py:612
  173.8 10.8 %collective-permute-start.20 = (bf16[128,1024]{1,0:T(8,128)(2,1)S(1)}, bf16[128,1024]{1,0:T(8,128)(2,1)S(1)}, u32[]{:S(2)}, u32[]{:S(2)}) collective-permute-start(bf16[128,1024]{1,0:T(8,128)(2,1)S(1)} %fusion.5.a), channel_id=1, source_target_pairs={{0,1},{1,0},{2,3},{3,2},{4,5},{5,4},{6,7},{7,6},{8,9},{9,8},{10,11... | collective-permute-start | bytes 786440 | tf_op jit(solution)/shard_map/ppermute | solution.py:613
  181.0 3.7 %collective-permute-start.21 = (bf16[128,1024]{1,0:T(8,128)(2,1)S(1)}, bf16[128,1024]{1,0:T(8,128)(2,1)S(1)}, u32[]{:S(2)}, u32[]{:S(2)}) collective-permute-start(bf16[128,1024]{1,0:T(8,128)(2,1)S(1)} %collective-permute-done.19.b), channel_id=1, source_target_pairs={{0,1},{1,0},{2,3},{3,2},{4,5},{5,4},{6,7},{7,6},{8,9},{9,8},{10,11... | collective-permute-start | bytes 786440 | tf_op jit(solution)/shard_map/ppermute | solution.py:614
  181.0 21.5 %collective-permute-start.22 = (bf16[128,1024]{1,0:T(8,128)(2,1)}, bf16[128,1024]{1,0:T(8,128)(2,1)S(1)}, u32[]{:S(2)}, u32[]{:S(2)}) collective-permute-start(bf16[128,1024]{1,0:T(8,128)(2,1)} %get-tuple-element.52), channel_id=1, source_target_pairs={{0,8},{4,12},{8,0},{12,4},{1,9},{5,13},{9,1},{13,5},{2,10},{6,14},... | collective-permute-start | bytes 786440 | tf_op jit(solution)/shard_map/ppermute | solution.py:622
  182.8 19.7 %collective-permute-start.23 = (bf16[128,1024]{1,0:T(8,128)(2,1)}, bf16[128,1024]{1,0:T(8,128)(2,1)S(1)}, u32[]{:S(2)}, u32[]{:S(2)}) collective-permute-start(bf16[128,1024]{1,0:T(8,128)(2,1)} %get-tuple-element.53), channel_id=1, source_target_pairs={{0,12},{4,8},{8,4},{12,0},{1,13},{5,9},{9,5},{13,1},{2,14},{6,10},... | collective-permute-start | bytes 786440 | tf_op jit(solution)/shard_map/ppermute | solution.py:623
  192.5 15.1 %collective-permute-start.24 = (bf16[128,1024]{1,0:T(8,128)(2,1)}, bf16[128,1024]{1,0:T(8,128)(2,1)S(1)}, u32[]{:S(2)}, u32[]{:S(2)}) collective-permute-start(bf16[128,1024]{1,0:T(8,128)(2,1)} %get-tuple-element.54), channel_id=1, source_target_pairs={{0,4},{4,0},{8,12},{12,8},{1,5},{5,1},{9,13},{13,9},{2,6},{6,2},{1... | collective-permute-start | bytes 786440 | tf_op jit(solution)/shard_map/ppermute | solution.py:625
  (13 other events, 70.9 us)
Sparse Core Ops, SparseCore 0:
  56.7 53.5 all-reduce.3

commit v5 on v3

--- a/solution.py
+++ b/solution.py
@@ -195,22 +195,30 @@
     return 2 * (lane & 1) + ((lane >> 1) ^ (device & 1))
 
 
-def turn(values, groups, lanes):
-    moves = [
-        (e * lanes + t, t * lanes + 2 * ((e ^ t) & 1) + (e >> 1))
-        for e in range(groups)
-        for t in range(lanes)
-    ]
-    return lax.ppermute(values, ("ep", "tp"), moves)
-
-
-def call(body, outs, scratch, flops, moved, **kwargs):
+def turn(question, keys_values, device, lane, n, meanwhile):
+    crosses = lambda e, t: ((e ^ t) & 1) != (t >> 1)
+    devices = [(e, t) for e in range(n) for t in range(n)]
+    swap = [(e * n + t, e * n + (t ^ 3)) for e, t in devices if crosses(e, t)]
+    crossed = lax.ppermute(question, ("ep", "tp"), swap)
+    crossed, *meanwhile = lax.optimization_barrier((crossed, *meanwhile))
+    heads = jnp.where(crosses(device, lane), lane ^ 3, lane)
+    picked = lax.dynamic_index_in_dim(keys_values, heads, 1, keepdims=False)
+    picked = jnp.transpose(picked, (1, 0, 2)).reshape(-1, question.shape[1])
+    held = jnp.where(crosses(device, lane), crossed, question)
+    moves = []
+    for e, t in devices:
+        h = t ^ 3 if crosses(e, t) else t
+        moves.append((e * n + t, h * n + 2 * ((e ^ h) & 1) + (e >> 1)))
+    return (lax.ppermute(jnp.concatenate([held, picked], axis=0), ("ep", "tp"), moves), meanwhile)
+
+
+def call(body, outs, scratch, **kwargs):
     return pl.pallas_call(
         body,
         out_shape=outs,
         **({} if scratch is None else {"scratch_shapes": scratch}),
-        compiler_params=pltpu.CompilerParams(vmem_limit_bytes=40 * 1024 * 1024),
-        cost_estimate=pl.CostEstimate(flops=flops, bytes_accessed=moved, transcendentals=0),
+        compiler_params=pltpu.CompilerParams(vmem_limit_bytes=20 * 1024 * 1024),
+        cost_estimate=pl.CostEstimate(flops=1 << 20, bytes_accessed=1 << 18, transcendentals=0),
         **kwargs,
     )
 
@@ -222,6 +230,19 @@
 
 def dot(a, b):
     return jnp.dot(a, b, preferred_element_type=jnp.float32)
+
+
+def document_slots(here, query_docs, pool_dev):
+    device, lane = (here[0], here[1])
+    query = query_of(device, lane)
+    slots = []
+    for d in range(4):
+        slot = jnp.int32(0)
+        for j in range(query_docs.shape[1]):
+            offset = query_docs[query, j] - (device ^ d) * pool_dev
+            slot = jnp.where(jnp.logical_and(offset >= 0, offset < pool_dev), j, slot)
+        slots.append(slot)
+    return (query, slots)
 
 
 def prepare_body(here, query_docs, pool, ids, *outs):
@@ -248,21 +269,57 @@
         prepare_body,
         [shape] * 4,
         [],
-        1024,
-        1024 * 1024,
         in_specs=[SMEM, SMEM, VMEM, VMEM],
         out_specs=[VMEM] * 4,
         name="prepare",
     )(here, query_docs, pool, ids)
 
 
-def attention_body(lens, q, c0, c1, c2, c3, cos_q, sin_q, cos_d, sin_d, out, wide, keys, vals):
+def angles_body(pool_dev, here, query_docs, ctx_pos, cos_q, sin_q, cos_d, sin_d):
+    query, slots = document_slots(here, query_docs, pool_dev)
+    docs_per = query_docs.shape[1]
+    head_dim = cos_q.shape[1]
+
+    def fill(starts, cosine, sine):
+        column = lax.broadcasted_iota(jnp.int32, cosine.shape, 1)
+        half = jnp.where(column < head_dim // 2, column, column - head_dim // 2)
+        freq = jnp.exp(half.astype(jnp.float32) * (-2.0 * math.log(rope_theta) / head_dim))
+        angle = starts.astype(jnp.float32) * freq
+        cosine[...] = jnp.cos(angle)
+        wave = jnp.sin(angle)
+        sine[...] = jnp.where(column < head_dim // 2, -wave, wave)
+
+    row = lax.broadcasted_iota(jnp.int32, cos_q.shape, 0)
+    fill(ctx_pos[query, docs_per] + row, cos_q, sin_q)
+    row = lax.broadcasted_iota(jnp.int32, cos_d.shape, 0)
+    starts = jnp.zeros(cos_d.shape, jnp.int32)
+    for d, slot in enumerate(slots):
+        starts = jnp.where(row == d, ctx_pos[query, slot], starts)
+    fill(starts, cos_d, sin_d)
+
+
+def angles(here, query_docs, ctx_pos, pool_dev, length, head_dim):
+    shapes = [jax.ShapeDtypeStruct((rows, head_dim), jnp.float32) for rows in (length, length, 8, 8)]
+    return call(
+        functools.partial(angles_body, pool_dev),
+        shapes,
+        [],
+        in_specs=[SMEM] * 3,
+        out_specs=[VMEM] * 4,
+        name="angles",
+    )(here, query_docs, ctx_pos)
+
+
+def attention_body(
+    pool_dev, here, query_docs, doc_lens, q, c0, c1, c2, c3, cos_q, sin_q, cos_d, sin_d, out, wide, keys, vals
+):
     length, head_dim = cos_q.shape
     heads = out.shape[1] // head_dim
     pieces = (c0, c1, c2, c3)
     docs = len(pieces)
     doc_max = (keys.shape[0] - length) // docs
     half = head_dim // 2
+    query, slots = document_slots(here, query_docs, pool_dev)
 
     def turned(x, cosine, sine):
         return x * cosine + pltpu.roll(x, half, 1) * sine
@@ -277,16 +334,16 @@
     keys[base:, :] = turned(q[first : first + length, :].astype(jnp.float32), cosine, sine).astype(
         jnp.bfloat16
     )
-    vals[base:, :] = q[first + length : first + 2 * length, :]
+    vals[base:, :] = q[first + length :, :]
     wide[...] = q[:first, :].astype(jnp.float32)
     column = lax.broadcasted_iota(jnp.int32, (1, doc_max), 1)
-    allowed = [column < lens[j] for j in range(docs)]
+    allowed = [column < doc_lens[query_docs[query, slot]] for slot in slots]
     causal = lax.broadcasted_iota(jnp.int32, (length, length), 0) >= lax.broadcasted_iota(
         jnp.int32, (length, length), 1
     )
     for h in range(heads):
-        query = turned(wide[pl.ds(h, length, stride=heads), :], cosine, sine).astype(jnp.bfloat16)
-        scores = lax.dot_general(query, keys[...], NT, preferred_element_type=jnp.float32)
+        rows = turned(wide[pl.ds(h, length, stride=heads), :], cosine, sine).astype(jnp.bfloat16)
+        scores = lax.dot_general(rows, keys[...], NT, preferred_element_type=jnp.float32)
         scores = scores * head_dim ** (-0.5)
         parts = [
             jnp.where(allowed[j], scores[:, j * doc_max : (j + 1) * doc_max], -jnp.inf)
@@ -300,129 +357,207 @@
         out[:, h * head_dim : (h + 1) * head_dim] = (mixed / denominator).astype(jnp.bfloat16)
 
 
-def attention(lens, q, pieces, heads, tables_q, tables_d):
-    length, head_dim = tables_q[0].shape
+def attention(here, query_docs, doc_lens, q, pieces, tables, pool_dev):
+    length, head_dim = tables[0].shape
+    heads = q.shape[0] // length - 2
     rows = 5 * length
     return call(
-        attention_body,
+        functools.partial(attention_body, pool_dev),
         jax.ShapeDtypeStruct((length, heads * head_dim), jnp.bfloat16),
         [
             pltpu.VMEM((heads * length, head_dim), jnp.float32),
             pltpu.VMEM((rows, head_dim), jnp.bfloat16),
             pltpu.VMEM((rows, head_dim), jnp.bfloat16),
         ],
-        4 * heads * length * rows * head_dim * 4,
-        4 * 1024 * 1024,
-        in_specs=[SMEM] + [VMEM] * 9,
+        in_specs=[SMEM] * 3 + [VMEM] * 9,
         out_specs=VMEM,
         name="attention",
-    )(lens, q, *pieces, *tables_q, *tables_d)
-
-
-def project_body(here, a, b, c, d, weight, hidden, out, rows):
+    )(here, query_docs, doc_lens, q, *pieces, *tables)
+
+
+def project_body(here, a, b, c, d, weight, *rest):
+    outs, rows = (rest[:-1], rest[-1])
     device, lane = (here[0], here[1])
     for flip, ref in zip((0, 2, 1, 3), (a, b, c, d)):
         rows[query_of(device, lane ^ flip)] = ref[...]
-    for s in range(4):
-        base = jnp.where(device == s, hidden[...].astype(jnp.float32), 0.0)
-        out[s] = (base + dot(rows[s], weight[...])).astype(jnp.bfloat16)
-
-
-def project(here, parts, weight, hidden):
+    for d in (2, 3, 1, 0):
+        outs[d][...] = dot(rows[device ^ d], weight[...]).astype(jnp.bfloat16)
+
+
+def project(here, parts, weight):
     length, depth = parts[0].shape
     return call(
         project_body,
-        jax.ShapeDtypeStruct((4, length, weight.shape[1]), jnp.bfloat16),
+        [jax.ShapeDtypeStruct((length, weight.shape[1]), jnp.bfloat16)] * 4,
         [pltpu.VMEM((4, length, depth), jnp.bfloat16)],
-        2 * 4 * length * depth * weight.shape[1],
-        4 * 1024 * 1024,
-        in_specs=[SMEM] + [VMEM] * 6,
-        out_specs=VMEM,
+        in_specs=[SMEM] + [VMEM] * 5,
+        out_specs=[VMEM] * 4,
         name="project",
-    )(here, *parts, weight, hidden)
-
-
-def assemble_body(here, tokens, gain, router, scaled, stats, residual):
-    length = tokens.shape[1]
-    experts = router.shape[0]
-    device = here[0]
-    ones = jnp.ones((8, tokens.shape[2]), jnp.float32)
-    residual[...] = tokens[device]
-    for d in range(4):
-        wide = tokens[device ^ d].astype(jnp.float32)
-        grown = wide * gain[...]
-        scaled[d] = grown.astype(jnp.bfloat16)
-        block = slice(d * length, (d + 1) * length)
-        stats[:experts, block] = lax.dot_general(
-            router[...], grown, NT, preferred_element_type=jnp.float32,
-            precision=lax.Precision.HIGHEST,
-        )
-        stats[experts:, block] = lax.dot_general(
-            ones, wide * wide, NT, preferred_element_type=jnp.float32,
-            precision=lax.Precision.HIGHEST,
-        )
-
-
-def assemble(here, tokens, gain, router):
-    n, length, width = tokens.shape
-    return call(
-        assemble_body,
+    )(here, *parts, weight)
+
+
+def routing_body(experts, here, c0, c1, c2, c3, pick, spread):
+    _, local, capacity, length = pick.shape
+    first = here[0] * local
+    before = (
+        lax.broadcasted_iota(jnp.int32, (length, length), 0)
+        < lax.broadcasted_iota(jnp.int32, (length, length), 1)
+    ).astype(jnp.bfloat16)
+    place = lax.broadcasted_iota(jnp.int32, (capacity, length), 0).astype(jnp.float32)
+    row = lax.broadcasted_iota(jnp.int32, (8, length), 0)
+    for d, piece in enumerate((c0, c1, c2, c3)):
+        ids = piece[piece.shape[0] - 16 :, :].astype(jnp.float32).astype(jnp.int32)
+        chosen = jnp.zeros((8, length), jnp.float32)
+        for k in range(8):
+            named = jnp.logical_and(ids[k : k + 1, :] == first + row, row < local)
+            chosen = jnp.where(named, 1.0, chosen)
+        rank = dot(chosen.astype(jnp.bfloat16), before)
+        wide = []
+        for e in range(local):
+            here_e = jnp.logical_and(rank[e : e + 1, :] == place, chosen[e : e + 1, :] > 0.0)
+            wide.append(jnp.where(here_e, 1.0, 0.0))
+            pick[d, e] = wide[-1].astype(jnp.bfloat16)
+        spread[d] = jnp.transpose(jnp.concatenate(wide, axis=0)).astype(jnp.bfloat16)
+
+
+def routing(here, pieces, experts, local, capacity):
+    length = pieces[0].shape[1]
+    rows = pieces[0].shape[0]
+    return call(
+        functools.partial(routing_body, experts),
         [
-            jax.ShapeDtypeStruct((n, length, width), jnp.bfloat16),
-            jax.ShapeDtypeStruct((router.shape[0] + 8, n * length), jnp.float32),
-            jax.ShapeDtypeStruct((length, width), jnp.bfloat16),
+            jax.ShapeDtypeStruct((4, local, capacity, length), jnp.bfloat16),
+            jax.ShapeDtypeStruct((4, length, local * capacity), jnp.bfloat16),
         ],
         [],
-        2 * n * length * width * 256,
-        3 * 1024 * 1024,
-        in_specs=[SMEM] + [VMEM] * 3,
-        out_specs=[VMEM] * 3,
-        name="assemble",
-    )(here, tokens, gain, router)
-
-
-def gate_up_body(first, order, tokens, pick, weight, *outs):
+        in_specs=[SMEM] + [VMEM] * 4,
+        out_specs=[VMEM] * 2,
+        name="routing",
+    )(here, *pieces)
+
+
+def residual_body(hidden, p0, p1, p2, p3, gain, router, after, out, stats):
+    rows = stats.shape[0]
+    total = hidden[...].astype(jnp.float32) + p0[...].astype(jnp.float32)
+    for part in (p1, p2, p3):
+        total = total + part[...].astype(jnp.float32)
+    narrow = total.astype(jnp.bfloat16)
+    out[...] = narrow
+    wide = narrow.astype(jnp.float32)
+    grown = wide * gain[...]
+    high = grown.astype(jnp.bfloat16)
+    rest = grown - high.astype(jnp.float32)
+    middle = rest.astype(jnp.bfloat16)
+    low = (rest - middle.astype(jnp.float32)).astype(jnp.bfloat16)
+    logits = dot(high, router[...]) + (dot(middle, router[...]) + dot(low, router[...]))
+    squares = jnp.sum(wide * wide, axis=1, keepdims=True)
+    column = lax.broadcasted_iota(jnp.int32, logits.shape, 1)
+    stats[...] = jnp.transpose(jnp.where(column == rows - 8, squares, logits))[:rows, :]
+
+
+def residual_and_stats(hidden, parts, gain, router, experts, after):
+    length, width = hidden.shape
+    return call(
+        residual_body,
+        [
+            jax.ShapeDtypeStruct((length, width), jnp.bfloat16),
+            jax.ShapeDtypeStruct((experts + 8, length), jnp.float32),
+        ],
+        [],
+        in_specs=[VMEM] * 7 + [pl.BlockSpec(memory_space=pl.ANY)],
+        out_specs=[VMEM] * 2,
+        name="residual",
+    )(hidden, *parts, gain, router, after)
+
+
+def gate_up_body(ds, order, *refs):
+    tokens = refs[: len(ds)]
+    gain, pick, weight, kept, given, rows = refs[len(ds) :]
     hid = weight.shape[3]
     capacity = pick.shape[2]
-    expert = order[pl.program_id(0)]
-    rows = jnp.concatenate(
-        [dot(pick[d, expert], tokens[d]).astype(jnp.bfloat16) for d in (first, first + 1)], axis=0
-    )
+    i = pl.program_id(0)
+    expert = order[i]
+    for k, d in enumerate(ds):
+        chosen = dot(pick[d, expert], tokens[k][...]) * gain[...]
+        rows[k * capacity : (k + 1) * capacity, :] = chosen.astype(jnp.bfloat16)
     for g in range(2):
-        term = dot(rows, weight[0, g]).astype(jnp.bfloat16)
-        for j, out in enumerate(outs):
-
-            @pl.when(pl.program_id(0) == j)
+        term = dot(rows[...], weight[0, g]).astype(jnp.bfloat16)
+        for j in range(4):
+            out = (kept, given)[j // 2]
+
+            @pl.when(i == j)
             def _():
-                out[:, g * hid : (g + 1) * hid] = term
-
-
-def gate_up(first, order, tokens, pick, weight):
+                out[j % 2, :, g * hid : (g + 1) * hid] = term
+
+
+def gate_up(ds, order, tokens, gain, pick, weight):
     local, _, width, hid = weight.shape
     capacity = pick.shape[2]
-    shape = jax.ShapeDtypeStruct((2 * capacity, 2 * hid), jnp.bfloat16)
+    shape = jax.ShapeDtypeStruct((2, len(ds) * capacity, 2 * hid), jnp.bfloat16)
     whole = lambda rank: lambda i, order: (0,) * rank
     return call(
-        functools.partial(gate_up_body, first),
-        [shape] * 4,
+        functools.partial(gate_up_body, ds),
+        [shape] * 2,
         None,
-        2 * local * 2 * capacity * width * 2 * hid,
-        20 * 1024 * 1024,
         grid_spec=pltpu.PrefetchScalarGridSpec(
             num_scalar_prefetch=1,
             grid=(local,),
-            in_specs=[
-                pl.BlockSpec(tokens.shape, whole(3)),
+            in_specs=[pl.BlockSpec(tokens[0].shape, whole(2))] * len(ds)
+            + [
+                pl.BlockSpec(gain.shape, whole(2)),
                 pl.BlockSpec(pick.shape, whole(4)),
                 pl.BlockSpec((1, 2, width, hid), lambda i, order: (order[i], 0, 0, 0)),
             ],
-            out_specs=[pl.BlockSpec(shape.shape, whole(2))] * 4,
+            out_specs=[pl.BlockSpec(shape.shape, whole(3))] * 2,
+            scratch_shapes=[pltpu.VMEM((len(ds) * capacity, width), jnp.bfloat16)],
         ),
         name="gate_up",
-    )(order, tokens, pick, weight)
-
-
-def down_body(order, a, b, c, d, spread, weight, *rest):
+    )(order, *tokens, gain, pick, weight)
+
+
+def activate_body(ds, features, here, kept, taken, across, pick, *refs):
+    stats = refs[: len(ds)]
+    pieces = refs[len(ds) : 2 * len(ds)]
+    out = refs[2 * len(ds)]
+    _, local, capacity, length = pick.shape
+    hid = out.shape[1]
+    experts = stats[0].shape[0] - 8
+    device, lane = (here[0], here[1])
+    expert = lax.broadcasted_iota(jnp.int32, (experts, length), 0)
+    for k, d in enumerate(ds):
+        ids = pieces[k][pieces[k].shape[0] - 16 :, :].astype(jnp.float32).astype(jnp.int32)
+        chosen = jnp.zeros((experts, length), jnp.float32)
+        for c in range(8):
+            chosen = jnp.where(ids[c : c + 1, :] == expert, 1.0, chosen)
+        inv_rms = lax.rsqrt(stats[k][experts : experts + 1, :] / features + norm_eps)
+        logits = jnp.where(chosen > 0.0, stats[k][:experts, :] * inv_rms, -jnp.inf)
+        grown = jnp.exp(logits - jnp.max(logits, axis=0, keepdims=True))
+        mix = grown / jnp.sum(grown, axis=0, keepdims=True)
+        mix = jnp.sum(jnp.where(expert == device * local + lane, mix, 0.0), axis=0, keepdims=True)
+        places = pick[d, lane].astype(jnp.float32)
+        inv_row = jnp.sum(places * inv_rms, axis=1, keepdims=True)
+        mix_row = jnp.sum(places * mix, axis=1, keepdims=True)
+        rows = slice(k * capacity, (k + 1) * capacity)
+        summed = kept[0, rows, :].astype(jnp.float32) + taken[0, rows, :].astype(jnp.float32)
+        summed = (summed + across[rows, :].astype(jnp.float32)) * inv_row
+        gate = summed[:, :hid]
+        act = gate / (1.0 + jnp.exp(-gate)) * summed[:, hid:] * mix_row
+        out[rows, :] = act.astype(jnp.bfloat16)
+
+
+def activate(ds, features, here, kept, taken, across, pick, stats, pieces):
+    rows, both = across.shape
+    return call(
+        functools.partial(activate_body, ds, features),
+        jax.ShapeDtypeStruct((rows, both // 2), jnp.bfloat16),
+        [],
+        in_specs=[SMEM] + [VMEM] * (4 + 2 * len(ds)),
+        out_specs=VMEM,
+        name="activate",
+    )(here, kept, taken, across, pick, *[stats[d] for d in ds], *[pieces[d] for d in ds])
+
+
+def down_body(ds, order, a, b, c, d, spread, weight, *rest):
     outs, results = (rest[:-1], rest[-1])
     i = pl.program_id(0)
     capacity = results.shape[2]
@@ -432,27 +567,26 @@
         @pl.when(i == j)
         def _():
             result = dot(ref[...], weight[0]).astype(jnp.bfloat16)
-            for k in range(2):
+            for k in range(len(ds)):
                 results[k, expert] = result[k * capacity : (k + 1) * capacity, :]
 
     @pl.when(i == pl.num_programs(0) - 1)
     def _():
         for k, out in enumerate(outs):
-            out[...] = dot(spread[k], results[k].reshape(-1, results.shape[3])).astype(jnp.bfloat16)
-
-
-def down(order, acts, spread, weight):
+            rows = results[k].reshape(-1, results.shape[3])
+            out[...] = dot(spread[ds[k]], rows).astype(jnp.bfloat16)
+
+
+def down(ds, order, acts, spread, weight):
     local, hid, width = weight.shape
-    capacity = acts[0].shape[0] // 2
+    capacity = acts[0].shape[0] // len(ds)
     length = spread.shape[1]
     shape = jax.ShapeDtypeStruct((length, width), jnp.bfloat16)
     whole = lambda rank: lambda i, order: (0,) * rank
     return call(
-        down_body,
-        [shape] * 2,
+        functools.partial(down_body, ds),
+        [shape] * len(ds),
         None,
-        2 * local * 2 * capacity * width * hid,
-        10 * 1024 * 1024,
         grid_spec=pltpu.PrefetchScalarGridSpec(
             num_scalar_prefetch=1,
             grid=(local,),
@@ -461,19 +595,11 @@
                 pl.BlockSpec(spread.shape, whole(3)),
                 pl.BlockSpec((1, hid, width), lambda i, order: (order[i], 0, 0)),
             ],
-            out_specs=[pl.BlockSpec(shape.shape, whole(2))] * 2,
-            scratch_shapes=[pltpu.VMEM((2, local, capacity, width), jnp.bfloat16)],
+            out_specs=[pl.BlockSpec(shape.shape, whole(2))] * len(ds),
+            scratch_shapes=[pltpu.VMEM((len(ds), local, capacity, width), jnp.bfloat16)],
         ),
         name="down",
     )(order, *acts, spread, weight)
-
-
-def signed_tables(positions, head_dim):
-    cosine, sine = tables(positions, head_dim)
-    return (
-        jnp.concatenate([cosine, cosine], axis=1),
-        jnp.concatenate([-sine, sine], axis=1),
-    )
 
 
 def per_device_square(
@@ -495,102 +621,84 @@
     lane = lax.axis_index("tp")
     device = lax.axis_index("ep")
     length, heads_here, head_dim = question_q.shape
-    pool_dev, doc_max, kv_heads, _, _ = doc_kv.shape
-    docs_per = query_docs.shape[1]
+    pool_dev = doc_kv.shape[0]
     width_here = hidden.shape[1]
     experts = router_weight.shape[1]
     local = w_gate_up.shape[0]
     capacity = length * expert_ids.shape[1] // experts
-    hid = w_gate_up.shape[3]
-    seats = jnp.arange(n, dtype=jnp.int32)
     here = jnp.stack([device, lane]).astype(jnp.int32)
     order = (lane ^ jnp.array([0, 2, 1, 3], jnp.int32)).astype(jnp.int32)
-    reach = device ^ seats
-
-    kv_head = lax.dynamic_index_in_dim(question_kv, lane, 1, keepdims=False)
-    kv_rows = jnp.transpose(kv_head, (1, 0, 2)).reshape(2 * length, head_dim)
-    q_rows = turn(
-        jnp.concatenate([question_q.reshape(length * heads_here, head_dim), kv_rows], axis=0), n, n
-    )
 
     pool = jnp.transpose(doc_kv, (0, 2, 3, 1, 4))
     ids_rows = jnp.pad(expert_ids.T.astype(jnp.bfloat16), ((0, 8), (0, 0)))
     pieces = prepare(here, query_docs, pool, ids_rows)
+    q_rows, pieces = turn(
+        question_q.reshape(length * heads_here, head_dim), question_kv, device, lane, n, pieces
+    )
     pieces = [pieces[0]] + [lax.ppermute(pieces[d], "ep", pairs(n, d)) for d in range(1, n)]
-
-    query = query_of(device, lane)
-    my_docs = lax.dynamic_index_in_dim(query_docs, query, 0, keepdims=False)
-    starts = lax.dynamic_index_in_dim(ctx_pos, query, 0, keepdims=False)
-    owned = (my_docs // pool_dev)[None, :] == reach[:, None]
-    lengths = jnp.sum(jnp.where(owned, jnp.take(doc_lens, my_docs)[None, :], 0), axis=1)
-    doc_starts = jnp.sum(jnp.where(owned, starts[None, :docs_per], 0), axis=1)
-    tables_q = signed_tables(starts[docs_per] + jnp.arange(length, dtype=jnp.int32), head_dim)
-    tables_d = signed_tables(doc_starts, head_dim)
-
-    attended = attention(lengths, q_rows, pieces, heads_here, tables_q, tables_d)
+    tables = list(angles(here, query_docs, ctx_pos, pool_dev, length, head_dim))
+
+    one = lax.optimization_barrier(jnp.ones((), jnp.bfloat16))
+    tables[0], out_proj = lax.optimization_barrier((tables[0], out_proj * one))
+    attended = attention(here, query_docs, doc_lens, q_rows, pieces, tables, pool_dev)
     far = lax.ppermute(attended, "tp", pairs(n, 2))
     near = lax.ppermute(attended, "tp", pairs(n, 1))
     farther = lax.ppermute(far, "tp", pairs(n, 1))
-    partial = project(here, (attended, far, near, farther), out_proj, hidden)
-    tokens = lax.psum(partial, "ep")
-
-    ids = jnp.stack([p[2 * doc_max : 2 * doc_max + expert_ids.shape[1]] for p in pieces])
-    ids = ids.astype(jnp.int32)
-    named = device * local + jnp.arange(local, dtype=jnp.int32)
-    chosen = jnp.any(ids[:, None, :, :] == named[None, :, None, None], axis=2)
-    before = (jnp.arange(length)[:, None] < jnp.arange(length)[None, :]).astype(jnp.bfloat16)
-    rank = jnp.einsum(
-        "men,nk->mek", chosen.astype(jnp.bfloat16), before, preferred_element_type=jnp.float32
-    ).astype(jnp.int32)
-    picked = jnp.logical_and(
-        chosen[:, :, None, :],
-        rank[:, :, None, :] == jnp.arange(capacity, dtype=jnp.int32)[None, None, :, None],
-    )
-    pick = picked.astype(jnp.bfloat16)
-    spread = jnp.transpose(pick.reshape(n, local * capacity, length), (0, 2, 1))
-    named_all = jnp.any(
-        ids[:, None, :, :] == jnp.arange(experts, dtype=jnp.int32)[None, :, None, None], axis=2
-    )
+    gain = norm_gain.astype(jnp.float32)[None, :]
+    router = jnp.pad(router_weight, ((0, 0), (0, 128 - experts)))
+    parts = project(here, (attended, far, near, farther), out_proj)
+    kept, w_gate_up = lax.optimization_barrier((parts[0], w_gate_up))
+    sent = [lax.ppermute(parts[d], "ep", pairs(n, d)) for d in (2, 3, 1)]
+    pick, spread = routing(here, pieces, experts, local, capacity)
     weight = jnp.transpose(w_gate_up, (0, 2, 1, 3))
-
-    scaled, stats, residual = assemble(
-        here, tokens, norm_gain.astype(jnp.float32)[None, :], router_weight.T.astype(jnp.float32)
-    )
-    stats = stats + lax.ppermute(stats, "tp", pairs(n, 2))
-    stats = stats + lax.ppermute(stats, "tp", pairs(n, 1))
-    stats = stats.reshape(experts + 8, n, length)
-    inv_rms = lax.rsqrt(stats[experts] / (width_here * n) + norm_eps)
-    logits = jnp.transpose(stats[:experts], (1, 0, 2)) * inv_rms[:, None, :]
-    top = jnp.max(jnp.where(named_all, logits, -jnp.inf), axis=1, keepdims=True)
-    grown = jnp.where(named_all, jnp.exp(logits - top), 0.0)
-    mine = device * local + lane
-    mix = lax.dynamic_index_in_dim(grown, mine, 1, keepdims=False) / jnp.sum(grown, axis=1)
-    picked_mine = lax.dynamic_index_in_dim(picked, lane, 1, keepdims=False)
-    inv_row = jnp.sum(jnp.where(picked_mine, inv_rms[:, None, :], 0.0), axis=2)
-    mix_row = jnp.sum(jnp.where(picked_mine, mix[:, None, :], 0.0), axis=2)
-
-    total = None
-    for first in (2, 0):
-        rows = slice(first, first + 2)
-        terms = gate_up(first, order, scaled, pick, weight)
-        for_far = lax.ppermute(terms[3], "tp", pairs(n, 1))
-        for_me = lax.ppermute(terms[2], "tp", pairs(n, 1))
-        chip_far = (terms[1].astype(jnp.float32) + for_far.astype(jnp.float32)).astype(jnp.bfloat16)
-        across = lax.ppermute(chip_far, "tp", pairs(n, 2))
-        summed = (
-            terms[0].astype(jnp.float32) + for_me.astype(jnp.float32) + across.astype(jnp.float32)
-        ) * inv_row[rows].reshape(-1, 1)
-        act = jax.nn.silu(summed[:, :hid]) * summed[:, hid:] * mix_row[rows].reshape(-1, 1)
-        act = act.astype(jnp.bfloat16)
+    residual, own_stats = residual_and_stats(
+        hidden, [kept] + sent, gain, router, experts, weight
+    )
+
+    residual, w_down = lax.optimization_barrier((residual, w_down))
+    w_down = w_down * one
+    tokens = {0: residual}
+    for d in (2, 3, 1):
+        tokens[d] = lax.ppermute(residual, "ep", pairs(n, d))
+    own_stats = own_stats + lax.ppermute(own_stats, "tp", pairs(n, 2))
+    own_stats = own_stats + lax.ppermute(own_stats, "tp", pairs(n, 1))
+    own_stats, w_down, tokens[1], tokens[2], tokens[3] = lax.optimization_barrier(
+        (own_stats, w_down, tokens[1], tokens[2], tokens[3])
+    )
+    stats = {0: own_stats}
+    for d in (2, 3, 1):
+        stats[d] = lax.ppermute(own_stats, "ep", pairs(n, d))
+
+    features = width_here * n
+
+    def exchange(ds, order, before):
+        kept, given = gate_up(ds, order, [tokens[d] for d in ds], gain, pick, weight)
+        given, *before = lax.optimization_barrier((given, *before))
+        taken = lax.ppermute(given, "tp", pairs(n, 1))
+        chip_far = (kept[1].astype(jnp.float32) + taken[1].astype(jnp.float32)).astype(jnp.bfloat16)
+        return (chip_far, before, kept, taken, lax.ppermute(chip_far, "tp", pairs(n, 2)))
+
+    def spread_act(act):
         far = lax.ppermute(act, "tp", pairs(n, 2))
         near = lax.ppermute(act, "tp", pairs(n, 1))
-        farther = lax.ppermute(far, "tp", pairs(n, 1))
-        parts = down(order, (act, far, near, farther), spread[rows], w_down)
-        for d, part in zip((first, first + 1), parts):
-            back = lax.ppermute(part, "ep", pairs(n, d)) if d else part
-            back = back.astype(jnp.float32)
-            total = back if total is None else total + back
-    return (residual.astype(jnp.float32) + total).astype(jnp.bfloat16)
+        return [act, far, near, lax.ppermute(far, "tp", pairs(n, 1))]
+
+    chip_far, _, *first = exchange((2, 3), order, [])
+    order, *_ = lax.optimization_barrier((order, chip_far, stats[1], stats[2], stats[3]))
+    _, first[2:], *second = exchange((0, 1), order, first[2:])
+    act = activate((2, 3), features, here, *first, pick, stats, pieces)
+    acts = spread_act(act)
+    act = activate((0, 1), features, here, *second, pick, stats, pieces)
+    acts[3], act = lax.optimization_barrier((acts[3], act))
+    others = spread_act(act)
+    parts = down((2, 3), order, acts, spread, w_down)
+    returned = [lax.ppermute(part, "ep", pairs(n, d)) for part, d in zip(parts, (2, 3))]
+    mine, near = down((0, 1), order, others, spread, w_down)
+    returned += [mine, lax.ppermute(near, "ep", pairs(n, 1))]
+    total = residual.astype(jnp.float32)
+    for part in returned:
+        total = total + part.astype(jnp.float32)
+    return total.astype(jnp.bfloat16)
 
 
 def solution(mesh):

time: 229 us -> 182 us (0.79)
  waiting for transfers between devices: 110 us -> 82.5 us
  starting transfers between devices: 19.6 us -> 39.7 us
  between operations: 13.7 us -> 0.32 us
  local copies, waits for them, and re-layouts: 34.2 us -> 21.3 us
  Pallas kernels: 34.9 us -> 25.7 us
  other arithmetic: 15.5 us -> 11.9 us
    psum x1 -> x0, waiting for transfers between devices: 50.5 us -> none  [per_device_square(): tokens = lax.psum(partial, 'ep')]
    ppermute x16 -> x26, waiting for transfers between devices: 45.2 us -> 70.4 us  [the longest x2 24 us: spread_act(): far = lax.ppermute(act, 'tp', pairs(n, 2))]
    unnamed x23 -> x31, local copies, waits for them, and re-layouts: 28.1 us -> 9.95 us
    ppermute x16 -> x26, starting transfers between devices: 11.1 us -> 25.2 us  [the longest x3 6.4 us: per_device_square(): tokens[d] = lax.ppermute(residual, 'ep', pairs(n, d))]
    optimization_barrier x0 -> x1, local copies, waits for them, and re-layouts: none -> 11.2 us  [per_device_square(): kept, w_gate_up = lax.optimization_barrier((parts[0], w_gate_up))]
    pallas_call x8 -> x12, Pallas kernels: 34.9 us -> 25.7 us  [the longest x2 9.95 us: gate_up(): call(functools.partial(gate_up_body, ds), [shape] * 2, None, grid_spec=pl...]
    mul x2, other arithmetic: 2.74 us -> 8.96 us  [the longest x1 7.23 us: per_device_square(): w_down = w_down * one]
    convert_element_type x9 -> x3, other arithmetic: 5.51 us -> 1.2 us  [the longest x1 0.92 us: per_device_square(): return total.astype(jnp.bfloat16)]
  transfers between devices with their start and end apart: 25 -> 32, of which waited for: 10 -> 16; matrix products, arithmetic and copies ran while one was open for 16% -> 12% of each run, Pallas kernels for 11% -> 8%
where the time goes in v5:
time: 182 us; the launch traced here: 181 us
  waiting for transfers between devices  82.5 us (45%)
  starting transfers between devices  39.7 us (22%)
  Pallas kernels  25.7 us (14%)
  local copies, waits for them, and re-layouts  21.3 us (12%)
  other arithmetic  11.9 us (7%)
    ppermute x2, waiting for transfers between devices, spread_act(): far = lax.ppermute(act, 'tp', pairs(n, 2))  24 us
    ppermute x2, waiting for transfers between devices, per_device_square(): lax.ppermute(part, 'ep', pairs(n, d))  14.1 us
    ppermute x3, waiting for transfers between devices, per_device_square(): tokens[d] = lax.ppermute(residual, 'ep', pairs(n, d))  11.4 us
    optimization_barrier x1, local copies, waits for them, and re-layouts, per_device_square(): kept, w_gate_up = lax.optimization_barrier((parts[0], w_gate_up))  11.2 us
    unnamed x31, local copies, waits for them, and re-layouts  9.95 us
    pallas_call x2, Pallas kernels, gate_up(): call(functools.partial(gate_up_body, ds), [shape] * 2, None, grid_spec=pl...  9.95 us
    ppermute x3, starting transfers between devices, per_device_square(): lax.ppermute(pieces[d], 'ep', pairs(n, d))  9.46 us
    mul x1, other arithmetic, per_device_square(): w_down = w_down * one  7.23 us
  transfers between devices with their start and end apart: 32, of which 16 were waited for; matrix products, arithmetic and copies ran while one was open for 12% of the time, Pallas kernels for 8%

profile of v5, /device:TPU:0, one launch (start us, length us, event | category | flops | bytes accessed | tf_op | source)
XLA Modules:
  0.0 181.3 jit_solution(8993516198041924979)
XLA Ops:
  5.3 6.9 %collective-permute-start.2 = (bf16[272,128]{1,0:T(8,128)(2,1)S(1)}, bf16[272,128]{1,0:T(8,128)(2,1)S(1)}, u32[]{:S(2)}, u32[]{:S(2)}) collective-permute-start(bf16[272,128]{1,0:T(8,128)(2,1)S(1)} %get-tuple-element.56), channel_id=1, source_target_pairs={{0,4},{4,0},{8,12},{12,8},{1,5},{5,1},{9,13},{13,9},{2,6},{6,2},{1... | collective-permute-start | bytes 208904 | tf_op jit(solution)/shard_map/ppermute | solution.py:638
  12.1 2.6 %collective-permute-start.3 = (bf16[272,128]{1,0:T(8,128)(2,1)S(1)}, bf16[272,128]{1,0:T(8,128)(2,1)S(1)}, u32[]{:S(2)}, u32[]{:S(2)}) collective-permute-start(bf16[272,128]{1,0:T(8,128)(2,1)S(1)} %get-tuple-element.57), channel_id=1, source_target_pairs={{0,8},{4,12},{8,0},{12,4},{1,9},{5,13},{9,1},{13,5},{2,10},{6,14},... | collective-permute-start | bytes 208904 | tf_op jit(solution)/shard_map/ppermute | solution.py:638
  15.4 1.7 broadcast_multiply_fusion.1.weight
  19.4 4.8 %collective-permute-done.3.c2.refs_2_ = bf16[272,128]{1,0:T(8,128)(2,1)S(1)} collective-permute-done((bf16[272,128]{1,0:T(8,128)(2,1)S(1)}, bf16[272,128]{1,0:T(8,128)(2,1)S(1)}, u32[]{:S(2)}, u32[]{:S(2)}) %collective-permute-start.3) | collective-permute-done | bytes 69664 | tf_op jit(solution)/shard_map/ppermute | solution.py:638
  24.9 3.4 %attention.1.a = bf16[128,1024]{1,0:T(8,128)(2,1)S(1)} custom-call(s32[2]{0:T(128)S(1)} %pad_add_fusion.here, s32[4,4]{1,0:T(4,128)S(1)} %copy-done.6, s32[8]{0:T(128)S(1)} %copy-done.8, bf16[1280,128]{1,0:T(8,128)(2,1)S(1)} %collective-permute-done.1.q, bf16[272,128]{1,0:T(8,128)(2,1)S(1)} %get-tuple-element.55.c0.refs_2_, ...), custom_call_target="tpu_custom_call" | custom-call | flops 1048576 | bytes 262144 | tf_op jit(solution)/shard_map/attention/pallas_call | solution.py:364
  28.3 4.2 %collective-permute-start.5 = (bf16[128,1024]{1,0:T(8,128)(2,1)S(1)}, bf16[128,1024]{1,0:T(8,128)(2,1)S(1)}, u32[]{:S(2)}, u32[]{:S(2)}) collective-permute-start(bf16[128,1024]{1,0:T(8,128)(2,1)S(1)} %attention.1.a), channel_id=1, source_target_pairs={{0,2},{1,3},{2,0},{3,1},{4,6},{5,7},{6,4},{7,5},{8,10},{9,11},{10,... | collective-permute-start | bytes 786440 | tf_op jit(solution)/shard_map/ppermute | solution.py:644
  32.5 6.1 %collective-permute-done.5.b = bf16[128,1024]{1,0:T(8,128)(2,1)S(1)} collective-permute-done((bf16[128,1024]{1,0:T(8,128)(2,1)S(1)}, bf16[128,1024]{1,0:T(8,128)(2,1)S(1)}, u32[]{:S(2)}, u32[]{:S(2)}) %collective-permute-start.5) | collective-permute-done | bytes 262176 | tf_op jit(solution)/shard_map/ppermute | solution.py:644
  40.6 1.9 %project.1 = (bf16[128,1024]{1,0:T(8,128)(2,1)S(1)}, bf16[128,1024]{1,0:T(8,128)(2,1)S(1)}, bf16[128,1024]{1,0:T(8,128)(2,1)S(1)}, bf16[128,1024]{1,0:T(8,128)(2,1)S(1)}) custom-call(s32[2]{0:T(128)S(1)} %pad_add_fusion.here, bf16[128,1024]{1,0:T(8,128)(2,1)S(1)} %attention.1.a, bf16[128,1024]{1,0:T(8,128)(2,1)S(1)} %collective-permute-done.5.b, ...), custom_call_target="tpu_custom_call" | custom-call | flops 1048576 | bytes 262144 | tf_op jit(solution)/shard_map/project/pallas_call | solution.py:389
  43.6 2.8 %collective-permute-start.9 = (bf16[128,1024]{1,0:T(8,128)(2,1)S(1)}, bf16[128,1024]{1,0:T(8,128)(2,1)S(1)}, u32[]{:S(2)}, u32[]{:S(2)}) collective-permute-start(bf16[128,1024]{1,0:T(8,128)(2,1)S(1)} %get-tuple-element.68), channel_id=1, source_target_pairs={{0,12},{4,8},{8,4},{12,0},{1,13},{5,9},{9,5},{13,1},{2,14},{6,10},... | collective-permute-start | bytes 786440 | tf_op jit(solution)/shard_map/ppermute | solution.py:651
  46.7 11.2 %copy.25 = bf16[4,1024,2,1024]{3,1,2,0:T(8,128)(2,1)S(1)} copy(bf16[4,1024,2,1024]{3,2,1,0:T(2,128)(2,1)} %param.24) | data formatting | bytes 33554432 | tf_op jit(solution)/shard_map/optimization_barrier | solution.py:650
  57.9 6.0 %collective-permute-done.8.p1 = bf16[128,1024]{1,0:T(8,128)(2,1)S(1)} collective-permute-done((bf16[128,1024]{1,0:T(8,128)(2,1)S(1)}, bf16[128,1024]{1,0:T(8,128)(2,1)S(1)}, u32[]{:S(2)}, u32[]{:S(2)}) %collective-permute-start.8) | collective-permute-done | bytes 262176 | tf_op jit(solution)/shard_map/ppermute | solution.py:651
  65.3 1.6 collective-permute-start.11
  67.8 1.9 %collective-permute-start.15 = (bf16[128,1024]{1,0:T(8,128)(2,1)S(1)}, bf16[128,1024]{1,0:T(8,128)(2,1)S(1)}, u32[]{:S(2)}, u32[]{:S(2)}) collective-permute-start(bf16[128,1024]{1,0:T(8,128)(2,1)S(1)} %get-tuple-element.72.refs_0_), channel_id=1, source_target_pairs={{0,12},{4,8},{8,4},{12,0},{1,13},{5,9},{9,5},{13,1},{2,14},{6,10},... | collective-permute-start | bytes 786440 | tf_op jit(solution)/shard_map/ppermute | solution.py:662
  69.7 4.5 %collective-permute-start.14 = (bf16[128,1024]{1,0:T(8,128)(2,1)S(1)}, bf16[128,1024]{1,0:T(8,128)(2,1)S(1)}, u32[]{:S(2)}, u32[]{:S(2)}) collective-permute-start(bf16[128,1024]{1,0:T(8,128)(2,1)S(1)} %get-tuple-element.72.refs_0_), channel_id=1, source_target_pairs={{0,8},{4,12},{8,0},{12,4},{1,9},{5,13},{9,1},{13,5},{2,10},{6,14},... | collective-permute-start | bytes 786440 | tf_op jit(solution)/shard_map/ppermute | solution.py:662
  74.2 7.2 %broadcast_multiply_fusion.weight = bf16[4,1024,1024]{2,1,0:T(8,128)(2,1)} fusion(bf16[4,1024,1024]{2,1,0:T(8,128)(2,1)} %param.25, bf16[]{:T(256)} %constant.23.clone.1), kind=kLoop, calls=%fused_computation.1 | loop fusion | flops 4194304 | bytes 16777218 | tf_op jit(solution)/shard_map/mul | solution.py:659
  81.5 11.4 %collective-permute-done.14.refs_0_ = bf16[128,1024]{1,0:T(8,128)(2,1)S(1)} collective-permute-done((bf16[128,1024]{1,0:T(8,128)(2,1)S(1)}, bf16[128,1024]{1,0:T(8,128)(2,1)S(1)}, u32[]{:S(2)}, u32[]{:S(2)}) %collective-permute-start.14) | collective-permute-done | bytes 262176 | tf_op jit(solution)/shard_map/ppermute | solution.py:662
  92.8 5.8 %copy-done.3 = bf16[4,1024,2,1024]{3,1,2,0:T(8,128)(2,1)S(1)} copy-done((bf16[4,1024,2,1024]{3,1,2,0:T(8,128)(2,1)S(1)}, bf16[4,1024,2,1024]{3,1,2,0:T(8,128)(2,1)}, u32[]{:S(2)}) %copy-start.3) | copy-done | bytes 16777240
  98.6 5.0 %gate_up.2 = (bf16[2,128,2048]{2,1,0:T(8,128)(2,1)S(1)}, bf16[2,128,2048]{2,1,0:T(8,128)(2,1)S(1)}) custom-call(s32[4]{0:T(128)S(1)} %broadcast_xor_fusion.order, bf16[128,1024]{1,0:T(8,128)(2,1)S(1)} %collective-permute-done.14.refs_0_, bf16[128,1024]{1,0:T(8,128)(2,1)S(1)} %collective-permute-done.15.refs_1_, f32[1,1024]{1,0:T(1,128)S(1)} %bitcast.29, ...), custom_call_target="tpu_custom_call" | custom-call | flops 1048576 | bytes 262144 | tf_op jit(solution)/shard_map/gate_up/pallas_call | solution.py:498
  103.7 2.6 %collective-permute-done.16.taken = bf16[2,128,2048]{2,1,0:T(8,128)(2,1)S(1)} collective-permute-done((bf16[2,128,2048]{2,1,0:T(8,128)(2,1)S(1)}, bf16[2,128,2048]{2,1,0:T(8,128)(2,1)S(1)}, u32[]{:S(2)}, u32[]{:S(2)}) %collective-permute-start.16) | collective-permute-done | bytes 1048608 | tf_op jit(solution)/shard_map/ppermute | solution.py:677
  107.0 2.0 %collective-permute-start.19 = (f32[24,128]{1,0:T(8,128)S(1)}, f32[24,128]{1,0:T(8,128)S(1)}, u32[]{:S(2)}, u32[]{:S(2)}) collective-permute-start(f32[24,128]{1,0:T(8,128)S(1)} %add.36.refs_0_), channel_id=1, source_target_pairs={{0,12},{4,8},{8,4},{12,0},{1,13},{5,9},{9,5},{13,1},{2,14},{6,10},... | collective-permute-start | bytes 36872 | tf_op jit(solution)/shard_map/ppermute | solution.py:670
  109.0 2.4 %collective-permute-start.17 = (f32[24,128]{1,0:T(8,128)S(1)}, f32[24,128]{1,0:T(8,128)S(1)}, u32[]{:S(2)}, u32[]{:S(2)}) collective-permute-start(f32[24,128]{1,0:T(8,128)S(1)} %add.36.refs_0_), channel_id=1, source_target_pairs={{0,4},{4,0},{8,12},{12,8},{1,5},{5,1},{9,13},{13,9},{2,6},{6,2},{1... | collective-permute-start | bytes 36872 | tf_op jit(solution)/shard_map/ppermute | solution.py:670
  113.6 5.0 %gate_up.3 = (bf16[2,128,2048]{2,1,0:T(8,128)(2,1)S(1)}, bf16[2,128,2048]{2,1,0:T(8,128)(2,1)S(1)}) custom-call(s32[4]{0:T(128)S(1)} %broadcast_xor_fusion.order, bf16[128,1024]{1,0:T(8,128)(2,1)S(1)} %get-tuple-element.72.refs_0_, bf16[128,1024]{1,0:T(8,128)(2,1)S(1)} %collective-permute-done.13.refs_1_, f32[1,1024]{1,0:T(1,128)S(1)} %bitcast.30, ...), custom_call_target="tpu_custom_call" | custom-call | flops 1048576 | bytes 262144 | tf_op jit(solution)/shard_map/gate_up/pallas_call | solution.py:498
  118.6 1.9 %collective-permute-done.20.across = bf16[128,2048]{1,0:T(8,128)(2,1)S(1)} collective-permute-done((bf16[128,2048]{1,0:T(8,128)(2,1)S(1)}, bf16[128,2048]{1,0:T(8,128)(2,1)S(1)}, u32[]{:S(2)}, u32[]{:S(2)}) %collective-permute-start.20) | collective-permute-done | bytes 524320 | tf_op jit(solution)/shard_map/ppermute | solution.py:679
  120.5 2.7 %collective-permute-done.24.taken = bf16[2,128,2048]{2,1,0:T(8,128)(2,1)S(1)} collective-permute-done((bf16[2,128,2048]{2,1,0:T(8,128)(2,1)S(1)}, bf16[2,128,2048]{2,1,0:T(8,128)(2,1)S(1)}, u32[]{:S(2)}, u32[]{:S(2)}) %collective-permute-start.24) | collective-permute-done | bytes 1048608 | tf_op jit(solution)/shard_map/ppermute | solution.py:677
  124.7 1.7 collective-permute-start.21
  126.4 16.6 %collective-permute-done.21.b = bf16[128,1024]{1,0:T(8,128)(2,1)S(1)} collective-permute-done((bf16[128,1024]{1,0:T(8,128)(2,1)S(1)}, bf16[128,1024]{1,0:T(8,128)(2,1)S(1)}, u32[]{:S(2)}, u32[]{:S(2)}) %collective-permute-start.21) | collective-permute-done | bytes 262176 | tf_op jit(solution)/shard_map/ppermute | solution.py:682
  145.4 7.4 %collective-permute-done.28.b = bf16[128,1024]{1,0:T(8,128)(2,1)S(1)} collective-permute-done((bf16[128,1024]{1,0:T(8,128)(2,1)S(1)}, bf16[128,1024]{1,0:T(8,128)(2,1)S(1)}, u32[]{:S(2)}, u32[]{:S(2)}) %collective-permute-start.28) | collective-permute-done | bytes 262176 | tf_op jit(solution)/shard_map/ppermute | solution.py:682
  152.9 2.8 %down.2 = (bf16[128,1024]{1,0:T(8,128)(2,1)S(1)}, bf16[128,1024]{1,0:T(8,128)(2,1)S(1)}) custom-call(s32[4]{0:T(128)S(1)} %broadcast_xor_fusion.order, bf16[128,1024]{1,0:T(8,128)(2,1)S(1)} %activate.2.a, bf16[128,1024]{1,0:T(8,128)(2,1)S(1)} %collective-permute-done.21.b, bf16[128,1024]{1,0:T(8,128)(2,1)S(1)} %collective-permute-done.22.c, ...), custom_call_target="tpu_custom_call" | custom-call | flops 1048576 | bytes 262144 | tf_op jit(solution)/shard_map/down/pallas_call | solution.py:586
  155.9 2.1 %collective-permute-start.27 = (bf16[128,1024]{1,0:T(8,128)(2,1)S(1)}, bf16[128,1024]{1,0:T(8,128)(2,1)S(1)}, u32[]{:S(2)}, u32[]{:S(2)}) collective-permute-start(bf16[128,1024]{1,0:T(8,128)(2,1)S(1)} %get-tuple-element.91), channel_id=1, source_target_pairs={{0,12},{4,8},{8,4},{12,0},{1,13},{5,9},{9,5},{13,1},{2,14},{6,10},... | collective-permute-start | bytes 786440 | tf_op jit(solution)/shard_map/ppermute | solution.py:695
  158.0 2.8 %down.3 = (bf16[128,1024]{1,0:T(8,128)(2,1)S(1)}, bf16[128,1024]{1,0:T(8,128)(2,1)S(1)}) custom-call(s32[4]{0:T(128)S(1)} %broadcast_xor_fusion.order, bf16[128,1024]{1,0:T(8,128)(2,1)S(1)} %activate.3.a, bf16[128,1024]{1,0:T(8,128)(2,1)S(1)} %collective-permute-done.28.b, bf16[128,1024]{1,0:T(8,128)(2,1)S(1)} %collective-permute-done.29.c, ...), custom_call_target="tpu_custom_call" | custom-call | flops 1048576 | bytes 262144 | tf_op jit(solution)/shard_map/down/pallas_call | solution.py:586
  162.1 14.0 %collective-permute-done.26 = bf16[128,1024]{1,0:T(8,128)(2,1)S(1)} collective-permute-done((bf16[128,1024]{1,0:T(8,128)(2,1)S(1)}, bf16[128,1024]{1,0:T(8,128)(2,1)S(1)}, u32[]{:S(2)}, u32[]{:S(2)}) %collective-permute-start.26) | collective-permute-done | bytes 262176 | tf_op jit(solution)/shard_map/ppermute | solution.py:695
  176.2 4.2 %collective-permute-done.31 = bf16[128,1024]{1,0:T(8,128)(2,1)S(1)} collective-permute-done((bf16[128,1024]{1,0:T(8,128)(2,1)S(1)}, bf16[128,1024]{1,0:T(8,128)(2,1)S(1)}, u32[]{:S(2)}, u32[]{:S(2)}) %collective-permute-start.31) | collective-permute-done | bytes 262176 | tf_op jit(solution)/shard_map/ppermute | solution.py:697
  (93 shorter events, 23.9 us)
Async XLA Ops:
  0.0 4.3 %collective-permute-start = (bf16[1024,128]{1,0:T(8,128)(2,1)}, bf16[1024,128]{1,0:T(8,128)(2,1)S(1)}, u32[]{:S(2)}, u32[]{:S(2)}) collective-permute-start(bf16[1024,128]{1,0:T(8,128)(2,1)} %bitcast.32), channel_id=1, source_target_pairs={{1,2},{2,1},{4,7},{7,4},{9,10},{10,9},{12,15},{15,12},{17,18},{18,... | collective-permute-start | bytes 786440 | tf_op jit(solution)/shard_map/ppermute | solution.py:202
  5.3 14.2 %collective-permute-start.2 = (bf16[272,128]{1,0:T(8,128)(2,1)S(1)}, bf16[272,128]{1,0:T(8,128)(2,1)S(1)}, u32[]{:S(2)}, u32[]{:S(2)}) collective-permute-start(bf16[272,128]{1,0:T(8,128)(2,1)S(1)} %get-tuple-element.56), channel_id=1, source_target_pairs={{0,4},{4,0},{8,12},{12,8},{1,5},{5,1},{9,13},{13,9},{2,6},{6,2},{1... | collective-permute-start | bytes 208904 | tf_op jit(solution)/shard_map/ppermute | solution.py:638
  12.1 12.1 %collective-permute-start.3 = (bf16[272,128]{1,0:T(8,128)(2,1)S(1)}, bf16[272,128]{1,0:T(8,128)(2,1)S(1)}, u32[]{:S(2)}, u32[]{:S(2)}) collective-permute-start(bf16[272,128]{1,0:T(8,128)(2,1)S(1)} %get-tuple-element.57), channel_id=1, source_target_pairs={{0,8},{4,12},{8,0},{12,4},{1,9},{5,13},{9,1},{13,5},{2,10},{6,14},... | collective-permute-start | bytes 208904 | tf_op jit(solution)/shard_map/ppermute | solution.py:638
  14.7 9.5 %collective-permute-start.4 = (bf16[272,128]{1,0:T(8,128)(2,1)S(1)}, bf16[272,128]{1,0:T(8,128)(2,1)S(1)}, u32[]{:S(2)}, u32[]{:S(2)}) collective-permute-start(bf16[272,128]{1,0:T(8,128)(2,1)S(1)} %get-tuple-element.58), channel_id=1, source_target_pairs={{0,12},{4,8},{8,4},{12,0},{1,13},{5,9},{9,5},{13,1},{2,14},{6,10},... | collective-permute-start | bytes 208904 | tf_op jit(solution)/shard_map/ppermute | solution.py:638
  14.7 9.5 %collective-permute-start.1 = (bf16[1280,128]{1,0:T(8,128)(2,1)S(1)}, bf16[1280,128]{1,0:T(8,128)(2,1)S(1)}, u32[]{:S(2)}, u32[]{:S(2)}) collective-permute-start(bf16[1280,128]{1,0:T(8,128)(2,1)S(1)} %pad_maximum_fusion), channel_id=1, source_target_pairs={{0,0},{1,8},{2,6},{3,14},{4,12},{5,4},{6,10},{7,2},{8,1},{9,9},{10... | collective-permute-start | bytes 983048 | tf_op jit(solution)/shard_map/ppermute | solution.py:212
  28.3 10.4 %collective-permute-start.5 = (bf16[128,1024]{1,0:T(8,128)(2,1)S(1)}, bf16[128,1024]{1,0:T(8,128)(2,1)S(1)}, u32[]{:S(2)}, u32[]{:S(2)}) collective-permute-start(bf16[128,1024]{1,0:T(8,128)(2,1)S(1)} %attention.1.a), channel_id=1, source_target_pairs={{0,2},{1,3},{2,0},{3,1},{4,6},{5,7},{6,4},{7,5},{8,10},{9,11},{10,... | collective-permute-start | bytes 786440 | tf_op jit(solution)/shard_map/ppermute | solution.py:644
  32.5 7.0 %collective-permute-start.6 = (bf16[128,1024]{1,0:T(8,128)(2,1)S(1)}, bf16[128,1024]{1,0:T(8,128)(2,1)S(1)}, u32[]{:S(2)}, u32[]{:S(2)}) collective-permute-start(bf16[128,1024]{1,0:T(8,128)(2,1)S(1)} %attention.1.a), channel_id=1, source_target_pairs={{0,1},{1,0},{2,3},{3,2},{4,5},{5,4},{6,7},{7,6},{8,9},{9,8},{10,11... | collective-permute-start | bytes 786440 | tf_op jit(solution)/shard_map/ppermute | solution.py:645
  38.6 2.0 %collective-permute-start.7 = (bf16[128,1024]{1,0:T(8,128)(2,1)S(1)}, bf16[128,1024]{1,0:T(8,128)(2,1)S(1)}, u32[]{:S(2)}, u32[]{:S(2)}) collective-permute-start(bf16[128,1024]{1,0:T(8,128)(2,1)S(1)} %collective-permute-done.5.b), channel_id=1, source_target_pairs={{0,1},{1,0},{2,3},{3,2},{4,5},{5,4},{6,7},{7,6},{8,9},{9,8},{10,11... | collective-permute-start | bytes 786440 | tf_op jit(solution)/shard_map/ppermute | solution.py:646
  42.5 21.4 %collective-permute-start.8 = (bf16[128,1024]{1,0:T(8,128)(2,1)S(1)}, bf16[128,1024]{1,0:T(8,128)(2,1)S(1)}, u32[]{:S(2)}, u32[]{:S(2)}) collective-permute-start(bf16[128,1024]{1,0:T(8,128)(2,1)S(1)} %get-tuple-element.67), channel_id=1, source_target_pairs={{0,8},{4,12},{8,0},{12,4},{1,9},{5,13},{9,1},{13,5},{2,10},{6,14},... | collective-permute-start | bytes 786440 | tf_op jit(solution)/shard_map/ppermute | solution.py:651
  43.6 20.3 %collective-permute-start.9 = (bf16[128,1024]{1,0:T(8,128)(2,1)S(1)}, bf16[128,1024]{1,0:T(8,128)(2,1)S(1)}, u32[]{:S(2)}, u32[]{:S(2)}) collective-permute-start(bf16[128,1024]{1,0:T(8,128)(2,1)S(1)} %get-tuple-element.68), channel_id=1, source_target_pairs={{0,12},{4,8},{8,4},{12,0},{1,13},{5,9},{9,5},{13,1},{2,14},{6,10},... | collective-permute-start | bytes 786440 | tf_op jit(solution)/shard_map/ppermute | solution.py:651
  46.4 18.2 %collective-permute-start.10 = (bf16[128,1024]{1,0:T(8,128)(2,1)S(1)}, bf16[128,1024]{1,0:T(8,128)(2,1)S(1)}, u32[]{:S(2)}, u32[]{:S(2)}) collective-permute-start(bf16[128,1024]{1,0:T(8,128)(2,1)S(1)} %get-tuple-element.69), channel_id=1, source_target_pairs={{0,4},{4,0},{8,12},{12,8},{1,5},{5,1},{9,13},{13,9},{2,6},{6,2},{1... | collective-permute-start | bytes 786440 | tf_op jit(solution)/shard_map/ppermute | solution.py:651
  65.3 8.9 %collective-permute-start.11 = (f32[24,128]{1,0:T(8,128)S(1)}, f32[24,128]{1,0:T(8,128)S(1)}, u32[]{:S(2)}, u32[]{:S(2)}) collective-permute-start(f32[24,128]{1,0:T(8,128)S(1)} %get-tuple-element.73), channel_id=1, source_target_pairs={{0,2},{1,3},{2,0},{3,1},{4,6},{5,7},{6,4},{7,5},{8,10},{9,11},{10,... | collective-permute-start | bytes 36872 | tf_op jit(solution)/shard_map/ppermute | solution.py:663
  67.8 13.7 %collective-permute-start.15 = (bf16[128,1024]{1,0:T(8,128)(2,1)S(1)}, bf16[128,1024]{1,0:T(8,128)(2,1)S(1)}, u32[]{:S(2)}, u32[]{:S(2)}) collective-permute-start(bf16[128,1024]{1,0:T(8,128)(2,1)S(1)} %get-tuple-element.72.refs_0_), channel_id=1, source_target_pairs={{0,12},{4,8},{8,4},{12,0},{1,13},{5,9},{9,5},{13,1},{2,14},{6,10},... | collective-permute-start | bytes 786440 | tf_op jit(solution)/shard_map/ppermute | solution.py:662
  69.7 23.2 %collective-permute-start.14 = (bf16[128,1024]{1,0:T(8,128)(2,1)S(1)}, bf16[128,1024]{1,0:T(8,128)(2,1)S(1)}, u32[]{:S(2)}, u32[]{:S(2)}) collective-permute-start(bf16[128,1024]{1,0:T(8,128)(2,1)S(1)} %get-tuple-element.72.refs_0_), channel_id=1, source_target_pairs={{0,8},{4,12},{8,0},{12,4},{1,9},{5,13},{9,1},{13,5},{2,10},{6,14},... | collective-permute-start | bytes 786440 | tf_op jit(solution)/shard_map/ppermute | solution.py:662
  74.2 18.7 %collective-permute-start.13 = (bf16[128,1024]{1,0:T(8,128)(2,1)S(1)}, bf16[128,1024]{1,0:T(8,128)(2,1)S(1)}, u32[]{:S(2)}, u32[]{:S(2)}) collective-permute-start(bf16[128,1024]{1,0:T(8,128)(2,1)S(1)} %get-tuple-element.72.refs_0_), channel_id=1, source_target_pairs={{0,4},{4,0},{8,12},{12,8},{1,5},{5,1},{9,13},{13,9},{2,6},{6,2},{1... | collective-permute-start | bytes 786440 | tf_op jit(solution)/shard_map/ppermute | solution.py:662
  74.2 7.3 %collective-permute-start.12 = (f32[24,128]{1,0:T(8,128)S(1)}, f32[24,128]{1,0:T(8,128)S(1)}, u32[]{:S(2)}, u32[]{:S(2)}) collective-permute-start(f32[24,128]{1,0:T(8,128)S(1)} %add.35), channel_id=1, source_target_pairs={{0,1},{1,0},{2,3},{3,2},{4,5},{5,4},{6,7},{7,6},{8,9},{9,8},{10,11... | collective-permute-start | bytes 36872 | tf_op jit(solution)/shard_map/ppermute | solution.py:664
  103.6 2.7 %collective-permute-start.16 = (bf16[2,128,2048]{2,1,0:T(8,128)(2,1)S(1)}, bf16[2,128,2048]{2,1,0:T(8,128)(2,1)S(1)}, u32[]{:S(2)}, u32[]{:S(2)}) collective-permute-start(bf16[2,128,2048]{2,1,0:T(8,128)(2,1)S(1)} %get-tuple-element.79), channel_id=1, source_target_pairs={{0,1},{1,0},{2,3},{3,2},{4,5},{5,4},{6,7},{7,6},{8,9},{9,8},{10,11... | collective-permute-start | bytes 3145736 | tf_op jit(solution)/shard_map/ppermute | solution.py:677
  106.5 14.0 %collective-permute-start.20 = (bf16[128,2048]{1,0:T(8,128)(2,1)S(1)}, bf16[128,2048]{1,0:T(8,128)(2,1)S(1)}, u32[]{:S(2)}, u32[]{:S(2)}) collective-permute-start(bf16[128,2048]{1,0:T(8,128)(2,1)S(1)} %fusion), channel_id=1, source_target_pairs={{0,2},{1,3},{2,0},{3,1},{4,6},{5,7},{6,4},{7,5},{8,10},{9,11},{10,... | collective-permute-start | bytes 1572872 | tf_op jit(solution)/shard_map/ppermute | solution.py:679
  107.0 5.5 %collective-permute-start.19 = (f32[24,128]{1,0:T(8,128)S(1)}, f32[24,128]{1,0:T(8,128)S(1)}, u32[]{:S(2)}, u32[]{:S(2)}) collective-permute-start(f32[24,128]{1,0:T(8,128)S(1)} %add.36.refs_0_), channel_id=1, source_target_pairs={{0,12},{4,8},{8,4},{12,0},{1,13},{5,9},{9,5},{13,1},{2,14},{6,10},... | collective-permute-start | bytes 36872 | tf_op jit(solution)/shard_map/ppermute | solution.py:670
  109.0 4.6 %collective-permute-start.18 = (f32[24,128]{1,0:T(8,128)S(1)}, f32[24,128]{1,0:T(8,128)S(1)}, u32[]{:S(2)}, u32[]{:S(2)}) collective-permute-start(f32[24,128]{1,0:T(8,128)S(1)} %add.36.refs_0_), channel_id=1, source_target_pairs={{0,8},{4,12},{8,0},{12,4},{1,9},{5,13},{9,1},{13,5},{2,10},{6,14},... | collective-permute-start | bytes 36872 | tf_op jit(solution)/shard_map/ppermute | solution.py:670
  109.0 4.6 %collective-permute-start.17 = (f32[24,128]{1,0:T(8,128)S(1)}, f32[24,128]{1,0:T(8,128)S(1)}, u32[]{:S(2)}, u32[]{:S(2)}) collective-permute-start(f32[24,128]{1,0:T(8,128)S(1)} %add.36.refs_0_), channel_id=1, source_target_pairs={{0,4},{4,0},{8,12},{12,8},{1,5},{5,1},{9,13},{13,9},{2,6},{6,2},{1... | collective-permute-start | bytes 36872 | tf_op jit(solution)/shard_map/ppermute | solution.py:670
  120.5 2.7 %collective-permute-start.24 = (bf16[2,128,2048]{2,1,0:T(8,128)(2,1)S(1)}, bf16[2,128,2048]{2,1,0:T(8,128)(2,1)S(1)}, u32[]{:S(2)}, u32[]{:S(2)}) collective-permute-start(bf16[2,128,2048]{2,1,0:T(8,128)(2,1)S(1)} %get-tuple-element.86), channel_id=1, source_target_pairs={{0,1},{1,0},{2,3},{3,2},{4,5},{5,4},{6,7},{7,6},{8,9},{9,8},{10,11... | collective-permute-start | bytes 3145736 | tf_op jit(solution)/shard_map/ppermute | solution.py:677
  123.3 19.7 %collective-permute-start.25 = (bf16[128,2048]{1,0:T(8,128)(2,1)S(1)}, bf16[128,2048]{1,0:T(8,128)(2,1)S(1)}, u32[]{:S(2)}, u32[]{:S(2)}) collective-permute-start(bf16[128,2048]{1,0:T(8,128)(2,1)S(1)} %fusion.1), channel_id=1, source_target_pairs={{0,2},{1,3},{2,0},{3,1},{4,6},{5,7},{6,4},{7,5},{8,10},{9,11},{10,... | collective-permute-start | bytes 1572872 | tf_op jit(solution)/shard_map/ppermute | solution.py:679
  124.7 18.2 %collective-permute-start.21 = (bf16[128,1024]{1,0:T(8,128)(2,1)S(1)}, bf16[128,1024]{1,0:T(8,128)(2,1)S(1)}, u32[]{:S(2)}, u32[]{:S(2)}) collective-permute-start(bf16[128,1024]{1,0:T(8,128)(2,1)S(1)} %activate.2.a), channel_id=1, source_target_pairs={{0,2},{1,3},{2,0},{3,1},{4,6},{5,7},{6,4},{7,5},{8,10},{9,11},{10,... | collective-permute-start | bytes 786440 | tf_op jit(solution)/shard_map/ppermute | solution.py:682
  143.0 1.5 collective-permute-start.23
  144.5 8.3 %collective-permute-start.28 = (bf16[128,1024]{1,0:T(8,128)(2,1)S(1)}, bf16[128,1024]{1,0:T(8,128)(2,1)S(1)}, u32[]{:S(2)}, u32[]{:S(2)}) collective-permute-start(bf16[128,1024]{1,0:T(8,128)(2,1)S(1)} %activate.3.a), channel_id=1, source_target_pairs={{0,2},{1,3},{2,0},{3,1},{4,6},{5,7},{6,4},{7,5},{8,10},{9,11},{10,... | collective-permute-start | bytes 786440 | tf_op jit(solution)/shard_map/ppermute | solution.py:682
  144.9 7.9 %collective-permute-start.22 = (bf16[128,1024]{1,0:T(8,128)(2,1)S(1)}, bf16[128,1024]{1,0:T(8,128)(2,1)S(1)}, u32[]{:S(2)}, u32[]{:S(2)}) collective-permute-start(bf16[128,1024]{1,0:T(8,128)(2,1)S(1)} %activate.2.a), channel_id=1, source_target_pairs={{0,1},{1,0},{2,3},{3,2},{4,5},{5,4},{6,7},{7,6},{8,9},{9,8},{10,11... | collective-permute-start | bytes 786440 | tf_op jit(solution)/shard_map/ppermute | solution.py:683
  144.9 13.0 %collective-permute-start.29 = (bf16[128,1024]{1,0:T(8,128)(2,1)S(1)}, bf16[128,1024]{1,0:T(8,128)(2,1)S(1)}, u32[]{:S(2)}, u32[]{:S(2)}) collective-permute-start(bf16[128,1024]{1,0:T(8,128)(2,1)S(1)} %activate.3.a), channel_id=1, source_target_pairs={{0,1},{1,0},{2,3},{3,2},{4,5},{5,4},{6,7},{7,6},{8,9},{9,8},{10,11... | collective-permute-start | bytes 786440 | tf_op jit(solution)/shard_map/ppermute | solution.py:683
  152.8 5.1 %collective-permute-start.30 = (bf16[128,1024]{1,0:T(8,128)(2,1)S(1)}, bf16[128,1024]{1,0:T(8,128)(2,1)S(1)}, u32[]{:S(2)}, u32[]{:S(2)}) collective-permute-start(bf16[128,1024]{1,0:T(8,128)(2,1)S(1)} %collective-permute-done.28.b), channel_id=1, source_target_pairs={{0,1},{1,0},{2,3},{3,2},{4,5},{5,4},{6,7},{7,6},{8,9},{9,8},{10,11... | collective-permute-start | bytes 786440 | tf_op jit(solution)/shard_map/ppermute | solution.py:684
  155.7 20.5 %collective-permute-start.26 = (bf16[128,1024]{1,0:T(8,128)(2,1)S(1)}, bf16[128,1024]{1,0:T(8,128)(2,1)S(1)}, u32[]{:S(2)}, u32[]{:S(2)}) collective-permute-start(bf16[128,1024]{1,0:T(8,128)(2,1)S(1)} %get-tuple-element.90), channel_id=1, source_target_pairs={{0,8},{4,12},{8,0},{12,4},{1,9},{5,13},{9,1},{13,5},{2,10},{6,14},... | collective-permute-start | bytes 786440 | tf_op jit(solution)/shard_map/ppermute | solution.py:695
  155.9 20.3 %collective-permute-start.27 = (bf16[128,1024]{1,0:T(8,128)(2,1)S(1)}, bf16[128,1024]{1,0:T(8,128)(2,1)S(1)}, u32[]{:S(2)}, u32[]{:S(2)}) collective-permute-start(bf16[128,1024]{1,0:T(8,128)(2,1)S(1)} %get-tuple-element.91), channel_id=1, source_target_pairs={{0,12},{4,8},{8,4},{12,0},{1,13},{5,9},{9,5},{13,1},{2,14},{6,10},... | collective-permute-start | bytes 786440 | tf_op jit(solution)/shard_map/ppermute | solution.py:695
  160.8 19.6 %collective-permute-start.31 = (bf16[128,1024]{1,0:T(8,128)(2,1)S(1)}, bf16[128,1024]{1,0:T(8,128)(2,1)S(1)}, u32[]{:S(2)}, u32[]{:S(2)}) collective-permute-start(bf16[128,1024]{1,0:T(8,128)(2,1)S(1)} %get-tuple-element.94), channel_id=1, source_target_pairs={{0,4},{4,0},{8,12},{12,8},{1,5},{5,1},{9,13},{13,9},{2,6},{6,2},{1... | collective-permute-start | bytes 786440 | tf_op jit(solution)/shard_map/ppermute | solution.py:697
  (14 other events, 251.3 us)

commit v6 on v5

--- a/solution.py
+++ b/solution.py
@@ -191,6 +191,12 @@
     return [(i, i ^ flip) for i in range(lanes)]
 
 
+def scatter_blocks(parts, n):
+    near = lax.ppermute(parts[3], "ep", pairs(n, 1))
+    far = (parts[2].astype(jnp.float32) + near.astype(jnp.float32)).astype(jnp.bfloat16)
+    return [parts[0], lax.ppermute(far, "ep", pairs(n, 2)), lax.ppermute(parts[1], "ep", pairs(n, 1))]
+
+
 def query_of(device, lane):
     return 2 * (lane & 1) + ((lane >> 1) ^ (device & 1))
 
@@ -436,10 +442,10 @@
     )(here, *pieces)
 
 
-def residual_body(hidden, p0, p1, p2, p3, gain, router, after, out, stats):
+def residual_body(hidden, p0, p1, p2, gain, router, after, out, stats):
     rows = stats.shape[0]
     total = hidden[...].astype(jnp.float32) + p0[...].astype(jnp.float32)
-    for part in (p1, p2, p3):
+    for part in (p1, p2):
         total = total + part[...].astype(jnp.float32)
     narrow = total.astype(jnp.bfloat16)
     out[...] = narrow
@@ -464,10 +470,28 @@
             jax.ShapeDtypeStruct((experts + 8, length), jnp.float32),
         ],
         [],
-        in_specs=[VMEM] * 7 + [pl.BlockSpec(memory_space=pl.ANY)],
+        in_specs=[VMEM] * 6 + [pl.BlockSpec(memory_space=pl.ANY)],
         out_specs=[VMEM] * 2,
         name="residual",
     )(hidden, *parts, gain, router, after)
+
+
+def join_body(a, b, c, d, out):
+    length = a.shape[1]
+    for j, ref in enumerate((a, b, c, d)):
+        out[:, j * length : (j + 1) * length] = ref[...]
+
+
+def join(parts):
+    rows, length = parts[0].shape
+    return call(
+        join_body,
+        jax.ShapeDtypeStruct((rows, 4 * length), parts[0].dtype),
+        [],
+        in_specs=[VMEM] * 4,
+        out_specs=VMEM,
+        name="join",
+    )(*parts)
 
 
 def gate_up_body(ds, order, *refs):
@@ -516,12 +540,12 @@
 
 
 def activate_body(ds, features, here, kept, taken, across, pick, *refs):
-    stats = refs[: len(ds)]
-    pieces = refs[len(ds) : 2 * len(ds)]
-    out = refs[2 * len(ds)]
+    stats = refs[0]
+    pieces = refs[1 : 1 + len(ds)]
+    out = refs[1 + len(ds)]
     _, local, capacity, length = pick.shape
     hid = out.shape[1]
-    experts = stats[0].shape[0] - 8
+    experts = stats.shape[0] - 8
     device, lane = (here[0], here[1])
     expert = lax.broadcasted_iota(jnp.int32, (experts, length), 0)
     for k, d in enumerate(ds):
@@ -529,8 +553,9 @@
         chosen = jnp.zeros((experts, length), jnp.float32)
         for c in range(8):
             chosen = jnp.where(ids[c : c + 1, :] == expert, 1.0, chosen)
-        inv_rms = lax.rsqrt(stats[k][experts : experts + 1, :] / features + norm_eps)
-        logits = jnp.where(chosen > 0.0, stats[k][:experts, :] * inv_rms, -jnp.inf)
+        block = slice(d * length, (d + 1) * length)
+        inv_rms = lax.rsqrt(stats[experts : experts + 1, block] / features + norm_eps)
+        logits = jnp.where(chosen > 0.0, stats[:experts, block] * inv_rms, -jnp.inf)
         grown = jnp.exp(logits - jnp.max(logits, axis=0, keepdims=True))
         mix = grown / jnp.sum(grown, axis=0, keepdims=True)
         mix = jnp.sum(jnp.where(expert == device * local + lane, mix, 0.0), axis=0, keepdims=True)
@@ -551,10 +576,10 @@
         functools.partial(activate_body, ds, features),
         jax.ShapeDtypeStruct((rows, both // 2), jnp.bfloat16),
         [],
-        in_specs=[SMEM] + [VMEM] * (4 + 2 * len(ds)),
+        in_specs=[SMEM] + [VMEM] * (5 + len(ds)),
         out_specs=VMEM,
         name="activate",
-    )(here, kept, taken, across, pick, *[stats[d] for d in ds], *[pieces[d] for d in ds])
+    )(here, kept, taken, across, pick, stats, *[pieces[d] for d in ds])
 
 
 def down_body(ds, order, a, b, c, d, spread, weight, *rest):
@@ -648,53 +673,60 @@
     router = jnp.pad(router_weight, ((0, 0), (0, 128 - experts)))
     parts = project(here, (attended, far, near, farther), out_proj)
     kept, w_gate_up = lax.optimization_barrier((parts[0], w_gate_up))
-    sent = [lax.ppermute(parts[d], "ep", pairs(n, d)) for d in (2, 3, 1)]
+    sent = scatter_blocks([kept] + list(parts[1:]), n)
     pick, spread = routing(here, pieces, experts, local, capacity)
     weight = jnp.transpose(w_gate_up, (0, 2, 1, 3))
-    residual, own_stats = residual_and_stats(
-        hidden, [kept] + sent, gain, router, experts, weight
-    )
-
-    residual, w_down = lax.optimization_barrier((residual, w_down))
-    w_down = w_down * one
-    tokens = {0: residual}
+    sent[0], pick = lax.optimization_barrier((sent[0], pick))
+    residual, own_stats = residual_and_stats(hidden, sent, gain, router, experts, weight)
+
+    tokens, stats = ({0: residual}, {0: own_stats})
     for d in (2, 3, 1):
         tokens[d] = lax.ppermute(residual, "ep", pairs(n, d))
-    own_stats = own_stats + lax.ppermute(own_stats, "tp", pairs(n, 2))
-    own_stats = own_stats + lax.ppermute(own_stats, "tp", pairs(n, 1))
-    own_stats, w_down, tokens[1], tokens[2], tokens[3] = lax.optimization_barrier(
-        (own_stats, w_down, tokens[1], tokens[2], tokens[3])
-    )
-    stats = {0: own_stats}
     for d in (2, 3, 1):
         stats[d] = lax.ppermute(own_stats, "ep", pairs(n, d))
+    tokens, stats = lax.optimization_barrier((tokens, stats))
+    stats = join([stats[d] for d in range(n)])
+    stats_far = lax.ppermute(stats, "tp", pairs(n, 2))
 
     features = width_here * n
-
-    def exchange(ds, order, before):
-        kept, given = gate_up(ds, order, [tokens[d] for d in ds], gain, pick, weight)
-        given, *before = lax.optimization_barrier((given, *before))
-        taken = lax.ppermute(given, "tp", pairs(n, 1))
-        chip_far = (kept[1].astype(jnp.float32) + taken[1].astype(jnp.float32)).astype(jnp.bfloat16)
-        return (chip_far, before, kept, taken, lax.ppermute(chip_far, "tp", pairs(n, 2)))
 
     def spread_act(act):
         far = lax.ppermute(act, "tp", pairs(n, 2))
         near = lax.ppermute(act, "tp", pairs(n, 1))
         return [act, far, near, lax.ppermute(far, "tp", pairs(n, 1))]
 
-    chip_far, _, *first = exchange((2, 3), order, [])
-    order, *_ = lax.optimization_barrier((order, chip_far, stats[1], stats[2], stats[3]))
-    _, first[2:], *second = exchange((0, 1), order, first[2:])
-    act = activate((2, 3), features, here, *first, pick, stats, pieces)
-    acts = spread_act(act)
-    act = activate((0, 1), features, here, *second, pick, stats, pieces)
-    acts[3], act = lax.optimization_barrier((acts[3], act))
-    others = spread_act(act)
-    parts = down((2, 3), order, acts, spread, w_down)
-    returned = [lax.ppermute(part, "ep", pairs(n, d)) for part, d in zip(parts, (2, 3))]
-    mine, near = down((0, 1), order, others, spread, w_down)
-    returned += [mine, lax.ppermute(near, "ep", pairs(n, 1))]
+    def chip_sum(kept, taken):
+        return (kept[1].astype(jnp.float32) + taken[1].astype(jnp.float32)).astype(jnp.bfloat16)
+
+    one_chunk, two_chunk = ((2, 3), (0, 1))
+    kept, given = gate_up(one_chunk, order, [tokens[d] for d in one_chunk], gain, pick, weight)
+    given, stats_far = lax.optimization_barrier((given, stats_far))
+    taken = lax.ppermute(given, "tp", pairs(n, 1))
+    stats = stats + stats_far
+    stats_near = lax.ppermute(stats, "tp", pairs(n, 1))
+    far_sum = chip_sum(kept, taken)
+    across = lax.ppermute(far_sum, "tp", pairs(n, 2))
+
+    order, _, stats_near = lax.optimization_barrier((order, far_sum, stats_near))
+    stats = stats + stats_near
+    kept_2, given = gate_up(two_chunk, order, [tokens[d] for d in two_chunk], gain, pick, weight)
+    given, across = lax.optimization_barrier((given, across))
+    taken_2 = lax.ppermute(given, "tp", pairs(n, 1))
+    acts = spread_act(activate(one_chunk, features, here, kept, taken, across, pick, stats, pieces))
+    far_sum = chip_sum(kept_2, taken_2)
+    far_sum, acts[1] = lax.optimization_barrier((far_sum, acts[1]))
+    acts[3] = lax.ppermute(acts[1], "tp", pairs(n, 1))
+    across = lax.ppermute(far_sum, "tp", pairs(n, 2))
+    parts = down(one_chunk, order, acts, spread, w_down)
+    near = lax.ppermute(parts[1], "ep", pairs(n, 1))
+    far = (parts[0].astype(jnp.float32) + near.astype(jnp.float32)).astype(jnp.bfloat16)
+    across, far = lax.optimization_barrier((across, far))
+    far = lax.ppermute(far, "ep", pairs(n, 2))
+    acts = spread_act(
+        activate(two_chunk, features, here, kept_2, taken_2, across, pick, stats, pieces)
+    )
+    mine, near = down(two_chunk, order, acts, spread, w_down)
+    returned = [mine, far, lax.ppermute(near, "ep", pairs(n, 1))]
     total = residual.astype(jnp.float32)
     for part in returned:
         total = total + part.astype(jnp.float32)

time: 182 us -> 168 us (0.923)
  local copies, waits for them, and re-layouts: 21.3 us -> 13.4 us
  other arithmetic: 11.9 us -> 4.78 us
    ppermute x3, waiting for transfers between devices: 2.21 us -> 15.6 us  [per_device_square(): stats[d] = lax.ppermute(own_stats, 'ep', pairs(n, d))]
    ppermute x3, waiting for transfers between devices: 11.4 us -> 0.01 us  [per_device_square(): tokens[d] = lax.ppermute(residual, 'ep', pairs(n, d))]
    ppermute x12 -> x13, waiting for transfers between devices: 32.3 us -> 42.3 us  [the longest x1 9.23 us: per_device_square(): far = lax.ppermute(far, 'ep', pairs(n, 2))]
    ppermute x2, waiting for transfers between devices: 24 us -> 14.6 us  [spread_act(): far = lax.ppermute(act, 'tp', pairs(n, 2))]
    unnamed x31, local copies, waits for them, and re-layouts: 9.95 us -> 2.09 us
    mul x1 -> x0, other arithmetic: 7.23 us -> none  [per_device_square(): w_down = w_down * one]
    ppermute x3, starting transfers between devices: 9.46 us -> 13.2 us  [per_device_square(): lax.ppermute(pieces[d], 'ep', pairs(n, d))]
    ppermute x3, starting transfers between devices: 6.4 us -> 4.42 us  [per_device_square(): tokens[d] = lax.ppermute(residual, 'ep', pairs(n, d))]
  transfers between devices with their start and end apart: 32 -> 32, of which waited for: 16 -> 17; matrix products, arithmetic and copies ran while one was open for 12% -> 9% of each run, Pallas kernels for 8% -> 11%
where the time goes in v6:
time: 168 us; the launch traced here: 167 us
  waiting for transfers between devices  81.7 us (49%)
  starting transfers between devices  41.2 us (25%)
  Pallas kernels  25.7 us (15%)
  local copies, waits for them, and re-layouts  13.4 us (8%)
  other arithmetic  4.78 us (3%)
    ppermute x3, waiting for transfers between devices, per_device_square(): stats[d] = lax.ppermute(own_stats, 'ep', pairs(n, d))  15.6 us
    ppermute x2, waiting for transfers between devices, spread_act(): far = lax.ppermute(act, 'tp', pairs(n, 2))  14.6 us
    ppermute x3, starting transfers between devices, per_device_square(): lax.ppermute(pieces[d], 'ep', pairs(n, d))  13.2 us
    optimization_barrier x1, local copies, waits for them, and re-layouts, per_device_square(): kept, w_gate_up = lax.optimization_barrier((parts[0], w_gate_up))  11.2 us
    pallas_call x2, Pallas kernels, gate_up(): call(functools.partial(gate_up_body, ds), [shape] * 2, None, grid_spec=pl...  9.97 us
    ppermute x1, waiting for transfers between devices, per_device_square(): far = lax.ppermute(far, 'ep', pairs(n, 2))  9.23 us
    ppermute x2, waiting for transfers between devices, per_device_square(): across = lax.ppermute(far_sum, 'tp', pairs(n, 2))  8.83 us
    ppermute x1, waiting for transfers between devices, per_device_square(): near = lax.ppermute(parts[1], 'ep', pairs(n, 1))  7.66 us
  transfers between devices with their start and end apart: 32, of which 17 were waited for; matrix products, arithmetic and copies ran while one was open for 9% of the time, Pallas kernels for 11%

profile of v6, /device:TPU:0, one launch (start us, length us, event | category | flops | bytes accessed | tf_op | source)
XLA Modules:
  0.0 167.3 jit_solution(1104529309166194953)
XLA Ops:
  6.0 10.8 %collective-permute-start.2 = (bf16[272,128]{1,0:T(8,128)(2,1)S(1)}, bf16[272,128]{1,0:T(8,128)(2,1)S(1)}, u32[]{:S(2)}, u32[]{:S(2)}) collective-permute-start(bf16[272,128]{1,0:T(8,128)(2,1)S(1)} %get-tuple-element.64), channel_id=1, source_target_pairs={{0,4},{4,0},{8,12},{12,8},{1,5},{5,1},{9,13},{13,9},{2,6},{6,2},{1... | collective-permute-start | bytes 208904 | tf_op jit(solution)/shard_map/ppermute | solution.py:663
  16.8 2.4 %collective-permute-start.4 = (bf16[272,128]{1,0:T(8,128)(2,1)S(1)}, bf16[272,128]{1,0:T(8,128)(2,1)S(1)}, u32[]{:S(2)}, u32[]{:S(2)}) collective-permute-start(bf16[272,128]{1,0:T(8,128)(2,1)S(1)} %get-tuple-element.66), channel_id=1, source_target_pairs={{0,12},{4,8},{8,4},{12,0},{1,13},{5,9},{9,5},{13,1},{2,14},{6,10},... | collective-permute-start | bytes 208904 | tf_op jit(solution)/shard_map/ppermute | solution.py:663
  19.2 1.7 %broadcast_multiply_fusion.weight = bf16[1024,1024]{1,0:T(8,128)(2,1)S(1)} fusion(bf16[1024,1024]{1,0:T(8,128)(2,1)} %param.21, bf16[]{:T(256)} %constant.23.clone.1), kind=kLoop, calls=%fused_computation.3 | loop fusion | flops 1048576 | bytes 4194306 | tf_op jit(solution)/shard_map/mul | solution.py:667
  21.9 3.4 %collective-permute-done.3.c2.refs_1_ = bf16[272,128]{1,0:T(8,128)(2,1)S(1)} collective-permute-done((bf16[272,128]{1,0:T(8,128)(2,1)S(1)}, bf16[272,128]{1,0:T(8,128)(2,1)S(1)}, u32[]{:S(2)}, u32[]{:S(2)}) %collective-permute-start.3) | collective-permute-done | bytes 69664 | tf_op jit(solution)/shard_map/ppermute | solution.py:663
  25.3 3.4 %attention.1.a = bf16[128,1024]{1,0:T(8,128)(2,1)S(1)} custom-call(s32[2]{0:T(128)S(1)} %pad_add_fusion.here, s32[4,4]{1,0:T(4,128)S(1)} %copy-done.4, s32[8]{0:T(128)S(1)} %copy-done.6, bf16[1280,128]{1,0:T(8,128)(2,1)S(1)} %collective-permute-done.1.q, bf16[272,128]{1,0:T(8,128)(2,1)S(1)} %get-tuple-element.63.c0.refs_1_, ...), custom_call_target="tpu_custom_call" | custom-call | flops 1048576 | bytes 262144 | tf_op jit(solution)/shard_map/attention/pallas_call | solution.py:370
  28.8 5.2 %collective-permute-start.5 = (bf16[128,1024]{1,0:T(8,128)(2,1)S(1)}, bf16[128,1024]{1,0:T(8,128)(2,1)S(1)}, u32[]{:S(2)}, u32[]{:S(2)}) collective-permute-start(bf16[128,1024]{1,0:T(8,128)(2,1)S(1)} %attention.1.a), channel_id=1, source_target_pairs={{0,2},{1,3},{2,0},{3,1},{4,6},{5,7},{6,4},{7,5},{8,10},{9,11},{10,... | collective-permute-start | bytes 786440 | tf_op jit(solution)/shard_map/ppermute | solution.py:669
  33.9 4.3 %collective-permute-done.5.b = bf16[128,1024]{1,0:T(8,128)(2,1)S(1)} collective-permute-done((bf16[128,1024]{1,0:T(8,128)(2,1)S(1)}, bf16[128,1024]{1,0:T(8,128)(2,1)S(1)}, u32[]{:S(2)}, u32[]{:S(2)}) %collective-permute-start.5) | collective-permute-done | bytes 262176 | tf_op jit(solution)/shard_map/ppermute | solution.py:669
  38.3 1.5 collective-permute-done.7.d
  39.8 1.9 %project.1 = (bf16[128,1024]{1,0:T(8,128)(2,1)S(1)}, bf16[128,1024]{1,0:T(8,128)(2,1)S(1)}, bf16[128,1024]{1,0:T(8,128)(2,1)S(1)}, bf16[128,1024]{1,0:T(8,128)(2,1)S(1)}) custom-call(s32[2]{0:T(128)S(1)} %pad_add_fusion.here, bf16[128,1024]{1,0:T(8,128)(2,1)S(1)} %attention.1.a, bf16[128,1024]{1,0:T(8,128)(2,1)S(1)} %collective-permute-done.5.b, ...), custom_call_target="tpu_custom_call" | custom-call | flops 1048576 | bytes 262144 | tf_op jit(solution)/shard_map/project/pallas_call | solution.py:395
  41.7 1.8 %collective-permute-start.8 = (bf16[128,1024]{1,0:T(8,128)(2,1)S(1)}, bf16[128,1024]{1,0:T(8,128)(2,1)S(1)}, u32[]{:S(2)}, u32[]{:S(2)}) collective-permute-start(bf16[128,1024]{1,0:T(8,128)(2,1)S(1)} %get-tuple-element.78), channel_id=1, source_target_pairs={{0,4},{4,0},{8,12},{12,8},{1,5},{5,1},{9,13},{13,9},{2,6},{6,2},{1... | collective-permute-start | bytes 786440 | tf_op jit(solution)/shard_map/ppermute | solution.py:195
  43.8 7.1 %collective-permute-done.8 = bf16[128,1024]{1,0:T(8,128)(2,1)S(1)} collective-permute-done((bf16[128,1024]{1,0:T(8,128)(2,1)S(1)}, bf16[128,1024]{1,0:T(8,128)(2,1)S(1)}, u32[]{:S(2)}, u32[]{:S(2)}) %collective-permute-start.8) | collective-permute-done | bytes 262176 | tf_op jit(solution)/shard_map/ppermute | solution.py:195
  53.2 11.2 %copy.25 = bf16[4,1024,2,1024]{3,1,2,0:T(8,128)(2,1)S(1)} copy(bf16[4,1024,2,1024]{3,2,1,0:T(2,128)(2,1)} %param.24) | data formatting | bytes 33554432 | tf_op jit(solution)/shard_map/optimization_barrier | solution.py:675
  65.9 2.9 %collective-permute-start.12 = (bf16[128,1024]{1,0:T(8,128)(2,1)S(1)}, bf16[128,1024]{1,0:T(8,128)(2,1)S(1)}, u32[]{:S(2)}, u32[]{:S(2)}) collective-permute-start(bf16[128,1024]{1,0:T(8,128)(2,1)S(1)} %get-tuple-element.95.refs_0_), channel_id=1, source_target_pairs={{0,8},{4,12},{8,0},{12,4},{1,9},{5,13},{9,1},{13,5},{2,10},{6,14},... | collective-permute-start | bytes 786440 | tf_op jit(solution)/shard_map/ppermute | solution.py:684
  69.5 3.6 %collective-permute-start.15 = (f32[24,128]{1,0:T(8,128)S(1)}, f32[24,128]{1,0:T(8,128)S(1)}, u32[]{:S(2)}, u32[]{:S(2)}) collective-permute-start(f32[24,128]{1,0:T(8,128)S(1)} %get-tuple-element.88.a), channel_id=1, source_target_pairs={{0,8},{4,12},{8,0},{12,4},{1,9},{5,13},{9,1},{13,5},{2,10},{6,14},... | collective-permute-start | bytes 36872 | tf_op jit(solution)/shard_map/ppermute | solution.py:686
  73.1 8.8 %collective-permute-done.14.b = f32[24,128]{1,0:T(8,128)S(1)} collective-permute-done((f32[24,128]{1,0:T(8,128)S(1)}, f32[24,128]{1,0:T(8,128)S(1)}, u32[]{:S(2)}, u32[]{:S(2)}) %collective-permute-start.14) | collective-permute-done | bytes 12320 | tf_op jit(solution)/shard_map/ppermute | solution.py:686
  81.9 2.3 %collective-permute-start.16 = (f32[24,128]{1,0:T(8,128)S(1)}, f32[24,128]{1,0:T(8,128)S(1)}, u32[]{:S(2)}, u32[]{:S(2)}) collective-permute-start(f32[24,128]{1,0:T(8,128)S(1)} %get-tuple-element.88.a), channel_id=1, source_target_pairs={{0,12},{4,8},{8,4},{12,0},{1,13},{5,9},{9,5},{13,1},{2,14},{6,10},... | collective-permute-start | bytes 36872 | tf_op jit(solution)/shard_map/ppermute | solution.py:686
  84.2 6.8 %collective-permute-done.15.c = f32[24,128]{1,0:T(8,128)S(1)} collective-permute-done((f32[24,128]{1,0:T(8,128)S(1)}, f32[24,128]{1,0:T(8,128)S(1)}, u32[]{:S(2)}, u32[]{:S(2)}) %collective-permute-start.15) | collective-permute-done | bytes 12320 | tf_op jit(solution)/shard_map/ppermute | solution.py:686
  91.1 1.8 %collective-permute-start.17 = (f32[24,512]{1,0:T(8,128)S(1)}, f32[24,512]{1,0:T(8,128)S(1)}, u32[]{:S(2)}, u32[]{:S(2)}) collective-permute-start(f32[24,512]{1,0:T(8,128)S(1)} %join.1), channel_id=1, source_target_pairs={{0,2},{1,3},{2,0},{3,1},{4,6},{5,7},{6,4},{7,5},{8,10},{9,11},{10,... | collective-permute-start | bytes 147464 | tf_op jit(solution)/shard_map/ppermute | solution.py:689
  92.9 5.0 %gate_up.2 = (bf16[2,128,2048]{2,1,0:T(8,128)(2,1)S(1)}, bf16[2,128,2048]{2,1,0:T(8,128)(2,1)S(1)}) custom-call(s32[4]{0:T(128)S(1)} %broadcast_xor_fusion.order, bf16[128,1024]{1,0:T(8,128)(2,1)S(1)} %collective-permute-done.12.refs_0_, bf16[128,1024]{1,0:T(8,128)(2,1)S(1)} %collective-permute-done.13.refs_1_, f32[1,1024]{1,0:T(1,128)S(1)} %bitcast.31, ...), custom_call_target="tpu_custom_call" | custom-call | flops 1048576 | bytes 262144 | tf_op jit(solution)/shard_map/gate_up/pallas_call | solution.py:522
  98.0 2.6 %collective-permute-done.18.taken = bf16[2,128,2048]{2,1,0:T(8,128)(2,1)S(1)} collective-permute-done((bf16[2,128,2048]{2,1,0:T(8,128)(2,1)S(1)}, bf16[2,128,2048]{2,1,0:T(8,128)(2,1)S(1)}, u32[]{:S(2)}, u32[]{:S(2)}) %collective-permute-start.18) | collective-permute-done | bytes 1048608 | tf_op jit(solution)/shard_map/ppermute | solution.py:704
  102.4 5.0 %gate_up.3 = (bf16[2,128,2048]{2,1,0:T(8,128)(2,1)S(1)}, bf16[2,128,2048]{2,1,0:T(8,128)(2,1)S(1)}) custom-call(s32[4]{0:T(128)S(1)} %broadcast_xor_fusion.order, bf16[128,1024]{1,0:T(8,128)(2,1)S(1)} %get-tuple-element.95.refs_0_, bf16[128,1024]{1,0:T(8,128)(2,1)S(1)} %collective-permute-done.11.refs_1_, f32[1,1024]{1,0:T(1,128)S(1)} %bitcast.32, ...), custom_call_target="tpu_custom_call" | custom-call | flops 1048576 | bytes 262144 | tf_op jit(solution)/shard_map/gate_up/pallas_call | solution.py:522
  107.4 7.3 %collective-permute-done.20.across = bf16[128,2048]{1,0:T(8,128)(2,1)S(1)} collective-permute-done((bf16[128,2048]{1,0:T(8,128)(2,1)S(1)}, bf16[128,2048]{1,0:T(8,128)(2,1)S(1)}, u32[]{:S(2)}, u32[]{:S(2)}) %collective-permute-start.20) | collective-permute-done | bytes 524320 | tf_op jit(solution)/shard_map/ppermute | solution.py:708
  117.6 6.9 %collective-permute-done.22.b = bf16[128,1024]{1,0:T(8,128)(2,1)S(1)} collective-permute-done((bf16[128,1024]{1,0:T(8,128)(2,1)S(1)}, bf16[128,1024]{1,0:T(8,128)(2,1)S(1)}, u32[]{:S(2)}, u32[]{:S(2)}) %collective-permute-start.22) | collective-permute-done | bytes 262176 | tf_op jit(solution)/shard_map/ppermute | solution.py:694
  126.1 2.8 %down.2 = (bf16[128,1024]{1,0:T(8,128)(2,1)S(1)}, bf16[128,1024]{1,0:T(8,128)(2,1)S(1)}) custom-call(s32[4]{0:T(128)S(1)} %broadcast_xor_fusion.order, bf16[128,1024]{1,0:T(8,128)(2,1)S(1)} %activate.2.a, bf16[128,1024]{1,0:T(8,128)(2,1)S(1)} %collective-permute-done.22.b, bf16[128,1024]{1,0:T(8,128)(2,1)S(1)} %collective-permute-done.24.c, ...), custom_call_target="tpu_custom_call" | custom-call | flops 1048576 | bytes 262144 | tf_op jit(solution)/shard_map/down/pallas_call | solution.py:611
  129.6 7.7 %collective-permute-done.26 = bf16[128,1024]{1,0:T(8,128)(2,1)S(1)} collective-permute-done((bf16[128,1024]{1,0:T(8,128)(2,1)S(1)}, bf16[128,1024]{1,0:T(8,128)(2,1)S(1)}, u32[]{:S(2)}, u32[]{:S(2)}) %collective-permute-start.26) | collective-permute-done | bytes 262176 | tf_op jit(solution)/shard_map/ppermute | solution.py:721
  137.4 1.5 collective-permute-done.23.across
  140.2 7.6 %collective-permute-done.27.b = bf16[128,1024]{1,0:T(8,128)(2,1)S(1)} collective-permute-done((bf16[128,1024]{1,0:T(8,128)(2,1)S(1)}, bf16[128,1024]{1,0:T(8,128)(2,1)S(1)}, u32[]{:S(2)}, u32[]{:S(2)}) %collective-permute-start.27) | collective-permute-done | bytes 262176 | tf_op jit(solution)/shard_map/ppermute | solution.py:694
  147.8 1.8 %collective-permute-start.30 = (bf16[128,1024]{1,0:T(8,128)(2,1)S(1)}, bf16[128,1024]{1,0:T(8,128)(2,1)S(1)}, u32[]{:S(2)}, u32[]{:S(2)}) collective-permute-start(bf16[128,1024]{1,0:T(8,128)(2,1)S(1)} %add_convert_fusion.3), channel_id=1, source_target_pairs={{0,8},{4,12},{8,0},{12,4},{1,9},{5,13},{9,1},{13,5},{2,10},{6,14},... | collective-permute-start | bytes 786440 | tf_op jit(solution)/shard_map/ppermute | solution.py:724
  149.7 2.8 %down.3 = (bf16[128,1024]{1,0:T(8,128)(2,1)S(1)}, bf16[128,1024]{1,0:T(8,128)(2,1)S(1)}) custom-call(s32[4]{0:T(128)S(1)} %broadcast_xor_fusion.order, bf16[128,1024]{1,0:T(8,128)(2,1)S(1)} %activate.3.a, bf16[128,1024]{1,0:T(8,128)(2,1)S(1)} %collective-permute-done.27.b, bf16[128,1024]{1,0:T(8,128)(2,1)S(1)} %collective-permute-done.28.c, ...), custom_call_target="tpu_custom_call" | custom-call | flops 1048576 | bytes 262144 | tf_op jit(solution)/shard_map/down/pallas_call | solution.py:611
  152.5 1.4 collective-permute-start.31
  153.9 9.2 %collective-permute-done.30 = bf16[128,1024]{1,0:T(8,128)(2,1)S(1)} collective-permute-done((bf16[128,1024]{1,0:T(8,128)(2,1)S(1)}, bf16[128,1024]{1,0:T(8,128)(2,1)S(1)}, u32[]{:S(2)}, u32[]{:S(2)}) %collective-permute-start.30) | collective-permute-done | bytes 262176 | tf_op jit(solution)/shard_map/ppermute | solution.py:724
  163.1 3.3 %collective-permute-done.31 = bf16[128,1024]{1,0:T(8,128)(2,1)S(1)} collective-permute-done((bf16[128,1024]{1,0:T(8,128)(2,1)S(1)}, bf16[128,1024]{1,0:T(8,128)(2,1)S(1)}, u32[]{:S(2)}, u32[]{:S(2)}) %collective-permute-start.31) | collective-permute-done | bytes 262176 | tf_op jit(solution)/shard_map/ppermute | solution.py:729
  (96 shorter events, 20.8 us)
Async XLA Ops:
  0.0 4.2 %collective-permute-start = (bf16[1024,128]{1,0:T(8,128)(2,1)}, bf16[1024,128]{1,0:T(8,128)(2,1)S(1)}, u32[]{:S(2)}, u32[]{:S(2)}) collective-permute-start(bf16[1024,128]{1,0:T(8,128)(2,1)} %bitcast.34), channel_id=1, source_target_pairs={{1,2},{2,1},{4,7},{7,4},{9,10},{10,9},{12,15},{15,12},{17,18},{18,... | collective-permute-start | bytes 786440 | tf_op jit(solution)/shard_map/ppermute | solution.py:208
  5.2 20.1 %collective-permute-start.1 = (bf16[1280,128]{1,0:T(8,128)(2,1)S(1)}, bf16[1280,128]{1,0:T(8,128)(2,1)S(1)}, u32[]{:S(2)}, u32[]{:S(2)}) collective-permute-start(bf16[1280,128]{1,0:T(8,128)(2,1)S(1)} %pad_maximum_fusion), channel_id=1, source_target_pairs={{0,0},{1,8},{2,6},{3,14},{4,12},{5,4},{6,10},{7,2},{8,1},{9,9},{10... | collective-permute-start | bytes 983048 | tf_op jit(solution)/shard_map/ppermute | solution.py:218
  6.0 15.9 %collective-permute-start.2 = (bf16[272,128]{1,0:T(8,128)(2,1)S(1)}, bf16[272,128]{1,0:T(8,128)(2,1)S(1)}, u32[]{:S(2)}, u32[]{:S(2)}) collective-permute-start(bf16[272,128]{1,0:T(8,128)(2,1)S(1)} %get-tuple-element.64), channel_id=1, source_target_pairs={{0,4},{4,0},{8,12},{12,8},{1,5},{5,1},{9,13},{13,9},{2,6},{6,2},{1... | collective-permute-start | bytes 208904 | tf_op jit(solution)/shard_map/ppermute | solution.py:663
  16.8 8.5 %collective-permute-start.3 = (bf16[272,128]{1,0:T(8,128)(2,1)S(1)}, bf16[272,128]{1,0:T(8,128)(2,1)S(1)}, u32[]{:S(2)}, u32[]{:S(2)}) collective-permute-start(bf16[272,128]{1,0:T(8,128)(2,1)S(1)} %get-tuple-element.65), channel_id=1, source_target_pairs={{0,8},{4,12},{8,0},{12,4},{1,9},{5,13},{9,1},{13,5},{2,10},{6,14},... | collective-permute-start | bytes 208904 | tf_op jit(solution)/shard_map/ppermute | solution.py:663
  16.8 8.5 %collective-permute-start.4 = (bf16[272,128]{1,0:T(8,128)(2,1)S(1)}, bf16[272,128]{1,0:T(8,128)(2,1)S(1)}, u32[]{:S(2)}, u32[]{:S(2)}) collective-permute-start(bf16[272,128]{1,0:T(8,128)(2,1)S(1)} %get-tuple-element.66), channel_id=1, source_target_pairs={{0,12},{4,8},{8,4},{12,0},{1,13},{5,9},{9,5},{13,1},{2,14},{6,10},... | collective-permute-start | bytes 208904 | tf_op jit(solution)/shard_map/ppermute | solution.py:663
  28.8 9.5 %collective-permute-start.5 = (bf16[128,1024]{1,0:T(8,128)(2,1)S(1)}, bf16[128,1024]{1,0:T(8,128)(2,1)S(1)}, u32[]{:S(2)}, u32[]{:S(2)}) collective-permute-start(bf16[128,1024]{1,0:T(8,128)(2,1)S(1)} %attention.1.a), channel_id=1, source_target_pairs={{0,2},{1,3},{2,0},{3,1},{4,6},{5,7},{6,4},{7,5},{8,10},{9,11},{10,... | collective-permute-start | bytes 786440 | tf_op jit(solution)/shard_map/ppermute | solution.py:669
  33.9 4.4 %collective-permute-start.6 = (bf16[128,1024]{1,0:T(8,128)(2,1)S(1)}, bf16[128,1024]{1,0:T(8,128)(2,1)S(1)}, u32[]{:S(2)}, u32[]{:S(2)}) collective-permute-start(bf16[128,1024]{1,0:T(8,128)(2,1)S(1)} %attention.1.a), channel_id=1, source_target_pairs={{0,1},{1,0},{2,3},{3,2},{4,5},{5,4},{6,7},{7,6},{8,9},{9,8},{10,11... | collective-permute-start | bytes 786440 | tf_op jit(solution)/shard_map/ppermute | solution.py:670
  38.3 1.5 collective-permute-start.7
  41.7 9.2 %collective-permute-start.8 = (bf16[128,1024]{1,0:T(8,128)(2,1)S(1)}, bf16[128,1024]{1,0:T(8,128)(2,1)S(1)}, u32[]{:S(2)}, u32[]{:S(2)}) collective-permute-start(bf16[128,1024]{1,0:T(8,128)(2,1)S(1)} %get-tuple-element.78), channel_id=1, source_target_pairs={{0,4},{4,0},{8,12},{12,8},{1,5},{5,1},{9,13},{13,9},{2,6},{6,2},{1... | collective-permute-start | bytes 786440 | tf_op jit(solution)/shard_map/ppermute | solution.py:195
  43.5 21.0 %collective-permute-start.10 = (bf16[128,1024]{1,0:T(8,128)(2,1)S(1)}, bf16[128,1024]{1,0:T(8,128)(2,1)S(1)}, u32[]{:S(2)}, u32[]{:S(2)}) collective-permute-start(bf16[128,1024]{1,0:T(8,128)(2,1)S(1)} %get-tuple-element.79), channel_id=1, source_target_pairs={{0,4},{4,0},{8,12},{12,8},{1,5},{5,1},{9,13},{13,9},{2,6},{6,2},{1... | collective-permute-start | bytes 786440 | tf_op jit(solution)/shard_map/ppermute | solution.py:197
  51.0 13.5 %collective-permute-start.9 = (bf16[128,1024]{1,0:T(8,128)(2,1)S(1)}, bf16[128,1024]{1,0:T(8,128)(2,1)S(1)}, u32[]{:S(2)}, u32[]{:S(2)}) collective-permute-start(bf16[128,1024]{1,0:T(8,128)(2,1)S(1)} %add_convert_fusion.4), channel_id=1, source_target_pairs={{0,8},{4,12},{8,0},{12,4},{1,9},{5,13},{9,1},{13,5},{2,10},{6,14},... | collective-permute-start | bytes 786440 | tf_op jit(solution)/shard_map/ppermute | solution.py:197
  65.1 25.9 %collective-permute-start.11 = (bf16[128,1024]{1,0:T(8,128)(2,1)S(1)}, bf16[128,1024]{1,0:T(8,128)(2,1)S(1)}, u32[]{:S(2)}, u32[]{:S(2)}) collective-permute-start(bf16[128,1024]{1,0:T(8,128)(2,1)S(1)} %get-tuple-element.95.refs_0_), channel_id=1, source_target_pairs={{0,4},{4,0},{8,12},{12,8},{1,5},{5,1},{9,13},{13,9},{2,6},{6,2},{1... | collective-permute-start | bytes 786440 | tf_op jit(solution)/shard_map/ppermute | solution.py:684
  65.9 25.2 %collective-permute-start.12 = (bf16[128,1024]{1,0:T(8,128)(2,1)S(1)}, bf16[128,1024]{1,0:T(8,128)(2,1)S(1)}, u32[]{:S(2)}, u32[]{:S(2)}) collective-permute-start(bf16[128,1024]{1,0:T(8,128)(2,1)S(1)} %get-tuple-element.95.refs_0_), channel_id=1, source_target_pairs={{0,8},{4,12},{8,0},{12,4},{1,9},{5,13},{9,1},{13,5},{2,10},{6,14},... | collective-permute-start | bytes 786440 | tf_op jit(solution)/shard_map/ppermute | solution.py:684
  68.7 22.3 %collective-permute-start.13 = (bf16[128,1024]{1,0:T(8,128)(2,1)S(1)}, bf16[128,1024]{1,0:T(8,128)(2,1)S(1)}, u32[]{:S(2)}, u32[]{:S(2)}) collective-permute-start(bf16[128,1024]{1,0:T(8,128)(2,1)S(1)} %get-tuple-element.95.refs_0_), channel_id=1, source_target_pairs={{0,12},{4,8},{8,4},{12,0},{1,13},{5,9},{9,5},{13,1},{2,14},{6,10},... | collective-permute-start | bytes 786440 | tf_op jit(solution)/shard_map/ppermute | solution.py:684
  69.5 12.4 %collective-permute-start.14 = (f32[24,128]{1,0:T(8,128)S(1)}, f32[24,128]{1,0:T(8,128)S(1)}, u32[]{:S(2)}, u32[]{:S(2)}) collective-permute-start(f32[24,128]{1,0:T(8,128)S(1)} %get-tuple-element.88.a), channel_id=1, source_target_pairs={{0,4},{4,0},{8,12},{12,8},{1,5},{5,1},{9,13},{13,9},{2,6},{6,2},{1... | collective-permute-start | bytes 36872 | tf_op jit(solution)/shard_map/ppermute | solution.py:686
  69.5 21.5 %collective-permute-start.15 = (f32[24,128]{1,0:T(8,128)S(1)}, f32[24,128]{1,0:T(8,128)S(1)}, u32[]{:S(2)}, u32[]{:S(2)}) collective-permute-start(f32[24,128]{1,0:T(8,128)S(1)} %get-tuple-element.88.a), channel_id=1, source_target_pairs={{0,8},{4,12},{8,0},{12,4},{1,9},{5,13},{9,1},{13,5},{2,10},{6,14},... | collective-permute-start | bytes 36872 | tf_op jit(solution)/shard_map/ppermute | solution.py:686
  81.9 9.1 %collective-permute-start.16 = (f32[24,128]{1,0:T(8,128)S(1)}, f32[24,128]{1,0:T(8,128)S(1)}, u32[]{:S(2)}, u32[]{:S(2)}) collective-permute-start(f32[24,128]{1,0:T(8,128)S(1)} %get-tuple-element.88.a), channel_id=1, source_target_pairs={{0,12},{4,8},{8,4},{12,0},{1,13},{5,9},{9,5},{13,1},{2,14},{6,10},... | collective-permute-start | bytes 36872 | tf_op jit(solution)/shard_map/ppermute | solution.py:686
  91.1 6.8 %collective-permute-start.17 = (f32[24,512]{1,0:T(8,128)S(1)}, f32[24,512]{1,0:T(8,128)S(1)}, u32[]{:S(2)}, u32[]{:S(2)}) collective-permute-start(f32[24,512]{1,0:T(8,128)S(1)} %join.1), channel_id=1, source_target_pairs={{0,2},{1,3},{2,0},{3,1},{4,6},{5,7},{6,4},{7,5},{8,10},{9,11},{10,... | collective-permute-start | bytes 147464 | tf_op jit(solution)/shard_map/ppermute | solution.py:689
  97.9 2.7 %collective-permute-start.18 = (bf16[2,128,2048]{2,1,0:T(8,128)(2,1)S(1)}, bf16[2,128,2048]{2,1,0:T(8,128)(2,1)S(1)}, u32[]{:S(2)}, u32[]{:S(2)}) collective-permute-start(bf16[2,128,2048]{2,1,0:T(8,128)(2,1)S(1)} %get-tuple-element.92), channel_id=1, source_target_pairs={{0,1},{1,0},{2,3},{3,2},{4,5},{5,4},{6,7},{7,6},{8,9},{9,8},{10,11... | collective-permute-start | bytes 3145736 | tf_op jit(solution)/shard_map/ppermute | solution.py:704
  100.7 14.0 %collective-permute-start.20 = (bf16[128,2048]{1,0:T(8,128)(2,1)S(1)}, bf16[128,2048]{1,0:T(8,128)(2,1)S(1)}, u32[]{:S(2)}, u32[]{:S(2)}) collective-permute-start(bf16[128,2048]{1,0:T(8,128)(2,1)S(1)} %fusion), channel_id=1, source_target_pairs={{0,2},{1,3},{2,0},{3,1},{4,6},{5,7},{6,4},{7,5},{8,10},{9,11},{10,... | collective-permute-start | bytes 1572872 | tf_op jit(solution)/shard_map/ppermute | solution.py:708
  101.1 1.3 collective-permute-start.19
  114.8 2.7 %collective-permute-start.21 = (bf16[2,128,2048]{2,1,0:T(8,128)(2,1)S(1)}, bf16[2,128,2048]{2,1,0:T(8,128)(2,1)S(1)}, u32[]{:S(2)}, u32[]{:S(2)}) collective-permute-start(bf16[2,128,2048]{2,1,0:T(8,128)(2,1)S(1)} %get-tuple-element.99), channel_id=1, source_target_pairs={{0,1},{1,0},{2,3},{3,2},{4,5},{5,4},{6,7},{7,6},{8,9},{9,8},{10,11... | collective-permute-start | bytes 3145736 | tf_op jit(solution)/shard_map/ppermute | solution.py:714
  115.7 8.8 %collective-permute-start.22 = (bf16[128,1024]{1,0:T(8,128)(2,1)S(1)}, bf16[128,1024]{1,0:T(8,128)(2,1)S(1)}, u32[]{:S(2)}, u32[]{:S(2)}) collective-permute-start(bf16[128,1024]{1,0:T(8,128)(2,1)S(1)} %activate.2.a), channel_id=1, source_target_pairs={{0,2},{1,3},{2,0},{3,1},{4,6},{5,7},{6,4},{7,5},{8,10},{9,11},{10,... | collective-permute-start | bytes 786440 | tf_op jit(solution)/shard_map/ppermute | solution.py:694
  116.1 8.7 %collective-permute-start.24 = (bf16[128,1024]{1,0:T(8,128)(2,1)S(1)}, bf16[128,1024]{1,0:T(8,128)(2,1)S(1)}, u32[]{:S(2)}, u32[]{:S(2)}) collective-permute-start(bf16[128,1024]{1,0:T(8,128)(2,1)S(1)} %activate.2.a), channel_id=1, source_target_pairs={{0,1},{1,0},{2,3},{3,2},{4,5},{5,4},{6,7},{7,6},{8,9},{9,8},{10,11... | collective-permute-start | bytes 786440 | tf_op jit(solution)/shard_map/ppermute | solution.py:695
  124.5 1.5 collective-permute-start.25
  124.5 14.3 %collective-permute-start.23 = (bf16[128,2048]{1,0:T(8,128)(2,1)S(1)}, bf16[128,2048]{1,0:T(8,128)(2,1)S(1)}, u32[]{:S(2)}, u32[]{:S(2)}) collective-permute-start(bf16[128,2048]{1,0:T(8,128)(2,1)S(1)} %fusion.1), channel_id=1, source_target_pairs={{0,2},{1,3},{2,0},{3,1},{4,6},{5,7},{6,4},{7,5},{8,10},{9,11},{10,... | collective-permute-start | bytes 1572872 | tf_op jit(solution)/shard_map/ppermute | solution.py:719
  128.9 8.4 %collective-permute-start.26 = (bf16[128,1024]{1,0:T(8,128)(2,1)S(1)}, bf16[128,1024]{1,0:T(8,128)(2,1)S(1)}, u32[]{:S(2)}, u32[]{:S(2)}) collective-permute-start(bf16[128,1024]{1,0:T(8,128)(2,1)S(1)} %get-tuple-element.106), channel_id=1, source_target_pairs={{0,4},{4,0},{8,12},{12,8},{1,5},{5,1},{9,13},{13,9},{2,6},{6,2},{1... | collective-permute-start | bytes 786440 | tf_op jit(solution)/shard_map/ppermute | solution.py:721
  139.8 8.0 %collective-permute-start.27 = (bf16[128,1024]{1,0:T(8,128)(2,1)S(1)}, bf16[128,1024]{1,0:T(8,128)(2,1)S(1)}, u32[]{:S(2)}, u32[]{:S(2)}) collective-permute-start(bf16[128,1024]{1,0:T(8,128)(2,1)S(1)} %activate.3.a), channel_id=1, source_target_pairs={{0,2},{1,3},{2,0},{3,1},{4,6},{5,7},{6,4},{7,5},{8,10},{9,11},{10,... | collective-permute-start | bytes 786440 | tf_op jit(solution)/shard_map/ppermute | solution.py:694
  140.2 9.5 %collective-permute-start.28 = (bf16[128,1024]{1,0:T(8,128)(2,1)S(1)}, bf16[128,1024]{1,0:T(8,128)(2,1)S(1)}, u32[]{:S(2)}, u32[]{:S(2)}) collective-permute-start(bf16[128,1024]{1,0:T(8,128)(2,1)S(1)} %activate.3.a), channel_id=1, source_target_pairs={{0,1},{1,0},{2,3},{3,2},{4,5},{5,4},{6,7},{7,6},{8,9},{9,8},{10,11... | collective-permute-start | bytes 786440 | tf_op jit(solution)/shard_map/ppermute | solution.py:695
  147.8 1.8 %collective-permute-start.29 = (bf16[128,1024]{1,0:T(8,128)(2,1)S(1)}, bf16[128,1024]{1,0:T(8,128)(2,1)S(1)}, u32[]{:S(2)}, u32[]{:S(2)}) collective-permute-start(bf16[128,1024]{1,0:T(8,128)(2,1)S(1)} %collective-permute-done.27.b), channel_id=1, source_target_pairs={{0,1},{1,0},{2,3},{3,2},{4,5},{5,4},{6,7},{7,6},{8,9},{9,8},{10,11... | collective-permute-start | bytes 786440 | tf_op jit(solution)/shard_map/ppermute | solution.py:696
  147.8 15.3 %collective-permute-start.30 = (bf16[128,1024]{1,0:T(8,128)(2,1)S(1)}, bf16[128,1024]{1,0:T(8,128)(2,1)S(1)}, u32[]{:S(2)}, u32[]{:S(2)}) collective-permute-start(bf16[128,1024]{1,0:T(8,128)(2,1)S(1)} %add_convert_fusion.3), channel_id=1, source_target_pairs={{0,8},{4,12},{8,0},{12,4},{1,9},{5,13},{9,1},{13,5},{2,10},{6,14},... | collective-permute-start | bytes 786440 | tf_op jit(solution)/shard_map/ppermute | solution.py:724
  152.5 13.9 %collective-permute-start.31 = (bf16[128,1024]{1,0:T(8,128)(2,1)S(1)}, bf16[128,1024]{1,0:T(8,128)(2,1)S(1)}, u32[]{:S(2)}, u32[]{:S(2)}) collective-permute-start(bf16[128,1024]{1,0:T(8,128)(2,1)S(1)} %get-tuple-element.110), channel_id=1, source_target_pairs={{0,4},{4,0},{8,12},{12,8},{1,5},{5,1},{9,13},{13,9},{2,6},{6,2},{1... | collective-permute-start | bytes 786440 | tf_op jit(solution)/shard_map/ppermute | solution.py:729
  (14 other events, 264.1 us)

commit v7 on v6

--- a/solution.py
+++ b/solution.py
@@ -442,56 +442,51 @@
     )(here, *pieces)
 
 
-def residual_body(hidden, p0, p1, p2, gain, router, after, out, stats):
-    rows = stats.shape[0]
+def residual_body(hidden, p0, p1, p2, after, out):
     total = hidden[...].astype(jnp.float32) + p0[...].astype(jnp.float32)
     for part in (p1, p2):
         total = total + part[...].astype(jnp.float32)
-    narrow = total.astype(jnp.bfloat16)
-    out[...] = narrow
-    wide = narrow.astype(jnp.float32)
-    grown = wide * gain[...]
-    high = grown.astype(jnp.bfloat16)
-    rest = grown - high.astype(jnp.float32)
-    middle = rest.astype(jnp.bfloat16)
-    low = (rest - middle.astype(jnp.float32)).astype(jnp.bfloat16)
-    logits = dot(high, router[...]) + (dot(middle, router[...]) + dot(low, router[...]))
-    squares = jnp.sum(wide * wide, axis=1, keepdims=True)
-    column = lax.broadcasted_iota(jnp.int32, logits.shape, 1)
-    stats[...] = jnp.transpose(jnp.where(column == rows - 8, squares, logits))[:rows, :]
-
-
-def residual_and_stats(hidden, parts, gain, router, experts, after):
-    length, width = hidden.shape
+    out[...] = total.astype(jnp.bfloat16)
+
+
+def add_parts(hidden, parts, after):
     return call(
         residual_body,
-        [
-            jax.ShapeDtypeStruct((length, width), jnp.bfloat16),
-            jax.ShapeDtypeStruct((experts + 8, length), jnp.float32),
-        ],
+        jax.ShapeDtypeStruct(hidden.shape, jnp.bfloat16),
         [],
-        in_specs=[VMEM] * 6 + [pl.BlockSpec(memory_space=pl.ANY)],
-        out_specs=[VMEM] * 2,
+        in_specs=[VMEM] * 4 + [pl.BlockSpec(memory_space=pl.ANY)],
+        out_specs=VMEM,
         name="residual",
-    )(hidden, *parts, gain, router, after)
-
-
-def join_body(a, b, c, d, out):
-    length = a.shape[1]
-    for j, ref in enumerate((a, b, c, d)):
-        out[:, j * length : (j + 1) * length] = ref[...]
-
-
-def join(parts):
-    rows, length = parts[0].shape
-    return call(
-        join_body,
-        jax.ShapeDtypeStruct((rows, 4 * length), parts[0].dtype),
+    )(hidden, *parts, after)
+
+
+def measure_body(t0, t1, t2, t3, gain, router, stats):
+    rows = stats.shape[0]
+    length = t0.shape[0]
+    for d, ref in enumerate((t0, t1, t2, t3)):
+        wide = ref[...].astype(jnp.float32)
+        grown = wide * gain[...]
+        high = grown.astype(jnp.bfloat16)
+        rest = grown - high.astype(jnp.float32)
+        middle = rest.astype(jnp.bfloat16)
+        low = (rest - middle.astype(jnp.float32)).astype(jnp.bfloat16)
+        logits = dot(high, router[...]) + (dot(middle, router[...]) + dot(low, router[...]))
+        squares = jnp.sum(wide * wide, axis=1, keepdims=True)
+        column = lax.broadcasted_iota(jnp.int32, logits.shape, 1)
+        both = jnp.where(column == rows - 8, squares, logits)
+        stats[:, d * length : (d + 1) * length] = jnp.transpose(both)[:rows, :]
+
+
+def squares_and_logits(tokens, gain, router, experts):
+    n, length = (len(tokens), tokens[0].shape[0])
+    return call(
+        measure_body,
+        jax.ShapeDtypeStruct((experts + 8, n * length), jnp.float32),
         [],
-        in_specs=[VMEM] * 4,
+        in_specs=[VMEM] * (n + 2),
         out_specs=VMEM,
-        name="join",
-    )(*parts)
+        name="stats",
+    )(*tokens, gain, router)
 
 
 def gate_up_body(ds, order, *refs):
@@ -539,47 +534,55 @@
     )(order, *tokens, gain, pick, weight)
 
 
-def activate_body(ds, features, here, kept, taken, across, pick, *refs):
-    stats = refs[0]
-    pieces = refs[1 : 1 + len(ds)]
-    out = refs[1 + len(ds)]
+def activate_body(groups, features, here, pick, stats, *refs):
+    out = refs[-1]
     _, local, capacity, length = pick.shape
     hid = out.shape[1]
     experts = stats.shape[0] - 8
     device, lane = (here[0], here[1])
     expert = lax.broadcasted_iota(jnp.int32, (experts, length), 0)
-    for k, d in enumerate(ds):
-        ids = pieces[k][pieces[k].shape[0] - 16 :, :].astype(jnp.float32).astype(jnp.int32)
-        chosen = jnp.zeros((experts, length), jnp.float32)
-        for c in range(8):
-            chosen = jnp.where(ids[c : c + 1, :] == expert, 1.0, chosen)
-        block = slice(d * length, (d + 1) * length)
-        inv_rms = lax.rsqrt(stats[experts : experts + 1, block] / features + norm_eps)
-        logits = jnp.where(chosen > 0.0, stats[:experts, block] * inv_rms, -jnp.inf)
-        grown = jnp.exp(logits - jnp.max(logits, axis=0, keepdims=True))
-        mix = grown / jnp.sum(grown, axis=0, keepdims=True)
-        mix = jnp.sum(jnp.where(expert == device * local + lane, mix, 0.0), axis=0, keepdims=True)
-        places = pick[d, lane].astype(jnp.float32)
-        inv_row = jnp.sum(places * inv_rms, axis=1, keepdims=True)
-        mix_row = jnp.sum(places * mix, axis=1, keepdims=True)
-        rows = slice(k * capacity, (k + 1) * capacity)
-        summed = kept[0, rows, :].astype(jnp.float32) + taken[0, rows, :].astype(jnp.float32)
-        summed = (summed + across[rows, :].astype(jnp.float32)) * inv_row
-        gate = summed[:, :hid]
-        act = gate / (1.0 + jnp.exp(-gate)) * summed[:, hid:] * mix_row
-        out[rows, :] = act.astype(jnp.bfloat16)
-
-
-def activate(ds, features, here, kept, taken, across, pick, stats, pieces):
-    rows, both = across.shape
-    return call(
-        functools.partial(activate_body, ds, features),
-        jax.ShapeDtypeStruct((rows, both // 2), jnp.bfloat16),
+    base, refs = (0, list(refs))
+    for ds in groups:
+        kept, taken, across = refs[:3]
+        pieces = refs[3 : 3 + len(ds)]
+        refs = refs[3 + len(ds) :]
+        for k, d in enumerate(ds):
+            ids = pieces[k][pieces[k].shape[0] - 16 :, :].astype(jnp.float32).astype(jnp.int32)
+            chosen = jnp.zeros((experts, length), jnp.float32)
+            for c in range(8):
+                chosen = jnp.where(ids[c : c + 1, :] == expert, 1.0, chosen)
+            block = slice(d * length, (d + 1) * length)
+            inv_rms = lax.rsqrt(stats[experts : experts + 1, block] / features + norm_eps)
+            logits = jnp.where(chosen > 0.0, stats[:experts, block] * inv_rms, -jnp.inf)
+            grown = jnp.exp(logits - jnp.max(logits, axis=0, keepdims=True))
+            mix = grown / jnp.sum(grown, axis=0, keepdims=True)
+            mine = jnp.where(expert == device * local + lane, mix, 0.0)
+            mix = jnp.sum(mine, axis=0, keepdims=True)
+            places = pick[d, lane].astype(jnp.float32)
+            inv_row = jnp.sum(places * inv_rms, axis=1, keepdims=True)
+            mix_row = jnp.sum(places * mix, axis=1, keepdims=True)
+            rows = slice(k * capacity, (k + 1) * capacity)
+            summed = kept[0, rows, :].astype(jnp.float32) + taken[0, rows, :].astype(jnp.float32)
+            summed = (summed + across[rows, :].astype(jnp.float32)) * inv_row
+            gate = summed[:, :hid]
+            act = gate / (1.0 + jnp.exp(-gate)) * summed[:, hid:] * mix_row
+            out[base + k * capacity : base + (k + 1) * capacity, :] = act.astype(jnp.bfloat16)
+        base += len(ds) * capacity
+
+
+def activate(groups, features, here, sums, pick, stats, pieces):
+    operands = []
+    for ds, terms in zip(groups, sums):
+        operands += list(terms) + [pieces[d] for d in ds]
+    rows = sum(terms[2].shape[0] for terms in sums)
+    return call(
+        functools.partial(activate_body, groups, features),
+        jax.ShapeDtypeStruct((rows, sums[0][2].shape[1] // 2), jnp.bfloat16),
         [],
-        in_specs=[SMEM] + [VMEM] * (5 + len(ds)),
+        in_specs=[SMEM] + [VMEM] * (2 + len(operands)),
         out_specs=VMEM,
         name="activate",
-    )(here, kept, taken, across, pick, stats, *[pieces[d] for d in ds])
+    )(here, pick, stats, *operands)
 
 
 def down_body(ds, order, a, b, c, d, spread, weight, *rest):
@@ -676,17 +679,12 @@
     sent = scatter_blocks([kept] + list(parts[1:]), n)
     pick, spread = routing(here, pieces, experts, local, capacity)
     weight = jnp.transpose(w_gate_up, (0, 2, 1, 3))
-    sent[0], pick = lax.optimization_barrier((sent[0], pick))
-    residual, own_stats = residual_and_stats(hidden, sent, gain, router, experts, weight)
-
-    tokens, stats = ({0: residual}, {0: own_stats})
+    sent[0], pick, router, gain = lax.optimization_barrier((sent[0], pick, router, gain))
+    residual = add_parts(hidden, sent, weight)
+
+    tokens = [residual] + [None] * (n - 1)
     for d in (2, 3, 1):
         tokens[d] = lax.ppermute(residual, "ep", pairs(n, d))
-    for d in (2, 3, 1):
-        stats[d] = lax.ppermute(own_stats, "ep", pairs(n, d))
-    tokens, stats = lax.optimization_barrier((tokens, stats))
-    stats = join([stats[d] for d in range(n)])
-    stats_far = lax.ppermute(stats, "tp", pairs(n, 2))
 
     features = width_here * n
 
@@ -698,34 +696,51 @@
     def chip_sum(kept, taken):
         return (kept[1].astype(jnp.float32) + taken[1].astype(jnp.float32)).astype(jnp.bfloat16)
 
-    one_chunk, two_chunk = ((2, 3), (0, 1))
-    kept, given = gate_up(one_chunk, order, [tokens[d] for d in one_chunk], gain, pick, weight)
-    given, stats_far = lax.optimization_barrier((given, stats_far))
-    taken = lax.ppermute(given, "tp", pairs(n, 1))
+    def terms_of(ds, order):
+        return gate_up(ds, order, [tokens[d] for d in ds], gain, pick, weight)
+
+    kept_0, given = terms_of((0,), order)
+    given, tokens = lax.optimization_barrier((given, tokens))
+    taken_0 = lax.ppermute(given, "tp", pairs(n, 1))
+    stats = squares_and_logits(tokens, gain, router, experts)
+    far_sum = chip_sum(kept_0, taken_0)
+    far_sum, stats = lax.optimization_barrier((far_sum, stats))
+    stats_far = lax.ppermute(stats, "tp", pairs(n, 2))
+    across_0 = lax.ppermute(far_sum, "tp", pairs(n, 2))
+
+    order, _ = lax.optimization_barrier((order, far_sum))
+    kept_2, given = terms_of((2, 3), order)
+    given, across_0, stats_far = lax.optimization_barrier((given, across_0, stats_far))
+    taken_2 = lax.ppermute(given, "tp", pairs(n, 1))
     stats = stats + stats_far
     stats_near = lax.ppermute(stats, "tp", pairs(n, 1))
-    far_sum = chip_sum(kept, taken)
-    across = lax.ppermute(far_sum, "tp", pairs(n, 2))
+    far_sum = chip_sum(kept_2, taken_2)
+    across_2 = lax.ppermute(far_sum, "tp", pairs(n, 2))
 
     order, _, stats_near = lax.optimization_barrier((order, far_sum, stats_near))
     stats = stats + stats_near
-    kept_2, given = gate_up(two_chunk, order, [tokens[d] for d in two_chunk], gain, pick, weight)
-    given, across = lax.optimization_barrier((given, across))
-    taken_2 = lax.ppermute(given, "tp", pairs(n, 1))
-    acts = spread_act(activate(one_chunk, features, here, kept, taken, across, pick, stats, pieces))
-    far_sum = chip_sum(kept_2, taken_2)
+    kept_1, given = terms_of((1,), order)
+    given, across_2 = lax.optimization_barrier((given, across_2))
+    taken_1 = lax.ppermute(given, "tp", pairs(n, 1))
+
+    groups = ((2, 3),)
+    sums = [(kept_2, taken_2, across_2)]
+    acts = spread_act(activate(groups, features, here, sums, pick, stats, pieces))
+    far_sum = chip_sum(kept_1, taken_1)
     far_sum, acts[1] = lax.optimization_barrier((far_sum, acts[1]))
     acts[3] = lax.ppermute(acts[1], "tp", pairs(n, 1))
-    across = lax.ppermute(far_sum, "tp", pairs(n, 2))
-    parts = down(one_chunk, order, acts, spread, w_down)
+    across_1 = lax.ppermute(far_sum, "tp", pairs(n, 2))
+    parts = down((2, 3), order, acts, spread, w_down)
+    across_1, *parts = lax.optimization_barrier((across_1, *parts))
     near = lax.ppermute(parts[1], "ep", pairs(n, 1))
     far = (parts[0].astype(jnp.float32) + near.astype(jnp.float32)).astype(jnp.bfloat16)
-    across, far = lax.optimization_barrier((across, far))
+    across_1, far = lax.optimization_barrier((across_1, far))
     far = lax.ppermute(far, "ep", pairs(n, 2))
-    acts = spread_act(
-        activate(two_chunk, features, here, kept_2, taken_2, across, pick, stats, pieces)
-    )
-    mine, near = down(two_chunk, order, acts, spread, w_down)
+
+    groups = ((0,), (1,))
+    sums = [(kept_0, taken_0, across_0), (kept_1, taken_1, across_1)]
+    acts = spread_act(activate(groups, features, here, sums, pick, stats, pieces))
+    mine, near = down((0, 1), order, acts, spread, w_down)
     returned = [mine, far, lax.ppermute(near, "ep", pairs(n, 1))]
     total = residual.astype(jnp.float32)
     for part in returned:

time: 168 us -> 171 us (1.018)
  Pallas kernels: 25.7 us -> 31.5 us
  waiting for transfers between devices: 81.7 us -> 77.1 us
  starting transfers between devices: 41.2 us -> 43.6 us
    ppermute x6 -> x5, waiting for transfers between devices: 27.1 us -> 10.6 us  [the longest x1 5.92 us: per_device_square(): across_2 = lax.ppermute(far_sum, 'tp', pairs(n, 2))]
    ppermute x3, waiting for transfers between devices: 0.01 us -> 12.5 us  [per_device_square(): tokens[d] = lax.ppermute(residual, 'ep', pairs(n, d))]
    pallas_call x2 -> x3, Pallas kernels: 9.97 us -> 14.9 us  [gate_up(): call(functools.partial(gate_up_body, ds), [shape] * 2, None, grid_spec=pl...]
    ppermute x2, starting transfers between devices: 0.75 us -> 3.61 us  [spread_act(): far = lax.ppermute(act, 'tp', pairs(n, 2))]
    ppermute x1, starting transfers between devices: 0.75 us -> 3.37 us  [per_device_square(): near = lax.ppermute(parts[1], 'ep', pairs(n, 1))]
    ppermute x1, waiting for transfers between devices: 0.01 us -> 2.59 us  [per_device_square(): stats_far = lax.ppermute(stats, 'tp', pairs(n, 2))]
    ppermute x2, waiting for transfers between devices: 14.6 us -> 12.3 us  [spread_act(): far = lax.ppermute(act, 'tp', pairs(n, 2))]
    ppermute x1, starting transfers between devices: 1.79 us -> 0.08 us  [per_device_square(): stats_far = lax.ppermute(stats, 'tp', pairs(n, 2))]
  transfers between devices with their start and end apart: 32 -> 31, of which waited for: 17 -> 17; matrix products, arithmetic and copies ran while one was open for 9% -> 9% of each run, Pallas kernels for 11% -> 15%
where the time goes in v7:
time: 171 us
  waiting for transfers between devices  77.1 us (45%)
  starting transfers between devices  43.6 us (25%)
  Pallas kernels  31.5 us (18%)
  local copies, waits for them, and re-layouts  13.6 us (8%)
  other arithmetic  4.79 us (3%)
    pallas_call x3, Pallas kernels, gate_up(): call(functools.partial(gate_up_body, ds), [shape] * 2, None, grid_spec=pl...  14.9 us
    ppermute x3, starting transfers between devices, per_device_square(): lax.ppermute(pieces[d], 'ep', pairs(n, d))  13.1 us
    ppermute x3, waiting for transfers between devices, per_device_square(): tokens[d] = lax.ppermute(residual, 'ep', pairs(n, d))  12.5 us
    ppermute x2, waiting for transfers between devices, spread_act(): far = lax.ppermute(act, 'tp', pairs(n, 2))  12.3 us
    optimization_barrier x1, local copies, waits for them, and re-layouts, per_device_square(): kept, w_gate_up = lax.optimization_barrier((parts[0], w_gate_up))  11.2 us
    ppermute x1, waiting for transfers between devices, per_device_square(): far = lax.ppermute(far, 'ep', pairs(n, 2))  9.4 us
    ppermute x1, waiting for transfers between devices, scatter_blocks(): near = lax.ppermute(parts[3], 'ep', pairs(n, 1))  7.12 us
    ppermute x1, waiting for transfers between devices, per_device_square(): near = lax.ppermute(parts[1], 'ep', pairs(n, 1))  6.19 us
  transfers between devices with their start and end apart: 31, of which 17 were waited for; matrix products, arithmetic and copies ran while one was open for 9% of the time, Pallas kernels for 15%

profile of v7, /device:TPU:0, one launch (start us, length us, event | category | flops | bytes accessed | tf_op | source)
XLA Modules:
  0.0 171.1 jit_solution(1216148986222934483)
XLA Ops:
  6.1 10.7 %collective-permute-start.2 = (bf16[272,128]{1,0:T(8,128)(2,1)S(1)}, bf16[272,128]{1,0:T(8,128)(2,1)S(1)}, u32[]{:S(2)}, u32[]{:S(2)}) collective-permute-start(bf16[272,128]{1,0:T(8,128)(2,1)S(1)} %get-tuple-element.70), channel_id=1, source_target_pairs={{0,4},{4,0},{8,12},{12,8},{1,5},{5,1},{9,13},{13,9},{2,6},{6,2},{1... | collective-permute-start | bytes 208904 | tf_op jit(solution)/shard_map/ppermute | solution.py:666
  16.8 2.4 %collective-permute-start.4 = (bf16[272,128]{1,0:T(8,128)(2,1)S(1)}, bf16[272,128]{1,0:T(8,128)(2,1)S(1)}, u32[]{:S(2)}, u32[]{:S(2)}) collective-permute-start(bf16[272,128]{1,0:T(8,128)(2,1)S(1)} %get-tuple-element.72), channel_id=1, source_target_pairs={{0,12},{4,8},{8,4},{12,0},{1,13},{5,9},{9,5},{13,1},{2,14},{6,10},... | collective-permute-start | bytes 208904 | tf_op jit(solution)/shard_map/ppermute | solution.py:666
  21.9 3.5 %collective-permute-done.3.c2.refs_3_ = bf16[272,128]{1,0:T(8,128)(2,1)S(1)} collective-permute-done((bf16[272,128]{1,0:T(8,128)(2,1)S(1)}, bf16[272,128]{1,0:T(8,128)(2,1)S(1)}, u32[]{:S(2)}, u32[]{:S(2)}) %collective-permute-start.3) | collective-permute-done | bytes 69664 | tf_op jit(solution)/shard_map/ppermute | solution.py:666
  25.4 3.4 %attention.1.a = bf16[128,1024]{1,0:T(8,128)(2,1)S(1)} custom-call(s32[2]{0:T(128)S(1)} %pad_add_fusion.here, s32[4,4]{1,0:T(4,128)S(1)} %copy-done.4, s32[8]{0:T(128)S(1)} %copy-done.6, bf16[1280,128]{1,0:T(8,128)(2,1)S(1)} %collective-permute-done.1.q, bf16[272,128]{1,0:T(8,128)(2,1)S(1)} %get-tuple-element.69.c0.refs_3_, ...), custom_call_target="tpu_custom_call" | custom-call | flops 1048576 | bytes 262144 | tf_op jit(solution)/shard_map/attention/pallas_call | solution.py:370
  28.9 5.1 %collective-permute-start.5 = (bf16[128,1024]{1,0:T(8,128)(2,1)S(1)}, bf16[128,1024]{1,0:T(8,128)(2,1)S(1)}, u32[]{:S(2)}, u32[]{:S(2)}) collective-permute-start(bf16[128,1024]{1,0:T(8,128)(2,1)S(1)} %attention.1.a), channel_id=1, source_target_pairs={{0,2},{1,3},{2,0},{3,1},{4,6},{5,7},{6,4},{7,5},{8,10},{9,11},{10,... | collective-permute-start | bytes 786440 | tf_op jit(solution)/shard_map/ppermute | solution.py:672
  33.9 4.3 %collective-permute-done.5.b = bf16[128,1024]{1,0:T(8,128)(2,1)S(1)} collective-permute-done((bf16[128,1024]{1,0:T(8,128)(2,1)S(1)}, bf16[128,1024]{1,0:T(8,128)(2,1)S(1)}, u32[]{:S(2)}, u32[]{:S(2)}) %collective-permute-start.5) | collective-permute-done | bytes 262176 | tf_op jit(solution)/shard_map/ppermute | solution.py:672
  39.8 1.9 %project.1 = (bf16[128,1024]{1,0:T(8,128)(2,1)S(1)}, bf16[128,1024]{1,0:T(8,128)(2,1)S(1)}, bf16[128,1024]{1,0:T(8,128)(2,1)S(1)}, bf16[128,1024]{1,0:T(8,128)(2,1)S(1)}) custom-call(s32[2]{0:T(128)S(1)} %pad_add_fusion.here, bf16[128,1024]{1,0:T(8,128)(2,1)S(1)} %attention.1.a, bf16[128,1024]{1,0:T(8,128)(2,1)S(1)} %collective-permute-done.5.b, ...), custom_call_target="tpu_custom_call" | custom-call | flops 1048576 | bytes 262144 | tf_op jit(solution)/shard_map/project/pallas_call | solution.py:395
  41.7 1.8 %collective-permute-start.8 = (bf16[128,1024]{1,0:T(8,128)(2,1)S(1)}, bf16[128,1024]{1,0:T(8,128)(2,1)S(1)}, u32[]{:S(2)}, u32[]{:S(2)}) collective-permute-start(bf16[128,1024]{1,0:T(8,128)(2,1)S(1)} %get-tuple-element.84), channel_id=1, source_target_pairs={{0,4},{4,0},{8,12},{12,8},{1,5},{5,1},{9,13},{13,9},{2,6},{6,2},{1... | collective-permute-start | bytes 786440 | tf_op jit(solution)/shard_map/ppermute | solution.py:195
  43.8 7.1 %collective-permute-done.8 = bf16[128,1024]{1,0:T(8,128)(2,1)S(1)} collective-permute-done((bf16[128,1024]{1,0:T(8,128)(2,1)S(1)}, bf16[128,1024]{1,0:T(8,128)(2,1)S(1)}, u32[]{:S(2)}, u32[]{:S(2)}) %collective-permute-start.8) | collective-permute-done | bytes 262176 | tf_op jit(solution)/shard_map/ppermute | solution.py:195
  53.4 11.2 %copy.25 = bf16[4,1024,2,1024]{3,1,2,0:T(8,128)(2,1)S(1)} copy(bf16[4,1024,2,1024]{3,2,1,0:T(2,128)(2,1)} %param.24) | data formatting | bytes 33554432 | tf_op jit(solution)/shard_map/optimization_barrier | solution.py:678
  65.6 2.8 %collective-permute-start.12 = (bf16[128,1024]{1,0:T(8,128)(2,1)S(1)}, bf16[128,1024]{1,0:T(8,128)(2,1)S(1)}, u32[]{:S(2)}, u32[]{:S(2)}) collective-permute-start(bf16[128,1024]{1,0:T(8,128)(2,1)S(1)} %residual.1.refs_0_.t0), channel_id=1, source_target_pairs={{0,8},{4,12},{8,0},{12,4},{1,9},{5,13},{9,1},{13,5},{2,10},{6,14},... | collective-permute-start | bytes 786440 | tf_op jit(solution)/shard_map/ppermute | solution.py:687
  69.2 5.0 %gate_up.3 = (bf16[2,64,2048]{2,1,0:T(8,128)(2,1)S(1)}, bf16[2,64,2048]{2,1,0:T(8,128)(2,1)S(1)}) custom-call(s32[4]{0:T(128)S(1)} %broadcast_xor_fusion.order, bf16[128,1024]{1,0:T(8,128)(2,1)S(1)} %residual.1.refs_0_.t0, f32[1,1024]{1,0:T(1,128)S(1)} %bitcast.33, bf16[4,4,64,128]{3,2,1,0:T(8,128)(2,1)S(1)} %get-tuple-element.88.refs_2_.refs_3_.pick, ...), custom_call_target="tpu_custom_call" | custom-call | flops 1048576 | bytes 262144 | tf_op jit(solution)/shard_map/gate_up/pallas_call | solution.py:517
  75.5 11.3 %collective-permute-done.12.t2.refs_0_ = bf16[128,1024]{1,0:T(8,128)(2,1)S(1)} collective-permute-done((bf16[128,1024]{1,0:T(8,128)(2,1)S(1)}, bf16[128,1024]{1,0:T(8,128)(2,1)S(1)}, u32[]{:S(2)}, u32[]{:S(2)}) %collective-permute-start.12) | collective-permute-done | bytes 262176 | tf_op jit(solution)/shard_map/ppermute | solution.py:687
  88.8 2.0 %collective-permute-start.15 = (bf16[64,2048]{1,0:T(8,128)(2,1)S(1)}, bf16[64,2048]{1,0:T(8,128)(2,1)S(1)}, u32[]{:S(2)}, u32[]{:S(2)}) collective-permute-start(bf16[64,2048]{1,0:T(8,128)(2,1)S(1)} %fusion.1), channel_id=1, source_target_pairs={{0,2},{1,3},{2,0},{3,1},{4,6},{5,7},{6,4},{7,5},{8,10},{9,11},{10,... | collective-permute-start | bytes 786440 | tf_op jit(solution)/shard_map/ppermute | solution.py:709
  90.9 5.0 %gate_up.4 = (bf16[2,128,2048]{2,1,0:T(8,128)(2,1)S(1)}, bf16[2,128,2048]{2,1,0:T(8,128)(2,1)S(1)}) custom-call(s32[4]{0:T(128)S(1)} %broadcast_xor_fusion.order, bf16[128,1024]{1,0:T(8,128)(2,1)S(1)} %collective-permute-done.12.t2.refs_0_, bf16[128,1024]{1,0:T(8,128)(2,1)S(1)} %collective-permute-done.13.t3.refs_1_, f32[1,1024]{1,0:T(1,128)S(1)} %bitcast.35, ...), custom_call_target="tpu_custom_call" | custom-call | flops 1048576 | bytes 262144 | tf_op jit(solution)/shard_map/gate_up/pallas_call | solution.py:517
  95.8 2.6 %collective-permute-done.16 = f32[24,512]{1,0:T(8,128)S(1)} collective-permute-done((f32[24,512]{1,0:T(8,128)S(1)}, f32[24,512]{1,0:T(8,128)S(1)}, u32[]{:S(2)}, u32[]{:S(2)}) %collective-permute-start.16) | collective-permute-done | bytes 49184 | tf_op jit(solution)/shard_map/ppermute | solution.py:708
  98.4 2.7 %collective-permute-done.17.refs_1_ = bf16[2,128,2048]{2,1,0:T(8,128)(2,1)S(1)} collective-permute-done((bf16[2,128,2048]{2,1,0:T(8,128)(2,1)S(1)}, bf16[2,128,2048]{2,1,0:T(8,128)(2,1)S(1)}, u32[]{:S(2)}, u32[]{:S(2)}) %collective-permute-start.17) | collective-permute-done | bytes 1048608 | tf_op jit(solution)/shard_map/ppermute | solution.py:714
  101.2 1.8 %collective-permute-start.19 = (bf16[128,2048]{1,0:T(8,128)(2,1)S(1)}, bf16[128,2048]{1,0:T(8,128)(2,1)S(1)}, u32[]{:S(2)}, u32[]{:S(2)}) collective-permute-start(bf16[128,2048]{1,0:T(8,128)(2,1)S(1)} %fusion), channel_id=1, source_target_pairs={{0,2},{1,3},{2,0},{3,1},{4,6},{5,7},{6,4},{7,5},{8,10},{9,11},{10,... | collective-permute-start | bytes 1572872 | tf_op jit(solution)/shard_map/ppermute | solution.py:718
  104.4 5.0 %gate_up.5 = (bf16[2,64,2048]{2,1,0:T(8,128)(2,1)S(1)}, bf16[2,64,2048]{2,1,0:T(8,128)(2,1)S(1)}) custom-call(s32[4]{0:T(128)S(1)} %broadcast_xor_fusion.order, bf16[128,1024]{1,0:T(8,128)(2,1)S(1)} %collective-permute-done.11.t1.refs_0_, f32[1,1024]{1,0:T(1,128)S(1)} %bitcast.36, bf16[4,4,64,128]{3,2,1,0:T(8,128)(2,1)S(1)} %get-tuple-element.88.refs_2_.refs_3_.pick, ...), custom_call_target="tpu_custom_call" | custom-call | flops 1048576 | bytes 262144 | tf_op jit(solution)/shard_map/gate_up/pallas_call | solution.py:517
  109.3 5.9 %collective-permute-done.19.refs_2_ = bf16[128,2048]{1,0:T(8,128)(2,1)S(1)} collective-permute-done((bf16[128,2048]{1,0:T(8,128)(2,1)S(1)}, bf16[128,2048]{1,0:T(8,128)(2,1)S(1)}, u32[]{:S(2)}, u32[]{:S(2)}) %collective-permute-start.19) | collective-permute-done | bytes 524320 | tf_op jit(solution)/shard_map/ppermute | solution.py:718
  116.2 1.8 %collective-permute-start.21 = (bf16[128,1024]{1,0:T(8,128)(2,1)S(1)}, bf16[128,1024]{1,0:T(8,128)(2,1)S(1)}, u32[]{:S(2)}, u32[]{:S(2)}) collective-permute-start(bf16[128,1024]{1,0:T(8,128)(2,1)S(1)} %activate.2.a), channel_id=1, source_target_pairs={{0,2},{1,3},{2,0},{3,1},{4,6},{5,7},{6,4},{7,5},{8,10},{9,11},{10,... | collective-permute-start | bytes 786440 | tf_op jit(solution)/shard_map/ppermute | solution.py:692
  118.3 6.7 %collective-permute-done.21.b = bf16[128,1024]{1,0:T(8,128)(2,1)S(1)} collective-permute-done((bf16[128,1024]{1,0:T(8,128)(2,1)S(1)}, bf16[128,1024]{1,0:T(8,128)(2,1)S(1)}, u32[]{:S(2)}, u32[]{:S(2)}) %collective-permute-start.21) | collective-permute-done | bytes 262176 | tf_op jit(solution)/shard_map/ppermute | solution.py:692
  126.8 2.8 %down.2 = (bf16[128,1024]{1,0:T(8,128)(2,1)S(1)}, bf16[128,1024]{1,0:T(8,128)(2,1)S(1)}) custom-call(s32[4]{0:T(128)S(1)} %broadcast_xor_fusion.order, bf16[128,1024]{1,0:T(8,128)(2,1)S(1)} %activate.2.a, bf16[128,1024]{1,0:T(8,128)(2,1)S(1)} %collective-permute-done.21.b, bf16[128,1024]{1,0:T(8,128)(2,1)S(1)} %collective-permute-done.23.c, ...), custom_call_target="tpu_custom_call" | custom-call | flops 1048576 | bytes 262144 | tf_op jit(solution)/shard_map/down/pallas_call | solution.py:614
  129.6 4.1 %collective-permute-done.22.refs_6_ = bf16[64,2048]{1,0:T(8,128)(2,1)S(1)} collective-permute-done((bf16[64,2048]{1,0:T(8,128)(2,1)S(1)}, bf16[64,2048]{1,0:T(8,128)(2,1)S(1)}, u32[]{:S(2)}, u32[]{:S(2)}) %collective-permute-start.22) | collective-permute-done | bytes 262176 | tf_op jit(solution)/shard_map/ppermute | solution.py:732
  133.7 3.4 %collective-permute-start.25 = (bf16[128,1024]{1,0:T(8,128)(2,1)S(1)}, bf16[128,1024]{1,0:T(8,128)(2,1)S(1)}, u32[]{:S(2)}, u32[]{:S(2)}) collective-permute-start(bf16[128,1024]{1,0:T(8,128)(2,1)S(1)} %get-tuple-element.118), channel_id=1, source_target_pairs={{0,4},{4,0},{8,12},{12,8},{1,5},{5,1},{9,13},{13,9},{2,6},{6,2},{1... | collective-permute-start | bytes 786440 | tf_op jit(solution)/shard_map/ppermute | solution.py:735
  137.1 6.2 %collective-permute-done.25 = bf16[128,1024]{1,0:T(8,128)(2,1)S(1)} collective-permute-done((bf16[128,1024]{1,0:T(8,128)(2,1)S(1)}, bf16[128,1024]{1,0:T(8,128)(2,1)S(1)}, u32[]{:S(2)}, u32[]{:S(2)}) %collective-permute-start.25) | collective-permute-done | bytes 262176 | tf_op jit(solution)/shard_map/ppermute | solution.py:735
  144.3 1.8 %collective-permute-start.26 = (bf16[128,1024]{1,0:T(8,128)(2,1)S(1)}, bf16[128,1024]{1,0:T(8,128)(2,1)S(1)}, u32[]{:S(2)}, u32[]{:S(2)}) collective-permute-start(bf16[128,1024]{1,0:T(8,128)(2,1)S(1)} %activate.3.a), channel_id=1, source_target_pairs={{0,2},{1,3},{2,0},{3,1},{4,6},{5,7},{6,4},{7,5},{8,10},{9,11},{10,... | collective-permute-start | bytes 786440 | tf_op jit(solution)/shard_map/ppermute | solution.py:692
  146.1 5.6 %collective-permute-done.26.b = bf16[128,1024]{1,0:T(8,128)(2,1)S(1)} collective-permute-done((bf16[128,1024]{1,0:T(8,128)(2,1)S(1)}, bf16[128,1024]{1,0:T(8,128)(2,1)S(1)}, u32[]{:S(2)}, u32[]{:S(2)}) %collective-permute-start.26) | collective-permute-done | bytes 262176 | tf_op jit(solution)/shard_map/ppermute | solution.py:692
  151.8 2.4 %collective-permute-start.29 = (bf16[128,1024]{1,0:T(8,128)(2,1)S(1)}, bf16[128,1024]{1,0:T(8,128)(2,1)S(1)}, u32[]{:S(2)}, u32[]{:S(2)}) collective-permute-start(bf16[128,1024]{1,0:T(8,128)(2,1)S(1)} %add_convert_fusion.2), channel_id=1, source_target_pairs={{0,8},{4,12},{8,0},{12,4},{1,9},{5,13},{9,1},{13,5},{2,10},{6,14},... | collective-permute-start | bytes 786440 | tf_op jit(solution)/shard_map/ppermute | solution.py:738
  154.2 2.8 %down.3 = (bf16[128,1024]{1,0:T(8,128)(2,1)S(1)}, bf16[128,1024]{1,0:T(8,128)(2,1)S(1)}) custom-call(s32[4]{0:T(128)S(1)} %broadcast_xor_fusion.order, bf16[128,1024]{1,0:T(8,128)(2,1)S(1)} %activate.3.a, bf16[128,1024]{1,0:T(8,128)(2,1)S(1)} %collective-permute-done.26.b, bf16[128,1024]{1,0:T(8,128)(2,1)S(1)} %collective-permute-done.27.c, ...), custom_call_target="tpu_custom_call" | custom-call | flops 1048576 | bytes 262144 | tf_op jit(solution)/shard_map/down/pallas_call | solution.py:614
  157.7 9.4 %collective-permute-done.29 = bf16[128,1024]{1,0:T(8,128)(2,1)S(1)} collective-permute-done((bf16[128,1024]{1,0:T(8,128)(2,1)S(1)}, bf16[128,1024]{1,0:T(8,128)(2,1)S(1)}, u32[]{:S(2)}, u32[]{:S(2)}) %collective-permute-start.29) | collective-permute-done | bytes 262176 | tf_op jit(solution)/shard_map/ppermute | solution.py:738
  167.1 3.1 %collective-permute-done.30 = bf16[128,1024]{1,0:T(8,128)(2,1)S(1)} collective-permute-done((bf16[128,1024]{1,0:T(8,128)(2,1)S(1)}, bf16[128,1024]{1,0:T(8,128)(2,1)S(1)}, u32[]{:S(2)}, u32[]{:S(2)}) %collective-permute-start.30) | collective-permute-done | bytes 262176 | tf_op jit(solution)/shard_map/ppermute | solution.py:744
  (96 shorter events, 25.0 us)
Async XLA Ops:
  0.0 4.3 %collective-permute-start = (bf16[1024,128]{1,0:T(8,128)(2,1)}, bf16[1024,128]{1,0:T(8,128)(2,1)S(1)}, u32[]{:S(2)}, u32[]{:S(2)}) collective-permute-start(bf16[1024,128]{1,0:T(8,128)(2,1)} %bitcast.38), channel_id=1, source_target_pairs={{1,2},{2,1},{4,7},{7,4},{9,10},{10,9},{12,15},{15,12},{17,18},{18,... | collective-permute-start | bytes 786440 | tf_op jit(solution)/shard_map/ppermute | solution.py:208
  5.3 20.1 %collective-permute-start.1 = (bf16[1280,128]{1,0:T(8,128)(2,1)S(1)}, bf16[1280,128]{1,0:T(8,128)(2,1)S(1)}, u32[]{:S(2)}, u32[]{:S(2)}) collective-permute-start(bf16[1280,128]{1,0:T(8,128)(2,1)S(1)} %pad_maximum_fusion), channel_id=1, source_target_pairs={{0,0},{1,8},{2,6},{3,14},{4,12},{5,4},{6,10},{7,2},{8,1},{9,9},{10... | collective-permute-start | bytes 983048 | tf_op jit(solution)/shard_map/ppermute | solution.py:218
  6.1 15.7 %collective-permute-start.2 = (bf16[272,128]{1,0:T(8,128)(2,1)S(1)}, bf16[272,128]{1,0:T(8,128)(2,1)S(1)}, u32[]{:S(2)}, u32[]{:S(2)}) collective-permute-start(bf16[272,128]{1,0:T(8,128)(2,1)S(1)} %get-tuple-element.70), channel_id=1, source_target_pairs={{0,4},{4,0},{8,12},{12,8},{1,5},{5,1},{9,13},{13,9},{2,6},{6,2},{1... | collective-permute-start | bytes 208904 | tf_op jit(solution)/shard_map/ppermute | solution.py:666
  16.8 8.6 %collective-permute-start.3 = (bf16[272,128]{1,0:T(8,128)(2,1)S(1)}, bf16[272,128]{1,0:T(8,128)(2,1)S(1)}, u32[]{:S(2)}, u32[]{:S(2)}) collective-permute-start(bf16[272,128]{1,0:T(8,128)(2,1)S(1)} %get-tuple-element.71), channel_id=1, source_target_pairs={{0,8},{4,12},{8,0},{12,4},{1,9},{5,13},{9,1},{13,5},{2,10},{6,14},... | collective-permute-start | bytes 208904 | tf_op jit(solution)/shard_map/ppermute | solution.py:666
  16.8 8.6 %collective-permute-start.4 = (bf16[272,128]{1,0:T(8,128)(2,1)S(1)}, bf16[272,128]{1,0:T(8,128)(2,1)S(1)}, u32[]{:S(2)}, u32[]{:S(2)}) collective-permute-start(bf16[272,128]{1,0:T(8,128)(2,1)S(1)} %get-tuple-element.72), channel_id=1, source_target_pairs={{0,12},{4,8},{8,4},{12,0},{1,13},{5,9},{9,5},{13,1},{2,14},{6,10},... | collective-permute-start | bytes 208904 | tf_op jit(solution)/shard_map/ppermute | solution.py:666
  28.9 9.4 %collective-permute-start.5 = (bf16[128,1024]{1,0:T(8,128)(2,1)S(1)}, bf16[128,1024]{1,0:T(8,128)(2,1)S(1)}, u32[]{:S(2)}, u32[]{:S(2)}) collective-permute-start(bf16[128,1024]{1,0:T(8,128)(2,1)S(1)} %attention.1.a), channel_id=1, source_target_pairs={{0,2},{1,3},{2,0},{3,1},{4,6},{5,7},{6,4},{7,5},{8,10},{9,11},{10,... | collective-permute-start | bytes 786440 | tf_op jit(solution)/shard_map/ppermute | solution.py:672
  33.9 4.4 %collective-permute-start.6 = (bf16[128,1024]{1,0:T(8,128)(2,1)S(1)}, bf16[128,1024]{1,0:T(8,128)(2,1)S(1)}, u32[]{:S(2)}, u32[]{:S(2)}) collective-permute-start(bf16[128,1024]{1,0:T(8,128)(2,1)S(1)} %attention.1.a), channel_id=1, source_target_pairs={{0,1},{1,0},{2,3},{3,2},{4,5},{5,4},{6,7},{7,6},{8,9},{9,8},{10,11... | collective-permute-start | bytes 786440 | tf_op jit(solution)/shard_map/ppermute | solution.py:673
  38.3 1.5 collective-permute-start.7
  41.7 9.2 %collective-permute-start.8 = (bf16[128,1024]{1,0:T(8,128)(2,1)S(1)}, bf16[128,1024]{1,0:T(8,128)(2,1)S(1)}, u32[]{:S(2)}, u32[]{:S(2)}) collective-permute-start(bf16[128,1024]{1,0:T(8,128)(2,1)S(1)} %get-tuple-element.84), channel_id=1, source_target_pairs={{0,4},{4,0},{8,12},{12,8},{1,5},{5,1},{9,13},{13,9},{2,6},{6,2},{1... | collective-permute-start | bytes 786440 | tf_op jit(solution)/shard_map/ppermute | solution.py:195
  43.5 21.1 %collective-permute-start.10 = (bf16[128,1024]{1,0:T(8,128)(2,1)S(1)}, bf16[128,1024]{1,0:T(8,128)(2,1)S(1)}, u32[]{:S(2)}, u32[]{:S(2)}) collective-permute-start(bf16[128,1024]{1,0:T(8,128)(2,1)S(1)} %get-tuple-element.85), channel_id=1, source_target_pairs={{0,4},{4,0},{8,12},{12,8},{1,5},{5,1},{9,13},{13,9},{2,6},{6,2},{1... | collective-permute-start | bytes 786440 | tf_op jit(solution)/shard_map/ppermute | solution.py:197
  51.0 13.6 %collective-permute-start.9 = (bf16[128,1024]{1,0:T(8,128)(2,1)S(1)}, bf16[128,1024]{1,0:T(8,128)(2,1)S(1)}, u32[]{:S(2)}, u32[]{:S(2)}) collective-permute-start(bf16[128,1024]{1,0:T(8,128)(2,1)S(1)} %add_convert_fusion.5), channel_id=1, source_target_pairs={{0,8},{4,12},{8,0},{12,4},{1,9},{5,13},{9,1},{13,5},{2,10},{6,14},... | collective-permute-start | bytes 786440 | tf_op jit(solution)/shard_map/ppermute | solution.py:197
  64.8 10.7 %collective-permute-start.11 = (bf16[128,1024]{1,0:T(8,128)(2,1)S(1)}, bf16[128,1024]{1,0:T(8,128)(2,1)S(1)}, u32[]{:S(2)}, u32[]{:S(2)}) collective-permute-start(bf16[128,1024]{1,0:T(8,128)(2,1)S(1)} %residual.1.refs_0_.t0), channel_id=1, source_target_pairs={{0,4},{4,0},{8,12},{12,8},{1,5},{5,1},{9,13},{13,9},{2,6},{6,2},{1... | collective-permute-start | bytes 786440 | tf_op jit(solution)/shard_map/ppermute | solution.py:687
  65.6 21.2 %collective-permute-start.12 = (bf16[128,1024]{1,0:T(8,128)(2,1)S(1)}, bf16[128,1024]{1,0:T(8,128)(2,1)S(1)}, u32[]{:S(2)}, u32[]{:S(2)}) collective-permute-start(bf16[128,1024]{1,0:T(8,128)(2,1)S(1)} %residual.1.refs_0_.t0), channel_id=1, source_target_pairs={{0,8},{4,12},{8,0},{12,4},{1,9},{5,13},{9,1},{13,5},{2,10},{6,14},... | collective-permute-start | bytes 786440 | tf_op jit(solution)/shard_map/ppermute | solution.py:687
  68.3 18.4 %collective-permute-start.13 = (bf16[128,1024]{1,0:T(8,128)(2,1)S(1)}, bf16[128,1024]{1,0:T(8,128)(2,1)S(1)}, u32[]{:S(2)}, u32[]{:S(2)}) collective-permute-start(bf16[128,1024]{1,0:T(8,128)(2,1)S(1)} %residual.1.refs_0_.t0), channel_id=1, source_target_pairs={{0,12},{4,8},{8,4},{12,0},{1,13},{5,9},{9,5},{13,1},{2,14},{6,10},... | collective-permute-start | bytes 786440 | tf_op jit(solution)/shard_map/ppermute | solution.py:687
  86.8 1.9 %collective-permute-start.14 = (bf16[2,64,2048]{2,1,0:T(8,128)(2,1)S(1)}, bf16[2,64,2048]{2,1,0:T(8,128)(2,1)S(1)}, u32[]{:S(2)}, u32[]{:S(2)}) collective-permute-start(bf16[2,64,2048]{2,1,0:T(8,128)(2,1)S(1)} %get-tuple-element.91), channel_id=1, source_target_pairs={{0,1},{1,0},{2,3},{3,2},{4,5},{5,4},{6,7},{7,6},{8,9},{9,8},{10,11... | collective-permute-start | bytes 1572872 | tf_op jit(solution)/shard_map/ppermute | solution.py:704
  88.8 9.7 %collective-permute-start.15 = (bf16[64,2048]{1,0:T(8,128)(2,1)S(1)}, bf16[64,2048]{1,0:T(8,128)(2,1)S(1)}, u32[]{:S(2)}, u32[]{:S(2)}) collective-permute-start(bf16[64,2048]{1,0:T(8,128)(2,1)S(1)} %fusion.1), channel_id=1, source_target_pairs={{0,2},{1,3},{2,0},{3,1},{4,6},{5,7},{6,4},{7,5},{8,10},{9,11},{10,... | collective-permute-start | bytes 786440 | tf_op jit(solution)/shard_map/ppermute | solution.py:709
  90.8 7.7 %collective-permute-start.16 = (f32[24,512]{1,0:T(8,128)S(1)}, f32[24,512]{1,0:T(8,128)S(1)}, u32[]{:S(2)}, u32[]{:S(2)}) collective-permute-start(f32[24,512]{1,0:T(8,128)S(1)} %stats.1), channel_id=1, source_target_pairs={{0,2},{1,3},{2,0},{3,1},{4,6},{5,7},{6,4},{7,5},{8,10},{9,11},{10,... | collective-permute-start | bytes 147464 | tf_op jit(solution)/shard_map/ppermute | solution.py:708
  98.4 2.7 %collective-permute-start.17 = (bf16[2,128,2048]{2,1,0:T(8,128)(2,1)S(1)}, bf16[2,128,2048]{2,1,0:T(8,128)(2,1)S(1)}, u32[]{:S(2)}, u32[]{:S(2)}) collective-permute-start(bf16[2,128,2048]{2,1,0:T(8,128)(2,1)S(1)} %get-tuple-element.102), channel_id=1, source_target_pairs={{0,1},{1,0},{2,3},{3,2},{4,5},{5,4},{6,7},{7,6},{8,9},{9,8},{10,11... | collective-permute-start | bytes 3145736 | tf_op jit(solution)/shard_map/ppermute | solution.py:714
  101.2 14.0 %collective-permute-start.19 = (bf16[128,2048]{1,0:T(8,128)(2,1)S(1)}, bf16[128,2048]{1,0:T(8,128)(2,1)S(1)}, u32[]{:S(2)}, u32[]{:S(2)}) collective-permute-start(bf16[128,2048]{1,0:T(8,128)(2,1)S(1)} %fusion), channel_id=1, source_target_pairs={{0,2},{1,3},{2,0},{3,1},{4,6},{5,7},{6,4},{7,5},{8,10},{9,11},{10,... | collective-permute-start | bytes 1572872 | tf_op jit(solution)/shard_map/ppermute | solution.py:718
  103.1 1.3 collective-permute-start.18
  115.3 3.0 %collective-permute-start.20 = (bf16[2,64,2048]{2,1,0:T(8,128)(2,1)S(1)}, bf16[2,64,2048]{2,1,0:T(8,128)(2,1)S(1)}, u32[]{:S(2)}, u32[]{:S(2)}) collective-permute-start(bf16[2,64,2048]{2,1,0:T(8,128)(2,1)S(1)} %get-tuple-element.109), channel_id=1, source_target_pairs={{0,1},{1,0},{2,3},{3,2},{4,5},{5,4},{6,7},{7,6},{8,9},{9,8},{10,11... | collective-permute-start | bytes 1572872 | tf_op jit(solution)/shard_map/ppermute | solution.py:724
  115.3 38.9 %slice-start.2 = ((s8[8388608]{0:T(1024)(128)(4,1)}), s8[4194304]{0:T(1024)(128)(4,1)S(1)}, s32[]{:S(2)}) async-start(s8[8388608]{0:T(1024)(128)(4,1)} %bitcast.30), calls=%async_computation.2 | async-start | bytes 8388608
  116.2 8.8 %collective-permute-start.21 = (bf16[128,1024]{1,0:T(8,128)(2,1)S(1)}, bf16[128,1024]{1,0:T(8,128)(2,1)S(1)}, u32[]{:S(2)}, u32[]{:S(2)}) collective-permute-start(bf16[128,1024]{1,0:T(8,128)(2,1)S(1)} %activate.2.a), channel_id=1, source_target_pairs={{0,2},{1,3},{2,0},{3,1},{4,6},{5,7},{6,4},{7,5},{8,10},{9,11},{10,... | collective-permute-start | bytes 786440 | tf_op jit(solution)/shard_map/ppermute | solution.py:692
  118.0 8.7 %collective-permute-start.23 = (bf16[128,1024]{1,0:T(8,128)(2,1)S(1)}, bf16[128,1024]{1,0:T(8,128)(2,1)S(1)}, u32[]{:S(2)}, u32[]{:S(2)}) collective-permute-start(bf16[128,1024]{1,0:T(8,128)(2,1)S(1)} %activate.2.a), channel_id=1, source_target_pairs={{0,1},{1,0},{2,3},{3,2},{4,5},{5,4},{6,7},{7,6},{8,9},{9,8},{10,11... | collective-permute-start | bytes 786440 | tf_op jit(solution)/shard_map/ppermute | solution.py:693
  125.0 1.8 %collective-permute-start.24 = (bf16[128,1024]{1,0:T(8,128)(2,1)S(1)}, bf16[128,1024]{1,0:T(8,128)(2,1)S(1)}, u32[]{:S(2)}, u32[]{:S(2)}) collective-permute-start(bf16[128,1024]{1,0:T(8,128)(2,1)S(1)} %collective-permute-done.21.b), channel_id=1, source_target_pairs={{0,1},{1,0},{2,3},{3,2},{4,5},{5,4},{6,7},{7,6},{8,9},{9,8},{10,11... | collective-permute-start | bytes 786440 | tf_op jit(solution)/shard_map/ppermute | solution.py:731
  125.0 8.7 %collective-permute-start.22 = (bf16[64,2048]{1,0:T(8,128)(2,1)S(1)}, bf16[64,2048]{1,0:T(8,128)(2,1)S(1)}, u32[]{:S(2)}, u32[]{:S(2)}) collective-permute-start(bf16[64,2048]{1,0:T(8,128)(2,1)S(1)} %fusion.2), channel_id=1, source_target_pairs={{0,2},{1,3},{2,0},{3,1},{4,6},{5,7},{6,4},{7,5},{8,10},{9,11},{10,... | collective-permute-start | bytes 786440 | tf_op jit(solution)/shard_map/ppermute | solution.py:732
  133.7 9.6 %collective-permute-start.25 = (bf16[128,1024]{1,0:T(8,128)(2,1)S(1)}, bf16[128,1024]{1,0:T(8,128)(2,1)S(1)}, u32[]{:S(2)}, u32[]{:S(2)}) collective-permute-start(bf16[128,1024]{1,0:T(8,128)(2,1)S(1)} %get-tuple-element.118), channel_id=1, source_target_pairs={{0,4},{4,0},{8,12},{12,8},{1,5},{5,1},{9,13},{13,9},{2,6},{6,2},{1... | collective-permute-start | bytes 786440 | tf_op jit(solution)/shard_map/ppermute | solution.py:735
  144.3 7.4 %collective-permute-start.26 = (bf16[128,1024]{1,0:T(8,128)(2,1)S(1)}, bf16[128,1024]{1,0:T(8,128)(2,1)S(1)}, u32[]{:S(2)}, u32[]{:S(2)}) collective-permute-start(bf16[128,1024]{1,0:T(8,128)(2,1)S(1)} %activate.3.a), channel_id=1, source_target_pairs={{0,2},{1,3},{2,0},{3,1},{4,6},{5,7},{6,4},{7,5},{8,10},{9,11},{10,... | collective-permute-start | bytes 786440 | tf_op jit(solution)/shard_map/ppermute | solution.py:692
  146.1 8.1 %collective-permute-start.27 = (bf16[128,1024]{1,0:T(8,128)(2,1)S(1)}, bf16[128,1024]{1,0:T(8,128)(2,1)S(1)}, u32[]{:S(2)}, u32[]{:S(2)}) collective-permute-start(bf16[128,1024]{1,0:T(8,128)(2,1)S(1)} %activate.3.a), channel_id=1, source_target_pairs={{0,1},{1,0},{2,3},{3,2},{4,5},{5,4},{6,7},{7,6},{8,9},{9,8},{10,11... | collective-permute-start | bytes 786440 | tf_op jit(solution)/shard_map/ppermute | solution.py:693
  151.7 2.4 %collective-permute-start.28 = (bf16[128,1024]{1,0:T(8,128)(2,1)S(1)}, bf16[128,1024]{1,0:T(8,128)(2,1)S(1)}, u32[]{:S(2)}, u32[]{:S(2)}) collective-permute-start(bf16[128,1024]{1,0:T(8,128)(2,1)S(1)} %collective-permute-done.26.b), channel_id=1, source_target_pairs={{0,1},{1,0},{2,3},{3,2},{4,5},{5,4},{6,7},{7,6},{8,9},{9,8},{10,11... | collective-permute-start | bytes 786440 | tf_op jit(solution)/shard_map/ppermute | solution.py:694
  151.8 15.3 %collective-permute-start.29 = (bf16[128,1024]{1,0:T(8,128)(2,1)S(1)}, bf16[128,1024]{1,0:T(8,128)(2,1)S(1)}, u32[]{:S(2)}, u32[]{:S(2)}) collective-permute-start(bf16[128,1024]{1,0:T(8,128)(2,1)S(1)} %add_convert_fusion.2), channel_id=1, source_target_pairs={{0,8},{4,12},{8,0},{12,4},{1,9},{5,13},{9,1},{13,5},{2,10},{6,14},... | collective-permute-start | bytes 786440 | tf_op jit(solution)/shard_map/ppermute | solution.py:738
  157.0 13.2 %collective-permute-start.30 = (bf16[128,1024]{1,0:T(8,128)(2,1)S(1)}, bf16[128,1024]{1,0:T(8,128)(2,1)S(1)}, u32[]{:S(2)}, u32[]{:S(2)}) collective-permute-start(bf16[128,1024]{1,0:T(8,128)(2,1)S(1)} %get-tuple-element.122), channel_id=1, source_target_pairs={{0,4},{4,0},{8,12},{12,8},{1,5},{5,1},{9,13},{13,9},{2,6},{6,2},{1... | collective-permute-start | bytes 786440 | tf_op jit(solution)/shard_map/ppermute | solution.py:744
  (13 other events, 207.8 us)

commit v8 on v7

--- a/solution.py
+++ b/solution.py
@@ -699,47 +699,35 @@
     def terms_of(ds, order):
         return gate_up(ds, order, [tokens[d] for d in ds], gain, pick, weight)
 
-    kept_0, given = terms_of((0,), order)
-    given, tokens = lax.optimization_barrier((given, tokens))
-    taken_0 = lax.ppermute(given, "tp", pairs(n, 1))
-    stats = squares_and_logits(tokens, gain, router, experts)
-    far_sum = chip_sum(kept_0, taken_0)
-    far_sum, stats = lax.optimization_barrier((far_sum, stats))
+    tokens = list(lax.optimization_barrier(tuple(tokens)))
+    kept, given = terms_of((2, 3), order)
+    taken = lax.ppermute(given, "tp", pairs(n, 1))
+    given, stats = lax.optimization_barrier((given, squares_and_logits(tokens, gain, router, experts)))
     stats_far = lax.ppermute(stats, "tp", pairs(n, 2))
-    across_0 = lax.ppermute(far_sum, "tp", pairs(n, 2))
-
-    order, _ = lax.optimization_barrier((order, far_sum))
-    kept_2, given = terms_of((2, 3), order)
-    given, across_0, stats_far = lax.optimization_barrier((given, across_0, stats_far))
-    taken_2 = lax.ppermute(given, "tp", pairs(n, 1))
+    taken, stats_far = lax.optimization_barrier((taken, stats_far))
     stats = stats + stats_far
     stats_near = lax.ppermute(stats, "tp", pairs(n, 1))
-    far_sum = chip_sum(kept_2, taken_2)
-    across_2 = lax.ppermute(far_sum, "tp", pairs(n, 2))
+    far_sum = chip_sum(kept, taken)
+    across = lax.ppermute(far_sum, "tp", pairs(n, 2))
 
     order, _, stats_near = lax.optimization_barrier((order, far_sum, stats_near))
     stats = stats + stats_near
-    kept_1, given = terms_of((1,), order)
-    given, across_2 = lax.optimization_barrier((given, across_2))
-    taken_1 = lax.ppermute(given, "tp", pairs(n, 1))
-
-    groups = ((2, 3),)
-    sums = [(kept_2, taken_2, across_2)]
-    acts = spread_act(activate(groups, features, here, sums, pick, stats, pieces))
-    far_sum = chip_sum(kept_1, taken_1)
+    kept_2, given = terms_of((0, 1), order)
+    given, across = lax.optimization_barrier((given, across))
+    taken_2 = lax.ppermute(given, "tp", pairs(n, 1))
+    sums = [(kept, taken, across)]
+    acts = spread_act(activate(((2, 3),), features, here, sums, pick, stats, pieces))
+    far_sum = chip_sum(kept_2, taken_2)
     far_sum, acts[1] = lax.optimization_barrier((far_sum, acts[1]))
     acts[3] = lax.ppermute(acts[1], "tp", pairs(n, 1))
-    across_1 = lax.ppermute(far_sum, "tp", pairs(n, 2))
+    across = lax.ppermute(far_sum, "tp", pairs(n, 2))
     parts = down((2, 3), order, acts, spread, w_down)
-    across_1, *parts = lax.optimization_barrier((across_1, *parts))
     near = lax.ppermute(parts[1], "ep", pairs(n, 1))
     far = (parts[0].astype(jnp.float32) + near.astype(jnp.float32)).astype(jnp.bfloat16)
-    across_1, far = lax.optimization_barrier((across_1, far))
+    across, far = lax.optimization_barrier((across, far))
     far = lax.ppermute(far, "ep", pairs(n, 2))
-
-    groups = ((0,), (1,))
-    sums = [(kept_0, taken_0, across_0), (kept_1, taken_1, across_1)]
-    acts = spread_act(activate(groups, features, here, sums, pick, stats, pieces))
+    sums = [(kept_2, taken_2, across)]
+    acts = spread_act(activate(((0, 1),), features, here, sums, pick, stats, pieces))
     mine, near = down((0, 1), order, acts, spread, w_down)
     returned = [mine, far, lax.ppermute(near, "ep", pairs(n, 1))]
     total = residual.astype(jnp.float32)

time: 171 us -> 166 us (0.971)
  Pallas kernels: 31.5 us -> 26.7 us
    ppermute x3, waiting for transfers between devices: 12.5 us -> 17.5 us  [per_device_square(): tokens[d] = lax.ppermute(residual, 'ep', pairs(n, d))]
    pallas_call x3 -> x2, Pallas kernels: 14.9 us -> 9.98 us  [gate_up(): call(functools.partial(gate_up_body, ds), [shape] * 2, None, grid_spec=pl...]
    ppermute x5 -> x3, waiting for transfers between devices: 10.6 us -> 5.65 us  [the longest x2 5.65 us: per_device_square(): across = lax.ppermute(far_sum, 'tp', pairs(n, 2))]
    ppermute x1, waiting for transfers between devices: 2.66 us -> 0.01 us  [per_device_square(): taken_2 = lax.ppermute(given, 'tp', pairs(n, 1))]
    ppermute x5 -> x3, starting transfers between devices: 5.58 us -> 3.45 us  [the longest x2 3.38 us: per_device_square(): across = lax.ppermute(far_sum, 'tp', pairs(n, 2))]
    ppermute x1, starting transfers between devices: 0.08 us -> 2.02 us  [per_device_square(): stats_far = lax.ppermute(stats, 'tp', pairs(n, 2))]
  transfers between devices with their start and end apart: 31 -> 29, of which waited for: 17 -> 14; matrix products, arithmetic and copies ran while one was open for 9% -> 9% of each run, Pallas kernels for 15% -> 9%
where the time goes in v8:
time: 166 us
  waiting for transfers between devices  75.8 us (46%)
  starting transfers between devices  44.4 us (27%)
  Pallas kernels  26.7 us (16%)
  local copies, waits for them, and re-layouts  13.6 us (8%)
  other arithmetic  4.78 us (3%)
    ppermute x3, waiting for transfers between devices, per_device_square(): tokens[d] = lax.ppermute(residual, 'ep', pairs(n, d))  17.5 us
    ppermute x2, waiting for transfers between devices, spread_act(): far = lax.ppermute(act, 'tp', pairs(n, 2))  13.3 us
    ppermute x3, starting transfers between devices, per_device_square(): lax.ppermute(pieces[d], 'ep', pairs(n, d))  13.1 us
    optimization_barrier x1, local copies, waits for them, and re-layouts, per_device_square(): kept, w_gate_up = lax.optimization_barrier((parts[0], w_gate_up))  11.2 us
    pallas_call x2, Pallas kernels, gate_up(): call(functools.partial(gate_up_body, ds), [shape] * 2, None, grid_spec=pl...  9.98 us
    ppermute x1, waiting for transfers between devices, per_device_square(): far = lax.ppermute(far, 'ep', pairs(n, 2))  9.26 us
    ppermute x1, waiting for transfers between devices, scatter_blocks(): near = lax.ppermute(parts[3], 'ep', pairs(n, 1))  7.12 us
    ppermute x1, waiting for transfers between devices, per_device_square(): near = lax.ppermute(parts[1], 'ep', pairs(n, 1))  6.71 us
  transfers between devices with their start and end apart: 29, of which 14 were waited for; matrix products, arithmetic and copies ran while one was open for 9% of the time, Pallas kernels for 9%

profile of v8, /device:TPU:0, one launch (start us, length us, event | category | flops | bytes accessed | tf_op | source)
XLA Modules:
  0.0 165.7 jit_solution(17134394073279778909)
XLA Ops:
  6.1 10.7 %collective-permute-start.2 = (bf16[272,128]{1,0:T(8,128)(2,1)S(1)}, bf16[272,128]{1,0:T(8,128)(2,1)S(1)}, u32[]{:S(2)}, u32[]{:S(2)}) collective-permute-start(bf16[272,128]{1,0:T(8,128)(2,1)S(1)} %get-tuple-element.61), channel_id=1, source_target_pairs={{0,4},{4,0},{8,12},{12,8},{1,5},{5,1},{9,13},{13,9},{2,6},{6,2},{1... | collective-permute-start | bytes 208904 | tf_op jit(solution)/shard_map/ppermute | solution.py:666
  16.8 2.4 %collective-permute-start.4 = (bf16[272,128]{1,0:T(8,128)(2,1)S(1)}, bf16[272,128]{1,0:T(8,128)(2,1)S(1)}, u32[]{:S(2)}, u32[]{:S(2)}) collective-permute-start(bf16[272,128]{1,0:T(8,128)(2,1)S(1)} %get-tuple-element.63), channel_id=1, source_target_pairs={{0,12},{4,8},{8,4},{12,0},{1,13},{5,9},{9,5},{13,1},{2,14},{6,10},... | collective-permute-start | bytes 208904 | tf_op jit(solution)/shard_map/ppermute | solution.py:666
  19.2 1.7 %broadcast_multiply_fusion.weight = bf16[1024,1024]{1,0:T(8,128)(2,1)S(1)} fusion(bf16[1024,1024]{1,0:T(8,128)(2,1)} %param.21, bf16[]{:T(256)} %constant.23.clone.1), kind=kLoop, calls=%fused_computation.3 | loop fusion | flops 1048576 | bytes 4194306 | tf_op jit(solution)/shard_map/mul | solution.py:670
  21.9 3.5 %collective-permute-done.3.c2.refs_3_ = bf16[272,128]{1,0:T(8,128)(2,1)S(1)} collective-permute-done((bf16[272,128]{1,0:T(8,128)(2,1)S(1)}, bf16[272,128]{1,0:T(8,128)(2,1)S(1)}, u32[]{:S(2)}, u32[]{:S(2)}) %collective-permute-start.3) | collective-permute-done | bytes 69664 | tf_op jit(solution)/shard_map/ppermute | solution.py:666
  25.4 3.4 %attention.1.a = bf16[128,1024]{1,0:T(8,128)(2,1)S(1)} custom-call(s32[2]{0:T(128)S(1)} %pad_add_fusion.here, s32[4,4]{1,0:T(4,128)S(1)} %copy-done.4, s32[8]{0:T(128)S(1)} %copy-done.6, bf16[1280,128]{1,0:T(8,128)(2,1)S(1)} %collective-permute-done.1.q, bf16[272,128]{1,0:T(8,128)(2,1)S(1)} %get-tuple-element.60.c0.refs_3_, ...), custom_call_target="tpu_custom_call" | custom-call | flops 1048576 | bytes 262144 | tf_op jit(solution)/shard_map/attention/pallas_call | solution.py:370
  28.9 5.1 %collective-permute-start.5 = (bf16[128,1024]{1,0:T(8,128)(2,1)S(1)}, bf16[128,1024]{1,0:T(8,128)(2,1)S(1)}, u32[]{:S(2)}, u32[]{:S(2)}) collective-permute-start(bf16[128,1024]{1,0:T(8,128)(2,1)S(1)} %attention.1.a), channel_id=1, source_target_pairs={{0,2},{1,3},{2,0},{3,1},{4,6},{5,7},{6,4},{7,5},{8,10},{9,11},{10,... | collective-permute-start | bytes 786440 | tf_op jit(solution)/shard_map/ppermute | solution.py:672
  33.9 4.3 %collective-permute-done.5.b = bf16[128,1024]{1,0:T(8,128)(2,1)S(1)} collective-permute-done((bf16[128,1024]{1,0:T(8,128)(2,1)S(1)}, bf16[128,1024]{1,0:T(8,128)(2,1)S(1)}, u32[]{:S(2)}, u32[]{:S(2)}) %collective-permute-start.5) | collective-permute-done | bytes 262176 | tf_op jit(solution)/shard_map/ppermute | solution.py:672
  38.3 1.5 collective-permute-done.7.d
  39.8 1.9 %project.1 = (bf16[128,1024]{1,0:T(8,128)(2,1)S(1)}, bf16[128,1024]{1,0:T(8,128)(2,1)S(1)}, bf16[128,1024]{1,0:T(8,128)(2,1)S(1)}, bf16[128,1024]{1,0:T(8,128)(2,1)S(1)}) custom-call(s32[2]{0:T(128)S(1)} %pad_add_fusion.here, bf16[128,1024]{1,0:T(8,128)(2,1)S(1)} %attention.1.a, bf16[128,1024]{1,0:T(8,128)(2,1)S(1)} %collective-permute-done.5.b, ...), custom_call_target="tpu_custom_call" | custom-call | flops 1048576 | bytes 262144 | tf_op jit(solution)/shard_map/project/pallas_call | solution.py:395
  41.7 1.8 %collective-permute-start.8 = (bf16[128,1024]{1,0:T(8,128)(2,1)S(1)}, bf16[128,1024]{1,0:T(8,128)(2,1)S(1)}, u32[]{:S(2)}, u32[]{:S(2)}) collective-permute-start(bf16[128,1024]{1,0:T(8,128)(2,1)S(1)} %get-tuple-element.75), channel_id=1, source_target_pairs={{0,4},{4,0},{8,12},{12,8},{1,5},{5,1},{9,13},{13,9},{2,6},{6,2},{1... | collective-permute-start | bytes 786440 | tf_op jit(solution)/shard_map/ppermute | solution.py:195
  43.8 7.1 %collective-permute-done.8 = bf16[128,1024]{1,0:T(8,128)(2,1)S(1)} collective-permute-done((bf16[128,1024]{1,0:T(8,128)(2,1)S(1)}, bf16[128,1024]{1,0:T(8,128)(2,1)S(1)}, u32[]{:S(2)}, u32[]{:S(2)}) %collective-permute-start.8) | collective-permute-done | bytes 262176 | tf_op jit(solution)/shard_map/ppermute | solution.py:195
  53.4 11.2 %copy.25 = bf16[4,1024,2,1024]{3,1,2,0:T(8,128)(2,1)S(1)} copy(bf16[4,1024,2,1024]{3,2,1,0:T(2,128)(2,1)} %param.24) | data formatting | bytes 33554432 | tf_op jit(solution)/shard_map/optimization_barrier | solution.py:678
  65.6 2.8 %collective-permute-start.12 = (bf16[128,1024]{1,0:T(8,128)(2,1)S(1)}, bf16[128,1024]{1,0:T(8,128)(2,1)S(1)}, u32[]{:S(2)}, u32[]{:S(2)}) collective-permute-start(bf16[128,1024]{1,0:T(8,128)(2,1)S(1)} %residual.1.t0.refs_0_), channel_id=1, source_target_pairs={{0,8},{4,12},{8,0},{12,4},{1,9},{5,13},{9,1},{13,5},{2,10},{6,14},... | collective-permute-start | bytes 786440 | tf_op jit(solution)/shard_map/ppermute | solution.py:687
  69.2 6.2 %collective-permute-done.11.t1.refs_1_ = bf16[128,1024]{1,0:T(8,128)(2,1)S(1)} collective-permute-done((bf16[128,1024]{1,0:T(8,128)(2,1)S(1)}, bf16[128,1024]{1,0:T(8,128)(2,1)S(1)}, u32[]{:S(2)}, u32[]{:S(2)}) %collective-permute-start.11) | collective-permute-done | bytes 262176 | tf_op jit(solution)/shard_map/ppermute | solution.py:687
  75.5 11.3 %collective-permute-done.12.refs_0_.t2 = bf16[128,1024]{1,0:T(8,128)(2,1)S(1)} collective-permute-done((bf16[128,1024]{1,0:T(8,128)(2,1)S(1)}, bf16[128,1024]{1,0:T(8,128)(2,1)S(1)}, u32[]{:S(2)}, u32[]{:S(2)}) %collective-permute-start.12) | collective-permute-done | bytes 262176 | tf_op jit(solution)/shard_map/ppermute | solution.py:687
  86.8 5.0 %gate_up.2 = (bf16[2,128,2048]{2,1,0:T(8,128)(2,1)S(1)}, bf16[2,128,2048]{2,1,0:T(8,128)(2,1)S(1)}) custom-call(s32[4]{0:T(128)S(1)} %broadcast_xor_fusion.order, bf16[128,1024]{1,0:T(8,128)(2,1)S(1)} %collective-permute-done.12.refs_0_.t2, bf16[128,1024]{1,0:T(8,128)(2,1)S(1)} %collective-permute-done.13.refs_1_.t3, f32[1,1024]{1,0:T(1,128)S(1)} %bitcast.30, ...), custom_call_target="tpu_custom_call" | custom-call | flops 1048576 | bytes 262144 | tf_op jit(solution)/shard_map/gate_up/pallas_call | solution.py:517
  93.3 2.0 %collective-permute-start.15 = (f32[24,512]{1,0:T(8,128)S(1)}, f32[24,512]{1,0:T(8,128)S(1)}, u32[]{:S(2)}, u32[]{:S(2)}) collective-permute-start(f32[24,512]{1,0:T(8,128)S(1)} %stats.1), channel_id=1, source_target_pairs={{0,2},{1,3},{2,0},{3,1},{4,6},{5,7},{6,4},{7,5},{8,10},{9,11},{10,... | collective-permute-start | bytes 147464 | tf_op jit(solution)/shard_map/ppermute | solution.py:706
  95.3 2.4 %collective-permute-done.15 = f32[24,512]{1,0:T(8,128)S(1)} collective-permute-done((f32[24,512]{1,0:T(8,128)S(1)}, f32[24,512]{1,0:T(8,128)S(1)}, u32[]{:S(2)}, u32[]{:S(2)}) %collective-permute-start.15) | collective-permute-done | bytes 49184 | tf_op jit(solution)/shard_map/ppermute | solution.py:706
  97.8 1.8 %collective-permute-start.17 = (bf16[128,2048]{1,0:T(8,128)(2,1)S(1)}, bf16[128,2048]{1,0:T(8,128)(2,1)S(1)}, u32[]{:S(2)}, u32[]{:S(2)}) collective-permute-start(bf16[128,2048]{1,0:T(8,128)(2,1)S(1)} %fusion), channel_id=1, source_target_pairs={{0,2},{1,3},{2,0},{3,1},{4,6},{5,7},{6,4},{7,5},{8,10},{9,11},{10,... | collective-permute-start | bytes 1572872 | tf_op jit(solution)/shard_map/ppermute | solution.py:711
  100.9 5.0 %gate_up.3 = (bf16[2,128,2048]{2,1,0:T(8,128)(2,1)S(1)}, bf16[2,128,2048]{2,1,0:T(8,128)(2,1)S(1)}) custom-call(s32[4]{0:T(128)S(1)} %broadcast_xor_fusion.order, bf16[128,1024]{1,0:T(8,128)(2,1)S(1)} %residual.1.t0.refs_0_, bf16[128,1024]{1,0:T(8,128)(2,1)S(1)} %collective-permute-done.11.t1.refs_1_, f32[1,1024]{1,0:T(1,128)S(1)} %bitcast.32, ...), custom_call_target="tpu_custom_call" | custom-call | flops 1048576 | bytes 262144 | tf_op jit(solution)/shard_map/gate_up/pallas_call | solution.py:517
  105.9 5.6 %collective-permute-done.17.refs_2_ = bf16[128,2048]{1,0:T(8,128)(2,1)S(1)} collective-permute-done((bf16[128,2048]{1,0:T(8,128)(2,1)S(1)}, bf16[128,2048]{1,0:T(8,128)(2,1)S(1)}, u32[]{:S(2)}, u32[]{:S(2)}) %collective-permute-start.17) | collective-permute-done | bytes 524320 | tf_op jit(solution)/shard_map/ppermute | solution.py:711
  112.5 1.6 collective-permute-start.19
  114.6 6.8 %collective-permute-done.19.b = bf16[128,1024]{1,0:T(8,128)(2,1)S(1)} collective-permute-done((bf16[128,1024]{1,0:T(8,128)(2,1)S(1)}, bf16[128,1024]{1,0:T(8,128)(2,1)S(1)}, u32[]{:S(2)}, u32[]{:S(2)}) %collective-permute-start.19) | collective-permute-done | bytes 262176 | tf_op jit(solution)/shard_map/ppermute | solution.py:692
  121.3 1.6 collective-permute-start.20
  123.0 2.8 %down.2 = (bf16[128,1024]{1,0:T(8,128)(2,1)S(1)}, bf16[128,1024]{1,0:T(8,128)(2,1)S(1)}) custom-call(s32[4]{0:T(128)S(1)} %broadcast_xor_fusion.order, bf16[128,1024]{1,0:T(8,128)(2,1)S(1)} %activate.2.a, bf16[128,1024]{1,0:T(8,128)(2,1)S(1)} %collective-permute-done.19.b, bf16[128,1024]{1,0:T(8,128)(2,1)S(1)} %collective-permute-done.21.c, ...), custom_call_target="tpu_custom_call" | custom-call | flops 1048576 | bytes 262144 | tf_op jit(solution)/shard_map/down/pallas_call | solution.py:614
  125.8 3.4 %collective-permute-start.23 = (bf16[128,1024]{1,0:T(8,128)(2,1)S(1)}, bf16[128,1024]{1,0:T(8,128)(2,1)S(1)}, u32[]{:S(2)}, u32[]{:S(2)}) collective-permute-start(bf16[128,1024]{1,0:T(8,128)(2,1)S(1)} %get-tuple-element.100), channel_id=1, source_target_pairs={{0,4},{4,0},{8,12},{12,8},{1,5},{5,1},{9,13},{13,9},{2,6},{6,2},{1... | collective-permute-start | bytes 786440 | tf_op jit(solution)/shard_map/ppermute | solution.py:725
  129.2 6.7 %collective-permute-done.23 = bf16[128,1024]{1,0:T(8,128)(2,1)S(1)} collective-permute-done((bf16[128,1024]{1,0:T(8,128)(2,1)S(1)}, bf16[128,1024]{1,0:T(8,128)(2,1)S(1)}, u32[]{:S(2)}, u32[]{:S(2)}) %collective-permute-start.23) | collective-permute-done | bytes 262176 | tf_op jit(solution)/shard_map/ppermute | solution.py:725
  138.4 6.6 %collective-permute-done.24.b = bf16[128,1024]{1,0:T(8,128)(2,1)S(1)} collective-permute-done((bf16[128,1024]{1,0:T(8,128)(2,1)S(1)}, bf16[128,1024]{1,0:T(8,128)(2,1)S(1)}, u32[]{:S(2)}, u32[]{:S(2)}) %collective-permute-start.24) | collective-permute-done | bytes 262176 | tf_op jit(solution)/shard_map/ppermute | solution.py:692
  144.9 4.0 %collective-permute-start.27 = (bf16[128,1024]{1,0:T(8,128)(2,1)S(1)}, bf16[128,1024]{1,0:T(8,128)(2,1)S(1)}, u32[]{:S(2)}, u32[]{:S(2)}) collective-permute-start(bf16[128,1024]{1,0:T(8,128)(2,1)S(1)} %add_convert_fusion.3), channel_id=1, source_target_pairs={{0,8},{4,12},{8,0},{12,4},{1,9},{5,13},{9,1},{13,5},{2,10},{6,14},... | collective-permute-start | bytes 786440 | tf_op jit(solution)/shard_map/ppermute | solution.py:728
  149.0 2.8 %down.3 = (bf16[128,1024]{1,0:T(8,128)(2,1)S(1)}, bf16[128,1024]{1,0:T(8,128)(2,1)S(1)}) custom-call(s32[4]{0:T(128)S(1)} %broadcast_xor_fusion.order, bf16[128,1024]{1,0:T(8,128)(2,1)S(1)} %activate.3.a, bf16[128,1024]{1,0:T(8,128)(2,1)S(1)} %collective-permute-done.24.b, bf16[128,1024]{1,0:T(8,128)(2,1)S(1)} %collective-permute-done.25.c, ...), custom_call_target="tpu_custom_call" | custom-call | flops 1048576 | bytes 262144 | tf_op jit(solution)/shard_map/down/pallas_call | solution.py:614
  152.4 9.3 %collective-permute-done.27 = bf16[128,1024]{1,0:T(8,128)(2,1)S(1)} collective-permute-done((bf16[128,1024]{1,0:T(8,128)(2,1)S(1)}, bf16[128,1024]{1,0:T(8,128)(2,1)S(1)}, u32[]{:S(2)}, u32[]{:S(2)}) %collective-permute-start.27) | collective-permute-done | bytes 262176 | tf_op jit(solution)/shard_map/ppermute | solution.py:728
  161.6 3.2 %collective-permute-done.28 = bf16[128,1024]{1,0:T(8,128)(2,1)S(1)} collective-permute-done((bf16[128,1024]{1,0:T(8,128)(2,1)S(1)}, bf16[128,1024]{1,0:T(8,128)(2,1)S(1)}, u32[]{:S(2)}, u32[]{:S(2)}) %collective-permute-start.28) | collective-permute-done | bytes 262176 | tf_op jit(solution)/shard_map/ppermute | solution.py:732
  (90 shorter events, 19.6 us)
Async XLA Ops:
  0.0 4.3 %collective-permute-start = (bf16[1024,128]{1,0:T(8,128)(2,1)}, bf16[1024,128]{1,0:T(8,128)(2,1)S(1)}, u32[]{:S(2)}, u32[]{:S(2)}) collective-permute-start(bf16[1024,128]{1,0:T(8,128)(2,1)} %bitcast.34), channel_id=1, source_target_pairs={{1,2},{2,1},{4,7},{7,4},{9,10},{10,9},{12,15},{15,12},{17,18},{18,... | collective-permute-start | bytes 786440 | tf_op jit(solution)/shard_map/ppermute | solution.py:208
  5.3 20.1 %collective-permute-start.1 = (bf16[1280,128]{1,0:T(8,128)(2,1)S(1)}, bf16[1280,128]{1,0:T(8,128)(2,1)S(1)}, u32[]{:S(2)}, u32[]{:S(2)}) collective-permute-start(bf16[1280,128]{1,0:T(8,128)(2,1)S(1)} %pad_maximum_fusion), channel_id=1, source_target_pairs={{0,0},{1,8},{2,6},{3,14},{4,12},{5,4},{6,10},{7,2},{8,1},{9,9},{10... | collective-permute-start | bytes 983048 | tf_op jit(solution)/shard_map/ppermute | solution.py:218
  6.1 15.7 %collective-permute-start.2 = (bf16[272,128]{1,0:T(8,128)(2,1)S(1)}, bf16[272,128]{1,0:T(8,128)(2,1)S(1)}, u32[]{:S(2)}, u32[]{:S(2)}) collective-permute-start(bf16[272,128]{1,0:T(8,128)(2,1)S(1)} %get-tuple-element.61), channel_id=1, source_target_pairs={{0,4},{4,0},{8,12},{12,8},{1,5},{5,1},{9,13},{13,9},{2,6},{6,2},{1... | collective-permute-start | bytes 208904 | tf_op jit(solution)/shard_map/ppermute | solution.py:666
  16.8 8.6 %collective-permute-start.3 = (bf16[272,128]{1,0:T(8,128)(2,1)S(1)}, bf16[272,128]{1,0:T(8,128)(2,1)S(1)}, u32[]{:S(2)}, u32[]{:S(2)}) collective-permute-start(bf16[272,128]{1,0:T(8,128)(2,1)S(1)} %get-tuple-element.62), channel_id=1, source_target_pairs={{0,8},{4,12},{8,0},{12,4},{1,9},{5,13},{9,1},{13,5},{2,10},{6,14},... | collective-permute-start | bytes 208904 | tf_op jit(solution)/shard_map/ppermute | solution.py:666
  16.8 8.6 %collective-permute-start.4 = (bf16[272,128]{1,0:T(8,128)(2,1)S(1)}, bf16[272,128]{1,0:T(8,128)(2,1)S(1)}, u32[]{:S(2)}, u32[]{:S(2)}) collective-permute-start(bf16[272,128]{1,0:T(8,128)(2,1)S(1)} %get-tuple-element.63), channel_id=1, source_target_pairs={{0,12},{4,8},{8,4},{12,0},{1,13},{5,9},{9,5},{13,1},{2,14},{6,10},... | collective-permute-start | bytes 208904 | tf_op jit(solution)/shard_map/ppermute | solution.py:666
  28.9 23.7 %copy-start.8 = (bf16[1024]{0:T(1024)(128)(2,1)S(1)}, bf16[1024]{0:T(1024)(128)(2,1)}, u32[]{:S(2)}) copy-start(bf16[1024]{0:T(1024)(128)(2,1)} %param.22) | copy-start | bytes 6148
  28.9 9.4 %collective-permute-start.5 = (bf16[128,1024]{1,0:T(8,128)(2,1)S(1)}, bf16[128,1024]{1,0:T(8,128)(2,1)S(1)}, u32[]{:S(2)}, u32[]{:S(2)}) collective-permute-start(bf16[128,1024]{1,0:T(8,128)(2,1)S(1)} %attention.1.a), channel_id=1, source_target_pairs={{0,2},{1,3},{2,0},{3,1},{4,6},{5,7},{6,4},{7,5},{8,10},{9,11},{10,... | collective-permute-start | bytes 786440 | tf_op jit(solution)/shard_map/ppermute | solution.py:672
  33.9 4.4 %collective-permute-start.6 = (bf16[128,1024]{1,0:T(8,128)(2,1)S(1)}, bf16[128,1024]{1,0:T(8,128)(2,1)S(1)}, u32[]{:S(2)}, u32[]{:S(2)}) collective-permute-start(bf16[128,1024]{1,0:T(8,128)(2,1)S(1)} %attention.1.a), channel_id=1, source_target_pairs={{0,1},{1,0},{2,3},{3,2},{4,5},{5,4},{6,7},{7,6},{8,9},{9,8},{10,11... | collective-permute-start | bytes 786440 | tf_op jit(solution)/shard_map/ppermute | solution.py:673
  38.3 1.5 collective-permute-start.7
  41.7 9.2 %collective-permute-start.8 = (bf16[128,1024]{1,0:T(8,128)(2,1)S(1)}, bf16[128,1024]{1,0:T(8,128)(2,1)S(1)}, u32[]{:S(2)}, u32[]{:S(2)}) collective-permute-start(bf16[128,1024]{1,0:T(8,128)(2,1)S(1)} %get-tuple-element.75), channel_id=1, source_target_pairs={{0,4},{4,0},{8,12},{12,8},{1,5},{5,1},{9,13},{13,9},{2,6},{6,2},{1... | collective-permute-start | bytes 786440 | tf_op jit(solution)/shard_map/ppermute | solution.py:195
  43.5 21.1 %collective-permute-start.10 = (bf16[128,1024]{1,0:T(8,128)(2,1)S(1)}, bf16[128,1024]{1,0:T(8,128)(2,1)S(1)}, u32[]{:S(2)}, u32[]{:S(2)}) collective-permute-start(bf16[128,1024]{1,0:T(8,128)(2,1)S(1)} %get-tuple-element.76), channel_id=1, source_target_pairs={{0,4},{4,0},{8,12},{12,8},{1,5},{5,1},{9,13},{13,9},{2,6},{6,2},{1... | collective-permute-start | bytes 786440 | tf_op jit(solution)/shard_map/ppermute | solution.py:197
  51.0 13.6 %collective-permute-start.9 = (bf16[128,1024]{1,0:T(8,128)(2,1)S(1)}, bf16[128,1024]{1,0:T(8,128)(2,1)S(1)}, u32[]{:S(2)}, u32[]{:S(2)}) collective-permute-start(bf16[128,1024]{1,0:T(8,128)(2,1)S(1)} %add_convert_fusion.4), channel_id=1, source_target_pairs={{0,8},{4,12},{8,0},{12,4},{1,9},{5,13},{9,1},{13,5},{2,10},{6,14},... | collective-permute-start | bytes 786440 | tf_op jit(solution)/shard_map/ppermute | solution.py:197
  64.8 10.7 %collective-permute-start.11 = (bf16[128,1024]{1,0:T(8,128)(2,1)S(1)}, bf16[128,1024]{1,0:T(8,128)(2,1)S(1)}, u32[]{:S(2)}, u32[]{:S(2)}) collective-permute-start(bf16[128,1024]{1,0:T(8,128)(2,1)S(1)} %residual.1.t0.refs_0_), channel_id=1, source_target_pairs={{0,4},{4,0},{8,12},{12,8},{1,5},{5,1},{9,13},{13,9},{2,6},{6,2},{1... | collective-permute-start | bytes 786440 | tf_op jit(solution)/shard_map/ppermute | solution.py:687
  65.6 21.2 %collective-permute-start.12 = (bf16[128,1024]{1,0:T(8,128)(2,1)S(1)}, bf16[128,1024]{1,0:T(8,128)(2,1)S(1)}, u32[]{:S(2)}, u32[]{:S(2)}) collective-permute-start(bf16[128,1024]{1,0:T(8,128)(2,1)S(1)} %residual.1.t0.refs_0_), channel_id=1, source_target_pairs={{0,8},{4,12},{8,0},{12,4},{1,9},{5,13},{9,1},{13,5},{2,10},{6,14},... | collective-permute-start | bytes 786440 | tf_op jit(solution)/shard_map/ppermute | solution.py:687
  68.3 18.4 %collective-permute-start.13 = (bf16[128,1024]{1,0:T(8,128)(2,1)S(1)}, bf16[128,1024]{1,0:T(8,128)(2,1)S(1)}, u32[]{:S(2)}, u32[]{:S(2)}) collective-permute-start(bf16[128,1024]{1,0:T(8,128)(2,1)S(1)} %residual.1.t0.refs_0_), channel_id=1, source_target_pairs={{0,12},{4,8},{8,4},{12,0},{1,13},{5,9},{9,5},{13,1},{2,14},{6,10},... | collective-permute-start | bytes 786440 | tf_op jit(solution)/shard_map/ppermute | solution.py:687
  91.8 5.9 %collective-permute-start.14 = (bf16[2,128,2048]{2,1,0:T(8,128)(2,1)S(1)}, bf16[2,128,2048]{2,1,0:T(8,128)(2,1)S(1)}, u32[]{:S(2)}, u32[]{:S(2)}) collective-permute-start(bf16[2,128,2048]{2,1,0:T(8,128)(2,1)S(1)} %get-tuple-element.83), channel_id=1, source_target_pairs={{0,1},{1,0},{2,3},{3,2},{4,5},{5,4},{6,7},{7,6},{8,9},{9,8},{10,11... | collective-permute-start | bytes 3145736 | tf_op jit(solution)/shard_map/ppermute | solution.py:704
  93.3 4.4 %collective-permute-start.15 = (f32[24,512]{1,0:T(8,128)S(1)}, f32[24,512]{1,0:T(8,128)S(1)}, u32[]{:S(2)}, u32[]{:S(2)}) collective-permute-start(f32[24,512]{1,0:T(8,128)S(1)} %stats.1), channel_id=1, source_target_pairs={{0,2},{1,3},{2,0},{3,1},{4,6},{5,7},{6,4},{7,5},{8,10},{9,11},{10,... | collective-permute-start | bytes 147464 | tf_op jit(solution)/shard_map/ppermute | solution.py:706
  97.8 13.8 %collective-permute-start.17 = (bf16[128,2048]{1,0:T(8,128)(2,1)S(1)}, bf16[128,2048]{1,0:T(8,128)(2,1)S(1)}, u32[]{:S(2)}, u32[]{:S(2)}) collective-permute-start(bf16[128,2048]{1,0:T(8,128)(2,1)S(1)} %fusion), channel_id=1, source_target_pairs={{0,2},{1,3},{2,0},{3,1},{4,6},{5,7},{6,4},{7,5},{8,10},{9,11},{10,... | collective-permute-start | bytes 1572872 | tf_op jit(solution)/shard_map/ppermute | solution.py:711
  99.6 1.3 collective-permute-start.16
  111.6 2.8 %collective-permute-start.18 = (bf16[2,128,2048]{2,1,0:T(8,128)(2,1)S(1)}, bf16[2,128,2048]{2,1,0:T(8,128)(2,1)S(1)}, u32[]{:S(2)}, u32[]{:S(2)}) collective-permute-start(bf16[2,128,2048]{2,1,0:T(8,128)(2,1)S(1)} %get-tuple-element.94), channel_id=1, source_target_pairs={{0,1},{1,0},{2,3},{3,2},{4,5},{5,4},{6,7},{7,6},{8,9},{9,8},{10,11... | collective-permute-start | bytes 3145736 | tf_op jit(solution)/shard_map/ppermute | solution.py:717
  112.5 8.8 %collective-permute-start.19 = (bf16[128,1024]{1,0:T(8,128)(2,1)S(1)}, bf16[128,1024]{1,0:T(8,128)(2,1)S(1)}, u32[]{:S(2)}, u32[]{:S(2)}) collective-permute-start(bf16[128,1024]{1,0:T(8,128)(2,1)S(1)} %activate.2.a), channel_id=1, source_target_pairs={{0,2},{1,3},{2,0},{3,1},{4,6},{5,7},{6,4},{7,5},{8,10},{9,11},{10,... | collective-permute-start | bytes 786440 | tf_op jit(solution)/shard_map/ppermute | solution.py:692
  114.2 8.7 %collective-permute-start.21 = (bf16[128,1024]{1,0:T(8,128)(2,1)S(1)}, bf16[128,1024]{1,0:T(8,128)(2,1)S(1)}, u32[]{:S(2)}, u32[]{:S(2)}) collective-permute-start(bf16[128,1024]{1,0:T(8,128)(2,1)S(1)} %activate.2.a), channel_id=1, source_target_pairs={{0,1},{1,0},{2,3},{3,2},{4,5},{5,4},{6,7},{7,6},{8,9},{9,8},{10,11... | collective-permute-start | bytes 786440 | tf_op jit(solution)/shard_map/ppermute | solution.py:693
  114.4 34.5 %slice-start.2 = ((s8[8388608]{0:T(1024)(128)(4,1)}), s8[4194304]{0:T(1024)(128)(4,1)S(1)}, s32[]{:S(2)}) async-start(s8[8388608]{0:T(1024)(128)(4,1)} %bitcast.27), calls=%async_computation.2 | async-start | bytes 8388608
  121.3 1.6 collective-permute-start.22
  121.3 14.6 %collective-permute-start.20 = (bf16[128,2048]{1,0:T(8,128)(2,1)S(1)}, bf16[128,2048]{1,0:T(8,128)(2,1)S(1)}, u32[]{:S(2)}, u32[]{:S(2)}) collective-permute-start(bf16[128,2048]{1,0:T(8,128)(2,1)S(1)} %fusion.1), channel_id=1, source_target_pairs={{0,2},{1,3},{2,0},{3,1},{4,6},{5,7},{6,4},{7,5},{8,10},{9,11},{10,... | collective-permute-start | bytes 1572872 | tf_op jit(solution)/shard_map/ppermute | solution.py:723
  122.9 26.0 %slice-start.3 = ((s8[8388608]{0:T(1024)(128)(4,1)}), s8[4194304]{0:T(1024)(128)(4,1)S(1)}, s32[]{:S(2)}) async-start(s8[8388608]{0:T(1024)(128)(4,1)} %bitcast.27), calls=%async_computation.3 | async-start | bytes 8388608
  125.8 10.1 %collective-permute-start.23 = (bf16[128,1024]{1,0:T(8,128)(2,1)S(1)}, bf16[128,1024]{1,0:T(8,128)(2,1)S(1)}, u32[]{:S(2)}, u32[]{:S(2)}) collective-permute-start(bf16[128,1024]{1,0:T(8,128)(2,1)S(1)} %get-tuple-element.100), channel_id=1, source_target_pairs={{0,4},{4,0},{8,12},{12,8},{1,5},{5,1},{9,13},{13,9},{2,6},{6,2},{1... | collective-permute-start | bytes 786440 | tf_op jit(solution)/shard_map/ppermute | solution.py:725
  136.9 8.0 %collective-permute-start.24 = (bf16[128,1024]{1,0:T(8,128)(2,1)S(1)}, bf16[128,1024]{1,0:T(8,128)(2,1)S(1)}, u32[]{:S(2)}, u32[]{:S(2)}) collective-permute-start(bf16[128,1024]{1,0:T(8,128)(2,1)S(1)} %activate.3.a), channel_id=1, source_target_pairs={{0,2},{1,3},{2,0},{3,1},{4,6},{5,7},{6,4},{7,5},{8,10},{9,11},{10,... | collective-permute-start | bytes 786440 | tf_op jit(solution)/shard_map/ppermute | solution.py:692
  138.4 10.6 %collective-permute-start.25 = (bf16[128,1024]{1,0:T(8,128)(2,1)S(1)}, bf16[128,1024]{1,0:T(8,128)(2,1)S(1)}, u32[]{:S(2)}, u32[]{:S(2)}) collective-permute-start(bf16[128,1024]{1,0:T(8,128)(2,1)S(1)} %activate.3.a), channel_id=1, source_target_pairs={{0,1},{1,0},{2,3},{3,2},{4,5},{5,4},{6,7},{7,6},{8,9},{9,8},{10,11... | collective-permute-start | bytes 786440 | tf_op jit(solution)/shard_map/ppermute | solution.py:693
  144.9 4.0 %collective-permute-start.26 = (bf16[128,1024]{1,0:T(8,128)(2,1)S(1)}, bf16[128,1024]{1,0:T(8,128)(2,1)S(1)}, u32[]{:S(2)}, u32[]{:S(2)}) collective-permute-start(bf16[128,1024]{1,0:T(8,128)(2,1)S(1)} %collective-permute-done.24.b), channel_id=1, source_target_pairs={{0,1},{1,0},{2,3},{3,2},{4,5},{5,4},{6,7},{7,6},{8,9},{9,8},{10,11... | collective-permute-start | bytes 786440 | tf_op jit(solution)/shard_map/ppermute | solution.py:694
  144.9 16.7 %collective-permute-start.27 = (bf16[128,1024]{1,0:T(8,128)(2,1)S(1)}, bf16[128,1024]{1,0:T(8,128)(2,1)S(1)}, u32[]{:S(2)}, u32[]{:S(2)}) collective-permute-start(bf16[128,1024]{1,0:T(8,128)(2,1)S(1)} %add_convert_fusion.3), channel_id=1, source_target_pairs={{0,8},{4,12},{8,0},{12,4},{1,9},{5,13},{9,1},{13,5},{2,10},{6,14},... | collective-permute-start | bytes 786440 | tf_op jit(solution)/shard_map/ppermute | solution.py:728
  151.8 13.0 %collective-permute-start.28 = (bf16[128,1024]{1,0:T(8,128)(2,1)S(1)}, bf16[128,1024]{1,0:T(8,128)(2,1)S(1)}, u32[]{:S(2)}, u32[]{:S(2)}) collective-permute-start(bf16[128,1024]{1,0:T(8,128)(2,1)S(1)} %get-tuple-element.104), channel_id=1, source_target_pairs={{0,4},{4,0},{8,12},{12,8},{1,5},{5,1},{9,13},{13,9},{2,6},{6,2},{1... | collective-permute-start | bytes 786440 | tf_op jit(solution)/shard_map/ppermute | solution.py:732
  (11 other events, 155.7 us)

commit v9 on v8

--- a/solution.py
+++ b/solution.py
@@ -460,10 +460,11 @@
     )(hidden, *parts, after)
 
 
-def measure_body(t0, t1, t2, t3, gain, router, stats):
+def measure_body(*refs):
+    *tokens, gain, router, stats = refs
     rows = stats.shape[0]
-    length = t0.shape[0]
-    for d, ref in enumerate((t0, t1, t2, t3)):
+    length = tokens[0].shape[0]
+    for d, ref in enumerate(tokens):
         wide = ref[...].astype(jnp.float32)
         grown = wide * gain[...]
         high = grown.astype(jnp.bfloat16)
@@ -551,7 +552,7 @@
             chosen = jnp.zeros((experts, length), jnp.float32)
             for c in range(8):
                 chosen = jnp.where(ids[c : c + 1, :] == expert, 1.0, chosen)
-            block = slice(d * length, (d + 1) * length)
+            block = slice((base // capacity + k) * length, (base // capacity + k + 1) * length)
             inv_rms = lax.rsqrt(stats[experts : experts + 1, block] / features + norm_eps)
             logits = jnp.where(chosen > 0.0, stats[:experts, block] * inv_rms, -jnp.inf)
             grown = jnp.exp(logits - jnp.max(logits, axis=0, keepdims=True))
@@ -600,20 +601,30 @@
 
     @pl.when(i == pl.num_programs(0) - 1)
     def _():
-        for k, out in enumerate(outs):
+        half = spread.shape[1] // 2
+        for k, d in enumerate(ds):
             rows = results[k].reshape(-1, results.shape[3])
-            out[...] = dot(spread[ds[k]], rows).astype(jnp.bfloat16)
-
-
-def down(ds, order, acts, spread, weight):
+            block = dot(spread[d], rows).astype(jnp.bfloat16)
+            if k < len(ds) - 1:
+                outs[k][...] = block
+            elif len(outs) == len(ds):
+                outs[k][...] = block
+            else:
+                outs[k][...] = block[:half]
+                outs[k + 1][...] = block[half:]
+
+
+def down(ds, order, acts, spread, weight, halved=False):
     local, hid, width = weight.shape
     capacity = acts[0].shape[0] // len(ds)
     length = spread.shape[1]
     shape = jax.ShapeDtypeStruct((length, width), jnp.bfloat16)
+    half = jax.ShapeDtypeStruct((length // 2, width), jnp.bfloat16)
+    shapes = [shape] * (len(ds) - 1) + [half] * 2 if halved else [shape] * len(ds)
     whole = lambda rank: lambda i, order: (0,) * rank
     return call(
         functools.partial(down_body, ds),
-        [shape] * len(ds),
+        shapes,
         None,
         grid_spec=pltpu.PrefetchScalarGridSpec(
             num_scalar_prefetch=1,
@@ -623,7 +634,7 @@
                 pl.BlockSpec(spread.shape, whole(3)),
                 pl.BlockSpec((1, hid, width), lambda i, order: (order[i], 0, 0)),
             ],
-            out_specs=[pl.BlockSpec(shape.shape, whole(2))] * len(ds),
+            out_specs=[pl.BlockSpec(s.shape, whole(2)) for s in shapes],
             scratch_shapes=[pltpu.VMEM((len(ds), local, capacity, width), jnp.bfloat16)],
         ),
         name="down",
@@ -683,8 +694,9 @@
     residual = add_parts(hidden, sent, weight)
 
     tokens = [residual] + [None] * (n - 1)
-    for d in (2, 3, 1):
+    for d in (2, 1):
         tokens[d] = lax.ppermute(residual, "ep", pairs(n, d))
+    tokens[3] = lax.ppermute(tokens[2], "ep", pairs(n, 1))
 
     features = width_here * n
 
@@ -699,10 +711,13 @@
     def terms_of(ds, order):
         return gate_up(ds, order, [tokens[d] for d in ds], gain, pick, weight)
 
-    tokens = list(lax.optimization_barrier(tuple(tokens)))
-    kept, given = terms_of((2, 3), order)
+    def stats_of(ds):
+        return squares_and_logits([tokens[d] for d in ds], gain, router, experts)
+
+    one_chunk, two_chunk = ((1, 2), (0, 3))
+    kept, given = terms_of(one_chunk, order)
     taken = lax.ppermute(given, "tp", pairs(n, 1))
-    given, stats = lax.optimization_barrier((given, squares_and_logits(tokens, gain, router, experts)))
+    _, stats = lax.optimization_barrier((given, stats_of(one_chunk)))
     stats_far = lax.ppermute(stats, "tp", pairs(n, 2))
     taken, stats_far = lax.optimization_barrier((taken, stats_far))
     stats = stats + stats_far
@@ -712,24 +727,30 @@
 
     order, _, stats_near = lax.optimization_barrier((order, far_sum, stats_near))
     stats = stats + stats_near
-    kept_2, given = terms_of((0, 1), order)
-    given, across = lax.optimization_barrier((given, across))
+    kept_2, given = terms_of(two_chunk, order)
+    stats_2 = stats_of(two_chunk)
+    given, across, stats_2 = lax.optimization_barrier((given, across, stats_2))
+    stats_far = lax.ppermute(stats_2, "tp", pairs(n, 2))
     taken_2 = lax.ppermute(given, "tp", pairs(n, 1))
     sums = [(kept, taken, across)]
-    acts = spread_act(activate(((2, 3),), features, here, sums, pick, stats, pieces))
+    acts = spread_act(activate((one_chunk,), features, here, sums, pick, stats, pieces))
     far_sum = chip_sum(kept_2, taken_2)
-    far_sum, acts[1] = lax.optimization_barrier((far_sum, acts[1]))
+    far_sum, stats_far, acts[1] = lax.optimization_barrier((far_sum, stats_far, acts[1]))
+    stats_2 = stats_2 + stats_far
+    stats_near = lax.ppermute(stats_2, "tp", pairs(n, 1))
     acts[3] = lax.ppermute(acts[1], "tp", pairs(n, 1))
     across = lax.ppermute(far_sum, "tp", pairs(n, 2))
-    parts = down((2, 3), order, acts, spread, w_down)
-    near = lax.ppermute(parts[1], "ep", pairs(n, 1))
-    far = (parts[0].astype(jnp.float32) + near.astype(jnp.float32)).astype(jnp.bfloat16)
-    across, far = lax.optimization_barrier((across, far))
-    far = lax.ppermute(far, "ep", pairs(n, 2))
+    near, *far = down(one_chunk, order, acts, spread, w_down, halved=True)
+    far = [lax.ppermute(part, "ep", pairs(n, 2)) for part in far]
+    across, far[0] = lax.optimization_barrier((across, far[0]))
+    near = lax.ppermute(near, "ep", pairs(n, 1))
     sums = [(kept_2, taken_2, across)]
-    acts = spread_act(activate(((0, 1),), features, here, sums, pick, stats, pieces))
-    mine, near = down((0, 1), order, acts, spread, w_down)
-    returned = [mine, far, lax.ppermute(near, "ep", pairs(n, 1))]
+    stats_2 = stats_2 + stats_near
+    acts = spread_act(activate((two_chunk,), features, here, sums, pick, stats_2, pieces))
+    acts[3], far[1] = lax.optimization_barrier((acts[3], far[1]))
+    mine, last = down(two_chunk, order, acts, spread, w_down)
+    last = lax.ppermute(last, "ep", pairs(n, 3))
+    returned = [mine, near, jnp.concatenate(far, axis=0), last]
     total = residual.astype(jnp.float32)
     for part in returned:
         total = total + part.astype(jnp.float32)

time: 166 us -> 161 us (0.970)
  waiting for transfers between devices: 75.8 us -> 72.8 us
  starting transfers between devices: 44.4 us -> 42.3 us
    ppermute x3 -> x7, waiting for transfers between devices: 19.1 us -> 36.3 us  [the longest x2 12.7 us: per_device_square(): far = [lax.ppermute(part, 'ep', pairs(n, 2)) for part in far]]
    ppermute x3 -> x2, waiting for transfers between devices: 17.5 us -> 10.1 us  [per_device_square(): tokens[d] = lax.ppermute(residual, 'ep', pairs(n, d))]
    ppermute x2, waiting for transfers between devices: 13.3 us -> 6.51 us  [spread_act(): far = lax.ppermute(act, 'tp', pairs(n, 2))]
    ppermute x2, waiting for transfers between devices: 5.65 us -> 0.01 us  [per_device_square(): across = lax.ppermute(far_sum, 'tp', pairs(n, 2))]
    ppermute x3 -> x2, starting transfers between devices: 4.45 us -> 3.63 us  [per_device_square(): tokens[d] = lax.ppermute(residual, 'ep', pairs(n, d))]
    ppermute x3 -> x7, starting transfers between devices: 7.95 us -> 8.11 us  [the longest x1 2.94 us: per_device_square(): near = lax.ppermute(near, 'ep', pairs(n, 1))]
  transfers between devices with their start and end apart: 29 -> 32, of which waited for: 14 -> 16; matrix products, arithmetic and copies ran while one was open for 9% -> 10% of each run, Pallas kernels for 9% -> 10%
where the time goes in v9:
time: 161 us; the launch traced here: 160 us
  waiting for transfers between devices  72.8 us (45%)
  starting transfers between devices  42.3 us (26%)
  Pallas kernels  26.7 us (17%)
  local copies, waits for them, and re-layouts  13.4 us (8%)
  other arithmetic  4.77 us (3%)
    ppermute x3, starting transfers between devices, per_device_square(): lax.ppermute(pieces[d], 'ep', pairs(n, d))  13.2 us
    ppermute x2, waiting for transfers between devices, per_device_square(): far = [lax.ppermute(part, 'ep', pairs(n, 2)) for part in far]  12.7 us
    optimization_barrier x1, local copies, waits for them, and re-layouts, per_device_square(): kept, w_gate_up = lax.optimization_barrier((parts[0], w_gate_up))  11.2 us
    ppermute x2, waiting for transfers between devices, per_device_square(): tokens[d] = lax.ppermute(residual, 'ep', pairs(n, d))  10.1 us
    pallas_call x2, Pallas kernels, gate_up(): call(functools.partial(gate_up_body, ds), [shape] * 2, None, grid_spec=pl...  9.99 us
    ppermute x1, waiting for transfers between devices, per_device_square(): last = lax.ppermute(last, 'ep', pairs(n, 3))  8.62 us
    ppermute x1, waiting for transfers between devices, scatter_blocks(): near = lax.ppermute(parts[3], 'ep', pairs(n, 1))  7.13 us
    ppermute x1, waiting for transfers between devices, per_device_square(): stats_far = lax.ppermute(stats_2, 'tp', pairs(n, 2))  7.05 us
  transfers between devices with their start and end apart: 32, of which 16 were waited for; matrix products, arithmetic and copies ran while one was open for 10% of the time, Pallas kernels for 10%

profile of v9, /device:TPU:0, one launch (start us, length us, event | category | flops | bytes accessed | tf_op | source)
XLA Modules:
  0.0 160.4 jit_solution(213299594183059672)
XLA Ops:
  6.0 10.8 %collective-permute-start.2 = (bf16[272,128]{1,0:T(8,128)(2,1)S(1)}, bf16[272,128]{1,0:T(8,128)(2,1)S(1)}, u32[]{:S(2)}, u32[]{:S(2)}) collective-permute-start(bf16[272,128]{1,0:T(8,128)(2,1)S(1)} %get-tuple-element.62), channel_id=1, source_target_pairs={{0,4},{4,0},{8,12},{12,8},{1,5},{5,1},{9,13},{13,9},{2,6},{6,2},{1... | collective-permute-start | bytes 208904 | tf_op jit(solution)/shard_map/ppermute | solution.py:677
  16.8 2.4 %collective-permute-start.4 = (bf16[272,128]{1,0:T(8,128)(2,1)S(1)}, bf16[272,128]{1,0:T(8,128)(2,1)S(1)}, u32[]{:S(2)}, u32[]{:S(2)}) collective-permute-start(bf16[272,128]{1,0:T(8,128)(2,1)S(1)} %get-tuple-element.64), channel_id=1, source_target_pairs={{0,12},{4,8},{8,4},{12,0},{1,13},{5,9},{9,5},{13,1},{2,14},{6,10},... | collective-permute-start | bytes 208904 | tf_op jit(solution)/shard_map/ppermute | solution.py:677
  19.2 1.7 %broadcast_multiply_fusion.weight = bf16[1024,1024]{1,0:T(8,128)(2,1)S(1)} fusion(bf16[1024,1024]{1,0:T(8,128)(2,1)} %param.21, bf16[]{:T(256)} %constant.23.clone.1), kind=kLoop, calls=%fused_computation.3 | loop fusion | flops 1048576 | bytes 4194306 | tf_op jit(solution)/shard_map/mul | solution.py:681
  21.9 3.4 %collective-permute-done.3.c2.refs_4_ = bf16[272,128]{1,0:T(8,128)(2,1)S(1)} collective-permute-done((bf16[272,128]{1,0:T(8,128)(2,1)S(1)}, bf16[272,128]{1,0:T(8,128)(2,1)S(1)}, u32[]{:S(2)}, u32[]{:S(2)}) %collective-permute-start.3) | collective-permute-done | bytes 69664 | tf_op jit(solution)/shard_map/ppermute | solution.py:677
  25.3 3.4 %attention.1.a = bf16[128,1024]{1,0:T(8,128)(2,1)S(1)} custom-call(s32[2]{0:T(128)S(1)} %pad_add_fusion.here, s32[4,4]{1,0:T(4,128)S(1)} %copy-done.4, s32[8]{0:T(128)S(1)} %copy-done.6, bf16[1280,128]{1,0:T(8,128)(2,1)S(1)} %collective-permute-done.1.q, bf16[272,128]{1,0:T(8,128)(2,1)S(1)} %get-tuple-element.61.c0.refs_3_, ...), custom_call_target="tpu_custom_call" | custom-call | flops 1048576 | bytes 262144 | tf_op jit(solution)/shard_map/attention/pallas_call | solution.py:370
  28.8 5.2 %collective-permute-start.5 = (bf16[128,1024]{1,0:T(8,128)(2,1)S(1)}, bf16[128,1024]{1,0:T(8,128)(2,1)S(1)}, u32[]{:S(2)}, u32[]{:S(2)}) collective-permute-start(bf16[128,1024]{1,0:T(8,128)(2,1)S(1)} %attention.1.a), channel_id=1, source_target_pairs={{0,2},{1,3},{2,0},{3,1},{4,6},{5,7},{6,4},{7,5},{8,10},{9,11},{10,... | collective-permute-start | bytes 786440 | tf_op jit(solution)/shard_map/ppermute | solution.py:683
  33.9 4.3 %collective-permute-done.5.b = bf16[128,1024]{1,0:T(8,128)(2,1)S(1)} collective-permute-done((bf16[128,1024]{1,0:T(8,128)(2,1)S(1)}, bf16[128,1024]{1,0:T(8,128)(2,1)S(1)}, u32[]{:S(2)}, u32[]{:S(2)}) %collective-permute-start.5) | collective-permute-done | bytes 262176 | tf_op jit(solution)/shard_map/ppermute | solution.py:683
  38.3 1.5 collective-permute-done.7.d
  39.8 1.9 %project.1 = (bf16[128,1024]{1,0:T(8,128)(2,1)S(1)}, bf16[128,1024]{1,0:T(8,128)(2,1)S(1)}, bf16[128,1024]{1,0:T(8,128)(2,1)S(1)}, bf16[128,1024]{1,0:T(8,128)(2,1)S(1)}) custom-call(s32[2]{0:T(128)S(1)} %pad_add_fusion.here, bf16[128,1024]{1,0:T(8,128)(2,1)S(1)} %attention.1.a, bf16[128,1024]{1,0:T(8,128)(2,1)S(1)} %collective-permute-done.5.b, ...), custom_call_target="tpu_custom_call" | custom-call | flops 1048576 | bytes 262144 | tf_op jit(solution)/shard_map/project/pallas_call | solution.py:395
  41.7 1.8 %collective-permute-start.8 = (bf16[128,1024]{1,0:T(8,128)(2,1)S(1)}, bf16[128,1024]{1,0:T(8,128)(2,1)S(1)}, u32[]{:S(2)}, u32[]{:S(2)}) collective-permute-start(bf16[128,1024]{1,0:T(8,128)(2,1)S(1)} %get-tuple-element.76), channel_id=1, source_target_pairs={{0,4},{4,0},{8,12},{12,8},{1,5},{5,1},{9,13},{13,9},{2,6},{6,2},{1... | collective-permute-start | bytes 786440 | tf_op jit(solution)/shard_map/ppermute | solution.py:195
  43.8 7.1 %collective-permute-done.8 = bf16[128,1024]{1,0:T(8,128)(2,1)S(1)} collective-permute-done((bf16[128,1024]{1,0:T(8,128)(2,1)S(1)}, bf16[128,1024]{1,0:T(8,128)(2,1)S(1)}, u32[]{:S(2)}, u32[]{:S(2)}) %collective-permute-start.8) | collective-permute-done | bytes 262176 | tf_op jit(solution)/shard_map/ppermute | solution.py:195
  53.3 11.2 %copy.25 = bf16[4,1024,2,1024]{3,1,2,0:T(8,128)(2,1)S(1)} copy(bf16[4,1024,2,1024]{3,2,1,0:T(2,128)(2,1)} %param.24) | data formatting | bytes 33554432 | tf_op jit(solution)/shard_map/optimization_barrier | solution.py:689
  65.5 2.9 %collective-permute-start.12 = (bf16[128,1024]{1,0:T(8,128)(2,1)S(1)}, bf16[128,1024]{1,0:T(8,128)(2,1)S(1)}, u32[]{:S(2)}, u32[]{:S(2)}) collective-permute-start(bf16[128,1024]{1,0:T(8,128)(2,1)S(1)} %residual.1.refs_0_), channel_id=1, source_target_pairs={{0,8},{4,12},{8,0},{12,4},{1,9},{5,13},{9,1},{13,5},{2,10},{6,14},... | collective-permute-start | bytes 786440 | tf_op jit(solution)/shard_map/ppermute | solution.py:698
  68.3 8.1 %collective-permute-done.11.refs_0_ = bf16[128,1024]{1,0:T(8,128)(2,1)S(1)} collective-permute-done((bf16[128,1024]{1,0:T(8,128)(2,1)S(1)}, bf16[128,1024]{1,0:T(8,128)(2,1)S(1)}, u32[]{:S(2)}, u32[]{:S(2)}) %collective-permute-start.11) | collective-permute-done | bytes 262176 | tf_op jit(solution)/shard_map/ppermute | solution.py:698
  76.4 2.0 %collective-permute-done.12.refs_1_ = bf16[128,1024]{1,0:T(8,128)(2,1)S(1)} collective-permute-done((bf16[128,1024]{1,0:T(8,128)(2,1)S(1)}, bf16[128,1024]{1,0:T(8,128)(2,1)S(1)}, u32[]{:S(2)}, u32[]{:S(2)}) %collective-permute-start.12) | collective-permute-done | bytes 262176 | tf_op jit(solution)/shard_map/ppermute | solution.py:698
  78.4 5.0 %gate_up.2 = (bf16[2,128,2048]{2,1,0:T(8,128)(2,1)S(1)}, bf16[2,128,2048]{2,1,0:T(8,128)(2,1)S(1)}) custom-call(s32[4]{0:T(128)S(1)} %broadcast_xor_fusion.order, bf16[128,1024]{1,0:T(8,128)(2,1)S(1)} %collective-permute-done.11.refs_0_, bf16[128,1024]{1,0:T(8,128)(2,1)S(1)} %collective-permute-done.12.refs_1_, f32[1,1024]{1,0:T(1,128)S(1)} %bitcast.30, ...), custom_call_target="tpu_custom_call" | custom-call | flops 1048576 | bytes 262144 | tf_op jit(solution)/shard_map/gate_up/pallas_call | solution.py:518
  84.2 1.9 %collective-permute-start.14 = (f32[24,256]{1,0:T(8,128)S(1)}, f32[24,256]{1,0:T(8,128)S(1)}, u32[]{:S(2)}, u32[]{:S(2)}) collective-permute-start(f32[24,256]{1,0:T(8,128)S(1)} %stats.2), channel_id=1, source_target_pairs={{0,2},{1,3},{2,0},{3,1},{4,6},{5,7},{6,4},{7,5},{8,10},{9,11},{10,... | collective-permute-start | bytes 73736 | tf_op jit(solution)/shard_map/ppermute | solution.py:721
  86.1 2.0 %collective-permute-done.14 = f32[24,256]{1,0:T(8,128)S(1)} collective-permute-done((f32[24,256]{1,0:T(8,128)S(1)}, f32[24,256]{1,0:T(8,128)S(1)}, u32[]{:S(2)}, u32[]{:S(2)}) %collective-permute-start.14) | collective-permute-done | bytes 24608 | tf_op jit(solution)/shard_map/ppermute | solution.py:721
  88.2 1.9 %collective-permute-start.17 = (bf16[128,2048]{1,0:T(8,128)(2,1)S(1)}, bf16[128,2048]{1,0:T(8,128)(2,1)S(1)}, u32[]{:S(2)}, u32[]{:S(2)}) collective-permute-start(bf16[128,2048]{1,0:T(8,128)(2,1)S(1)} %fusion), channel_id=1, source_target_pairs={{0,2},{1,3},{2,0},{3,1},{4,6},{5,7},{6,4},{7,5},{8,10},{9,11},{10,... | collective-permute-start | bytes 1572872 | tf_op jit(solution)/shard_map/ppermute | solution.py:726
  90.7 6.7 %collective-permute-done.16.refs_1_ = bf16[128,1024]{1,0:T(8,128)(2,1)S(1)} collective-permute-done((bf16[128,1024]{1,0:T(8,128)(2,1)S(1)}, bf16[128,1024]{1,0:T(8,128)(2,1)S(1)}, u32[]{:S(2)}, u32[]{:S(2)}) %collective-permute-start.16) | collective-permute-done | bytes 262176 | tf_op jit(solution)/shard_map/ppermute | solution.py:699
  98.1 5.0 %gate_up.3 = (bf16[2,128,2048]{2,1,0:T(8,128)(2,1)S(1)}, bf16[2,128,2048]{2,1,0:T(8,128)(2,1)S(1)}) custom-call(s32[4]{0:T(128)S(1)} %broadcast_xor_fusion.order, bf16[128,1024]{1,0:T(8,128)(2,1)S(1)} %residual.1.refs_0_, bf16[128,1024]{1,0:T(8,128)(2,1)S(1)} %collective-permute-done.16.refs_1_, f32[1,1024]{1,0:T(1,128)S(1)} %bitcast.33, ...), custom_call_target="tpu_custom_call" | custom-call | flops 1048576 | bytes 262144 | tf_op jit(solution)/shard_map/gate_up/pallas_call | solution.py:518
  104.6 1.7 %collective-permute-start.19 = (f32[24,256]{1,0:T(8,128)S(1)}, f32[24,256]{1,0:T(8,128)S(1)}, u32[]{:S(2)}, u32[]{:S(2)}) collective-permute-start(f32[24,256]{1,0:T(8,128)S(1)} %stats.3), channel_id=1, source_target_pairs={{0,2},{1,3},{2,0},{3,1},{4,6},{5,7},{6,4},{7,5},{8,10},{9,11},{10,... | collective-permute-start | bytes 73736 | tf_op jit(solution)/shard_map/ppermute | solution.py:733
  106.4 7.0 %collective-permute-done.19 = f32[24,256]{1,0:T(8,128)S(1)} collective-permute-done((f32[24,256]{1,0:T(8,128)S(1)}, f32[24,256]{1,0:T(8,128)S(1)}, u32[]{:S(2)}, u32[]{:S(2)}) %collective-permute-start.19) | collective-permute-done | bytes 24608 | tf_op jit(solution)/shard_map/ppermute | solution.py:733
  115.7 2.8 %down.2 = (bf16[128,1024]{1,0:T(8,128)(2,1)S(1)}, bf16[64,1024]{1,0:T(8,128)(2,1)S(1)}, bf16[64,1024]{1,0:T(8,128)(2,1)S(1)}) custom-call(s32[4]{0:T(128)S(1)} %broadcast_xor_fusion.order, bf16[128,1024]{1,0:T(8,128)(2,1)S(1)} %activate.2.a, bf16[128,1024]{1,0:T(8,128)(2,1)S(1)} %collective-permute-done.20.b, ...), custom_call_target="tpu_custom_call" | custom-call | flops 1048576 | bytes 262144 | tf_op jit(solution)/shard_map/down/pallas_call | solution.py:625
  121.2 6.7 %collective-permute-done.25 = bf16[64,1024]{1,0:T(8,128)(2,1)S(1)} collective-permute-done((bf16[64,1024]{1,0:T(8,128)(2,1)S(1)}, bf16[64,1024]{1,0:T(8,128)(2,1)S(1)}, u32[]{:S(2)}, u32[]{:S(2)}) %collective-permute-start.25) | collective-permute-done | bytes 131104 | tf_op jit(solution)/shard_map/ppermute | solution.py:744
  128.8 1.7 %collective-permute-start.26 = (bf16[128,1024]{1,0:T(8,128)(2,1)S(1)}, bf16[128,1024]{1,0:T(8,128)(2,1)S(1)}, u32[]{:S(2)}, u32[]{:S(2)}) collective-permute-start(bf16[128,1024]{1,0:T(8,128)(2,1)S(1)} %activate.3.a), channel_id=1, source_target_pairs={{0,2},{1,3},{2,0},{3,1},{4,6},{5,7},{6,4},{7,5},{8,10},{9,11},{10,... | collective-permute-start | bytes 786440 | tf_op jit(solution)/shard_map/ppermute | solution.py:704
  130.5 6.5 %collective-permute-done.26.b = bf16[128,1024]{1,0:T(8,128)(2,1)S(1)} collective-permute-done((bf16[128,1024]{1,0:T(8,128)(2,1)S(1)}, bf16[128,1024]{1,0:T(8,128)(2,1)S(1)}, u32[]{:S(2)}, u32[]{:S(2)}) %collective-permute-start.26) | collective-permute-done | bytes 262176 | tf_op jit(solution)/shard_map/ppermute | solution.py:704
  137.5 2.9 %collective-permute-start.30 = (bf16[128,1024]{1,0:T(8,128)(2,1)S(1)}, bf16[128,1024]{1,0:T(8,128)(2,1)S(1)}, u32[]{:S(2)}, u32[]{:S(2)}) collective-permute-start(bf16[128,1024]{1,0:T(8,128)(2,1)S(1)} %get-tuple-element.103), channel_id=1, source_target_pairs={{0,4},{4,0},{8,12},{12,8},{1,5},{5,1},{9,13},{13,9},{2,6},{6,2},{1... | collective-permute-start | bytes 786440 | tf_op jit(solution)/shard_map/ppermute | solution.py:746
  140.5 6.0 %collective-permute-done.29 = bf16[64,1024]{1,0:T(8,128)(2,1)S(1)} collective-permute-done((bf16[64,1024]{1,0:T(8,128)(2,1)S(1)}, bf16[64,1024]{1,0:T(8,128)(2,1)S(1)}, u32[]{:S(2)}, u32[]{:S(2)}) %collective-permute-start.29) | collective-permute-done | bytes 131104 | tf_op jit(solution)/shard_map/ppermute | solution.py:744
  146.5 2.8 %down.3 = (bf16[128,1024]{1,0:T(8,128)(2,1)S(1)}, bf16[128,1024]{1,0:T(8,128)(2,1)S(1)}) custom-call(s32[4]{0:T(128)S(1)} %broadcast_xor_fusion.order, bf16[128,1024]{1,0:T(8,128)(2,1)S(1)} %activate.3.a, bf16[128,1024]{1,0:T(8,128)(2,1)S(1)} %collective-permute-done.26.b, bf16[128,1024]{1,0:T(8,128)(2,1)S(1)} %collective-permute-done.27.c, ...), custom_call_target="tpu_custom_call" | custom-call | flops 1048576 | bytes 262144 | tf_op jit(solution)/shard_map/down/pallas_call | solution.py:625
  149.4 1.5 collective-permute-start.31
  150.9 8.6 %collective-permute-done.31 = bf16[128,1024]{1,0:T(8,128)(2,1)S(1)} collective-permute-done((bf16[128,1024]{1,0:T(8,128)(2,1)S(1)}, bf16[128,1024]{1,0:T(8,128)(2,1)S(1)}, u32[]{:S(2)}, u32[]{:S(2)}) %collective-permute-start.31) | collective-permute-done | bytes 262176 | tf_op jit(solution)/shard_map/ppermute | solution.py:752
  (98 shorter events, 21.4 us)
Async XLA Ops:
  0.0 4.2 %collective-permute-start = (bf16[1024,128]{1,0:T(8,128)(2,1)}, bf16[1024,128]{1,0:T(8,128)(2,1)S(1)}, u32[]{:S(2)}, u32[]{:S(2)}) collective-permute-start(bf16[1024,128]{1,0:T(8,128)(2,1)} %bitcast.35), channel_id=1, source_target_pairs={{1,2},{2,1},{4,7},{7,4},{9,10},{10,9},{12,15},{15,12},{17,18},{18,... | collective-permute-start | bytes 786440 | tf_op jit(solution)/shard_map/ppermute | solution.py:208
  5.2 20.1 %collective-permute-start.1 = (bf16[1280,128]{1,0:T(8,128)(2,1)S(1)}, bf16[1280,128]{1,0:T(8,128)(2,1)S(1)}, u32[]{:S(2)}, u32[]{:S(2)}) collective-permute-start(bf16[1280,128]{1,0:T(8,128)(2,1)S(1)} %pad_maximum_fusion), channel_id=1, source_target_pairs={{0,0},{1,8},{2,6},{3,14},{4,12},{5,4},{6,10},{7,2},{8,1},{9,9},{10... | collective-permute-start | bytes 983048 | tf_op jit(solution)/shard_map/ppermute | solution.py:218
  6.0 15.9 %collective-permute-start.2 = (bf16[272,128]{1,0:T(8,128)(2,1)S(1)}, bf16[272,128]{1,0:T(8,128)(2,1)S(1)}, u32[]{:S(2)}, u32[]{:S(2)}) collective-permute-start(bf16[272,128]{1,0:T(8,128)(2,1)S(1)} %get-tuple-element.62), channel_id=1, source_target_pairs={{0,4},{4,0},{8,12},{12,8},{1,5},{5,1},{9,13},{13,9},{2,6},{6,2},{1... | collective-permute-start | bytes 208904 | tf_op jit(solution)/shard_map/ppermute | solution.py:677
  16.8 8.5 %collective-permute-start.3 = (bf16[272,128]{1,0:T(8,128)(2,1)S(1)}, bf16[272,128]{1,0:T(8,128)(2,1)S(1)}, u32[]{:S(2)}, u32[]{:S(2)}) collective-permute-start(bf16[272,128]{1,0:T(8,128)(2,1)S(1)} %get-tuple-element.63), channel_id=1, source_target_pairs={{0,8},{4,12},{8,0},{12,4},{1,9},{5,13},{9,1},{13,5},{2,10},{6,14},... | collective-permute-start | bytes 208904 | tf_op jit(solution)/shard_map/ppermute | solution.py:677
  16.8 8.5 %collective-permute-start.4 = (bf16[272,128]{1,0:T(8,128)(2,1)S(1)}, bf16[272,128]{1,0:T(8,128)(2,1)S(1)}, u32[]{:S(2)}, u32[]{:S(2)}) collective-permute-start(bf16[272,128]{1,0:T(8,128)(2,1)S(1)} %get-tuple-element.64), channel_id=1, source_target_pairs={{0,12},{4,8},{8,4},{12,0},{1,13},{5,9},{9,5},{13,1},{2,14},{6,10},... | collective-permute-start | bytes 208904 | tf_op jit(solution)/shard_map/ppermute | solution.py:677
  28.8 9.5 %collective-permute-start.5 = (bf16[128,1024]{1,0:T(8,128)(2,1)S(1)}, bf16[128,1024]{1,0:T(8,128)(2,1)S(1)}, u32[]{:S(2)}, u32[]{:S(2)}) collective-permute-start(bf16[128,1024]{1,0:T(8,128)(2,1)S(1)} %attention.1.a), channel_id=1, source_target_pairs={{0,2},{1,3},{2,0},{3,1},{4,6},{5,7},{6,4},{7,5},{8,10},{9,11},{10,... | collective-permute-start | bytes 786440 | tf_op jit(solution)/shard_map/ppermute | solution.py:683
  33.9 4.4 %collective-permute-start.6 = (bf16[128,1024]{1,0:T(8,128)(2,1)S(1)}, bf16[128,1024]{1,0:T(8,128)(2,1)S(1)}, u32[]{:S(2)}, u32[]{:S(2)}) collective-permute-start(bf16[128,1024]{1,0:T(8,128)(2,1)S(1)} %attention.1.a), channel_id=1, source_target_pairs={{0,1},{1,0},{2,3},{3,2},{4,5},{5,4},{6,7},{7,6},{8,9},{9,8},{10,11... | collective-permute-start | bytes 786440 | tf_op jit(solution)/shard_map/ppermute | solution.py:684
  38.3 1.5 collective-permute-start.7
  41.7 9.2 %collective-permute-start.8 = (bf16[128,1024]{1,0:T(8,128)(2,1)S(1)}, bf16[128,1024]{1,0:T(8,128)(2,1)S(1)}, u32[]{:S(2)}, u32[]{:S(2)}) collective-permute-start(bf16[128,1024]{1,0:T(8,128)(2,1)S(1)} %get-tuple-element.76), channel_id=1, source_target_pairs={{0,4},{4,0},{8,12},{12,8},{1,5},{5,1},{9,13},{13,9},{2,6},{6,2},{1... | collective-permute-start | bytes 786440 | tf_op jit(solution)/shard_map/ppermute | solution.py:195
  43.5 21.0 %collective-permute-start.10 = (bf16[128,1024]{1,0:T(8,128)(2,1)S(1)}, bf16[128,1024]{1,0:T(8,128)(2,1)S(1)}, u32[]{:S(2)}, u32[]{:S(2)}) collective-permute-start(bf16[128,1024]{1,0:T(8,128)(2,1)S(1)} %get-tuple-element.77), channel_id=1, source_target_pairs={{0,4},{4,0},{8,12},{12,8},{1,5},{5,1},{9,13},{13,9},{2,6},{6,2},{1... | collective-permute-start | bytes 786440 | tf_op jit(solution)/shard_map/ppermute | solution.py:197
  51.0 13.5 %collective-permute-start.9 = (bf16[128,1024]{1,0:T(8,128)(2,1)S(1)}, bf16[128,1024]{1,0:T(8,128)(2,1)S(1)}, u32[]{:S(2)}, u32[]{:S(2)}) collective-permute-start(bf16[128,1024]{1,0:T(8,128)(2,1)S(1)} %add_convert_fusion.3), channel_id=1, source_target_pairs={{0,8},{4,12},{8,0},{12,4},{1,9},{5,13},{9,1},{13,5},{2,10},{6,14},... | collective-permute-start | bytes 786440 | tf_op jit(solution)/shard_map/ppermute | solution.py:197
  64.7 11.7 %collective-permute-start.11 = (bf16[128,1024]{1,0:T(8,128)(2,1)S(1)}, bf16[128,1024]{1,0:T(8,128)(2,1)S(1)}, u32[]{:S(2)}, u32[]{:S(2)}) collective-permute-start(bf16[128,1024]{1,0:T(8,128)(2,1)S(1)} %residual.1.refs_0_), channel_id=1, source_target_pairs={{0,4},{4,0},{8,12},{12,8},{1,5},{5,1},{9,13},{13,9},{2,6},{6,2},{1... | collective-permute-start | bytes 786440 | tf_op jit(solution)/shard_map/ppermute | solution.py:698
  65.5 12.9 %collective-permute-start.12 = (bf16[128,1024]{1,0:T(8,128)(2,1)S(1)}, bf16[128,1024]{1,0:T(8,128)(2,1)S(1)}, u32[]{:S(2)}, u32[]{:S(2)}) collective-permute-start(bf16[128,1024]{1,0:T(8,128)(2,1)S(1)} %residual.1.refs_0_), channel_id=1, source_target_pairs={{0,8},{4,12},{8,0},{12,4},{1,9},{5,13},{9,1},{13,5},{2,10},{6,14},... | collective-permute-start | bytes 786440 | tf_op jit(solution)/shard_map/ppermute | solution.py:698
  83.4 4.7 %collective-permute-start.13 = (bf16[2,128,2048]{2,1,0:T(8,128)(2,1)S(1)}, bf16[2,128,2048]{2,1,0:T(8,128)(2,1)S(1)}, u32[]{:S(2)}, u32[]{:S(2)}) collective-permute-start(bf16[2,128,2048]{2,1,0:T(8,128)(2,1)S(1)} %get-tuple-element.82), channel_id=1, source_target_pairs={{0,1},{1,0},{2,3},{3,2},{4,5},{5,4},{6,7},{7,6},{8,9},{9,8},{10,11... | collective-permute-start | bytes 3145736 | tf_op jit(solution)/shard_map/ppermute | solution.py:719
  84.2 3.9 %collective-permute-start.14 = (f32[24,256]{1,0:T(8,128)S(1)}, f32[24,256]{1,0:T(8,128)S(1)}, u32[]{:S(2)}, u32[]{:S(2)}) collective-permute-start(f32[24,256]{1,0:T(8,128)S(1)} %stats.2), channel_id=1, source_target_pairs={{0,2},{1,3},{2,0},{3,1},{4,6},{5,7},{6,4},{7,5},{8,10},{9,11},{10,... | collective-permute-start | bytes 73736 | tf_op jit(solution)/shard_map/ppermute | solution.py:721
  88.2 14.9 %collective-permute-start.17 = (bf16[128,2048]{1,0:T(8,128)(2,1)S(1)}, bf16[128,2048]{1,0:T(8,128)(2,1)S(1)}, u32[]{:S(2)}, u32[]{:S(2)}) collective-permute-start(bf16[128,2048]{1,0:T(8,128)(2,1)S(1)} %fusion), channel_id=1, source_target_pairs={{0,2},{1,3},{2,0},{3,1},{4,6},{5,7},{6,4},{7,5},{8,10},{9,11},{10,... | collective-permute-start | bytes 1572872 | tf_op jit(solution)/shard_map/ppermute | solution.py:726
  90.1 7.3 %collective-permute-start.16 = (bf16[128,1024]{1,0:T(8,128)(2,1)S(1)}, bf16[128,1024]{1,0:T(8,128)(2,1)S(1)}, u32[]{:S(2)}, u32[]{:S(2)}) collective-permute-start(bf16[128,1024]{1,0:T(8,128)(2,1)S(1)} %collective-permute-done.12.refs_1_), channel_id=1, source_target_pairs={{0,4},{4,0},{8,12},{12,8},{1,5},{5,1},{9,13},{13,9},{2,6},{6,2},{1... | collective-permute-start | bytes 786440 | tf_op jit(solution)/shard_map/ppermute | solution.py:699
  90.7 7.5 %collective-permute-start.15 = (f32[24,256]{1,0:T(8,128)S(1)}, f32[24,256]{1,0:T(8,128)S(1)}, u32[]{:S(2)}, u32[]{:S(2)}) collective-permute-start(f32[24,256]{1,0:T(8,128)S(1)} %add.46), channel_id=1, source_target_pairs={{0,1},{1,0},{2,3},{3,2},{4,5},{5,4},{6,7},{7,6},{8,9},{9,8},{10,11... | collective-permute-start | bytes 73736 | tf_op jit(solution)/shard_map/ppermute | solution.py:724
  103.2 3.1 %collective-permute-start.18 = (bf16[2,128,2048]{2,1,0:T(8,128)(2,1)S(1)}, bf16[2,128,2048]{2,1,0:T(8,128)(2,1)S(1)}, u32[]{:S(2)}, u32[]{:S(2)}) collective-permute-start(bf16[2,128,2048]{2,1,0:T(8,128)(2,1)S(1)} %get-tuple-element.91), channel_id=1, source_target_pairs={{0,1},{1,0},{2,3},{3,2},{4,5},{5,4},{6,7},{7,6},{8,9},{9,8},{10,11... | collective-permute-start | bytes 3145736 | tf_op jit(solution)/shard_map/ppermute | solution.py:734
  104.2 9.3 %collective-permute-start.20 = (bf16[128,1024]{1,0:T(8,128)(2,1)S(1)}, bf16[128,1024]{1,0:T(8,128)(2,1)S(1)}, u32[]{:S(2)}, u32[]{:S(2)}) collective-permute-start(bf16[128,1024]{1,0:T(8,128)(2,1)S(1)} %activate.2.a), channel_id=1, source_target_pairs={{0,2},{1,3},{2,0},{3,1},{4,6},{5,7},{6,4},{7,5},{8,10},{9,11},{10,... | collective-permute-start | bytes 786440 | tf_op jit(solution)/shard_map/ppermute | solution.py:704
  104.6 8.9 %collective-permute-start.19 = (f32[24,256]{1,0:T(8,128)S(1)}, f32[24,256]{1,0:T(8,128)S(1)}, u32[]{:S(2)}, u32[]{:S(2)}) collective-permute-start(f32[24,256]{1,0:T(8,128)S(1)} %stats.3), channel_id=1, source_target_pairs={{0,2},{1,3},{2,0},{3,1},{4,6},{5,7},{6,4},{7,5},{8,10},{9,11},{10,... | collective-permute-start | bytes 73736 | tf_op jit(solution)/shard_map/ppermute | solution.py:733
  113.5 14.4 %collective-permute-start.22 = (bf16[128,2048]{1,0:T(8,128)(2,1)S(1)}, bf16[128,2048]{1,0:T(8,128)(2,1)S(1)}, u32[]{:S(2)}, u32[]{:S(2)}) collective-permute-start(bf16[128,2048]{1,0:T(8,128)(2,1)S(1)} %fusion.1), channel_id=1, source_target_pairs={{0,2},{1,3},{2,0},{3,1},{4,6},{5,7},{6,4},{7,5},{8,10},{9,11},{10,... | collective-permute-start | bytes 1572872 | tf_op jit(solution)/shard_map/ppermute | solution.py:742
  113.8 1.5 collective-permute-start.23
  113.8 1.9 %collective-permute-start.24 = (bf16[128,1024]{1,0:T(8,128)(2,1)S(1)}, bf16[128,1024]{1,0:T(8,128)(2,1)S(1)}, u32[]{:S(2)}, u32[]{:S(2)}) collective-permute-start(bf16[128,1024]{1,0:T(8,128)(2,1)S(1)} %collective-permute-done.20.b), channel_id=1, source_target_pairs={{0,1},{1,0},{2,3},{3,2},{4,5},{5,4},{6,7},{7,6},{8,9},{9,8},{10,11... | collective-permute-start | bytes 786440 | tf_op jit(solution)/shard_map/ppermute | solution.py:741
  118.5 9.3 %collective-permute-start.25 = (bf16[64,1024]{1,0:T(8,128)(2,1)S(1)}, bf16[64,1024]{1,0:T(8,128)(2,1)S(1)}, u32[]{:S(2)}, u32[]{:S(2)}) collective-permute-start(bf16[64,1024]{1,0:T(8,128)(2,1)S(1)} %get-tuple-element.98), channel_id=1, source_target_pairs={{0,8},{4,12},{8,0},{12,4},{1,9},{5,13},{9,1},{13,5},{2,10},{6,14},... | collective-permute-start | bytes 393224 | tf_op jit(solution)/shard_map/ppermute | solution.py:744
  120.0 1.2 collective-permute-start.21
  128.8 8.2 %collective-permute-start.26 = (bf16[128,1024]{1,0:T(8,128)(2,1)S(1)}, bf16[128,1024]{1,0:T(8,128)(2,1)S(1)}, u32[]{:S(2)}, u32[]{:S(2)}) collective-permute-start(bf16[128,1024]{1,0:T(8,128)(2,1)S(1)} %activate.3.a), channel_id=1, source_target_pairs={{0,2},{1,3},{2,0},{3,1},{4,6},{5,7},{6,4},{7,5},{8,10},{9,11},{10,... | collective-permute-start | bytes 786440 | tf_op jit(solution)/shard_map/ppermute | solution.py:704
  137.0 9.5 %collective-permute-start.28 = (bf16[128,1024]{1,0:T(8,128)(2,1)S(1)}, bf16[128,1024]{1,0:T(8,128)(2,1)S(1)}, u32[]{:S(2)}, u32[]{:S(2)}) collective-permute-start(bf16[128,1024]{1,0:T(8,128)(2,1)S(1)} %collective-permute-done.26.b), channel_id=1, source_target_pairs={{0,1},{1,0},{2,3},{3,2},{4,5},{5,4},{6,7},{7,6},{8,9},{9,8},{10,11... | collective-permute-start | bytes 786440 | tf_op jit(solution)/shard_map/ppermute | solution.py:706
  137.0 9.5 %collective-permute-start.27 = (bf16[128,1024]{1,0:T(8,128)(2,1)S(1)}, bf16[128,1024]{1,0:T(8,128)(2,1)S(1)}, u32[]{:S(2)}, u32[]{:S(2)}) collective-permute-start(bf16[128,1024]{1,0:T(8,128)(2,1)S(1)} %activate.3.a), channel_id=1, source_target_pairs={{0,1},{1,0},{2,3},{3,2},{4,5},{5,4},{6,7},{7,6},{8,9},{9,8},{10,11... | collective-permute-start | bytes 786440 | tf_op jit(solution)/shard_map/ppermute | solution.py:705
  137.5 9.0 %collective-permute-start.29 = (bf16[64,1024]{1,0:T(8,128)(2,1)S(1)}, bf16[64,1024]{1,0:T(8,128)(2,1)S(1)}, u32[]{:S(2)}, u32[]{:S(2)}) collective-permute-start(bf16[64,1024]{1,0:T(8,128)(2,1)S(1)} %get-tuple-element.100), channel_id=1, source_target_pairs={{0,8},{4,12},{8,0},{12,4},{1,9},{5,13},{9,1},{13,5},{2,10},{6,14},... | collective-permute-start | bytes 393224 | tf_op jit(solution)/shard_map/ppermute | solution.py:744
  137.5 13.3 %collective-permute-start.30 = (bf16[128,1024]{1,0:T(8,128)(2,1)S(1)}, bf16[128,1024]{1,0:T(8,128)(2,1)S(1)}, u32[]{:S(2)}, u32[]{:S(2)}) collective-permute-start(bf16[128,1024]{1,0:T(8,128)(2,1)S(1)} %get-tuple-element.103), channel_id=1, source_target_pairs={{0,4},{4,0},{8,12},{12,8},{1,5},{5,1},{9,13},{13,9},{2,6},{6,2},{1... | collective-permute-start | bytes 786440 | tf_op jit(solution)/shard_map/ppermute | solution.py:746
  149.4 10.1 %collective-permute-start.31 = (bf16[128,1024]{1,0:T(8,128)(2,1)S(1)}, bf16[128,1024]{1,0:T(8,128)(2,1)S(1)}, u32[]{:S(2)}, u32[]{:S(2)}) collective-permute-start(bf16[128,1024]{1,0:T(8,128)(2,1)S(1)} %get-tuple-element.106), channel_id=1, source_target_pairs={{0,12},{4,8},{8,4},{12,0},{1,13},{5,9},{9,5},{13,1},{2,14},{6,10},... | collective-permute-start | bytes 786440 | tf_op jit(solution)/shard_map/ppermute | solution.py:752
  (14 other events, 240.4 us)

commit v10 on v9

--- a/solution.py
+++ b/solution.py
@@ -191,12 +191,6 @@
     return [(i, i ^ flip) for i in range(lanes)]
 
 
-def scatter_blocks(parts, n):
-    near = lax.ppermute(parts[3], "ep", pairs(n, 1))
-    far = (parts[2].astype(jnp.float32) + near.astype(jnp.float32)).astype(jnp.bfloat16)
-    return [parts[0], lax.ppermute(far, "ep", pairs(n, 2)), lax.ppermute(parts[1], "ep", pairs(n, 1))]
-
-
 def query_of(device, lane):
     return 2 * (lane & 1) + ((lane >> 1) ^ (device & 1))
 
@@ -381,25 +375,38 @@
     )(here, query_docs, doc_lens, q, *pieces, *tables)
 
 
-def project_body(here, a, b, c, d, weight, *rest):
-    outs, rows = (rest[:-1], rest[-1])
+def project_rows(here, flip, a, b, rows):
     device, lane = (here[0], here[1])
-    for flip, ref in zip((0, 2, 1, 3), (a, b, c, d)):
-        rows[query_of(device, lane ^ flip)] = ref[...]
-    for d in (2, 3, 1, 0):
-        outs[d][...] = dot(rows[device ^ d], weight[...]).astype(jnp.bfloat16)
-
-
-def project(here, parts, weight):
+    high = (device ^ query_of(device, lane ^ flip)) >> 1
+    rows[high] = a[...]
+    rows[1 - high] = b[...]
+
+
+def project_early_body(here, a, b, weight, close, far, rows):
+    project_rows(here, 0, a, b, rows)
+    far[...] = dot(rows[1], weight[...]).astype(jnp.bfloat16)
+    close[...] = dot(rows[0], weight[...]).astype(jnp.bfloat16)
+
+
+def project_late_body(here, a, b, weight, early, own, near, far, rows):
+    project_rows(here, 2, a, b, rows)
+    far[...] = dot(rows[1], weight[...]).astype(jnp.bfloat16)
+    late = dot(rows[0], weight[...]).astype(jnp.bfloat16)
+    first = here[1] < 2
+    own[...] = jnp.where(first, early[...], late)
+    near[...] = jnp.where(first, late, early[...])
+
+
+def project(body, here, parts, weight, outs, *early):
     length, depth = parts[0].shape
     return call(
-        project_body,
-        [jax.ShapeDtypeStruct((length, weight.shape[1]), jnp.bfloat16)] * 4,
-        [pltpu.VMEM((4, length, depth), jnp.bfloat16)],
-        in_specs=[SMEM] + [VMEM] * 5,
-        out_specs=[VMEM] * 4,
+        body,
+        [jax.ShapeDtypeStruct((length, weight.shape[1]), jnp.bfloat16)] * outs,
+        [pltpu.VMEM((2, length, depth), jnp.bfloat16)],
+        in_specs=[SMEM] + [VMEM] * (3 + len(early)),
+        out_specs=[VMEM] * outs,
         name="project",
-    )(here, *parts, weight)
+    )(here, *parts, weight, *early)
 
 
 def routing_body(experts, here, c0, c1, c2, c3, pick, spread):
@@ -492,44 +499,38 @@
 
 def gate_up_body(ds, order, *refs):
     tokens = refs[: len(ds)]
-    gain, pick, weight, kept, given, rows = refs[len(ds) :]
+    gain, pick, weight, out, rows = refs[len(ds) :]
     hid = weight.shape[3]
     capacity = pick.shape[2]
-    i = pl.program_id(0)
-    expert = order[i]
+    expert = order[pl.program_id(0)]
     for k, d in enumerate(ds):
         chosen = dot(pick[d, expert], tokens[k][...]) * gain[...]
         rows[k * capacity : (k + 1) * capacity, :] = chosen.astype(jnp.bfloat16)
     for g in range(2):
-        term = dot(rows[...], weight[0, g]).astype(jnp.bfloat16)
-        for j in range(4):
-            out = (kept, given)[j // 2]
-
-            @pl.when(i == j)
-            def _():
-                out[j % 2, :, g * hid : (g + 1) * hid] = term
+        out[0, :, g * hid : (g + 1) * hid] = dot(rows[...], weight[0, g]).astype(jnp.bfloat16)
 
 
 def gate_up(ds, order, tokens, gain, pick, weight):
-    local, _, width, hid = weight.shape
+    _, _, width, hid = weight.shape
+    count = order.shape[0]
     capacity = pick.shape[2]
-    shape = jax.ShapeDtypeStruct((2, len(ds) * capacity, 2 * hid), jnp.bfloat16)
+    rows = len(ds) * capacity
     whole = lambda rank: lambda i, order: (0,) * rank
     return call(
         functools.partial(gate_up_body, ds),
-        [shape] * 2,
+        jax.ShapeDtypeStruct((count, rows, 2 * hid), jnp.bfloat16),
         None,
         grid_spec=pltpu.PrefetchScalarGridSpec(
             num_scalar_prefetch=1,
-            grid=(local,),
+            grid=(count,),
             in_specs=[pl.BlockSpec(tokens[0].shape, whole(2))] * len(ds)
             + [
                 pl.BlockSpec(gain.shape, whole(2)),
                 pl.BlockSpec(pick.shape, whole(4)),
                 pl.BlockSpec((1, 2, width, hid), lambda i, order: (order[i], 0, 0, 0)),
             ],
-            out_specs=[pl.BlockSpec(shape.shape, whole(3))] * 2,
-            scratch_shapes=[pltpu.VMEM((len(ds) * capacity, width), jnp.bfloat16)],
+            out_specs=pl.BlockSpec((1, rows, 2 * hid), lambda i, order: (i, 0, 0)),
+            scratch_shapes=[pltpu.VMEM((rows, width), jnp.bfloat16)],
         ),
         name="gate_up",
     )(order, *tokens, gain, pick, weight)
@@ -685,9 +686,15 @@
     farther = lax.ppermute(far, "tp", pairs(n, 1))
     gain = norm_gain.astype(jnp.float32)[None, :]
     router = jnp.pad(router_weight, ((0, 0), (0, 128 - experts)))
-    parts = project(here, (attended, far, near, farther), out_proj)
-    kept, w_gate_up = lax.optimization_barrier((parts[0], w_gate_up))
-    sent = scatter_blocks([kept] + list(parts[1:]), n)
+    close, early = project(project_early_body, here, (attended, near), out_proj, 2)
+    given = lax.ppermute(early, "ep", pairs(n, 1))
+    kept, near, late = project(project_late_body, here, (far, farther), out_proj, 3, close)
+    kept, w_gate_up = lax.optimization_barrier((kept, w_gate_up))
+    late = (late.astype(jnp.float32) + given.astype(jnp.float32)).astype(jnp.bfloat16)
+    moves = [
+        (e * n + t, (e ^ (3 if t < 2 else 2)) * n + t) for e in range(n) for t in range(n)
+    ]
+    sent = [kept, lax.ppermute(late, ("ep", "tp"), moves), lax.ppermute(near, "ep", pairs(n, 1))]
     pick, spread = routing(here, pieces, experts, local, capacity)
     weight = jnp.transpose(w_gate_up, (0, 2, 1, 3))
     sent[0], pick, router, gain = lax.optimization_barrier((sent[0], pick, router, gain))
@@ -700,8 +707,9 @@
 
     features = width_here * n
 
-    def spread_act(act):
+    def spread_act(act, before=()):
         far = lax.ppermute(act, "tp", pairs(n, 2))
+        far, *before = lax.optimization_barrier((far, *before))
         near = lax.ppermute(act, "tp", pairs(n, 1))
         return [act, far, near, lax.ppermute(far, "tp", pairs(n, 1))]
 
@@ -709,7 +717,9 @@
         return (kept[1].astype(jnp.float32) + taken[1].astype(jnp.float32)).astype(jnp.bfloat16)
 
     def terms_of(ds, order):
-        return gate_up(ds, order, [tokens[d] for d in ds], gain, pick, weight)
+        blocks = [tokens[d] for d in ds]
+        given = gate_up(ds, order[2:], blocks, gain, pick, weight)
+        return (gate_up(ds, order[:2], blocks, gain, pick, weight), given)
 
     def stats_of(ds):
         return squares_and_logits([tokens[d] for d in ds], gain, router, experts)
@@ -746,8 +756,9 @@
     near = lax.ppermute(near, "ep", pairs(n, 1))
     sums = [(kept_2, taken_2, across)]
     stats_2 = stats_2 + stats_near
-    acts = spread_act(activate((two_chunk,), features, here, sums, pick, stats_2, pieces))
-    acts[3], far[1] = lax.optimization_barrier((acts[3], far[1]))
+    acts = spread_act(
+        activate((two_chunk,), features, here, sums, pick, stats_2, pieces), far[1:]
+    )
     mine, last = down(two_chunk, order, acts, spread, w_down)
     last = lax.ppermute(last, "ep", pairs(n, 3))
     returned = [mine, near, jnp.concatenate(far, axis=0), last]

time: 161 us -> 154 us (0.957)
  waiting for transfers between devices: 72.8 us -> 61.9 us
  local copies, waits for them, and re-layouts: 13.4 us -> 16.9 us
    ppermute x1, waiting for transfers between devices: 7.05 us -> 0.13 us  [per_device_square(): stats_far = lax.ppermute(stats_2, 'tp', pairs(n, 2))]
    unnamed x31 -> x29, local copies, waits for them, and re-layouts: 2.08 us -> 5.45 us
    ppermute x1, starting transfers between devices: 2.94 us -> 0.01 us  [per_device_square(): near = lax.ppermute(near, 'ep', pairs(n, 1))]
    ppermute x1, waiting for transfers between devices: 2.01 us -> 0.01 us  [per_device_square(): stats_far = lax.ppermute(stats, 'tp', pairs(n, 2))]
    ppermute x2, waiting for transfers between devices: 6.51 us -> 4.56 us  [spread_act(): far = lax.ppermute(act, 'tp', pairs(n, 2))]
    ppermute x1, starting transfers between devices: 0.53 us -> 2.37 us  [per_device_square(): tokens[3] = lax.ppermute(tokens[2], 'ep', pairs(n, 1))]
    pallas_call x3 -> x6, Pallas kernels: 11.9 us -> 11.9 us  [the longest x4 9.27 us: gate_up(): call(functools.partial(gate_up_body, ds), jax.ShapeDtypeStruct((count, ro...]
  transfers between devices with their start and end apart: 32 -> 32, of which waited for: 16 -> 16; matrix products, arithmetic and copies ran while one was open for 10% -> 10% of each run, Pallas kernels for 10% -> 13%
where the time goes in v10:
time: 154 us; the launch traced here: 152 us
  waiting for transfers between devices  61.9 us (40%)
  starting transfers between devices  41.7 us (27%)
  Pallas kernels  26.6 us (17%)
  local copies, waits for them, and re-layouts  16.9 us (11%)
  other arithmetic  4.77 us (3%)
    ppermute x2, waiting for transfers between devices, per_device_square(): far = [lax.ppermute(part, 'ep', pairs(n, 2)) for part in far]  13.9 us
    ppermute x3, starting transfers between devices, per_device_square(): lax.ppermute(pieces[d], 'ep', pairs(n, d))  13.2 us
    optimization_barrier x1, local copies, waits for them, and re-layouts, per_device_square(): kept, w_gate_up = lax.optimization_barrier((kept, w_gate_up))  11.2 us
    ppermute x2, waiting for transfers between devices, per_device_square(): tokens[d] = lax.ppermute(residual, 'ep', pairs(n, d))  9.79 us
    pallas_call x4, Pallas kernels, gate_up(): call(functools.partial(gate_up_body, ds), jax.ShapeDtypeStruct((count, ro...  9.27 us
    ppermute x1, waiting for transfers between devices, per_device_square(): last = lax.ppermute(last, 'ep', pairs(n, 3))  8.56 us
    ppermute x1, waiting for transfers between devices, per_device_square(): given = lax.ppermute(early, 'ep', pairs(n, 1))  5.66 us
    pallas_call x2, Pallas kernels, down(): call(functools.partial(down_body, ds), shapes, None, grid_spec=pltpu.Pref...  5.59 us
  transfers between devices with their start and end apart: 32, of which 16 were waited for; matrix products, arithmetic and copies ran while one was open for 10% of the time, Pallas kernels for 13%

profile of v10, /device:TPU:0, one launch (start us, length us, event | category | flops | bytes accessed | tf_op | source)
XLA Modules:
  0.0 152.3 jit_solution(6291418943404040323)
XLA Ops:
  6.0 10.8 %collective-permute-start.2 = (bf16[272,128]{1,0:T(8,128)(2,1)S(1)}, bf16[272,128]{1,0:T(8,128)(2,1)S(1)}, u32[]{:S(2)}, u32[]{:S(2)}) collective-permute-start(bf16[272,128]{1,0:T(8,128)(2,1)S(1)} %get-tuple-element.58), channel_id=1, source_target_pairs={{0,4},{4,0},{8,12},{12,8},{1,5},{5,1},{9,13},{13,9},{2,6},{6,2},{1... | collective-permute-start | bytes 208904 | tf_op jit(solution)/shard_map/ppermute | solution.py:678
  16.8 2.4 %collective-permute-start.4 = (bf16[272,128]{1,0:T(8,128)(2,1)S(1)}, bf16[272,128]{1,0:T(8,128)(2,1)S(1)}, u32[]{:S(2)}, u32[]{:S(2)}) collective-permute-start(bf16[272,128]{1,0:T(8,128)(2,1)S(1)} %get-tuple-element.60), channel_id=1, source_target_pairs={{0,12},{4,8},{8,4},{12,0},{1,13},{5,9},{9,5},{13,1},{2,14},{6,10},... | collective-permute-start | bytes 208904 | tf_op jit(solution)/shard_map/ppermute | solution.py:678
  19.2 1.7 %broadcast_multiply_fusion.weight = bf16[1024,1024]{1,0:T(8,128)(2,1)S(1)} fusion(bf16[1024,1024]{1,0:T(8,128)(2,1)} %param.21, bf16[]{:T(256)} %constant.23.clone.1), kind=kLoop, calls=%fused_computation.3 | loop fusion | flops 1048576 | bytes 4194306 | tf_op jit(solution)/shard_map/mul | solution.py:682
  21.9 3.4 %collective-permute-done.3.c2.refs_4_ = bf16[272,128]{1,0:T(8,128)(2,1)S(1)} collective-permute-done((bf16[272,128]{1,0:T(8,128)(2,1)S(1)}, bf16[272,128]{1,0:T(8,128)(2,1)S(1)}, u32[]{:S(2)}, u32[]{:S(2)}) %collective-permute-start.3) | collective-permute-done | bytes 69664 | tf_op jit(solution)/shard_map/ppermute | solution.py:678
  25.3 3.4 %attention.1.a = bf16[128,1024]{1,0:T(8,128)(2,1)S(1)} custom-call(s32[2]{0:T(128)S(1)} %pad_add_fusion.here, s32[4,4]{1,0:T(4,128)S(1)} %copy-done.5, s32[8]{0:T(128)S(1)} %copy-done.7, bf16[1280,128]{1,0:T(8,128)(2,1)S(1)} %collective-permute-done.1.q, bf16[272,128]{1,0:T(8,128)(2,1)S(1)} %get-tuple-element.57.c0.refs_3_, ...), custom_call_target="tpu_custom_call" | custom-call | flops 1048576 | bytes 262144 | tf_op jit(solution)/shard_map/attention/pallas_call | solution.py:364
  28.7 5.2 %collective-permute-start.5 = (bf16[128,1024]{1,0:T(8,128)(2,1)S(1)}, bf16[128,1024]{1,0:T(8,128)(2,1)S(1)}, u32[]{:S(2)}, u32[]{:S(2)}) collective-permute-start(bf16[128,1024]{1,0:T(8,128)(2,1)S(1)} %attention.1.a), channel_id=1, source_target_pairs={{0,2},{1,3},{2,0},{3,1},{4,6},{5,7},{6,4},{7,5},{8,10},{9,11},{10,... | collective-permute-start | bytes 786440 | tf_op jit(solution)/shard_map/ppermute | solution.py:684
  33.9 4.3 %collective-permute-done.5.a = bf16[128,1024]{1,0:T(8,128)(2,1)S(1)} collective-permute-done((bf16[128,1024]{1,0:T(8,128)(2,1)S(1)}, bf16[128,1024]{1,0:T(8,128)(2,1)S(1)}, u32[]{:S(2)}, u32[]{:S(2)}) %collective-permute-start.5) | collective-permute-done | bytes 262176 | tf_op jit(solution)/shard_map/ppermute | solution.py:684
  39.6 1.8 %collective-permute-start.8 = (bf16[128,1024]{1,0:T(8,128)(2,1)S(1)}, bf16[128,1024]{1,0:T(8,128)(2,1)S(1)}, u32[]{:S(2)}, u32[]{:S(2)}) collective-permute-start(bf16[128,1024]{1,0:T(8,128)(2,1)S(1)} %get-tuple-element.73), channel_id=1, source_target_pairs={{0,4},{4,0},{8,12},{12,8},{1,5},{5,1},{9,13},{13,9},{2,6},{6,2},{1... | collective-permute-start | bytes 786440 | tf_op jit(solution)/shard_map/ppermute | solution.py:690
  42.7 5.7 %collective-permute-done.8 = bf16[128,1024]{1,0:T(8,128)(2,1)S(1)} collective-permute-done((bf16[128,1024]{1,0:T(8,128)(2,1)S(1)}, bf16[128,1024]{1,0:T(8,128)(2,1)S(1)}, u32[]{:S(2)}, u32[]{:S(2)}) %collective-permute-start.8) | collective-permute-done | bytes 262176 | tf_op jit(solution)/shard_map/ppermute | solution.py:690
  51.4 11.2 %copy.25 = bf16[4,1024,2,1024]{3,1,2,0:T(8,128)(2,1)S(1)} copy(bf16[4,1024,2,1024]{3,2,1,0:T(2,128)(2,1)} %param.24) | data formatting | bytes 33554432 | tf_op jit(solution)/shard_map/optimization_barrier | solution.py:692
  64.3 2.0 %collective-permute-start.12 = (bf16[128,1024]{1,0:T(8,128)(2,1)S(1)}, bf16[128,1024]{1,0:T(8,128)(2,1)S(1)}, u32[]{:S(2)}, u32[]{:S(2)}) collective-permute-start(bf16[128,1024]{1,0:T(8,128)(2,1)S(1)} %residual.1.refs_0_), channel_id=1, source_target_pairs={{0,8},{4,12},{8,0},{12,4},{1,9},{5,13},{9,1},{13,5},{2,10},{6,14},... | collective-permute-start | bytes 786440 | tf_op jit(solution)/shard_map/ppermute | solution.py:705
  66.4 9.8 %collective-permute-done.11.refs_0_ = bf16[128,1024]{1,0:T(8,128)(2,1)S(1)} collective-permute-done((bf16[128,1024]{1,0:T(8,128)(2,1)S(1)}, bf16[128,1024]{1,0:T(8,128)(2,1)S(1)}, u32[]{:S(2)}, u32[]{:S(2)}) %collective-permute-start.11) | collective-permute-done | bytes 262176 | tf_op jit(solution)/shard_map/ppermute | solution.py:705
  76.2 2.3 %gate_up.5 = bf16[2,128,2048]{2,1,0:T(8,128)(2,1)S(1)} custom-call(s32[2]{0:T(128)S(1)} %get-tuple-element.101.order, bf16[128,1024]{1,0:T(8,128)(2,1)S(1)} %collective-permute-done.11.refs_0_, bf16[128,1024]{1,0:T(8,128)(2,1)S(1)} %collective-permute-done.12.refs_1_, f32[1,1024]{1,0:T(1,128)S(1)} %bitcast.30, ...), custom_call_target="tpu_custom_call" | custom-call | flops 1048576 | bytes 262144 | tf_op jit(solution)/shard_map/gate_up/pallas_call | solution.py:519
  79.3 2.0 %collective-permute-start.14 = (f32[24,256]{1,0:T(8,128)S(1)}, f32[24,256]{1,0:T(8,128)S(1)}, u32[]{:S(2)}, u32[]{:S(2)}) collective-permute-start(f32[24,256]{1,0:T(8,128)S(1)} %stats.2), channel_id=1, source_target_pairs={{0,2},{1,3},{2,0},{3,1},{4,6},{5,7},{6,4},{7,5},{8,10},{9,11},{10,... | collective-permute-start | bytes 73736 | tf_op jit(solution)/shard_map/ppermute | solution.py:731
  81.3 2.3 %gate_up.4.refs_0_ = bf16[2,128,2048]{2,1,0:T(8,128)(2,1)S(1)} custom-call(s32[2]{0:T(128)S(1)} %get-tuple-element.102.order, bf16[128,1024]{1,0:T(8,128)(2,1)S(1)} %collective-permute-done.11.refs_0_, bf16[128,1024]{1,0:T(8,128)(2,1)S(1)} %collective-permute-done.12.refs_1_, f32[1,1024]{1,0:T(1,128)S(1)} %bitcast.32, ...), custom_call_target="tpu_custom_call" | custom-call | flops 1048576 | bytes 262144 | tf_op jit(solution)/shard_map/gate_up/pallas_call | solution.py:519
  83.7 1.6 %collective-permute-start.17 = (bf16[128,2048]{1,0:T(8,128)(2,1)S(1)}, bf16[128,2048]{1,0:T(8,128)(2,1)S(1)}, u32[]{:S(2)}, u32[]{:S(2)}) collective-permute-start(bf16[128,2048]{1,0:T(8,128)(2,1)S(1)} %fusion), channel_id=1, source_target_pairs={{0,2},{1,3},{2,0},{3,1},{4,6},{5,7},{6,4},{7,5},{8,10},{9,11},{10,... | collective-permute-start | bytes 1572872 | tf_op jit(solution)/shard_map/ppermute | solution.py:736
  85.3 2.4 %collective-permute-start.16 = (bf16[128,1024]{1,0:T(8,128)(2,1)S(1)}, bf16[128,1024]{1,0:T(8,128)(2,1)S(1)}, u32[]{:S(2)}, u32[]{:S(2)}) collective-permute-start(bf16[128,1024]{1,0:T(8,128)(2,1)S(1)} %collective-permute-done.12.refs_1_), channel_id=1, source_target_pairs={{0,4},{4,0},{8,12},{12,8},{1,5},{5,1},{9,13},{13,9},{2,6},{6,2},{1... | collective-permute-start | bytes 786440 | tf_op jit(solution)/shard_map/ppermute | solution.py:706
  87.7 5.5 %collective-permute-done.16.refs_1_ = bf16[128,1024]{1,0:T(8,128)(2,1)S(1)} collective-permute-done((bf16[128,1024]{1,0:T(8,128)(2,1)S(1)}, bf16[128,1024]{1,0:T(8,128)(2,1)S(1)}, u32[]{:S(2)}, u32[]{:S(2)}) %collective-permute-start.16) | collective-permute-done | bytes 262176 | tf_op jit(solution)/shard_map/ppermute | solution.py:706
  94.0 2.3 %gate_up.6 = bf16[2,128,2048]{2,1,0:T(8,128)(2,1)S(1)} custom-call(s32[2]{0:T(128)S(1)} %get-tuple-element.100.order, bf16[128,1024]{1,0:T(8,128)(2,1)S(1)} %residual.1.refs_0_, bf16[128,1024]{1,0:T(8,128)(2,1)S(1)} %collective-permute-done.16.refs_1_, f32[1,1024]{1,0:T(1,128)S(1)} %bitcast.34, bf16[4,4,64,128]{3,2,1,0:T(8,128)(2,1)S(1)} %get-tuple-element.77.refs_3_.pick, ...), custom_call_target="tpu_custom_call" | custom-call | flops 1048576 | bytes 262144 | tf_op jit(solution)/shard_map/gate_up/pallas_call | solution.py:519
  96.4 1.5 collective-permute-done.17.refs_2_
  99.5 2.3 %gate_up.7.refs_0_ = bf16[2,128,2048]{2,1,0:T(8,128)(2,1)S(1)} custom-call(s32[2]{0:T(128)S(1)} %get-tuple-element.99.order, bf16[128,1024]{1,0:T(8,128)(2,1)S(1)} %residual.1.refs_0_, bf16[128,1024]{1,0:T(8,128)(2,1)S(1)} %collective-permute-done.16.refs_1_, f32[1,1024]{1,0:T(1,128)S(1)} %bitcast.35, ...), custom_call_target="tpu_custom_call" | custom-call | flops 1048576 | bytes 262144 | tf_op jit(solution)/shard_map/gate_up/pallas_call | solution.py:519
  103.3 4.6 %collective-permute-done.20.b = bf16[128,1024]{1,0:T(8,128)(2,1)S(1)} collective-permute-done((bf16[128,1024]{1,0:T(8,128)(2,1)S(1)}, bf16[128,1024]{1,0:T(8,128)(2,1)S(1)}, u32[]{:S(2)}, u32[]{:S(2)}) %collective-permute-start.20) | collective-permute-done | bytes 262176 | tf_op jit(solution)/shard_map/ppermute | solution.py:711
  110.7 2.8 %down.2 = (bf16[128,1024]{1,0:T(8,128)(2,1)S(1)}, bf16[64,1024]{1,0:T(8,128)(2,1)S(1)}, bf16[64,1024]{1,0:T(8,128)(2,1)S(1)}) custom-call(s32[4]{0:T(128)S(1)} %broadcast_xor_fusion.order, bf16[128,1024]{1,0:T(8,128)(2,1)S(1)} %activate.2.a, bf16[128,1024]{1,0:T(8,128)(2,1)S(1)} %collective-permute-done.20.b, ...), custom_call_target="tpu_custom_call" | custom-call | flops 1048576 | bytes 262144 | tf_op jit(solution)/shard_map/down/pallas_call | solution.py:626
  113.5 2.2 %collective-permute-start.25 = (bf16[64,1024]{1,0:T(8,128)(2,1)S(1)}, bf16[64,1024]{1,0:T(8,128)(2,1)S(1)}, u32[]{:S(2)}, u32[]{:S(2)}) collective-permute-start(bf16[64,1024]{1,0:T(8,128)(2,1)S(1)} %get-tuple-element.91), channel_id=1, source_target_pairs={{0,8},{4,12},{8,0},{12,4},{1,9},{5,13},{9,1},{13,5},{2,10},{6,14},... | collective-permute-start | bytes 393224 | tf_op jit(solution)/shard_map/ppermute | solution.py:754
  116.8 6.0 %collective-permute-done.25 = bf16[64,1024]{1,0:T(8,128)(2,1)S(1)} collective-permute-done((bf16[64,1024]{1,0:T(8,128)(2,1)S(1)}, bf16[64,1024]{1,0:T(8,128)(2,1)S(1)}, u32[]{:S(2)}, u32[]{:S(2)}) %collective-permute-start.25) | collective-permute-done | bytes 131104 | tf_op jit(solution)/shard_map/ppermute | solution.py:754
  123.7 1.5 collective-permute-start.26
  125.4 7.9 %collective-permute-done.27 = bf16[64,1024]{1,0:T(8,128)(2,1)S(1)} collective-permute-done((bf16[64,1024]{1,0:T(8,128)(2,1)S(1)}, bf16[64,1024]{1,0:T(8,128)(2,1)S(1)}, u32[]{:S(2)}, u32[]{:S(2)}) %collective-permute-start.27) | collective-permute-done | bytes 131104 | tf_op jit(solution)/shard_map/ppermute | solution.py:754
  133.4 1.5 collective-permute-done.29.d
  134.9 3.4 %copy-done.2 = bf16[4,1024,1024]{2,1,0:T(8,128)(2,1)S(1)} copy-done((bf16[4,1024,1024]{2,1,0:T(8,128)(2,1)S(1)}, bf16[4,1024,1024]{2,1,0:T(8,128)(2,1)}, u32[]{:S(2)}) %copy-start.2) | copy-done | bytes 8388632
  138.3 2.8 %down.3 = (bf16[128,1024]{1,0:T(8,128)(2,1)S(1)}, bf16[128,1024]{1,0:T(8,128)(2,1)S(1)}) custom-call(s32[4]{0:T(128)S(1)} %broadcast_xor_fusion.order, bf16[128,1024]{1,0:T(8,128)(2,1)S(1)} %activate.3.a, bf16[128,1024]{1,0:T(8,128)(2,1)S(1)} %collective-permute-done.26.b, bf16[128,1024]{1,0:T(8,128)(2,1)S(1)} %collective-permute-done.28.c, ...), custom_call_target="tpu_custom_call" | custom-call | flops 1048576 | bytes 262144 | tf_op jit(solution)/shard_map/down/pallas_call | solution.py:626
  141.1 1.8 %collective-permute-start.31 = (bf16[128,1024]{1,0:T(8,128)(2,1)S(1)}, bf16[128,1024]{1,0:T(8,128)(2,1)S(1)}, u32[]{:S(2)}, u32[]{:S(2)}) collective-permute-start(bf16[128,1024]{1,0:T(8,128)(2,1)S(1)} %get-tuple-element.98), channel_id=1, source_target_pairs={{0,12},{4,8},{8,4},{12,0},{1,13},{5,9},{9,5},{13,1},{2,14},{6,10},... | collective-permute-start | bytes 786440 | tf_op jit(solution)/shard_map/ppermute | solution.py:763
  142.8 8.6 %collective-permute-done.31 = bf16[128,1024]{1,0:T(8,128)(2,1)S(1)} collective-permute-done((bf16[128,1024]{1,0:T(8,128)(2,1)S(1)}, bf16[128,1024]{1,0:T(8,128)(2,1)S(1)}, u32[]{:S(2)}, u32[]{:S(2)}) %collective-permute-start.31) | collective-permute-done | bytes 262176 | tf_op jit(solution)/shard_map/ppermute | solution.py:763
  (100 shorter events, 25.1 us)
Async XLA Ops:
  0.0 4.2 %collective-permute-start = (bf16[1024,128]{1,0:T(8,128)(2,1)}, bf16[1024,128]{1,0:T(8,128)(2,1)S(1)}, u32[]{:S(2)}, u32[]{:S(2)}) collective-permute-start(bf16[1024,128]{1,0:T(8,128)(2,1)} %bitcast.37), channel_id=1, source_target_pairs={{1,2},{2,1},{4,7},{7,4},{9,10},{10,9},{12,15},{15,12},{17,18},{18,... | collective-permute-start | bytes 786440 | tf_op jit(solution)/shard_map/ppermute | solution.py:202
  5.2 20.1 %collective-permute-start.1 = (bf16[1280,128]{1,0:T(8,128)(2,1)S(1)}, bf16[1280,128]{1,0:T(8,128)(2,1)S(1)}, u32[]{:S(2)}, u32[]{:S(2)}) collective-permute-start(bf16[1280,128]{1,0:T(8,128)(2,1)S(1)} %pad_maximum_fusion), channel_id=1, source_target_pairs={{0,0},{1,8},{2,6},{3,14},{4,12},{5,4},{6,10},{7,2},{8,1},{9,9},{10... | collective-permute-start | bytes 983048 | tf_op jit(solution)/shard_map/ppermute | solution.py:212
  6.0 15.9 %collective-permute-start.2 = (bf16[272,128]{1,0:T(8,128)(2,1)S(1)}, bf16[272,128]{1,0:T(8,128)(2,1)S(1)}, u32[]{:S(2)}, u32[]{:S(2)}) collective-permute-start(bf16[272,128]{1,0:T(8,128)(2,1)S(1)} %get-tuple-element.58), channel_id=1, source_target_pairs={{0,4},{4,0},{8,12},{12,8},{1,5},{5,1},{9,13},{13,9},{2,6},{6,2},{1... | collective-permute-start | bytes 208904 | tf_op jit(solution)/shard_map/ppermute | solution.py:678
  16.8 8.5 %collective-permute-start.3 = (bf16[272,128]{1,0:T(8,128)(2,1)S(1)}, bf16[272,128]{1,0:T(8,128)(2,1)S(1)}, u32[]{:S(2)}, u32[]{:S(2)}) collective-permute-start(bf16[272,128]{1,0:T(8,128)(2,1)S(1)} %get-tuple-element.59), channel_id=1, source_target_pairs={{0,8},{4,12},{8,0},{12,4},{1,9},{5,13},{9,1},{13,5},{2,10},{6,14},... | collective-permute-start | bytes 208904 | tf_op jit(solution)/shard_map/ppermute | solution.py:678
  16.8 8.5 %collective-permute-start.4 = (bf16[272,128]{1,0:T(8,128)(2,1)S(1)}, bf16[272,128]{1,0:T(8,128)(2,1)S(1)}, u32[]{:S(2)}, u32[]{:S(2)}) collective-permute-start(bf16[272,128]{1,0:T(8,128)(2,1)S(1)} %get-tuple-element.60), channel_id=1, source_target_pairs={{0,12},{4,8},{8,4},{12,0},{1,13},{5,9},{9,5},{13,1},{2,14},{6,10},... | collective-permute-start | bytes 208904 | tf_op jit(solution)/shard_map/ppermute | solution.py:678
  28.7 9.5 %collective-permute-start.5 = (bf16[128,1024]{1,0:T(8,128)(2,1)S(1)}, bf16[128,1024]{1,0:T(8,128)(2,1)S(1)}, u32[]{:S(2)}, u32[]{:S(2)}) collective-permute-start(bf16[128,1024]{1,0:T(8,128)(2,1)S(1)} %attention.1.a), channel_id=1, source_target_pairs={{0,2},{1,3},{2,0},{3,1},{4,6},{5,7},{6,4},{7,5},{8,10},{9,11},{10,... | collective-permute-start | bytes 786440 | tf_op jit(solution)/shard_map/ppermute | solution.py:684
  33.9 4.4 %collective-permute-start.7 = (bf16[128,1024]{1,0:T(8,128)(2,1)S(1)}, bf16[128,1024]{1,0:T(8,128)(2,1)S(1)}, u32[]{:S(2)}, u32[]{:S(2)}) collective-permute-start(bf16[128,1024]{1,0:T(8,128)(2,1)S(1)} %attention.1.a), channel_id=1, source_target_pairs={{0,1},{1,0},{2,3},{3,2},{4,5},{5,4},{6,7},{7,6},{8,9},{9,8},{10,11... | collective-permute-start | bytes 786440 | tf_op jit(solution)/shard_map/ppermute | solution.py:685
  38.3 3.1 %collective-permute-start.6 = (bf16[128,1024]{1,0:T(8,128)(2,1)S(1)}, bf16[128,1024]{1,0:T(8,128)(2,1)S(1)}, u32[]{:S(2)}, u32[]{:S(2)}) collective-permute-start(bf16[128,1024]{1,0:T(8,128)(2,1)S(1)} %collective-permute-done.5.a), channel_id=1, source_target_pairs={{0,1},{1,0},{2,3},{3,2},{4,5},{5,4},{6,7},{7,6},{8,9},{9,8},{10,11... | collective-permute-start | bytes 786440 | tf_op jit(solution)/shard_map/ppermute | solution.py:686
  39.6 8.8 %collective-permute-start.8 = (bf16[128,1024]{1,0:T(8,128)(2,1)S(1)}, bf16[128,1024]{1,0:T(8,128)(2,1)S(1)}, u32[]{:S(2)}, u32[]{:S(2)}) collective-permute-start(bf16[128,1024]{1,0:T(8,128)(2,1)S(1)} %get-tuple-element.73), channel_id=1, source_target_pairs={{0,4},{4,0},{8,12},{12,8},{1,5},{5,1},{9,13},{13,9},{2,6},{6,2},{1... | collective-permute-start | bytes 786440 | tf_op jit(solution)/shard_map/ppermute | solution.py:690
  48.4 14.2 %collective-permute-start.9 = (bf16[128,1024]{1,0:T(8,128)(2,1)S(1)}, bf16[128,1024]{1,0:T(8,128)(2,1)S(1)}, u32[]{:S(2)}, u32[]{:S(2)}) collective-permute-start(bf16[128,1024]{1,0:T(8,128)(2,1)S(1)} %add_convert_fusion.3), channel_id=1, source_target_pairs={{0,12},{1,13},{2,10},{3,11},{4,8},{5,9},{6,14},{7,15},{8,4},{9,5},... | collective-permute-start | bytes 786440 | tf_op jit(solution)/shard_map/ppermute | solution.py:697
  49.7 13.3 %collective-permute-start.10 = (bf16[128,1024]{1,0:T(8,128)(2,1)S(1)}, bf16[128,1024]{1,0:T(8,128)(2,1)S(1)}, u32[]{:S(2)}, u32[]{:S(2)}) collective-permute-start(bf16[128,1024]{1,0:T(8,128)(2,1)S(1)} %get-tuple-element.74), channel_id=1, source_target_pairs={{0,4},{4,0},{8,12},{12,8},{1,5},{5,1},{9,13},{13,9},{2,6},{6,2},{1... | collective-permute-start | bytes 786440 | tf_op jit(solution)/shard_map/ppermute | solution.py:697
  63.1 13.0 %collective-permute-start.11 = (bf16[128,1024]{1,0:T(8,128)(2,1)S(1)}, bf16[128,1024]{1,0:T(8,128)(2,1)S(1)}, u32[]{:S(2)}, u32[]{:S(2)}) collective-permute-start(bf16[128,1024]{1,0:T(8,128)(2,1)S(1)} %residual.1.refs_0_), channel_id=1, source_target_pairs={{0,4},{4,0},{8,12},{12,8},{1,5},{5,1},{9,13},{13,9},{2,6},{6,2},{1... | collective-permute-start | bytes 786440 | tf_op jit(solution)/shard_map/ppermute | solution.py:705
  64.3 11.8 %collective-permute-start.12 = (bf16[128,1024]{1,0:T(8,128)(2,1)S(1)}, bf16[128,1024]{1,0:T(8,128)(2,1)S(1)}, u32[]{:S(2)}, u32[]{:S(2)}) collective-permute-start(bf16[128,1024]{1,0:T(8,128)(2,1)S(1)} %residual.1.refs_0_), channel_id=1, source_target_pairs={{0,8},{4,12},{8,0},{12,4},{1,9},{5,13},{9,1},{13,5},{2,10},{6,14},... | collective-permute-start | bytes 786440 | tf_op jit(solution)/shard_map/ppermute | solution.py:705
  78.5 5.1 %collective-permute-start.13 = (bf16[2,128,2048]{2,1,0:T(8,128)(2,1)S(1)}, bf16[2,128,2048]{2,1,0:T(8,128)(2,1)S(1)}, u32[]{:S(2)}, u32[]{:S(2)}) collective-permute-start(bf16[2,128,2048]{2,1,0:T(8,128)(2,1)S(1)} %gate_up.5), channel_id=1, source_target_pairs={{0,1},{1,0},{2,3},{3,2},{4,5},{5,4},{6,7},{7,6},{8,9},{9,8},{10,11... | collective-permute-start | bytes 3145736 | tf_op jit(solution)/shard_map/ppermute | solution.py:729
  79.3 4.3 %collective-permute-start.14 = (f32[24,256]{1,0:T(8,128)S(1)}, f32[24,256]{1,0:T(8,128)S(1)}, u32[]{:S(2)}, u32[]{:S(2)}) collective-permute-start(f32[24,256]{1,0:T(8,128)S(1)} %stats.2), channel_id=1, source_target_pairs={{0,2},{1,3},{2,0},{3,1},{4,6},{5,7},{6,4},{7,5},{8,10},{9,11},{10,... | collective-permute-start | bytes 73736 | tf_op jit(solution)/shard_map/ppermute | solution.py:731
  83.7 14.1 %collective-permute-start.17 = (bf16[128,2048]{1,0:T(8,128)(2,1)S(1)}, bf16[128,2048]{1,0:T(8,128)(2,1)S(1)}, u32[]{:S(2)}, u32[]{:S(2)}) collective-permute-start(bf16[128,2048]{1,0:T(8,128)(2,1)S(1)} %fusion), channel_id=1, source_target_pairs={{0,2},{1,3},{2,0},{3,1},{4,6},{5,7},{6,4},{7,5},{8,10},{9,11},{10,... | collective-permute-start | bytes 1572872 | tf_op jit(solution)/shard_map/ppermute | solution.py:736
  85.3 7.9 %collective-permute-start.16 = (bf16[128,1024]{1,0:T(8,128)(2,1)S(1)}, bf16[128,1024]{1,0:T(8,128)(2,1)S(1)}, u32[]{:S(2)}, u32[]{:S(2)}) collective-permute-start(bf16[128,1024]{1,0:T(8,128)(2,1)S(1)} %collective-permute-done.12.refs_1_), channel_id=1, source_target_pairs={{0,4},{4,0},{8,12},{12,8},{1,5},{5,1},{9,13},{13,9},{2,6},{6,2},{1... | collective-permute-start | bytes 786440 | tf_op jit(solution)/shard_map/ppermute | solution.py:706
  87.7 6.3 %collective-permute-start.15 = (f32[24,256]{1,0:T(8,128)S(1)}, f32[24,256]{1,0:T(8,128)S(1)}, u32[]{:S(2)}, u32[]{:S(2)}) collective-permute-start(f32[24,256]{1,0:T(8,128)S(1)} %add.46), channel_id=1, source_target_pairs={{0,1},{1,0},{2,3},{3,2},{4,5},{5,4},{6,7},{7,6},{8,9},{9,8},{10,11... | collective-permute-start | bytes 73736 | tf_op jit(solution)/shard_map/ppermute | solution.py:734
  97.9 10.0 %collective-permute-start.18 = (bf16[2,128,2048]{2,1,0:T(8,128)(2,1)S(1)}, bf16[2,128,2048]{2,1,0:T(8,128)(2,1)S(1)}, u32[]{:S(2)}, u32[]{:S(2)}) collective-permute-start(bf16[2,128,2048]{2,1,0:T(8,128)(2,1)S(1)} %gate_up.6), channel_id=1, source_target_pairs={{0,1},{1,0},{2,3},{3,2},{4,5},{5,4},{6,7},{7,6},{8,9},{9,8},{10,11... | collective-permute-start | bytes 3145736 | tf_op jit(solution)/shard_map/ppermute | solution.py:744
  98.8 9.0 %collective-permute-start.20 = (bf16[128,1024]{1,0:T(8,128)(2,1)S(1)}, bf16[128,1024]{1,0:T(8,128)(2,1)S(1)}, u32[]{:S(2)}, u32[]{:S(2)}) collective-permute-start(bf16[128,1024]{1,0:T(8,128)(2,1)S(1)} %activate.2.a), channel_id=1, source_target_pairs={{0,2},{1,3},{2,0},{3,1},{4,6},{5,7},{6,4},{7,5},{8,10},{9,11},{10,... | collective-permute-start | bytes 786440 | tf_op jit(solution)/shard_map/ppermute | solution.py:711
  101.8 6.3 %collective-permute-start.19 = (f32[24,256]{1,0:T(8,128)S(1)}, f32[24,256]{1,0:T(8,128)S(1)}, u32[]{:S(2)}, u32[]{:S(2)}) collective-permute-start(f32[24,256]{1,0:T(8,128)S(1)} %stats.3), channel_id=1, source_target_pairs={{0,2},{1,3},{2,0},{3,1},{4,6},{5,7},{6,4},{7,5},{8,10},{9,11},{10,... | collective-permute-start | bytes 73736 | tf_op jit(solution)/shard_map/ppermute | solution.py:743
  108.1 14.7 %collective-permute-start.22 = (bf16[128,2048]{1,0:T(8,128)(2,1)S(1)}, bf16[128,2048]{1,0:T(8,128)(2,1)S(1)}, u32[]{:S(2)}, u32[]{:S(2)}) collective-permute-start(bf16[128,2048]{1,0:T(8,128)(2,1)S(1)} %fusion.1), channel_id=1, source_target_pairs={{0,2},{1,3},{2,0},{3,1},{4,6},{5,7},{6,4},{7,5},{8,10},{9,11},{10,... | collective-permute-start | bytes 1572872 | tf_op jit(solution)/shard_map/ppermute | solution.py:752
  108.7 1.5 %collective-permute-start.23 = (bf16[128,1024]{1,0:T(8,128)(2,1)S(1)}, bf16[128,1024]{1,0:T(8,128)(2,1)S(1)}, u32[]{:S(2)}, u32[]{:S(2)}) collective-permute-start(bf16[128,1024]{1,0:T(8,128)(2,1)S(1)} %activate.2.a), channel_id=1, source_target_pairs={{0,1},{1,0},{2,3},{3,2},{4,5},{5,4},{6,7},{7,6},{8,9},{9,8},{10,11... | collective-permute-start | bytes 786440 | tf_op jit(solution)/shard_map/ppermute | solution.py:713
  108.7 1.9 %collective-permute-start.24 = (bf16[128,1024]{1,0:T(8,128)(2,1)S(1)}, bf16[128,1024]{1,0:T(8,128)(2,1)S(1)}, u32[]{:S(2)}, u32[]{:S(2)}) collective-permute-start(bf16[128,1024]{1,0:T(8,128)(2,1)S(1)} %collective-permute-done.20.b), channel_id=1, source_target_pairs={{0,1},{1,0},{2,3},{3,2},{4,5},{5,4},{6,7},{7,6},{8,9},{9,8},{10,11... | collective-permute-start | bytes 786440 | tf_op jit(solution)/shard_map/ppermute | solution.py:751
  113.5 9.3 %collective-permute-start.25 = (bf16[64,1024]{1,0:T(8,128)(2,1)S(1)}, bf16[64,1024]{1,0:T(8,128)(2,1)S(1)}, u32[]{:S(2)}, u32[]{:S(2)}) collective-permute-start(bf16[64,1024]{1,0:T(8,128)(2,1)S(1)} %get-tuple-element.91), channel_id=1, source_target_pairs={{0,8},{4,12},{8,0},{12,4},{1,9},{5,13},{9,1},{13,5},{2,10},{6,14},... | collective-permute-start | bytes 393224 | tf_op jit(solution)/shard_map/ppermute | solution.py:754
  115.6 1.2 collective-permute-start.21
  123.7 9.6 %collective-permute-start.26 = (bf16[128,1024]{1,0:T(8,128)(2,1)S(1)}, bf16[128,1024]{1,0:T(8,128)(2,1)S(1)}, u32[]{:S(2)}, u32[]{:S(2)}) collective-permute-start(bf16[128,1024]{1,0:T(8,128)(2,1)S(1)} %activate.3.a), channel_id=1, source_target_pairs={{0,2},{1,3},{2,0},{3,1},{4,6},{5,7},{6,4},{7,5},{8,10},{9,11},{10,... | collective-permute-start | bytes 786440 | tf_op jit(solution)/shard_map/ppermute | solution.py:711
  125.2 8.1 %collective-permute-start.27 = (bf16[64,1024]{1,0:T(8,128)(2,1)S(1)}, bf16[64,1024]{1,0:T(8,128)(2,1)S(1)}, u32[]{:S(2)}, u32[]{:S(2)}) collective-permute-start(bf16[64,1024]{1,0:T(8,128)(2,1)S(1)} %get-tuple-element.93), channel_id=1, source_target_pairs={{0,8},{4,12},{8,0},{12,4},{1,9},{5,13},{9,1},{13,5},{2,10},{6,14},... | collective-permute-start | bytes 393224 | tf_op jit(solution)/shard_map/ppermute | solution.py:754
  125.4 8.0 %collective-permute-start.28 = (bf16[128,1024]{1,0:T(8,128)(2,1)S(1)}, bf16[128,1024]{1,0:T(8,128)(2,1)S(1)}, u32[]{:S(2)}, u32[]{:S(2)}) collective-permute-start(bf16[128,1024]{1,0:T(8,128)(2,1)S(1)} %activate.3.a), channel_id=1, source_target_pairs={{0,1},{1,0},{2,3},{3,2},{4,5},{5,4},{6,7},{7,6},{8,9},{9,8},{10,11... | collective-permute-start | bytes 786440 | tf_op jit(solution)/shard_map/ppermute | solution.py:713
  133.3 1.5 %collective-permute-start.29 = (bf16[128,1024]{1,0:T(8,128)(2,1)S(1)}, bf16[128,1024]{1,0:T(8,128)(2,1)S(1)}, u32[]{:S(2)}, u32[]{:S(2)}) collective-permute-start(bf16[128,1024]{1,0:T(8,128)(2,1)S(1)} %collective-permute-done.26.b), channel_id=1, source_target_pairs={{0,1},{1,0},{2,3},{3,2},{4,5},{5,4},{6,7},{7,6},{8,9},{9,8},{10,11... | collective-permute-start | bytes 786440 | tf_op jit(solution)/shard_map/ppermute | solution.py:714
  133.3 9.5 %collective-permute-start.30 = (bf16[128,1024]{1,0:T(8,128)(2,1)S(1)}, bf16[128,1024]{1,0:T(8,128)(2,1)S(1)}, u32[]{:S(2)}, u32[]{:S(2)}) collective-permute-start(bf16[128,1024]{1,0:T(8,128)(2,1)S(1)} %get-tuple-element.96), channel_id=1, source_target_pairs={{0,4},{4,0},{8,12},{12,8},{1,5},{5,1},{9,13},{13,9},{2,6},{6,2},{1... | collective-permute-start | bytes 786440 | tf_op jit(solution)/shard_map/ppermute | solution.py:756
  141.1 10.3 %collective-permute-start.31 = (bf16[128,1024]{1,0:T(8,128)(2,1)S(1)}, bf16[128,1024]{1,0:T(8,128)(2,1)S(1)}, u32[]{:S(2)}, u32[]{:S(2)}) collective-permute-start(bf16[128,1024]{1,0:T(8,128)(2,1)S(1)} %get-tuple-element.98), channel_id=1, source_target_pairs={{0,12},{4,8},{8,4},{12,0},{1,13},{5,9},{9,5},{13,1},{2,14},{6,10},... | collective-permute-start | bytes 786440 | tf_op jit(solution)/shard_map/ppermute | solution.py:763
  (13 other events, 129.0 us)

commit v11 on v10

--- a/solution.py
+++ b/solution.py
@@ -212,13 +212,13 @@
     return (lax.ppermute(jnp.concatenate([held, picked], axis=0), ("ep", "tp"), moves), meanwhile)
 
 
-def call(body, outs, scratch, **kwargs):
+def call(body, outs, scratch, flops=1 << 20, **kwargs):
     return pl.pallas_call(
         body,
         out_shape=outs,
         **({} if scratch is None else {"scratch_shapes": scratch}),
         compiler_params=pltpu.CompilerParams(vmem_limit_bytes=20 * 1024 * 1024),
-        cost_estimate=pl.CostEstimate(flops=1 << 20, bytes_accessed=1 << 18, transcendentals=0),
+        cost_estimate=pl.CostEstimate(flops=flops, bytes_accessed=1 << 18, transcendentals=0),
         **kwargs,
     )
 
@@ -583,6 +583,7 @@
         [],
         in_specs=[SMEM] + [VMEM] * (2 + len(operands)),
         out_specs=VMEM,
+        flops=1 << 32,
         name="activate",
     )(here, pick, stats, *operands)
 
@@ -683,11 +684,12 @@
     attended = attention(here, query_docs, doc_lens, q_rows, pieces, tables, pool_dev)
     far = lax.ppermute(attended, "tp", pairs(n, 2))
     near = lax.ppermute(attended, "tp", pairs(n, 1))
-    farther = lax.ppermute(far, "tp", pairs(n, 1))
     gain = norm_gain.astype(jnp.float32)[None, :]
     router = jnp.pad(router_weight, ((0, 0), (0, 128 - experts)))
     close, early = project(project_early_body, here, (attended, near), out_proj, 2)
+    early, far = lax.optimization_barrier((early, far))
     given = lax.ppermute(early, "ep", pairs(n, 1))
+    farther = lax.ppermute(far, "tp", pairs(n, 1))
     kept, near, late = project(project_late_body, here, (far, farther), out_proj, 3, close)
     kept, w_gate_up = lax.optimization_barrier((kept, w_gate_up))
     late = (late.astype(jnp.float32) + given.astype(jnp.float32)).astype(jnp.bfloat16)
@@ -725,19 +727,25 @@
         return squares_and_logits([tokens[d] for d in ds], gain, router, experts)
 
     one_chunk, two_chunk = ((1, 2), (0, 3))
+    kept_0, given_0 = terms_of((0,), order)
+    order, kept_0, given_0 = lax.optimization_barrier((order, kept_0, given_0))
     kept, given = terms_of(one_chunk, order)
+    given, given_0 = lax.optimization_barrier((given, given_0))
+    taken_0 = lax.ppermute(given_0, "tp", pairs(n, 1))
     taken = lax.ppermute(given, "tp", pairs(n, 1))
+    across_0 = lax.ppermute(chip_sum(kept_0, taken_0), "tp", pairs(n, 2))
     _, stats = lax.optimization_barrier((given, stats_of(one_chunk)))
     stats_far = lax.ppermute(stats, "tp", pairs(n, 2))
     taken, stats_far = lax.optimization_barrier((taken, stats_far))
     stats = stats + stats_far
     stats_near = lax.ppermute(stats, "tp", pairs(n, 1))
     far_sum = chip_sum(kept, taken)
+    far_sum, across_0 = lax.optimization_barrier((far_sum, across_0))
     across = lax.ppermute(far_sum, "tp", pairs(n, 2))
 
     order, _, stats_near = lax.optimization_barrier((order, far_sum, stats_near))
     stats = stats + stats_near
-    kept_2, given = terms_of(two_chunk, order)
+    kept_2, given = terms_of((3,), order)
     stats_2 = stats_of(two_chunk)
     given, across, stats_2 = lax.optimization_barrier((given, across, stats_2))
     stats_far = lax.ppermute(stats_2, "tp", pairs(n, 2))
@@ -752,12 +760,11 @@
     across = lax.ppermute(far_sum, "tp", pairs(n, 2))
     near, *far = down(one_chunk, order, acts, spread, w_down, halved=True)
     far = [lax.ppermute(part, "ep", pairs(n, 2)) for part in far]
-    across, far[0] = lax.optimization_barrier((across, far[0]))
     near = lax.ppermute(near, "ep", pairs(n, 1))
-    sums = [(kept_2, taken_2, across)]
+    sums = [(kept_0, taken_0, across_0), (kept_2, taken_2, across)]
     stats_2 = stats_2 + stats_near
     acts = spread_act(
-        activate((two_chunk,), features, here, sums, pick, stats_2, pieces), far[1:]
+        activate(((0,), (3,)), features, here, sums, pick, stats_2, pieces), far[:1]
     )
     mine, last = down(two_chunk, order, acts, spread, w_down)
     last = lax.ppermute(last, "ep", pairs(n, 3))

time: 154 us -> 162 us (1.052); the launches traced: 152 us -> 162 us
  waiting for transfers between devices: 61.9 us -> 77.1 us
  starting transfers between devices: 41.7 us -> 34 us
  Pallas kernels: 26.6 us -> 32 us
  local copies, waits for them, and re-layouts: 16.9 us -> 13.7 us
    ppermute x2, waiting for transfers between devices: 13.9 us -> 23.2 us  [per_device_square(): far = [lax.ppermute(part, 'ep', pairs(n, 2)) for part in far]]
    ppermute x1, waiting for transfers between devices: 8.56 us -> 0.01 us  [per_device_square(): last = lax.ppermute(last, 'ep', pairs(n, 3))]
    ppermute x0 -> x2, waiting for transfers between devices: none -> 6.14 us  [the longest x1 6.14 us: per_device_square(): across_0 = lax.ppermute(chip_sum(kept_0, taken_0), 'tp', pairs(n, 2))]
    pallas_call x4 -> x6, Pallas kernels: 9.27 us -> 14.6 us  [gate_up(): call(functools.partial(gate_up_body, ds), jax.ShapeDtypeStruct((count, ro...]
    ppermute x2, waiting for transfers between devices: 1.5 us -> 6.46 us  [per_device_square(): across = lax.ppermute(far_sum, 'tp', pairs(n, 2))]
    ppermute x1, starting transfers between devices: 5.18 us -> 0.33 us  [per_device_square(): far = lax.ppermute(attended, 'tp', pairs(n, 2))]
    ppermute x1, starting transfers between devices: 0.01 us -> 4.14 us  [per_device_square(): near = lax.ppermute(attended, 'tp', pairs(n, 1))]
    ppermute x3, starting transfers between devices: 13.2 us -> 9.44 us  [per_device_square(): lax.ppermute(pieces[d], 'ep', pairs(n, d))]
  transfers between devices with their start and end apart: 32 -> 34, of which waited for: 16 -> 17; matrix products, arithmetic and copies ran while one was open for 10% -> 10% of each run, Pallas kernels for 13% -> 16%
where the time goes in v11:
time: 162 us
  waiting for transfers between devices  77.1 us (48%)
  starting transfers between devices  34 us (21%)
  Pallas kernels  32 us (20%)
  local copies, waits for them, and re-layouts  13.7 us (8%)
  other arithmetic  4.78 us (3%)
    ppermute x2, waiting for transfers between devices, per_device_square(): far = [lax.ppermute(part, 'ep', pairs(n, 2)) for part in far]  23.2 us
    pallas_call x6, Pallas kernels, gate_up(): call(functools.partial(gate_up_body, ds), jax.ShapeDtypeStruct((count, ro...  14.6 us
    optimization_barrier x1, local copies, waits for them, and re-layouts, per_device_square(): kept, w_gate_up = lax.optimization_barrier((kept, w_gate_up))  11.2 us
    ppermute x3, starting transfers between devices, per_device_square(): lax.ppermute(pieces[d], 'ep', pairs(n, d))  9.44 us
    ppermute x2, waiting for transfers between devices, per_device_square(): tokens[d] = lax.ppermute(residual, 'ep', pairs(n, d))  7.4 us
    ppermute x1, waiting for transfers between devices, per_device_square(): tokens[3] = lax.ppermute(tokens[2], 'ep', pairs(n, 1))  6.75 us
    ppermute x2, waiting for transfers between devices, per_device_square(): across = lax.ppermute(far_sum, 'tp', pairs(n, 2))  6.46 us
    ppermute x1, waiting for transfers between devices, per_device_square(): across_0 = lax.ppermute(chip_sum(kept_0, taken_0), 'tp', pairs(n, 2))  6.14 us
  transfers between devices with their start and end apart: 34, of which 17 were waited for; matrix products, arithmetic and copies ran while one was open for 10% of the time, Pallas kernels for 16%

profile of v11, /device:TPU:0, one launch (start us, length us, event | category | flops | bytes accessed | tf_op | source)
XLA Modules:
  0.0 162.0 jit_solution(17570656318255330982)
XLA Ops:
  5.3 6.8 %collective-permute-start.2 = (bf16[272,128]{1,0:T(8,128)(2,1)S(1)}, bf16[272,128]{1,0:T(8,128)(2,1)S(1)}, u32[]{:S(2)}, u32[]{:S(2)}) collective-permute-start(bf16[272,128]{1,0:T(8,128)(2,1)S(1)} %get-tuple-element.65), channel_id=1, source_target_pairs={{0,4},{4,0},{8,12},{12,8},{1,5},{5,1},{9,13},{13,9},{2,6},{6,2},{1... | collective-permute-start | bytes 208904 | tf_op jit(solution)/shard_map/ppermute | solution.py:679
  12.1 2.6 %collective-permute-start.3 = (bf16[272,128]{1,0:T(8,128)(2,1)S(1)}, bf16[272,128]{1,0:T(8,128)(2,1)S(1)}, u32[]{:S(2)}, u32[]{:S(2)}) collective-permute-start(bf16[272,128]{1,0:T(8,128)(2,1)S(1)} %get-tuple-element.66), channel_id=1, source_target_pairs={{0,8},{4,12},{8,0},{12,4},{1,9},{5,13},{9,1},{13,5},{2,10},{6,14},... | collective-permute-start | bytes 208904 | tf_op jit(solution)/shard_map/ppermute | solution.py:679
  15.6 1.7 %broadcast_multiply_fusion.weight = bf16[1024,1024]{1,0:T(8,128)(2,1)S(1)} fusion(bf16[1024,1024]{1,0:T(8,128)(2,1)} %param.21, bf16[]{:T(256)} %constant.23.clone.1), kind=kLoop, calls=%fused_computation.2 | loop fusion | flops 1048576 | bytes 4194306 | tf_op jit(solution)/shard_map/mul | solution.py:683
  18.2 5.9 %collective-permute-done.3.c2.refs_4_ = bf16[272,128]{1,0:T(8,128)(2,1)S(1)} collective-permute-done((bf16[272,128]{1,0:T(8,128)(2,1)S(1)}, bf16[272,128]{1,0:T(8,128)(2,1)S(1)}, u32[]{:S(2)}, u32[]{:S(2)}) %collective-permute-start.3) | collective-permute-done | bytes 69664 | tf_op jit(solution)/shard_map/ppermute | solution.py:679
  24.2 3.4 %attention.1.a = bf16[128,1024]{1,0:T(8,128)(2,1)S(1)} custom-call(s32[2]{0:T(128)S(1)} %pad_add_fusion.here, s32[4,4]{1,0:T(4,128)S(1)} %copy-done.4, s32[8]{0:T(128)S(1)} %copy-done.6, bf16[1280,128]{1,0:T(8,128)(2,1)S(1)} %collective-permute-done.1.q, bf16[272,128]{1,0:T(8,128)(2,1)S(1)} %get-tuple-element.64.c0.refs_3_, ...), custom_call_target="tpu_custom_call" | custom-call | flops 1048576 | bytes 262144 | tf_op jit(solution)/shard_map/attention/pallas_call | solution.py:364
  27.6 4.1 %collective-permute-start.5 = (bf16[128,1024]{1,0:T(8,128)(2,1)S(1)}, bf16[128,1024]{1,0:T(8,128)(2,1)S(1)}, u32[]{:S(2)}, u32[]{:S(2)}) collective-permute-start(bf16[128,1024]{1,0:T(8,128)(2,1)S(1)} %attention.1.a), channel_id=1, source_target_pairs={{0,1},{1,0},{2,3},{3,2},{4,5},{5,4},{6,7},{7,6},{8,9},{9,8},{10,11... | collective-permute-start | bytes 786440 | tf_op jit(solution)/shard_map/ppermute | solution.py:686
  34.2 5.8 %collective-permute-done.6.a = bf16[128,1024]{1,0:T(8,128)(2,1)S(1)} collective-permute-done((bf16[128,1024]{1,0:T(8,128)(2,1)S(1)}, bf16[128,1024]{1,0:T(8,128)(2,1)S(1)}, u32[]{:S(2)}, u32[]{:S(2)}) %collective-permute-start.6) | collective-permute-done | bytes 262176 | tf_op jit(solution)/shard_map/ppermute | solution.py:685
  40.0 1.5 collective-permute-done.7.b
  42.9 5.9 %collective-permute-done.8 = bf16[128,1024]{1,0:T(8,128)(2,1)S(1)} collective-permute-done((bf16[128,1024]{1,0:T(8,128)(2,1)S(1)}, bf16[128,1024]{1,0:T(8,128)(2,1)S(1)}, u32[]{:S(2)}, u32[]{:S(2)}) %collective-permute-start.8) | collective-permute-done | bytes 262176 | tf_op jit(solution)/shard_map/ppermute | solution.py:691
  48.8 2.8 %collective-permute-start.9 = (bf16[128,1024]{1,0:T(8,128)(2,1)S(1)}, bf16[128,1024]{1,0:T(8,128)(2,1)S(1)}, u32[]{:S(2)}, u32[]{:S(2)}) collective-permute-start(bf16[128,1024]{1,0:T(8,128)(2,1)S(1)} %add_convert_fusion.4), channel_id=1, source_target_pairs={{0,12},{1,13},{2,10},{3,11},{4,8},{5,9},{6,14},{7,15},{8,4},{9,5},... | collective-permute-start | bytes 786440 | tf_op jit(solution)/shard_map/ppermute | solution.py:699
  52.8 11.2 %copy.25 = bf16[4,1024,2,1024]{3,1,2,0:T(8,128)(2,1)S(1)} copy(bf16[4,1024,2,1024]{3,2,1,0:T(2,128)(2,1)} %param.24) | data formatting | bytes 33554432 | tf_op jit(solution)/shard_map/optimization_barrier | solution.py:694
  66.8 2.5 %gate_up.7 = bf16[2,64,2048]{2,1,0:T(8,128)(2,1)S(1)} custom-call(s32[2]{0:T(128)S(1)} %get-tuple-element.117.order, bf16[128,1024]{1,0:T(8,128)(2,1)S(1)} %residual.1.refs_0_, f32[1,1024]{1,0:T(1,128)S(1)} %bitcast.34, bf16[4,4,64,128]{3,2,1,0:T(8,128)(2,1)S(1)} %get-tuple-element.86.refs_2_.refs_3_.pick, bf16[4,2,1024,1024]{3,2,1,0:T(8,128)(2,1)S(1)} %bitcast.25), custom_call_target="tpu_custom_call" | custom-call | flops 1048576 | bytes 262144 | tf_op jit(solution)/shard_map/gate_up/pallas_call | solution.py:519
  69.3 2.5 %gate_up.6.refs_0_ = bf16[2,64,2048]{2,1,0:T(8,128)(2,1)S(1)} custom-call(s32[2]{0:T(128)S(1)} %get-tuple-element.118.order, bf16[128,1024]{1,0:T(8,128)(2,1)S(1)} %residual.1.refs_0_, f32[1,1024]{1,0:T(1,128)S(1)} %bitcast.35, bf16[4,4,64,128]{3,2,1,0:T(8,128)(2,1)S(1)} %get-tuple-element.86.refs_2_.refs_3_.pick, bf16[4,2,1024,1024]{3,2,1,0:T(8,128)(2,1)S(1)} %bitcast.26), custom_call_target="tpu_custom_call" | custom-call | flops 1048576 | bytes 262144 | tf_op jit(solution)/shard_map/gate_up/pallas_call | solution.py:519
  71.9 7.4 %collective-permute-done.12.refs_1_ = bf16[128,1024]{1,0:T(8,128)(2,1)S(1)} collective-permute-done((bf16[128,1024]{1,0:T(8,128)(2,1)S(1)}, bf16[128,1024]{1,0:T(8,128)(2,1)S(1)}, u32[]{:S(2)}, u32[]{:S(2)}) %collective-permute-start.12) | collective-permute-done | bytes 262176 | tf_op jit(solution)/shard_map/ppermute | solution.py:707
  79.3 2.3 %gate_up.9 = bf16[2,128,2048]{2,1,0:T(8,128)(2,1)S(1)} custom-call(s32[2]{0:T(128)S(1)} %get-tuple-element.115.order, bf16[128,1024]{1,0:T(8,128)(2,1)S(1)} %collective-permute-done.11.refs_0_, bf16[128,1024]{1,0:T(8,128)(2,1)S(1)} %collective-permute-done.12.refs_1_, f32[1,1024]{1,0:T(1,128)S(1)} %bitcast.36, ...), custom_call_target="tpu_custom_call" | custom-call | flops 1048576 | bytes 262144 | tf_op jit(solution)/shard_map/gate_up/pallas_call | solution.py:519
  83.0 2.3 %gate_up.8.refs_0_ = bf16[2,128,2048]{2,1,0:T(8,128)(2,1)S(1)} custom-call(s32[2]{0:T(128)S(1)} %get-tuple-element.116.order, bf16[128,1024]{1,0:T(8,128)(2,1)S(1)} %collective-permute-done.11.refs_0_, bf16[128,1024]{1,0:T(8,128)(2,1)S(1)} %collective-permute-done.12.refs_1_, f32[1,1024]{1,0:T(1,128)S(1)} %bitcast.38, ...), custom_call_target="tpu_custom_call" | custom-call | flops 1048576 | bytes 262144 | tf_op jit(solution)/shard_map/gate_up/pallas_call | solution.py:519
  85.4 2.1 %collective-permute-start.16 = (bf16[64,2048]{1,0:T(8,128)(2,1)S(1)}, bf16[64,2048]{1,0:T(8,128)(2,1)S(1)}, u32[]{:S(2)}, u32[]{:S(2)}) collective-permute-start(bf16[64,2048]{1,0:T(8,128)(2,1)S(1)} %fusion.1), channel_id=1, source_target_pairs={{0,2},{1,3},{2,0},{3,1},{4,6},{5,7},{6,4},{7,5},{8,10},{9,11},{10,... | collective-permute-start | bytes 786440 | tf_op jit(solution)/shard_map/ppermute | solution.py:736
  87.6 6.1 %collective-permute-done.16.refs_2_ = bf16[64,2048]{1,0:T(8,128)(2,1)S(1)} collective-permute-done((bf16[64,2048]{1,0:T(8,128)(2,1)S(1)}, bf16[64,2048]{1,0:T(8,128)(2,1)S(1)}, u32[]{:S(2)}, u32[]{:S(2)}) %collective-permute-start.16) | collective-permute-done | bytes 262176 | tf_op jit(solution)/shard_map/ppermute | solution.py:736
  93.8 1.7 %collective-permute-start.19 = (bf16[128,2048]{1,0:T(8,128)(2,1)S(1)}, bf16[128,2048]{1,0:T(8,128)(2,1)S(1)}, u32[]{:S(2)}, u32[]{:S(2)}) collective-permute-start(bf16[128,2048]{1,0:T(8,128)(2,1)S(1)} %fusion), channel_id=1, source_target_pairs={{0,2},{1,3},{2,0},{3,1},{4,6},{5,7},{6,4},{7,5},{8,10},{9,11},{10,... | collective-permute-start | bytes 1572872 | tf_op jit(solution)/shard_map/ppermute | solution.py:744
  95.6 6.8 %collective-permute-done.18.refs_0_.refs_1_ = bf16[128,1024]{1,0:T(8,128)(2,1)S(1)} collective-permute-done((bf16[128,1024]{1,0:T(8,128)(2,1)S(1)}, bf16[128,1024]{1,0:T(8,128)(2,1)S(1)}, u32[]{:S(2)}, u32[]{:S(2)}) %collective-permute-start.18) | collective-permute-done | bytes 262176 | tf_op jit(solution)/shard_map/ppermute | solution.py:708
  103.2 2.5 %gate_up.10 = bf16[2,64,2048]{2,1,0:T(8,128)(2,1)S(1)} custom-call(s32[2]{0:T(128)S(1)} %get-tuple-element.114.order, bf16[128,1024]{1,0:T(8,128)(2,1)S(1)} %collective-permute-done.18.refs_0_.refs_1_, f32[1,1024]{1,0:T(1,128)S(1)} %bitcast.40, bf16[4,4,64,128]{3,2,1,0:T(8,128)(2,1)S(1)} %get-tuple-element.86.refs_2_.refs_3_.pick, ...), custom_call_target="tpu_custom_call" | custom-call | flops 1048576 | bytes 262144 | tf_op jit(solution)/shard_map/gate_up/pallas_call | solution.py:519
  107.8 1.5 collective-permute-start.22
  109.2 2.5 %gate_up.11.refs_4_ = bf16[2,64,2048]{2,1,0:T(8,128)(2,1)S(1)} custom-call(s32[2]{0:T(128)S(1)} %get-tuple-element.113.order, bf16[128,1024]{1,0:T(8,128)(2,1)S(1)} %collective-permute-done.18.refs_0_.refs_1_, f32[1,1024]{1,0:T(1,128)S(1)} %bitcast.41, bf16[4,4,64,128]{3,2,1,0:T(8,128)(2,1)S(1)} %get-tuple-element.86.refs_2_.refs_3_.pick, ...), custom_call_target="tpu_custom_call" | custom-call | flops 1048576 | bytes 262144 | tf_op jit(solution)/shard_map/gate_up/pallas_call | solution.py:519
  112.4 4.4 %collective-permute-done.22.b = bf16[128,1024]{1,0:T(8,128)(2,1)S(1)} collective-permute-done((bf16[128,1024]{1,0:T(8,128)(2,1)S(1)}, bf16[128,1024]{1,0:T(8,128)(2,1)S(1)}, u32[]{:S(2)}, u32[]{:S(2)}) %collective-permute-start.22) | collective-permute-done | bytes 262176 | tf_op jit(solution)/shard_map/ppermute | solution.py:713
  119.7 5.3 %collective-permute-done.24.refs_6_ = bf16[64,2048]{1,0:T(8,128)(2,1)S(1)} collective-permute-done((bf16[64,2048]{1,0:T(8,128)(2,1)S(1)}, bf16[64,2048]{1,0:T(8,128)(2,1)S(1)}, u32[]{:S(2)}, u32[]{:S(2)}) %collective-permute-start.24) | collective-permute-done | bytes 262176 | tf_op jit(solution)/shard_map/ppermute | solution.py:760
  125.9 1.5 collective-permute-start.25
  127.5 2.8 %down.2 = (bf16[128,1024]{1,0:T(8,128)(2,1)S(1)}, bf16[64,1024]{1,0:T(8,128)(2,1)S(1)}, bf16[64,1024]{1,0:T(8,128)(2,1)S(1)}) custom-call(s32[4]{0:T(128)S(1)} %broadcast_xor_fusion.order, bf16[128,1024]{1,0:T(8,128)(2,1)S(1)} %activate.2.a, bf16[128,1024]{1,0:T(8,128)(2,1)S(1)} %collective-permute-done.22.b, ...), custom_call_target="tpu_custom_call" | custom-call | flops 1048576 | bytes 262144 | tf_op jit(solution)/shard_map/down/pallas_call | solution.py:627
  131.3 5.8 %collective-permute-done.28 = bf16[64,1024]{1,0:T(8,128)(2,1)S(1)} collective-permute-done((bf16[64,1024]{1,0:T(8,128)(2,1)S(1)}, bf16[64,1024]{1,0:T(8,128)(2,1)S(1)}, u32[]{:S(2)}, u32[]{:S(2)}) %collective-permute-start.28) | collective-permute-done | bytes 131104 | tf_op jit(solution)/shard_map/ppermute | solution.py:762
  137.1 1.5 collective-permute-done.30.d
  138.6 2.8 %down.3 = (bf16[128,1024]{1,0:T(8,128)(2,1)S(1)}, bf16[128,1024]{1,0:T(8,128)(2,1)S(1)}) custom-call(s32[4]{0:T(128)S(1)} %broadcast_xor_fusion.order, bf16[128,1024]{1,0:T(8,128)(2,1)S(1)} %activate.3.a, bf16[128,1024]{1,0:T(8,128)(2,1)S(1)} %collective-permute-done.25.b, bf16[128,1024]{1,0:T(8,128)(2,1)S(1)} %collective-permute-done.29.c, ...), custom_call_target="tpu_custom_call" | custom-call | flops 1048576 | bytes 262144 | tf_op jit(solution)/shard_map/down/pallas_call | solution.py:627
  141.4 2.2 %collective-permute-start.33 = (bf16[128,1024]{1,0:T(8,128)(2,1)S(1)}, bf16[128,1024]{1,0:T(8,128)(2,1)S(1)}, u32[]{:S(2)}, u32[]{:S(2)}) collective-permute-start(bf16[128,1024]{1,0:T(8,128)(2,1)S(1)} %get-tuple-element.112), channel_id=1, source_target_pairs={{0,12},{4,8},{8,4},{12,0},{1,13},{5,9},{9,5},{13,1},{2,14},{6,10},... | collective-permute-start | bytes 786440 | tf_op jit(solution)/shard_map/ppermute | solution.py:770
  143.6 17.5 %collective-permute-done.32 = bf16[64,1024]{1,0:T(8,128)(2,1)S(1)} collective-permute-done((bf16[64,1024]{1,0:T(8,128)(2,1)S(1)}, bf16[64,1024]{1,0:T(8,128)(2,1)S(1)}, u32[]{:S(2)}, u32[]{:S(2)}) %collective-permute-start.32) | collective-permute-done | bytes 131104 | tf_op jit(solution)/shard_map/ppermute | solution.py:762
  (106 shorter events, 25.7 us)
Async XLA Ops:
  0.0 4.3 %collective-permute-start = (bf16[1024,128]{1,0:T(8,128)(2,1)}, bf16[1024,128]{1,0:T(8,128)(2,1)S(1)}, u32[]{:S(2)}, u32[]{:S(2)}) collective-permute-start(bf16[1024,128]{1,0:T(8,128)(2,1)} %bitcast.43), channel_id=1, source_target_pairs={{1,2},{2,1},{4,7},{7,4},{9,10},{10,9},{12,15},{15,12},{17,18},{18,... | collective-permute-start | bytes 786440 | tf_op jit(solution)/shard_map/ppermute | solution.py:202
  5.3 13.0 %collective-permute-start.2 = (bf16[272,128]{1,0:T(8,128)(2,1)S(1)}, bf16[272,128]{1,0:T(8,128)(2,1)S(1)}, u32[]{:S(2)}, u32[]{:S(2)}) collective-permute-start(bf16[272,128]{1,0:T(8,128)(2,1)S(1)} %get-tuple-element.65), channel_id=1, source_target_pairs={{0,4},{4,0},{8,12},{12,8},{1,5},{5,1},{9,13},{13,9},{2,6},{6,2},{1... | collective-permute-start | bytes 208904 | tf_op jit(solution)/shard_map/ppermute | solution.py:679
  12.1 12.1 %collective-permute-start.3 = (bf16[272,128]{1,0:T(8,128)(2,1)S(1)}, bf16[272,128]{1,0:T(8,128)(2,1)S(1)}, u32[]{:S(2)}, u32[]{:S(2)}) collective-permute-start(bf16[272,128]{1,0:T(8,128)(2,1)S(1)} %get-tuple-element.66), channel_id=1, source_target_pairs={{0,8},{4,12},{8,0},{12,4},{1,9},{5,13},{9,1},{13,5},{2,10},{6,14},... | collective-permute-start | bytes 208904 | tf_op jit(solution)/shard_map/ppermute | solution.py:679
  14.7 9.5 %collective-permute-start.4 = (bf16[272,128]{1,0:T(8,128)(2,1)S(1)}, bf16[272,128]{1,0:T(8,128)(2,1)S(1)}, u32[]{:S(2)}, u32[]{:S(2)}) collective-permute-start(bf16[272,128]{1,0:T(8,128)(2,1)S(1)} %get-tuple-element.67), channel_id=1, source_target_pairs={{0,12},{4,8},{8,4},{12,0},{1,13},{5,9},{9,5},{13,1},{2,14},{6,10},... | collective-permute-start | bytes 208904 | tf_op jit(solution)/shard_map/ppermute | solution.py:679
  14.8 9.4 %collective-permute-start.1 = (bf16[1280,128]{1,0:T(8,128)(2,1)S(1)}, bf16[1280,128]{1,0:T(8,128)(2,1)S(1)}, u32[]{:S(2)}, u32[]{:S(2)}) collective-permute-start(bf16[1280,128]{1,0:T(8,128)(2,1)S(1)} %pad_maximum_fusion), channel_id=1, source_target_pairs={{0,0},{1,8},{2,6},{3,14},{4,12},{5,4},{6,10},{7,2},{8,1},{9,9},{10... | collective-permute-start | bytes 983048 | tf_op jit(solution)/shard_map/ppermute | solution.py:212
  27.6 5.3 %collective-permute-start.5 = (bf16[128,1024]{1,0:T(8,128)(2,1)S(1)}, bf16[128,1024]{1,0:T(8,128)(2,1)S(1)}, u32[]{:S(2)}, u32[]{:S(2)}) collective-permute-start(bf16[128,1024]{1,0:T(8,128)(2,1)S(1)} %attention.1.a), channel_id=1, source_target_pairs={{0,1},{1,0},{2,3},{3,2},{4,5},{5,4},{6,7},{7,6},{8,9},{9,8},{10,11... | collective-permute-start | bytes 786440 | tf_op jit(solution)/shard_map/ppermute | solution.py:686
  31.7 8.3 %collective-permute-start.6 = (bf16[128,1024]{1,0:T(8,128)(2,1)S(1)}, bf16[128,1024]{1,0:T(8,128)(2,1)S(1)}, u32[]{:S(2)}, u32[]{:S(2)}) collective-permute-start(bf16[128,1024]{1,0:T(8,128)(2,1)S(1)} %attention.1.a), channel_id=1, source_target_pairs={{0,2},{1,3},{2,0},{3,1},{4,6},{5,7},{6,4},{7,5},{8,10},{9,11},{10,... | collective-permute-start | bytes 786440 | tf_op jit(solution)/shard_map/ppermute | solution.py:685
  40.0 8.7 %collective-permute-start.8 = (bf16[128,1024]{1,0:T(8,128)(2,1)S(1)}, bf16[128,1024]{1,0:T(8,128)(2,1)S(1)}, u32[]{:S(2)}, u32[]{:S(2)}) collective-permute-start(bf16[128,1024]{1,0:T(8,128)(2,1)S(1)} %get-tuple-element.82), channel_id=1, source_target_pairs={{0,4},{4,0},{8,12},{12,8},{1,5},{5,1},{9,13},{13,9},{2,6},{6,2},{1... | collective-permute-start | bytes 786440 | tf_op jit(solution)/shard_map/ppermute | solution.py:691
  48.8 15.2 %collective-permute-start.9 = (bf16[128,1024]{1,0:T(8,128)(2,1)S(1)}, bf16[128,1024]{1,0:T(8,128)(2,1)S(1)}, u32[]{:S(2)}, u32[]{:S(2)}) collective-permute-start(bf16[128,1024]{1,0:T(8,128)(2,1)S(1)} %add_convert_fusion.4), channel_id=1, source_target_pairs={{0,12},{1,13},{2,10},{3,11},{4,8},{5,9},{6,14},{7,15},{8,4},{9,5},... | collective-permute-start | bytes 786440 | tf_op jit(solution)/shard_map/ppermute | solution.py:699
  51.6 12.7 %collective-permute-start.10 = (bf16[128,1024]{1,0:T(8,128)(2,1)S(1)}, bf16[128,1024]{1,0:T(8,128)(2,1)S(1)}, u32[]{:S(2)}, u32[]{:S(2)}) collective-permute-start(bf16[128,1024]{1,0:T(8,128)(2,1)S(1)} %get-tuple-element.83), channel_id=1, source_target_pairs={{0,4},{4,0},{8,12},{12,8},{1,5},{5,1},{9,13},{13,9},{2,6},{6,2},{1... | collective-permute-start | bytes 786440 | tf_op jit(solution)/shard_map/ppermute | solution.py:699
  64.5 14.8 %collective-permute-start.12 = (bf16[128,1024]{1,0:T(8,128)(2,1)S(1)}, bf16[128,1024]{1,0:T(8,128)(2,1)S(1)}, u32[]{:S(2)}, u32[]{:S(2)}) collective-permute-start(bf16[128,1024]{1,0:T(8,128)(2,1)S(1)} %residual.1.refs_0_), channel_id=1, source_target_pairs={{0,8},{4,12},{8,0},{12,4},{1,9},{5,13},{9,1},{13,5},{2,10},{6,14},... | collective-permute-start | bytes 786440 | tf_op jit(solution)/shard_map/ppermute | solution.py:707
  65.8 13.4 %collective-permute-start.11 = (bf16[128,1024]{1,0:T(8,128)(2,1)S(1)}, bf16[128,1024]{1,0:T(8,128)(2,1)S(1)}, u32[]{:S(2)}, u32[]{:S(2)}) collective-permute-start(bf16[128,1024]{1,0:T(8,128)(2,1)S(1)} %residual.1.refs_0_), channel_id=1, source_target_pairs={{0,4},{4,0},{8,12},{12,8},{1,5},{5,1},{9,13},{13,9},{2,6},{6,2},{1... | collective-permute-start | bytes 786440 | tf_op jit(solution)/shard_map/ppermute | solution.py:707
  81.6 5.9 %collective-permute-start.13 = (bf16[2,128,2048]{2,1,0:T(8,128)(2,1)S(1)}, bf16[2,128,2048]{2,1,0:T(8,128)(2,1)S(1)}, u32[]{:S(2)}, u32[]{:S(2)}) collective-permute-start(bf16[2,128,2048]{2,1,0:T(8,128)(2,1)S(1)} %gate_up.9), channel_id=1, source_target_pairs={{0,1},{1,0},{2,3},{3,2},{4,5},{5,4},{6,7},{7,6},{8,9},{9,8},{10,11... | collective-permute-start | bytes 3145736 | tf_op jit(solution)/shard_map/ppermute | solution.py:735
  81.7 3.6 %collective-permute-start.15 = (bf16[2,64,2048]{2,1,0:T(8,128)(2,1)S(1)}, bf16[2,64,2048]{2,1,0:T(8,128)(2,1)S(1)}, u32[]{:S(2)}, u32[]{:S(2)}) collective-permute-start(bf16[2,64,2048]{2,1,0:T(8,128)(2,1)S(1)} %gate_up.7), channel_id=1, source_target_pairs={{0,1},{1,0},{2,3},{3,2},{4,5},{5,4},{6,7},{7,6},{8,9},{9,8},{10,11... | collective-permute-start | bytes 1572872 | tf_op jit(solution)/shard_map/ppermute | solution.py:734
  82.9 4.6 %collective-permute-start.14 = (f32[24,256]{1,0:T(8,128)S(1)}, f32[24,256]{1,0:T(8,128)S(1)}, u32[]{:S(2)}, u32[]{:S(2)}) collective-permute-start(f32[24,256]{1,0:T(8,128)S(1)} %stats.2), channel_id=1, source_target_pairs={{0,2},{1,3},{2,0},{3,1},{4,6},{5,7},{6,4},{7,5},{8,10},{9,11},{10,... | collective-permute-start | bytes 73736 | tf_op jit(solution)/shard_map/ppermute | solution.py:738
  85.4 8.3 %collective-permute-start.16 = (bf16[64,2048]{1,0:T(8,128)(2,1)S(1)}, bf16[64,2048]{1,0:T(8,128)(2,1)S(1)}, u32[]{:S(2)}, u32[]{:S(2)}) collective-permute-start(bf16[64,2048]{1,0:T(8,128)(2,1)S(1)} %fusion.1), channel_id=1, source_target_pairs={{0,2},{1,3},{2,0},{3,1},{4,6},{5,7},{6,4},{7,5},{8,10},{9,11},{10,... | collective-permute-start | bytes 786440 | tf_op jit(solution)/shard_map/ppermute | solution.py:736
  93.8 13.1 %collective-permute-start.19 = (bf16[128,2048]{1,0:T(8,128)(2,1)S(1)}, bf16[128,2048]{1,0:T(8,128)(2,1)S(1)}, u32[]{:S(2)}, u32[]{:S(2)}) collective-permute-start(bf16[128,2048]{1,0:T(8,128)(2,1)S(1)} %fusion), channel_id=1, source_target_pairs={{0,2},{1,3},{2,0},{3,1},{4,6},{5,7},{6,4},{7,5},{8,10},{9,11},{10,... | collective-permute-start | bytes 1572872 | tf_op jit(solution)/shard_map/ppermute | solution.py:744
  95.5 6.8 %collective-permute-start.18 = (bf16[128,1024]{1,0:T(8,128)(2,1)S(1)}, bf16[128,1024]{1,0:T(8,128)(2,1)S(1)}, u32[]{:S(2)}, u32[]{:S(2)}) collective-permute-start(bf16[128,1024]{1,0:T(8,128)(2,1)S(1)} %collective-permute-done.12.refs_1_), channel_id=1, source_target_pairs={{0,4},{4,0},{8,12},{12,8},{1,5},{5,1},{9,13},{13,9},{2,6},{6,2},{1... | collective-permute-start | bytes 786440 | tf_op jit(solution)/shard_map/ppermute | solution.py:708
  95.5 7.6 %collective-permute-start.17 = (f32[24,256]{1,0:T(8,128)S(1)}, f32[24,256]{1,0:T(8,128)S(1)}, u32[]{:S(2)}, u32[]{:S(2)}) collective-permute-start(f32[24,256]{1,0:T(8,128)S(1)} %add.51), channel_id=1, source_target_pairs={{0,1},{1,0},{2,3},{3,2},{4,5},{5,4},{6,7},{7,6},{8,9},{9,8},{10,11... | collective-permute-start | bytes 73736 | tf_op jit(solution)/shard_map/ppermute | solution.py:741
  106.8 10.0 %collective-permute-start.20 = (bf16[2,64,2048]{2,1,0:T(8,128)(2,1)S(1)}, bf16[2,64,2048]{2,1,0:T(8,128)(2,1)S(1)}, u32[]{:S(2)}, u32[]{:S(2)}) collective-permute-start(bf16[2,64,2048]{2,1,0:T(8,128)(2,1)S(1)} %gate_up.10), channel_id=1, source_target_pairs={{0,1},{1,0},{2,3},{3,2},{4,5},{5,4},{6,7},{7,6},{8,9},{9,8},{10,11... | collective-permute-start | bytes 1572872 | tf_op jit(solution)/shard_map/ppermute | solution.py:752
  107.8 9.0 %collective-permute-start.22 = (bf16[128,1024]{1,0:T(8,128)(2,1)S(1)}, bf16[128,1024]{1,0:T(8,128)(2,1)S(1)}, u32[]{:S(2)}, u32[]{:S(2)}) collective-permute-start(bf16[128,1024]{1,0:T(8,128)(2,1)S(1)} %activate.2.a), channel_id=1, source_target_pairs={{0,2},{1,3},{2,0},{3,1},{4,6},{5,7},{6,4},{7,5},{8,10},{9,11},{10,... | collective-permute-start | bytes 786440 | tf_op jit(solution)/shard_map/ppermute | solution.py:713
  111.7 5.3 %collective-permute-start.21 = (f32[24,256]{1,0:T(8,128)S(1)}, f32[24,256]{1,0:T(8,128)S(1)}, u32[]{:S(2)}, u32[]{:S(2)}) collective-permute-start(f32[24,256]{1,0:T(8,128)S(1)} %stats.3), channel_id=1, source_target_pairs={{0,2},{1,3},{2,0},{3,1},{4,6},{5,7},{6,4},{7,5},{8,10},{9,11},{10,... | collective-permute-start | bytes 73736 | tf_op jit(solution)/shard_map/ppermute | solution.py:751
  117.1 7.9 %collective-permute-start.24 = (bf16[64,2048]{1,0:T(8,128)(2,1)S(1)}, bf16[64,2048]{1,0:T(8,128)(2,1)S(1)}, u32[]{:S(2)}, u32[]{:S(2)}) collective-permute-start(bf16[64,2048]{1,0:T(8,128)(2,1)S(1)} %fusion.2), channel_id=1, source_target_pairs={{0,2},{1,3},{2,0},{3,1},{4,6},{5,7},{6,4},{7,5},{8,10},{9,11},{10,... | collective-permute-start | bytes 786440 | tf_op jit(solution)/shard_map/ppermute | solution.py:760
  118.5 8.9 %collective-permute-start.26 = (bf16[128,1024]{1,0:T(8,128)(2,1)S(1)}, bf16[128,1024]{1,0:T(8,128)(2,1)S(1)}, u32[]{:S(2)}, u32[]{:S(2)}) collective-permute-start(bf16[128,1024]{1,0:T(8,128)(2,1)S(1)} %activate.2.a), channel_id=1, source_target_pairs={{0,1},{1,0},{2,3},{3,2},{4,5},{5,4},{6,7},{7,6},{8,9},{9,8},{10,11... | collective-permute-start | bytes 786440 | tf_op jit(solution)/shard_map/ppermute | solution.py:715
  119.0 8.4 %collective-permute-start.27 = (bf16[128,1024]{1,0:T(8,128)(2,1)S(1)}, bf16[128,1024]{1,0:T(8,128)(2,1)S(1)}, u32[]{:S(2)}, u32[]{:S(2)}) collective-permute-start(bf16[128,1024]{1,0:T(8,128)(2,1)S(1)} %collective-permute-done.22.b), channel_id=1, source_target_pairs={{0,1},{1,0},{2,3},{3,2},{4,5},{5,4},{6,7},{7,6},{8,9},{9,8},{10,11... | collective-permute-start | bytes 786440 | tf_op jit(solution)/shard_map/ppermute | solution.py:759
  125.9 11.1 %collective-permute-start.25 = (bf16[128,1024]{1,0:T(8,128)(2,1)S(1)}, bf16[128,1024]{1,0:T(8,128)(2,1)S(1)}, u32[]{:S(2)}, u32[]{:S(2)}) collective-permute-start(bf16[128,1024]{1,0:T(8,128)(2,1)S(1)} %activate.3.a), channel_id=1, source_target_pairs={{0,2},{1,3},{2,0},{3,1},{4,6},{5,7},{6,4},{7,5},{8,10},{9,11},{10,... | collective-permute-start | bytes 786440 | tf_op jit(solution)/shard_map/ppermute | solution.py:713
  130.3 6.8 %collective-permute-start.28 = (bf16[64,1024]{1,0:T(8,128)(2,1)S(1)}, bf16[64,1024]{1,0:T(8,128)(2,1)S(1)}, u32[]{:S(2)}, u32[]{:S(2)}) collective-permute-start(bf16[64,1024]{1,0:T(8,128)(2,1)S(1)} %get-tuple-element.107), channel_id=1, source_target_pairs={{0,8},{4,12},{8,0},{12,4},{1,9},{5,13},{9,1},{13,5},{2,10},{6,14},... | collective-permute-start | bytes 393224 | tf_op jit(solution)/shard_map/ppermute | solution.py:762
  131.3 5.8 %collective-permute-start.29 = (bf16[128,1024]{1,0:T(8,128)(2,1)S(1)}, bf16[128,1024]{1,0:T(8,128)(2,1)S(1)}, u32[]{:S(2)}, u32[]{:S(2)}) collective-permute-start(bf16[128,1024]{1,0:T(8,128)(2,1)S(1)} %activate.3.a), channel_id=1, source_target_pairs={{0,1},{1,0},{2,3},{3,2},{4,5},{5,4},{6,7},{7,6},{8,9},{9,8},{10,11... | collective-permute-start | bytes 786440 | tf_op jit(solution)/shard_map/ppermute | solution.py:715
  137.0 1.5 collective-permute-start.30
  137.0 24.0 %collective-permute-start.31 = (bf16[128,1024]{1,0:T(8,128)(2,1)S(1)}, bf16[128,1024]{1,0:T(8,128)(2,1)S(1)}, u32[]{:S(2)}, u32[]{:S(2)}) collective-permute-start(bf16[128,1024]{1,0:T(8,128)(2,1)S(1)} %get-tuple-element.110), channel_id=1, source_target_pairs={{0,4},{4,0},{8,12},{12,8},{1,5},{5,1},{9,13},{13,9},{2,6},{6,2},{1... | collective-permute-start | bytes 786440 | tf_op jit(solution)/shard_map/ppermute | solution.py:763
  141.4 19.7 %collective-permute-start.33 = (bf16[128,1024]{1,0:T(8,128)(2,1)S(1)}, bf16[128,1024]{1,0:T(8,128)(2,1)S(1)}, u32[]{:S(2)}, u32[]{:S(2)}) collective-permute-start(bf16[128,1024]{1,0:T(8,128)(2,1)S(1)} %get-tuple-element.112), channel_id=1, source_target_pairs={{0,12},{4,8},{8,4},{12,0},{1,13},{5,9},{9,5},{13,1},{2,14},{6,10},... | collective-permute-start | bytes 786440 | tf_op jit(solution)/shard_map/ppermute | solution.py:770
  143.6 17.5 %collective-permute-start.32 = (bf16[64,1024]{1,0:T(8,128)(2,1)S(1)}, bf16[64,1024]{1,0:T(8,128)(2,1)S(1)}, u32[]{:S(2)}, u32[]{:S(2)}) collective-permute-start(bf16[64,1024]{1,0:T(8,128)(2,1)S(1)} %get-tuple-element.111), channel_id=1, source_target_pairs={{0,8},{4,12},{8,0},{12,4},{1,9},{5,13},{9,1},{13,5},{2,10},{6,14},... | collective-permute-start | bytes 393224 | tf_op jit(solution)/shard_map/ppermute | solution.py:762
  (14 other events, 114.8 us)

commit v12 on v10

--- a/solution.py
+++ b/solution.py
@@ -212,13 +212,13 @@
     return (lax.ppermute(jnp.concatenate([held, picked], axis=0), ("ep", "tp"), moves), meanwhile)
 
 
-def call(body, outs, scratch, **kwargs):
+def call(body, outs, scratch, flops=1 << 20, **kwargs):
     return pl.pallas_call(
         body,
         out_shape=outs,
         **({} if scratch is None else {"scratch_shapes": scratch}),
         compiler_params=pltpu.CompilerParams(vmem_limit_bytes=20 * 1024 * 1024),
-        cost_estimate=pl.CostEstimate(flops=1 << 20, bytes_accessed=1 << 18, transcendentals=0),
+        cost_estimate=pl.CostEstimate(flops=flops, bytes_accessed=1 << 18, transcendentals=0),
         **kwargs,
     )
 
@@ -572,7 +572,7 @@
         base += len(ds) * capacity
 
 
-def activate(groups, features, here, sums, pick, stats, pieces):
+def activate(groups, features, here, sums, pick, stats, pieces, flops=1 << 20):
     operands = []
     for ds, terms in zip(groups, sums):
         operands += list(terms) + [pieces[d] for d in ds]
@@ -583,6 +583,7 @@
         [],
         in_specs=[SMEM] + [VMEM] * (2 + len(operands)),
         out_specs=VMEM,
+        flops=flops,
         name="activate",
     )(here, pick, stats, *operands)
 
@@ -753,14 +754,15 @@
     near, *far = down(one_chunk, order, acts, spread, w_down, halved=True)
     far = [lax.ppermute(part, "ep", pairs(n, 2)) for part in far]
     across, far[0] = lax.optimization_barrier((across, far[0]))
-    near = lax.ppermute(near, "ep", pairs(n, 1))
     sums = [(kept_2, taken_2, across)]
     stats_2 = stats_2 + stats_near
     acts = spread_act(
-        activate((two_chunk,), features, here, sums, pick, stats_2, pieces), far[1:]
+        activate((two_chunk,), features, here, sums, pick, stats_2, pieces, 1 << 32), far[1:]
     )
     mine, last = down(two_chunk, order, acts, spread, w_down)
+    last, near = lax.optimization_barrier((last, near))
     last = lax.ppermute(last, "ep", pairs(n, 3))
+    near = lax.ppermute(near, "ep", pairs(n, 1))
     returned = [mine, near, jnp.concatenate(far, axis=0), last]
     total = residual.astype(jnp.float32)
     for part in returned:

time: 154 us -> 153 us (level)
  waiting for transfers between devices: 61.9 us -> 65.6 us
  local copies, waits for them, and re-layouts: 16.9 us -> 13.6 us
    ppermute x1, waiting for transfers between devices: 0.01 us -> 7.06 us  [per_device_square(): near = lax.ppermute(near, 'ep', pairs(n, 1))]
    unnamed x29 -> x31, local copies, waits for them, and re-layouts: 5.45 us -> 2.07 us
    ppermute x1, waiting for transfers between devices: 8.56 us -> 5.19 us  [per_device_square(): last = lax.ppermute(last, 'ep', pairs(n, 3))]
  transfers between devices with their start and end apart: 32 -> 32, of which waited for: 16 -> 17; matrix products, arithmetic and copies ran while one was open for 10% -> 10% of each run, Pallas kernels for 13% -> 11%
where the time goes in v12:
time: 153 us
  waiting for transfers between devices  65.6 us (43%)
  starting transfers between devices  41.8 us (27%)
  Pallas kernels  26.6 us (17%)
  local copies, waits for them, and re-layouts  13.6 us (9%)
  other arithmetic  4.77 us (3%)
    ppermute x2, waiting for transfers between devices, per_device_square(): far = [lax.ppermute(part, 'ep', pairs(n, 2)) for part in far]  13.9 us
    ppermute x3, starting transfers between devices, per_device_square(): lax.ppermute(pieces[d], 'ep', pairs(n, d))  13.2 us
    optimization_barrier x1, local copies, waits for them, and re-layouts, per_device_square(): kept, w_gate_up = lax.optimization_barrier((kept, w_gate_up))  11.2 us
    ppermute x2, waiting for transfers between devices, per_device_square(): tokens[d] = lax.ppermute(residual, 'ep', pairs(n, d))  9.79 us
    pallas_call x4, Pallas kernels, gate_up(): call(functools.partial(gate_up_body, ds), jax.ShapeDtypeStruct((count, ro...  9.27 us
    ppermute x1, waiting for transfers between devices, per_device_square(): near = lax.ppermute(near, 'ep', pairs(n, 1))  7.06 us
    ppermute x1, waiting for transfers between devices, per_device_square(): given = lax.ppermute(early, 'ep', pairs(n, 1))  5.66 us
    pallas_call x2, Pallas kernels, down(): call(functools.partial(down_body, ds), shapes, None, grid_spec=pltpu.Pref...  5.59 us
  transfers between devices with their start and end apart: 32, of which 17 were waited for; matrix products, arithmetic and copies ran while one was open for 10% of the time, Pallas kernels for 11%

profile of v12, /device:TPU:0, one launch (start us, length us, event | category | flops | bytes accessed | tf_op | source)
XLA Modules:
  0.0 152.7 jit_solution(1497253038823642724)
XLA Ops:
  6.0 10.8 %collective-permute-start.2 = (bf16[272,128]{1,0:T(8,128)(2,1)S(1)}, bf16[272,128]{1,0:T(8,128)(2,1)S(1)}, u32[]{:S(2)}, u32[]{:S(2)}) collective-permute-start(bf16[272,128]{1,0:T(8,128)(2,1)S(1)} %get-tuple-element.60), channel_id=1, source_target_pairs={{0,4},{4,0},{8,12},{12,8},{1,5},{5,1},{9,13},{13,9},{2,6},{6,2},{1... | collective-permute-start | bytes 208904 | tf_op jit(solution)/shard_map/ppermute | solution.py:679
  16.8 2.4 %collective-permute-start.4 = (bf16[272,128]{1,0:T(8,128)(2,1)S(1)}, bf16[272,128]{1,0:T(8,128)(2,1)S(1)}, u32[]{:S(2)}, u32[]{:S(2)}) collective-permute-start(bf16[272,128]{1,0:T(8,128)(2,1)S(1)} %get-tuple-element.62), channel_id=1, source_target_pairs={{0,12},{4,8},{8,4},{12,0},{1,13},{5,9},{9,5},{13,1},{2,14},{6,10},... | collective-permute-start | bytes 208904 | tf_op jit(solution)/shard_map/ppermute | solution.py:679
  19.2 1.7 %broadcast_multiply_fusion.weight = bf16[1024,1024]{1,0:T(8,128)(2,1)S(1)} fusion(bf16[1024,1024]{1,0:T(8,128)(2,1)} %param.21, bf16[]{:T(256)} %constant.23.clone.1), kind=kLoop, calls=%fused_computation.3 | loop fusion | flops 1048576 | bytes 4194306 | tf_op jit(solution)/shard_map/mul | solution.py:683
  21.9 3.4 %collective-permute-done.3.c2.refs_4_ = bf16[272,128]{1,0:T(8,128)(2,1)S(1)} collective-permute-done((bf16[272,128]{1,0:T(8,128)(2,1)S(1)}, bf16[272,128]{1,0:T(8,128)(2,1)S(1)}, u32[]{:S(2)}, u32[]{:S(2)}) %collective-permute-start.3) | collective-permute-done | bytes 69664 | tf_op jit(solution)/shard_map/ppermute | solution.py:679
  25.3 3.4 %attention.1.a = bf16[128,1024]{1,0:T(8,128)(2,1)S(1)} custom-call(s32[2]{0:T(128)S(1)} %pad_add_fusion.here, s32[4,4]{1,0:T(4,128)S(1)} %copy-done.4, s32[8]{0:T(128)S(1)} %copy-done.6, bf16[1280,128]{1,0:T(8,128)(2,1)S(1)} %collective-permute-done.1.q, bf16[272,128]{1,0:T(8,128)(2,1)S(1)} %get-tuple-element.59.c0.refs_3_, ...), custom_call_target="tpu_custom_call" | custom-call | flops 1048576 | bytes 262144 | tf_op jit(solution)/shard_map/attention/pallas_call | solution.py:364
  28.7 5.2 %collective-permute-start.5 = (bf16[128,1024]{1,0:T(8,128)(2,1)S(1)}, bf16[128,1024]{1,0:T(8,128)(2,1)S(1)}, u32[]{:S(2)}, u32[]{:S(2)}) collective-permute-start(bf16[128,1024]{1,0:T(8,128)(2,1)S(1)} %attention.1.a), channel_id=1, source_target_pairs={{0,2},{1,3},{2,0},{3,1},{4,6},{5,7},{6,4},{7,5},{8,10},{9,11},{10,... | collective-permute-start | bytes 786440 | tf_op jit(solution)/shard_map/ppermute | solution.py:685
  33.9 4.3 %collective-permute-done.5.a = bf16[128,1024]{1,0:T(8,128)(2,1)S(1)} collective-permute-done((bf16[128,1024]{1,0:T(8,128)(2,1)S(1)}, bf16[128,1024]{1,0:T(8,128)(2,1)S(1)}, u32[]{:S(2)}, u32[]{:S(2)}) %collective-permute-start.5) | collective-permute-done | bytes 262176 | tf_op jit(solution)/shard_map/ppermute | solution.py:685
  39.6 1.8 %collective-permute-start.8 = (bf16[128,1024]{1,0:T(8,128)(2,1)S(1)}, bf16[128,1024]{1,0:T(8,128)(2,1)S(1)}, u32[]{:S(2)}, u32[]{:S(2)}) collective-permute-start(bf16[128,1024]{1,0:T(8,128)(2,1)S(1)} %get-tuple-element.75), channel_id=1, source_target_pairs={{0,4},{4,0},{8,12},{12,8},{1,5},{5,1},{9,13},{13,9},{2,6},{6,2},{1... | collective-permute-start | bytes 786440 | tf_op jit(solution)/shard_map/ppermute | solution.py:691
  42.7 5.7 %collective-permute-done.8 = bf16[128,1024]{1,0:T(8,128)(2,1)S(1)} collective-permute-done((bf16[128,1024]{1,0:T(8,128)(2,1)S(1)}, bf16[128,1024]{1,0:T(8,128)(2,1)S(1)}, u32[]{:S(2)}, u32[]{:S(2)}) %collective-permute-start.8) | collective-permute-done | bytes 262176 | tf_op jit(solution)/shard_map/ppermute | solution.py:691
  51.4 11.2 %copy.25 = bf16[4,1024,2,1024]{3,1,2,0:T(8,128)(2,1)S(1)} copy(bf16[4,1024,2,1024]{3,2,1,0:T(2,128)(2,1)} %param.24) | data formatting | bytes 33554432 | tf_op jit(solution)/shard_map/optimization_barrier | solution.py:693
  64.3 2.0 %collective-permute-start.12 = (bf16[128,1024]{1,0:T(8,128)(2,1)S(1)}, bf16[128,1024]{1,0:T(8,128)(2,1)S(1)}, u32[]{:S(2)}, u32[]{:S(2)}) collective-permute-start(bf16[128,1024]{1,0:T(8,128)(2,1)S(1)} %residual.1.refs_0_), channel_id=1, source_target_pairs={{0,8},{4,12},{8,0},{12,4},{1,9},{5,13},{9,1},{13,5},{2,10},{6,14},... | collective-permute-start | bytes 786440 | tf_op jit(solution)/shard_map/ppermute | solution.py:706
  66.4 9.8 %collective-permute-done.11.refs_0_ = bf16[128,1024]{1,0:T(8,128)(2,1)S(1)} collective-permute-done((bf16[128,1024]{1,0:T(8,128)(2,1)S(1)}, bf16[128,1024]{1,0:T(8,128)(2,1)S(1)}, u32[]{:S(2)}, u32[]{:S(2)}) %collective-permute-start.11) | collective-permute-done | bytes 262176 | tf_op jit(solution)/shard_map/ppermute | solution.py:706
  76.2 2.3 %gate_up.5 = bf16[2,128,2048]{2,1,0:T(8,128)(2,1)S(1)} custom-call(s32[2]{0:T(128)S(1)} %get-tuple-element.105.order, bf16[128,1024]{1,0:T(8,128)(2,1)S(1)} %collective-permute-done.11.refs_0_, bf16[128,1024]{1,0:T(8,128)(2,1)S(1)} %collective-permute-done.12.refs_1_, f32[1,1024]{1,0:T(1,128)S(1)} %bitcast.32, ...), custom_call_target="tpu_custom_call" | custom-call | flops 1048576 | bytes 262144 | tf_op jit(solution)/shard_map/gate_up/pallas_call | solution.py:519
  79.3 2.0 %collective-permute-start.14 = (f32[24,256]{1,0:T(8,128)S(1)}, f32[24,256]{1,0:T(8,128)S(1)}, u32[]{:S(2)}, u32[]{:S(2)}) collective-permute-start(f32[24,256]{1,0:T(8,128)S(1)} %stats.2), channel_id=1, source_target_pairs={{0,2},{1,3},{2,0},{3,1},{4,6},{5,7},{6,4},{7,5},{8,10},{9,11},{10,... | collective-permute-start | bytes 73736 | tf_op jit(solution)/shard_map/ppermute | solution.py:732
  81.3 2.3 %gate_up.4.refs_0_ = bf16[2,128,2048]{2,1,0:T(8,128)(2,1)S(1)} custom-call(s32[2]{0:T(128)S(1)} %get-tuple-element.106.order, bf16[128,1024]{1,0:T(8,128)(2,1)S(1)} %collective-permute-done.11.refs_0_, bf16[128,1024]{1,0:T(8,128)(2,1)S(1)} %collective-permute-done.12.refs_1_, f32[1,1024]{1,0:T(1,128)S(1)} %bitcast.34, ...), custom_call_target="tpu_custom_call" | custom-call | flops 1048576 | bytes 262144 | tf_op jit(solution)/shard_map/gate_up/pallas_call | solution.py:519
  83.7 1.6 %collective-permute-start.17 = (bf16[128,2048]{1,0:T(8,128)(2,1)S(1)}, bf16[128,2048]{1,0:T(8,128)(2,1)S(1)}, u32[]{:S(2)}, u32[]{:S(2)}) collective-permute-start(bf16[128,2048]{1,0:T(8,128)(2,1)S(1)} %fusion), channel_id=1, source_target_pairs={{0,2},{1,3},{2,0},{3,1},{4,6},{5,7},{6,4},{7,5},{8,10},{9,11},{10,... | collective-permute-start | bytes 1572872 | tf_op jit(solution)/shard_map/ppermute | solution.py:737
  85.3 2.4 %collective-permute-start.16 = (bf16[128,1024]{1,0:T(8,128)(2,1)S(1)}, bf16[128,1024]{1,0:T(8,128)(2,1)S(1)}, u32[]{:S(2)}, u32[]{:S(2)}) collective-permute-start(bf16[128,1024]{1,0:T(8,128)(2,1)S(1)} %collective-permute-done.12.refs_1_), channel_id=1, source_target_pairs={{0,4},{4,0},{8,12},{12,8},{1,5},{5,1},{9,13},{13,9},{2,6},{6,2},{1... | collective-permute-start | bytes 786440 | tf_op jit(solution)/shard_map/ppermute | solution.py:707
  87.7 5.5 %collective-permute-done.16.refs_1_ = bf16[128,1024]{1,0:T(8,128)(2,1)S(1)} collective-permute-done((bf16[128,1024]{1,0:T(8,128)(2,1)S(1)}, bf16[128,1024]{1,0:T(8,128)(2,1)S(1)}, u32[]{:S(2)}, u32[]{:S(2)}) %collective-permute-start.16) | collective-permute-done | bytes 262176 | tf_op jit(solution)/shard_map/ppermute | solution.py:707
  94.0 2.3 %gate_up.6 = bf16[2,128,2048]{2,1,0:T(8,128)(2,1)S(1)} custom-call(s32[2]{0:T(128)S(1)} %get-tuple-element.104.order, bf16[128,1024]{1,0:T(8,128)(2,1)S(1)} %residual.1.refs_0_, bf16[128,1024]{1,0:T(8,128)(2,1)S(1)} %collective-permute-done.16.refs_1_, f32[1,1024]{1,0:T(1,128)S(1)} %bitcast.36, bf16[4,4,64,128]{3,2,1,0:T(8,128)(2,1)S(1)} %get-tuple-element.79.refs_3_.pick, ...), custom_call_target="tpu_custom_call" | custom-call | flops 1048576 | bytes 262144 | tf_op jit(solution)/shard_map/gate_up/pallas_call | solution.py:519
  96.4 1.5 collective-permute-done.17.refs_2_
  99.5 2.3 %gate_up.7.refs_0_ = bf16[2,128,2048]{2,1,0:T(8,128)(2,1)S(1)} custom-call(s32[2]{0:T(128)S(1)} %get-tuple-element.103.order, bf16[128,1024]{1,0:T(8,128)(2,1)S(1)} %residual.1.refs_0_, bf16[128,1024]{1,0:T(8,128)(2,1)S(1)} %collective-permute-done.16.refs_1_, f32[1,1024]{1,0:T(1,128)S(1)} %bitcast.37, ...), custom_call_target="tpu_custom_call" | custom-call | flops 1048576 | bytes 262144 | tf_op jit(solution)/shard_map/gate_up/pallas_call | solution.py:519
  103.3 4.6 %collective-permute-done.20.b = bf16[128,1024]{1,0:T(8,128)(2,1)S(1)} collective-permute-done((bf16[128,1024]{1,0:T(8,128)(2,1)S(1)}, bf16[128,1024]{1,0:T(8,128)(2,1)S(1)}, u32[]{:S(2)}, u32[]{:S(2)}) %collective-permute-start.20) | collective-permute-done | bytes 262176 | tf_op jit(solution)/shard_map/ppermute | solution.py:712
  110.7 2.8 %down.2 = (bf16[128,1024]{1,0:T(8,128)(2,1)S(1)}, bf16[64,1024]{1,0:T(8,128)(2,1)S(1)}, bf16[64,1024]{1,0:T(8,128)(2,1)S(1)}) custom-call(s32[4]{0:T(128)S(1)} %broadcast_xor_fusion.order, bf16[128,1024]{1,0:T(8,128)(2,1)S(1)} %activate.2.a, bf16[128,1024]{1,0:T(8,128)(2,1)S(1)} %collective-permute-done.20.b, ...), custom_call_target="tpu_custom_call" | custom-call | flops 1048576 | bytes 262144 | tf_op jit(solution)/shard_map/down/pallas_call | solution.py:627
  113.5 2.2 %collective-permute-start.25 = (bf16[64,1024]{1,0:T(8,128)(2,1)S(1)}, bf16[64,1024]{1,0:T(8,128)(2,1)S(1)}, u32[]{:S(2)}, u32[]{:S(2)}) collective-permute-start(bf16[64,1024]{1,0:T(8,128)(2,1)S(1)} %get-tuple-element.93), channel_id=1, source_target_pairs={{0,8},{4,12},{8,0},{12,4},{1,9},{5,13},{9,1},{13,5},{2,10},{6,14},... | collective-permute-start | bytes 393224 | tf_op jit(solution)/shard_map/ppermute | solution.py:755
  116.8 6.0 %collective-permute-done.25 = bf16[64,1024]{1,0:T(8,128)(2,1)S(1)} collective-permute-done((bf16[64,1024]{1,0:T(8,128)(2,1)S(1)}, bf16[64,1024]{1,0:T(8,128)(2,1)S(1)}, u32[]{:S(2)}, u32[]{:S(2)}) %collective-permute-start.25) | collective-permute-done | bytes 131104 | tf_op jit(solution)/shard_map/ppermute | solution.py:755
  123.7 1.5 collective-permute-start.26
  125.4 7.9 %collective-permute-done.27 = bf16[64,1024]{1,0:T(8,128)(2,1)S(1)} collective-permute-done((bf16[64,1024]{1,0:T(8,128)(2,1)S(1)}, bf16[64,1024]{1,0:T(8,128)(2,1)S(1)}, u32[]{:S(2)}, u32[]{:S(2)}) %collective-permute-start.27) | collective-permute-done | bytes 131104 | tf_op jit(solution)/shard_map/ppermute | solution.py:755
  133.4 1.5 %collective-permute-done.29.d = bf16[128,1024]{1,0:T(8,128)(2,1)S(1)} collective-permute-done((bf16[128,1024]{1,0:T(8,128)(2,1)S(1)}, bf16[128,1024]{1,0:T(8,128)(2,1)S(1)}, u32[]{:S(2)}, u32[]{:S(2)}) %collective-permute-start.29) | collective-permute-done | bytes 262176 | tf_op jit(solution)/shard_map/ppermute | solution.py:715
  134.9 2.8 %down.3 = (bf16[128,1024]{1,0:T(8,128)(2,1)S(1)}, bf16[128,1024]{1,0:T(8,128)(2,1)S(1)}) custom-call(s32[4]{0:T(128)S(1)} %broadcast_xor_fusion.order, bf16[128,1024]{1,0:T(8,128)(2,1)S(1)} %activate.3.a, bf16[128,1024]{1,0:T(8,128)(2,1)S(1)} %collective-permute-done.26.b, bf16[128,1024]{1,0:T(8,128)(2,1)S(1)} %collective-permute-done.28.c, ...), custom_call_target="tpu_custom_call" | custom-call | flops 1048576 | bytes 262144 | tf_op jit(solution)/shard_map/down/pallas_call | solution.py:627
  137.8 1.8 %collective-permute-start.31 = (bf16[128,1024]{1,0:T(8,128)(2,1)S(1)}, bf16[128,1024]{1,0:T(8,128)(2,1)S(1)}, u32[]{:S(2)}, u32[]{:S(2)}) collective-permute-start(bf16[128,1024]{1,0:T(8,128)(2,1)S(1)} %get-tuple-element.102), channel_id=1, source_target_pairs={{0,12},{4,8},{8,4},{12,0},{1,13},{5,9},{9,5},{13,1},{2,14},{6,10},... | collective-permute-start | bytes 786440 | tf_op jit(solution)/shard_map/ppermute | solution.py:764
  139.5 7.1 %collective-permute-done.30 = bf16[128,1024]{1,0:T(8,128)(2,1)S(1)} collective-permute-done((bf16[128,1024]{1,0:T(8,128)(2,1)S(1)}, bf16[128,1024]{1,0:T(8,128)(2,1)S(1)}, u32[]{:S(2)}, u32[]{:S(2)}) %collective-permute-start.30) | collective-permute-done | bytes 262176 | tf_op jit(solution)/shard_map/ppermute | solution.py:765
  146.6 5.2 %collective-permute-done.31 = bf16[128,1024]{1,0:T(8,128)(2,1)S(1)} collective-permute-done((bf16[128,1024]{1,0:T(8,128)(2,1)S(1)}, bf16[128,1024]{1,0:T(8,128)(2,1)S(1)}, u32[]{:S(2)}, u32[]{:S(2)}) %collective-permute-start.31) | collective-permute-done | bytes 262176 | tf_op jit(solution)/shard_map/ppermute | solution.py:764
  (103 shorter events, 25.2 us)
Async XLA Ops:
  0.0 4.2 %collective-permute-start = (bf16[1024,128]{1,0:T(8,128)(2,1)}, bf16[1024,128]{1,0:T(8,128)(2,1)S(1)}, u32[]{:S(2)}, u32[]{:S(2)}) collective-permute-start(bf16[1024,128]{1,0:T(8,128)(2,1)} %bitcast.39), channel_id=1, source_target_pairs={{1,2},{2,1},{4,7},{7,4},{9,10},{10,9},{12,15},{15,12},{17,18},{18,... | collective-permute-start | bytes 786440 | tf_op jit(solution)/shard_map/ppermute | solution.py:202
  5.2 20.1 %collective-permute-start.1 = (bf16[1280,128]{1,0:T(8,128)(2,1)S(1)}, bf16[1280,128]{1,0:T(8,128)(2,1)S(1)}, u32[]{:S(2)}, u32[]{:S(2)}) collective-permute-start(bf16[1280,128]{1,0:T(8,128)(2,1)S(1)} %pad_maximum_fusion), channel_id=1, source_target_pairs={{0,0},{1,8},{2,6},{3,14},{4,12},{5,4},{6,10},{7,2},{8,1},{9,9},{10... | collective-permute-start | bytes 983048 | tf_op jit(solution)/shard_map/ppermute | solution.py:212
  6.0 15.9 %collective-permute-start.2 = (bf16[272,128]{1,0:T(8,128)(2,1)S(1)}, bf16[272,128]{1,0:T(8,128)(2,1)S(1)}, u32[]{:S(2)}, u32[]{:S(2)}) collective-permute-start(bf16[272,128]{1,0:T(8,128)(2,1)S(1)} %get-tuple-element.60), channel_id=1, source_target_pairs={{0,4},{4,0},{8,12},{12,8},{1,5},{5,1},{9,13},{13,9},{2,6},{6,2},{1... | collective-permute-start | bytes 208904 | tf_op jit(solution)/shard_map/ppermute | solution.py:679
  16.8 8.5 %collective-permute-start.3 = (bf16[272,128]{1,0:T(8,128)(2,1)S(1)}, bf16[272,128]{1,0:T(8,128)(2,1)S(1)}, u32[]{:S(2)}, u32[]{:S(2)}) collective-permute-start(bf16[272,128]{1,0:T(8,128)(2,1)S(1)} %get-tuple-element.61), channel_id=1, source_target_pairs={{0,8},{4,12},{8,0},{12,4},{1,9},{5,13},{9,1},{13,5},{2,10},{6,14},... | collective-permute-start | bytes 208904 | tf_op jit(solution)/shard_map/ppermute | solution.py:679
  16.8 8.5 %collective-permute-start.4 = (bf16[272,128]{1,0:T(8,128)(2,1)S(1)}, bf16[272,128]{1,0:T(8,128)(2,1)S(1)}, u32[]{:S(2)}, u32[]{:S(2)}) collective-permute-start(bf16[272,128]{1,0:T(8,128)(2,1)S(1)} %get-tuple-element.62), channel_id=1, source_target_pairs={{0,12},{4,8},{8,4},{12,0},{1,13},{5,9},{9,5},{13,1},{2,14},{6,10},... | collective-permute-start | bytes 208904 | tf_op jit(solution)/shard_map/ppermute | solution.py:679
  28.7 9.5 %collective-permute-start.5 = (bf16[128,1024]{1,0:T(8,128)(2,1)S(1)}, bf16[128,1024]{1,0:T(8,128)(2,1)S(1)}, u32[]{:S(2)}, u32[]{:S(2)}) collective-permute-start(bf16[128,1024]{1,0:T(8,128)(2,1)S(1)} %attention.1.a), channel_id=1, source_target_pairs={{0,2},{1,3},{2,0},{3,1},{4,6},{5,7},{6,4},{7,5},{8,10},{9,11},{10,... | collective-permute-start | bytes 786440 | tf_op jit(solution)/shard_map/ppermute | solution.py:685
  33.9 4.4 %collective-permute-start.7 = (bf16[128,1024]{1,0:T(8,128)(2,1)S(1)}, bf16[128,1024]{1,0:T(8,128)(2,1)S(1)}, u32[]{:S(2)}, u32[]{:S(2)}) collective-permute-start(bf16[128,1024]{1,0:T(8,128)(2,1)S(1)} %attention.1.a), channel_id=1, source_target_pairs={{0,1},{1,0},{2,3},{3,2},{4,5},{5,4},{6,7},{7,6},{8,9},{9,8},{10,11... | collective-permute-start | bytes 786440 | tf_op jit(solution)/shard_map/ppermute | solution.py:686
  38.3 3.1 %collective-permute-start.6 = (bf16[128,1024]{1,0:T(8,128)(2,1)S(1)}, bf16[128,1024]{1,0:T(8,128)(2,1)S(1)}, u32[]{:S(2)}, u32[]{:S(2)}) collective-permute-start(bf16[128,1024]{1,0:T(8,128)(2,1)S(1)} %collective-permute-done.5.a), channel_id=1, source_target_pairs={{0,1},{1,0},{2,3},{3,2},{4,5},{5,4},{6,7},{7,6},{8,9},{9,8},{10,11... | collective-permute-start | bytes 786440 | tf_op jit(solution)/shard_map/ppermute | solution.py:687
  39.6 8.8 %collective-permute-start.8 = (bf16[128,1024]{1,0:T(8,128)(2,1)S(1)}, bf16[128,1024]{1,0:T(8,128)(2,1)S(1)}, u32[]{:S(2)}, u32[]{:S(2)}) collective-permute-start(bf16[128,1024]{1,0:T(8,128)(2,1)S(1)} %get-tuple-element.75), channel_id=1, source_target_pairs={{0,4},{4,0},{8,12},{12,8},{1,5},{5,1},{9,13},{13,9},{2,6},{6,2},{1... | collective-permute-start | bytes 786440 | tf_op jit(solution)/shard_map/ppermute | solution.py:691
  48.4 14.2 %collective-permute-start.9 = (bf16[128,1024]{1,0:T(8,128)(2,1)S(1)}, bf16[128,1024]{1,0:T(8,128)(2,1)S(1)}, u32[]{:S(2)}, u32[]{:S(2)}) collective-permute-start(bf16[128,1024]{1,0:T(8,128)(2,1)S(1)} %add_convert_fusion.3), channel_id=1, source_target_pairs={{0,12},{1,13},{2,10},{3,11},{4,8},{5,9},{6,14},{7,15},{8,4},{9,5},... | collective-permute-start | bytes 786440 | tf_op jit(solution)/shard_map/ppermute | solution.py:698
  49.7 13.3 %collective-permute-start.10 = (bf16[128,1024]{1,0:T(8,128)(2,1)S(1)}, bf16[128,1024]{1,0:T(8,128)(2,1)S(1)}, u32[]{:S(2)}, u32[]{:S(2)}) collective-permute-start(bf16[128,1024]{1,0:T(8,128)(2,1)S(1)} %get-tuple-element.76), channel_id=1, source_target_pairs={{0,4},{4,0},{8,12},{12,8},{1,5},{5,1},{9,13},{13,9},{2,6},{6,2},{1... | collective-permute-start | bytes 786440 | tf_op jit(solution)/shard_map/ppermute | solution.py:698
  63.1 13.0 %collective-permute-start.11 = (bf16[128,1024]{1,0:T(8,128)(2,1)S(1)}, bf16[128,1024]{1,0:T(8,128)(2,1)S(1)}, u32[]{:S(2)}, u32[]{:S(2)}) collective-permute-start(bf16[128,1024]{1,0:T(8,128)(2,1)S(1)} %residual.1.refs_0_), channel_id=1, source_target_pairs={{0,4},{4,0},{8,12},{12,8},{1,5},{5,1},{9,13},{13,9},{2,6},{6,2},{1... | collective-permute-start | bytes 786440 | tf_op jit(solution)/shard_map/ppermute | solution.py:706
  64.3 11.8 %collective-permute-start.12 = (bf16[128,1024]{1,0:T(8,128)(2,1)S(1)}, bf16[128,1024]{1,0:T(8,128)(2,1)S(1)}, u32[]{:S(2)}, u32[]{:S(2)}) collective-permute-start(bf16[128,1024]{1,0:T(8,128)(2,1)S(1)} %residual.1.refs_0_), channel_id=1, source_target_pairs={{0,8},{4,12},{8,0},{12,4},{1,9},{5,13},{9,1},{13,5},{2,10},{6,14},... | collective-permute-start | bytes 786440 | tf_op jit(solution)/shard_map/ppermute | solution.py:706
  78.5 5.1 %collective-permute-start.13 = (bf16[2,128,2048]{2,1,0:T(8,128)(2,1)S(1)}, bf16[2,128,2048]{2,1,0:T(8,128)(2,1)S(1)}, u32[]{:S(2)}, u32[]{:S(2)}) collective-permute-start(bf16[2,128,2048]{2,1,0:T(8,128)(2,1)S(1)} %gate_up.5), channel_id=1, source_target_pairs={{0,1},{1,0},{2,3},{3,2},{4,5},{5,4},{6,7},{7,6},{8,9},{9,8},{10,11... | collective-permute-start | bytes 3145736 | tf_op jit(solution)/shard_map/ppermute | solution.py:730
  79.3 4.3 %collective-permute-start.14 = (f32[24,256]{1,0:T(8,128)S(1)}, f32[24,256]{1,0:T(8,128)S(1)}, u32[]{:S(2)}, u32[]{:S(2)}) collective-permute-start(f32[24,256]{1,0:T(8,128)S(1)} %stats.2), channel_id=1, source_target_pairs={{0,2},{1,3},{2,0},{3,1},{4,6},{5,7},{6,4},{7,5},{8,10},{9,11},{10,... | collective-permute-start | bytes 73736 | tf_op jit(solution)/shard_map/ppermute | solution.py:732
  83.7 14.1 %collective-permute-start.17 = (bf16[128,2048]{1,0:T(8,128)(2,1)S(1)}, bf16[128,2048]{1,0:T(8,128)(2,1)S(1)}, u32[]{:S(2)}, u32[]{:S(2)}) collective-permute-start(bf16[128,2048]{1,0:T(8,128)(2,1)S(1)} %fusion), channel_id=1, source_target_pairs={{0,2},{1,3},{2,0},{3,1},{4,6},{5,7},{6,4},{7,5},{8,10},{9,11},{10,... | collective-permute-start | bytes 1572872 | tf_op jit(solution)/shard_map/ppermute | solution.py:737
  85.3 7.9 %collective-permute-start.16 = (bf16[128,1024]{1,0:T(8,128)(2,1)S(1)}, bf16[128,1024]{1,0:T(8,128)(2,1)S(1)}, u32[]{:S(2)}, u32[]{:S(2)}) collective-permute-start(bf16[128,1024]{1,0:T(8,128)(2,1)S(1)} %collective-permute-done.12.refs_1_), channel_id=1, source_target_pairs={{0,4},{4,0},{8,12},{12,8},{1,5},{5,1},{9,13},{13,9},{2,6},{6,2},{1... | collective-permute-start | bytes 786440 | tf_op jit(solution)/shard_map/ppermute | solution.py:707
  87.7 6.3 %collective-permute-start.15 = (f32[24,256]{1,0:T(8,128)S(1)}, f32[24,256]{1,0:T(8,128)S(1)}, u32[]{:S(2)}, u32[]{:S(2)}) collective-permute-start(f32[24,256]{1,0:T(8,128)S(1)} %add.46), channel_id=1, source_target_pairs={{0,1},{1,0},{2,3},{3,2},{4,5},{5,4},{6,7},{7,6},{8,9},{9,8},{10,11... | collective-permute-start | bytes 73736 | tf_op jit(solution)/shard_map/ppermute | solution.py:735
  97.9 10.0 %collective-permute-start.18 = (bf16[2,128,2048]{2,1,0:T(8,128)(2,1)S(1)}, bf16[2,128,2048]{2,1,0:T(8,128)(2,1)S(1)}, u32[]{:S(2)}, u32[]{:S(2)}) collective-permute-start(bf16[2,128,2048]{2,1,0:T(8,128)(2,1)S(1)} %gate_up.6), channel_id=1, source_target_pairs={{0,1},{1,0},{2,3},{3,2},{4,5},{5,4},{6,7},{7,6},{8,9},{9,8},{10,11... | collective-permute-start | bytes 3145736 | tf_op jit(solution)/shard_map/ppermute | solution.py:745
  98.8 9.0 %collective-permute-start.20 = (bf16[128,1024]{1,0:T(8,128)(2,1)S(1)}, bf16[128,1024]{1,0:T(8,128)(2,1)S(1)}, u32[]{:S(2)}, u32[]{:S(2)}) collective-permute-start(bf16[128,1024]{1,0:T(8,128)(2,1)S(1)} %activate.2.a), channel_id=1, source_target_pairs={{0,2},{1,3},{2,0},{3,1},{4,6},{5,7},{6,4},{7,5},{8,10},{9,11},{10,... | collective-permute-start | bytes 786440 | tf_op jit(solution)/shard_map/ppermute | solution.py:712
  101.8 6.3 %collective-permute-start.19 = (f32[24,256]{1,0:T(8,128)S(1)}, f32[24,256]{1,0:T(8,128)S(1)}, u32[]{:S(2)}, u32[]{:S(2)}) collective-permute-start(f32[24,256]{1,0:T(8,128)S(1)} %stats.3), channel_id=1, source_target_pairs={{0,2},{1,3},{2,0},{3,1},{4,6},{5,7},{6,4},{7,5},{8,10},{9,11},{10,... | collective-permute-start | bytes 73736 | tf_op jit(solution)/shard_map/ppermute | solution.py:744
  108.1 14.7 %collective-permute-start.22 = (bf16[128,2048]{1,0:T(8,128)(2,1)S(1)}, bf16[128,2048]{1,0:T(8,128)(2,1)S(1)}, u32[]{:S(2)}, u32[]{:S(2)}) collective-permute-start(bf16[128,2048]{1,0:T(8,128)(2,1)S(1)} %fusion.1), channel_id=1, source_target_pairs={{0,2},{1,3},{2,0},{3,1},{4,6},{5,7},{6,4},{7,5},{8,10},{9,11},{10,... | collective-permute-start | bytes 1572872 | tf_op jit(solution)/shard_map/ppermute | solution.py:753
  108.7 1.5 %collective-permute-start.23 = (bf16[128,1024]{1,0:T(8,128)(2,1)S(1)}, bf16[128,1024]{1,0:T(8,128)(2,1)S(1)}, u32[]{:S(2)}, u32[]{:S(2)}) collective-permute-start(bf16[128,1024]{1,0:T(8,128)(2,1)S(1)} %activate.2.a), channel_id=1, source_target_pairs={{0,1},{1,0},{2,3},{3,2},{4,5},{5,4},{6,7},{7,6},{8,9},{9,8},{10,11... | collective-permute-start | bytes 786440 | tf_op jit(solution)/shard_map/ppermute | solution.py:714
  108.7 1.9 %collective-permute-start.24 = (bf16[128,1024]{1,0:T(8,128)(2,1)S(1)}, bf16[128,1024]{1,0:T(8,128)(2,1)S(1)}, u32[]{:S(2)}, u32[]{:S(2)}) collective-permute-start(bf16[128,1024]{1,0:T(8,128)(2,1)S(1)} %collective-permute-done.20.b), channel_id=1, source_target_pairs={{0,1},{1,0},{2,3},{3,2},{4,5},{5,4},{6,7},{7,6},{8,9},{9,8},{10,11... | collective-permute-start | bytes 786440 | tf_op jit(solution)/shard_map/ppermute | solution.py:752
  113.5 9.3 %collective-permute-start.25 = (bf16[64,1024]{1,0:T(8,128)(2,1)S(1)}, bf16[64,1024]{1,0:T(8,128)(2,1)S(1)}, u32[]{:S(2)}, u32[]{:S(2)}) collective-permute-start(bf16[64,1024]{1,0:T(8,128)(2,1)S(1)} %get-tuple-element.93), channel_id=1, source_target_pairs={{0,8},{4,12},{8,0},{12,4},{1,9},{5,13},{9,1},{13,5},{2,10},{6,14},... | collective-permute-start | bytes 393224 | tf_op jit(solution)/shard_map/ppermute | solution.py:755
  115.6 1.2 collective-permute-start.21
  123.7 9.6 %collective-permute-start.26 = (bf16[128,1024]{1,0:T(8,128)(2,1)S(1)}, bf16[128,1024]{1,0:T(8,128)(2,1)S(1)}, u32[]{:S(2)}, u32[]{:S(2)}) collective-permute-start(bf16[128,1024]{1,0:T(8,128)(2,1)S(1)} %activate.3.a), channel_id=1, source_target_pairs={{0,2},{1,3},{2,0},{3,1},{4,6},{5,7},{6,4},{7,5},{8,10},{9,11},{10,... | collective-permute-start | bytes 786440 | tf_op jit(solution)/shard_map/ppermute | solution.py:712
  125.2 8.1 %collective-permute-start.27 = (bf16[64,1024]{1,0:T(8,128)(2,1)S(1)}, bf16[64,1024]{1,0:T(8,128)(2,1)S(1)}, u32[]{:S(2)}, u32[]{:S(2)}) collective-permute-start(bf16[64,1024]{1,0:T(8,128)(2,1)S(1)} %get-tuple-element.95), channel_id=1, source_target_pairs={{0,8},{4,12},{8,0},{12,4},{1,9},{5,13},{9,1},{13,5},{2,10},{6,14},... | collective-permute-start | bytes 393224 | tf_op jit(solution)/shard_map/ppermute | solution.py:755
  125.4 8.0 %collective-permute-start.28 = (bf16[128,1024]{1,0:T(8,128)(2,1)S(1)}, bf16[128,1024]{1,0:T(8,128)(2,1)S(1)}, u32[]{:S(2)}, u32[]{:S(2)}) collective-permute-start(bf16[128,1024]{1,0:T(8,128)(2,1)S(1)} %activate.3.a), channel_id=1, source_target_pairs={{0,1},{1,0},{2,3},{3,2},{4,5},{5,4},{6,7},{7,6},{8,9},{9,8},{10,11... | collective-permute-start | bytes 786440 | tf_op jit(solution)/shard_map/ppermute | solution.py:714
  133.3 1.5 %collective-permute-start.29 = (bf16[128,1024]{1,0:T(8,128)(2,1)S(1)}, bf16[128,1024]{1,0:T(8,128)(2,1)S(1)}, u32[]{:S(2)}, u32[]{:S(2)}) collective-permute-start(bf16[128,1024]{1,0:T(8,128)(2,1)S(1)} %collective-permute-done.26.b), channel_id=1, source_target_pairs={{0,1},{1,0},{2,3},{3,2},{4,5},{5,4},{6,7},{7,6},{8,9},{9,8},{10,11... | collective-permute-start | bytes 786440 | tf_op jit(solution)/shard_map/ppermute | solution.py:715
  137.7 8.9 %collective-permute-start.30 = (bf16[128,1024]{1,0:T(8,128)(2,1)S(1)}, bf16[128,1024]{1,0:T(8,128)(2,1)S(1)}, u32[]{:S(2)}, u32[]{:S(2)}) collective-permute-start(bf16[128,1024]{1,0:T(8,128)(2,1)S(1)} %get-tuple-element.100), channel_id=1, source_target_pairs={{0,4},{4,0},{8,12},{12,8},{1,5},{5,1},{9,13},{13,9},{2,6},{6,2},{1... | collective-permute-start | bytes 786440 | tf_op jit(solution)/shard_map/ppermute | solution.py:765
  137.8 14.0 %collective-permute-start.31 = (bf16[128,1024]{1,0:T(8,128)(2,1)S(1)}, bf16[128,1024]{1,0:T(8,128)(2,1)S(1)}, u32[]{:S(2)}, u32[]{:S(2)}) collective-permute-start(bf16[128,1024]{1,0:T(8,128)(2,1)S(1)} %get-tuple-element.102), channel_id=1, source_target_pairs={{0,12},{4,8},{8,4},{12,0},{1,13},{5,9},{9,5},{13,1},{2,14},{6,10},... | collective-permute-start | bytes 786440 | tf_op jit(solution)/shard_map/ppermute | solution.py:764
  (14 other events, 165.5 us)

commit v13 on v12

--- a/solution.py
+++ b/solution.py
@@ -607,13 +607,11 @@
         for k, d in enumerate(ds):
             rows = results[k].reshape(-1, results.shape[3])
             block = dot(spread[d], rows).astype(jnp.bfloat16)
-            if k < len(ds) - 1:
-                outs[k][...] = block
-            elif len(outs) == len(ds):
+            if len(outs) == len(ds):
                 outs[k][...] = block
             else:
-                outs[k][...] = block[:half]
-                outs[k + 1][...] = block[half:]
+                outs[2 * k][...] = block[:half]
+                outs[2 * k + 1][...] = block[half:]
 
 
 def down(ds, order, acts, spread, weight, halved=False):
@@ -622,7 +620,7 @@
     length = spread.shape[1]
     shape = jax.ShapeDtypeStruct((length, width), jnp.bfloat16)
     half = jax.ShapeDtypeStruct((length // 2, width), jnp.bfloat16)
-    shapes = [shape] * (len(ds) - 1) + [half] * 2 if halved else [shape] * len(ds)
+    shapes = [half] * (2 * len(ds)) if halved else [shape] * len(ds)
     whole = lambda rank: lambda i, order: (0,) * rank
     return call(
         functools.partial(down_body, ds),
@@ -751,19 +749,19 @@
     stats_near = lax.ppermute(stats_2, "tp", pairs(n, 1))
     acts[3] = lax.ppermute(acts[1], "tp", pairs(n, 1))
     across = lax.ppermute(far_sum, "tp", pairs(n, 2))
-    near, *far = down(one_chunk, order, acts, spread, w_down, halved=True)
-    far = [lax.ppermute(part, "ep", pairs(n, 2)) for part in far]
-    across, far[0] = lax.optimization_barrier((across, far[0]))
+    parts = down(one_chunk, order, acts, spread, w_down, halved=True)
+    far = [lax.ppermute(part, "ep", pairs(n, 2)) for part in parts[2:]]
+    near = [lax.ppermute(part, "ep", pairs(n, 1)) for part in parts[:2]]
+    across, far[0], near[0] = lax.optimization_barrier((across, far[0], near[0]))
     sums = [(kept_2, taken_2, across)]
     stats_2 = stats_2 + stats_near
     acts = spread_act(
-        activate((two_chunk,), features, here, sums, pick, stats_2, pieces, 1 << 32), far[1:]
+        activate((two_chunk,), features, here, sums, pick, stats_2, pieces, 1 << 32),
+        (far[1], near[1]),
     )
     mine, last = down(two_chunk, order, acts, spread, w_down)
-    last, near = lax.optimization_barrier((last, near))
     last = lax.ppermute(last, "ep", pairs(n, 3))
-    near = lax.ppermute(near, "ep", pairs(n, 1))
-    returned = [mine, near, jnp.concatenate(far, axis=0), last]
+    returned = [mine, jnp.concatenate(near, axis=0), jnp.concatenate(far, axis=0), last]
     total = residual.astype(jnp.float32)
     for part in returned:
         total = total + part.astype(jnp.float32)

time: 153 us -> 152 us (level); the launches traced: 153 us -> 149 us
  waiting for transfers between devices: 65.6 us -> 53.8 us
  starting transfers between devices: 41.8 us -> 50 us
    ppermute x3 -> x4, waiting for transfers between devices: 21 us -> 7.32 us  [the longest x2 6.89 us: per_device_square(): far = [lax.ppermute(part, 'ep', pairs(n, 2)) for part in parts[2:]]]
    ppermute x3 -> x4, starting transfers between devices: 2.42 us -> 9.21 us  [the longest x2 4.75 us: per_device_square(): near = [lax.ppermute(part, 'ep', pairs(n, 1)) for part in parts[:2]]]
    ppermute x1, waiting for transfers between devices: 5.19 us -> 7.08 us  [per_device_square(): last = lax.ppermute(last, 'ep', pairs(n, 3))]
  transfers between devices with their start and end apart: 32 -> 33, of which waited for: 17 -> 18; matrix products, arithmetic and copies ran while one was open for 10% -> 10% of each run, Pallas kernels for 11% -> 11%
where the time goes in v13:
time: 152 us; the launch traced here: 149 us
  waiting for transfers between devices  53.8 us (35%)
  starting transfers between devices  50 us (33%)
  Pallas kernels  26.7 us (18%)
  local copies, waits for them, and re-layouts  13.6 us (9%)
  other arithmetic  4.77 us (3%)
    ppermute x3, starting transfers between devices, per_device_square(): lax.ppermute(pieces[d], 'ep', pairs(n, d))  13.2 us
    optimization_barrier x1, local copies, waits for them, and re-layouts, per_device_square(): kept, w_gate_up = lax.optimization_barrier((kept, w_gate_up))  11.2 us
    ppermute x2, waiting for transfers between devices, per_device_square(): tokens[d] = lax.ppermute(residual, 'ep', pairs(n, d))  9.79 us
    pallas_call x4, Pallas kernels, gate_up(): call(functools.partial(gate_up_body, ds), jax.ShapeDtypeStruct((count, ro...  9.27 us
    ppermute x1, waiting for transfers between devices, per_device_square(): last = lax.ppermute(last, 'ep', pairs(n, 3))  7.08 us
    ppermute x2, waiting for transfers between devices, per_device_square(): far = [lax.ppermute(part, 'ep', pairs(n, 2)) for part in parts[2:]]  6.89 us
    ppermute x1, waiting for transfers between devices, per_device_square(): given = lax.ppermute(early, 'ep', pairs(n, 1))  5.66 us
    pallas_call x2, Pallas kernels, down(): call(functools.partial(down_body, ds), shapes, None, grid_spec=pltpu.Pref...  5.61 us
  transfers between devices with their start and end apart: 33, of which 18 were waited for; matrix products, arithmetic and copies ran while one was open for 10% of the time, Pallas kernels for 11%

profile of v13, /device:TPU:0, one launch (start us, length us, event | category | flops | bytes accessed | tf_op | source)
XLA Modules:
  0.0 149.2 jit_solution(9717909062119083585)
XLA Ops:
  6.0 10.8 %collective-permute-start.2 = (bf16[272,128]{1,0:T(8,128)(2,1)S(1)}, bf16[272,128]{1,0:T(8,128)(2,1)S(1)}, u32[]{:S(2)}, u32[]{:S(2)}) collective-permute-start(bf16[272,128]{1,0:T(8,128)(2,1)S(1)} %get-tuple-element.60), channel_id=1, source_target_pairs={{0,4},{4,0},{8,12},{12,8},{1,5},{5,1},{9,13},{13,9},{2,6},{6,2},{1... | collective-permute-start | bytes 208904 | tf_op jit(solution)/shard_map/ppermute | solution.py:677
  16.8 2.4 %collective-permute-start.4 = (bf16[272,128]{1,0:T(8,128)(2,1)S(1)}, bf16[272,128]{1,0:T(8,128)(2,1)S(1)}, u32[]{:S(2)}, u32[]{:S(2)}) collective-permute-start(bf16[272,128]{1,0:T(8,128)(2,1)S(1)} %get-tuple-element.62), channel_id=1, source_target_pairs={{0,12},{4,8},{8,4},{12,0},{1,13},{5,9},{9,5},{13,1},{2,14},{6,10},... | collective-permute-start | bytes 208904 | tf_op jit(solution)/shard_map/ppermute | solution.py:677
  19.2 1.7 %broadcast_multiply_fusion.weight = bf16[1024,1024]{1,0:T(8,128)(2,1)S(1)} fusion(bf16[1024,1024]{1,0:T(8,128)(2,1)} %param.21, bf16[]{:T(256)} %constant.23.clone.1), kind=kLoop, calls=%fused_computation.3 | loop fusion | flops 1048576 | bytes 4194306 | tf_op jit(solution)/shard_map/mul | solution.py:681
  21.9 3.4 %collective-permute-done.3.c2.refs_4_ = bf16[272,128]{1,0:T(8,128)(2,1)S(1)} collective-permute-done((bf16[272,128]{1,0:T(8,128)(2,1)S(1)}, bf16[272,128]{1,0:T(8,128)(2,1)S(1)}, u32[]{:S(2)}, u32[]{:S(2)}) %collective-permute-start.3) | collective-permute-done | bytes 69664 | tf_op jit(solution)/shard_map/ppermute | solution.py:677
  25.3 3.4 %attention.1.a = bf16[128,1024]{1,0:T(8,128)(2,1)S(1)} custom-call(s32[2]{0:T(128)S(1)} %pad_add_fusion.here, s32[4,4]{1,0:T(4,128)S(1)} %copy-done.4, s32[8]{0:T(128)S(1)} %copy-done.6, bf16[1280,128]{1,0:T(8,128)(2,1)S(1)} %collective-permute-done.1.q, bf16[272,128]{1,0:T(8,128)(2,1)S(1)} %get-tuple-element.59.c0.refs_3_, ...), custom_call_target="tpu_custom_call" | custom-call | flops 1048576 | bytes 262144 | tf_op jit(solution)/shard_map/attention/pallas_call | solution.py:364
  28.7 5.2 %collective-permute-start.5 = (bf16[128,1024]{1,0:T(8,128)(2,1)S(1)}, bf16[128,1024]{1,0:T(8,128)(2,1)S(1)}, u32[]{:S(2)}, u32[]{:S(2)}) collective-permute-start(bf16[128,1024]{1,0:T(8,128)(2,1)S(1)} %attention.1.a), channel_id=1, source_target_pairs={{0,2},{1,3},{2,0},{3,1},{4,6},{5,7},{6,4},{7,5},{8,10},{9,11},{10,... | collective-permute-start | bytes 786440 | tf_op jit(solution)/shard_map/ppermute | solution.py:683
  33.9 4.3 %collective-permute-done.5.a = bf16[128,1024]{1,0:T(8,128)(2,1)S(1)} collective-permute-done((bf16[128,1024]{1,0:T(8,128)(2,1)S(1)}, bf16[128,1024]{1,0:T(8,128)(2,1)S(1)}, u32[]{:S(2)}, u32[]{:S(2)}) %collective-permute-start.5) | collective-permute-done | bytes 262176 | tf_op jit(solution)/shard_map/ppermute | solution.py:683
  39.6 1.8 %collective-permute-start.8 = (bf16[128,1024]{1,0:T(8,128)(2,1)S(1)}, bf16[128,1024]{1,0:T(8,128)(2,1)S(1)}, u32[]{:S(2)}, u32[]{:S(2)}) collective-permute-start(bf16[128,1024]{1,0:T(8,128)(2,1)S(1)} %get-tuple-element.75), channel_id=1, source_target_pairs={{0,4},{4,0},{8,12},{12,8},{1,5},{5,1},{9,13},{13,9},{2,6},{6,2},{1... | collective-permute-start | bytes 786440 | tf_op jit(solution)/shard_map/ppermute | solution.py:689
  42.7 5.7 %collective-permute-done.8 = bf16[128,1024]{1,0:T(8,128)(2,1)S(1)} collective-permute-done((bf16[128,1024]{1,0:T(8,128)(2,1)S(1)}, bf16[128,1024]{1,0:T(8,128)(2,1)S(1)}, u32[]{:S(2)}, u32[]{:S(2)}) %collective-permute-start.8) | collective-permute-done | bytes 262176 | tf_op jit(solution)/shard_map/ppermute | solution.py:689
  51.4 11.2 %copy.25 = bf16[4,1024,2,1024]{3,1,2,0:T(8,128)(2,1)S(1)} copy(bf16[4,1024,2,1024]{3,2,1,0:T(2,128)(2,1)} %param.24) | data formatting | bytes 33554432 | tf_op jit(solution)/shard_map/optimization_barrier | solution.py:691
  64.3 2.0 %collective-permute-start.12 = (bf16[128,1024]{1,0:T(8,128)(2,1)S(1)}, bf16[128,1024]{1,0:T(8,128)(2,1)S(1)}, u32[]{:S(2)}, u32[]{:S(2)}) collective-permute-start(bf16[128,1024]{1,0:T(8,128)(2,1)S(1)} %residual.1.refs_0_), channel_id=1, source_target_pairs={{0,8},{4,12},{8,0},{12,4},{1,9},{5,13},{9,1},{13,5},{2,10},{6,14},... | collective-permute-start | bytes 786440 | tf_op jit(solution)/shard_map/ppermute | solution.py:704
  66.4 9.8 %collective-permute-done.11.refs_0_ = bf16[128,1024]{1,0:T(8,128)(2,1)S(1)} collective-permute-done((bf16[128,1024]{1,0:T(8,128)(2,1)S(1)}, bf16[128,1024]{1,0:T(8,128)(2,1)S(1)}, u32[]{:S(2)}, u32[]{:S(2)}) %collective-permute-start.11) | collective-permute-done | bytes 262176 | tf_op jit(solution)/shard_map/ppermute | solution.py:704
  76.2 2.3 %gate_up.5 = bf16[2,128,2048]{2,1,0:T(8,128)(2,1)S(1)} custom-call(s32[2]{0:T(128)S(1)} %get-tuple-element.105.order, bf16[128,1024]{1,0:T(8,128)(2,1)S(1)} %collective-permute-done.11.refs_0_, bf16[128,1024]{1,0:T(8,128)(2,1)S(1)} %collective-permute-done.12.refs_1_, f32[1,1024]{1,0:T(1,128)S(1)} %bitcast.32, ...), custom_call_target="tpu_custom_call" | custom-call | flops 1048576 | bytes 262144 | tf_op jit(solution)/shard_map/gate_up/pallas_call | solution.py:519
  79.3 2.0 %collective-permute-start.14 = (f32[24,256]{1,0:T(8,128)S(1)}, f32[24,256]{1,0:T(8,128)S(1)}, u32[]{:S(2)}, u32[]{:S(2)}) collective-permute-start(f32[24,256]{1,0:T(8,128)S(1)} %stats.2), channel_id=1, source_target_pairs={{0,2},{1,3},{2,0},{3,1},{4,6},{5,7},{6,4},{7,5},{8,10},{9,11},{10,... | collective-permute-start | bytes 73736 | tf_op jit(solution)/shard_map/ppermute | solution.py:730
  81.3 2.3 %gate_up.4.refs_0_ = bf16[2,128,2048]{2,1,0:T(8,128)(2,1)S(1)} custom-call(s32[2]{0:T(128)S(1)} %get-tuple-element.106.order, bf16[128,1024]{1,0:T(8,128)(2,1)S(1)} %collective-permute-done.11.refs_0_, bf16[128,1024]{1,0:T(8,128)(2,1)S(1)} %collective-permute-done.12.refs_1_, f32[1,1024]{1,0:T(1,128)S(1)} %bitcast.34, ...), custom_call_target="tpu_custom_call" | custom-call | flops 1048576 | bytes 262144 | tf_op jit(solution)/shard_map/gate_up/pallas_call | solution.py:519
  83.7 1.6 %collective-permute-start.17 = (bf16[128,2048]{1,0:T(8,128)(2,1)S(1)}, bf16[128,2048]{1,0:T(8,128)(2,1)S(1)}, u32[]{:S(2)}, u32[]{:S(2)}) collective-permute-start(bf16[128,2048]{1,0:T(8,128)(2,1)S(1)} %fusion), channel_id=1, source_target_pairs={{0,2},{1,3},{2,0},{3,1},{4,6},{5,7},{6,4},{7,5},{8,10},{9,11},{10,... | collective-permute-start | bytes 1572872 | tf_op jit(solution)/shard_map/ppermute | solution.py:735
  85.3 2.4 %collective-permute-start.16 = (bf16[128,1024]{1,0:T(8,128)(2,1)S(1)}, bf16[128,1024]{1,0:T(8,128)(2,1)S(1)}, u32[]{:S(2)}, u32[]{:S(2)}) collective-permute-start(bf16[128,1024]{1,0:T(8,128)(2,1)S(1)} %collective-permute-done.12.refs_1_), channel_id=1, source_target_pairs={{0,4},{4,0},{8,12},{12,8},{1,5},{5,1},{9,13},{13,9},{2,6},{6,2},{1... | collective-permute-start | bytes 786440 | tf_op jit(solution)/shard_map/ppermute | solution.py:705
  87.7 5.5 %collective-permute-done.16.refs_1_ = bf16[128,1024]{1,0:T(8,128)(2,1)S(1)} collective-permute-done((bf16[128,1024]{1,0:T(8,128)(2,1)S(1)}, bf16[128,1024]{1,0:T(8,128)(2,1)S(1)}, u32[]{:S(2)}, u32[]{:S(2)}) %collective-permute-start.16) | collective-permute-done | bytes 262176 | tf_op jit(solution)/shard_map/ppermute | solution.py:705
  94.0 2.3 %gate_up.6 = bf16[2,128,2048]{2,1,0:T(8,128)(2,1)S(1)} custom-call(s32[2]{0:T(128)S(1)} %get-tuple-element.104.order, bf16[128,1024]{1,0:T(8,128)(2,1)S(1)} %residual.1.refs_0_, bf16[128,1024]{1,0:T(8,128)(2,1)S(1)} %collective-permute-done.16.refs_1_, f32[1,1024]{1,0:T(1,128)S(1)} %bitcast.36, bf16[4,4,64,128]{3,2,1,0:T(8,128)(2,1)S(1)} %get-tuple-element.79.refs_3_.pick, ...), custom_call_target="tpu_custom_call" | custom-call | flops 1048576 | bytes 262144 | tf_op jit(solution)/shard_map/gate_up/pallas_call | solution.py:519
  99.5 2.3 %gate_up.7.refs_0_ = bf16[2,128,2048]{2,1,0:T(8,128)(2,1)S(1)} custom-call(s32[2]{0:T(128)S(1)} %get-tuple-element.103.order, bf16[128,1024]{1,0:T(8,128)(2,1)S(1)} %residual.1.refs_0_, bf16[128,1024]{1,0:T(8,128)(2,1)S(1)} %collective-permute-done.16.refs_1_, f32[1,1024]{1,0:T(1,128)S(1)} %bitcast.37, ...), custom_call_target="tpu_custom_call" | custom-call | flops 1048576 | bytes 262144 | tf_op jit(solution)/shard_map/gate_up/pallas_call | solution.py:519
  103.3 4.6 %collective-permute-done.20.b = bf16[128,1024]{1,0:T(8,128)(2,1)S(1)} collective-permute-done((bf16[128,1024]{1,0:T(8,128)(2,1)S(1)}, bf16[128,1024]{1,0:T(8,128)(2,1)S(1)}, u32[]{:S(2)}, u32[]{:S(2)}) %collective-permute-start.20) | collective-permute-done | bytes 262176 | tf_op jit(solution)/shard_map/ppermute | solution.py:710
  110.7 2.8 %down.2 = (bf16[64,1024]{1,0:T(8,128)(2,1)S(1)}, bf16[64,1024]{1,0:T(8,128)(2,1)S(1)}, bf16[64,1024]{1,0:T(8,128)(2,1)S(1)}, bf16[64,1024]{1,0:T(8,128)(2,1)S(1)}) custom-call(s32[4]{0:T(128)S(1)} %broadcast_xor_fusion.order, bf16[128,1024]{1,0:T(8,128)(2,1)S(1)} %activate.2.a, bf16[128,1024]{1,0:T(8,128)(2,1)S(1)} %collective-permute-done.20.b, ...), custom_call_target="tpu_custom_call" | custom-call | flops 1048576 | bytes 262144 | tf_op jit(solution)/shard_map/down/pallas_call | solution.py:625
  113.5 2.2 %collective-permute-start.25 = (bf16[64,1024]{1,0:T(8,128)(2,1)S(1)}, bf16[64,1024]{1,0:T(8,128)(2,1)S(1)}, u32[]{:S(2)}, u32[]{:S(2)}) collective-permute-start(bf16[64,1024]{1,0:T(8,128)(2,1)S(1)} %get-tuple-element.93), channel_id=1, source_target_pairs={{0,8},{4,12},{8,0},{12,4},{1,9},{5,13},{9,1},{13,5},{2,10},{6,14},... | collective-permute-start | bytes 393224 | tf_op jit(solution)/shard_map/ppermute | solution.py:753
  115.6 3.0 %collective-permute-start.26 = (bf16[64,1024]{1,0:T(8,128)(2,1)S(1)}, bf16[64,1024]{1,0:T(8,128)(2,1)S(1)}, u32[]{:S(2)}, u32[]{:S(2)}) collective-permute-start(bf16[64,1024]{1,0:T(8,128)(2,1)S(1)} %get-tuple-element.94), channel_id=1, source_target_pairs={{0,4},{4,0},{8,12},{12,8},{1,5},{5,1},{9,13},{13,9},{2,6},{6,2},{1... | collective-permute-start | bytes 393224 | tf_op jit(solution)/shard_map/ppermute | solution.py:754
  119.8 3.1 %collective-permute-done.25 = bf16[64,1024]{1,0:T(8,128)(2,1)S(1)} collective-permute-done((bf16[64,1024]{1,0:T(8,128)(2,1)S(1)}, bf16[64,1024]{1,0:T(8,128)(2,1)S(1)}, u32[]{:S(2)}, u32[]{:S(2)}) %collective-permute-start.25) | collective-permute-done | bytes 131104 | tf_op jit(solution)/shard_map/ppermute | solution.py:753
  125.4 2.3 %collective-permute-start.28 = (bf16[64,1024]{1,0:T(8,128)(2,1)S(1)}, bf16[64,1024]{1,0:T(8,128)(2,1)S(1)}, u32[]{:S(2)}, u32[]{:S(2)}) collective-permute-start(bf16[64,1024]{1,0:T(8,128)(2,1)S(1)} %get-tuple-element.96), channel_id=1, source_target_pairs={{0,8},{4,12},{8,0},{12,4},{1,9},{5,13},{9,1},{13,5},{2,10},{6,14},... | collective-permute-start | bytes 393224 | tf_op jit(solution)/shard_map/ppermute | solution.py:753
  127.7 1.8 %collective-permute-start.29 = (bf16[64,1024]{1,0:T(8,128)(2,1)S(1)}, bf16[64,1024]{1,0:T(8,128)(2,1)S(1)}, u32[]{:S(2)}, u32[]{:S(2)}) collective-permute-start(bf16[64,1024]{1,0:T(8,128)(2,1)S(1)} %get-tuple-element.97), channel_id=1, source_target_pairs={{0,4},{4,0},{8,12},{12,8},{1,5},{5,1},{9,13},{13,9},{2,6},{6,2},{1... | collective-permute-start | bytes 393224 | tf_op jit(solution)/shard_map/ppermute | solution.py:754
  129.5 3.8 %collective-permute-done.28 = bf16[64,1024]{1,0:T(8,128)(2,1)S(1)} collective-permute-done((bf16[64,1024]{1,0:T(8,128)(2,1)S(1)}, bf16[64,1024]{1,0:T(8,128)(2,1)S(1)}, u32[]{:S(2)}, u32[]{:S(2)}) %collective-permute-start.28) | collective-permute-done | bytes 131104 | tf_op jit(solution)/shard_map/ppermute | solution.py:753
  133.6 1.5 %collective-permute-done.31.d = bf16[128,1024]{1,0:T(8,128)(2,1)S(1)} collective-permute-done((bf16[128,1024]{1,0:T(8,128)(2,1)S(1)}, bf16[128,1024]{1,0:T(8,128)(2,1)S(1)}, u32[]{:S(2)}, u32[]{:S(2)}) %collective-permute-start.31) | collective-permute-done | bytes 262176 | tf_op jit(solution)/shard_map/ppermute | solution.py:713
  135.2 2.8 %down.3 = (bf16[128,1024]{1,0:T(8,128)(2,1)S(1)}, bf16[128,1024]{1,0:T(8,128)(2,1)S(1)}) custom-call(s32[4]{0:T(128)S(1)} %broadcast_xor_fusion.order, bf16[128,1024]{1,0:T(8,128)(2,1)S(1)} %activate.3.a, bf16[128,1024]{1,0:T(8,128)(2,1)S(1)} %collective-permute-done.27.b, bf16[128,1024]{1,0:T(8,128)(2,1)S(1)} %collective-permute-done.30.c, ...), custom_call_target="tpu_custom_call" | custom-call | flops 1048576 | bytes 262144 | tf_op jit(solution)/shard_map/down/pallas_call | solution.py:625
  138.0 3.2 %collective-permute-start.32 = (bf16[128,1024]{1,0:T(8,128)(2,1)S(1)}, bf16[128,1024]{1,0:T(8,128)(2,1)S(1)}, u32[]{:S(2)}, u32[]{:S(2)}) collective-permute-start(bf16[128,1024]{1,0:T(8,128)(2,1)S(1)} %get-tuple-element.102), channel_id=1, source_target_pairs={{0,12},{4,8},{8,4},{12,0},{1,13},{5,9},{9,5},{13,1},{2,14},{6,10},... | collective-permute-start | bytes 786440 | tf_op jit(solution)/shard_map/ppermute | solution.py:763
  141.2 7.1 %collective-permute-done.32 = bf16[128,1024]{1,0:T(8,128)(2,1)S(1)} collective-permute-done((bf16[128,1024]{1,0:T(8,128)(2,1)S(1)}, bf16[128,1024]{1,0:T(8,128)(2,1)S(1)}, u32[]{:S(2)}, u32[]{:S(2)}) %collective-permute-start.32) | collective-permute-done | bytes 262176 | tf_op jit(solution)/shard_map/ppermute | solution.py:763
  (105 shorter events, 28.3 us)
Async XLA Ops:
  0.0 4.2 %collective-permute-start = (bf16[1024,128]{1,0:T(8,128)(2,1)}, bf16[1024,128]{1,0:T(8,128)(2,1)S(1)}, u32[]{:S(2)}, u32[]{:S(2)}) collective-permute-start(bf16[1024,128]{1,0:T(8,128)(2,1)} %bitcast.39), channel_id=1, source_target_pairs={{1,2},{2,1},{4,7},{7,4},{9,10},{10,9},{12,15},{15,12},{17,18},{18,... | collective-permute-start | bytes 786440 | tf_op jit(solution)/shard_map/ppermute | solution.py:202
  5.2 20.1 %collective-permute-start.1 = (bf16[1280,128]{1,0:T(8,128)(2,1)S(1)}, bf16[1280,128]{1,0:T(8,128)(2,1)S(1)}, u32[]{:S(2)}, u32[]{:S(2)}) collective-permute-start(bf16[1280,128]{1,0:T(8,128)(2,1)S(1)} %pad_maximum_fusion), channel_id=1, source_target_pairs={{0,0},{1,8},{2,6},{3,14},{4,12},{5,4},{6,10},{7,2},{8,1},{9,9},{10... | collective-permute-start | bytes 983048 | tf_op jit(solution)/shard_map/ppermute | solution.py:212
  6.0 15.9 %collective-permute-start.2 = (bf16[272,128]{1,0:T(8,128)(2,1)S(1)}, bf16[272,128]{1,0:T(8,128)(2,1)S(1)}, u32[]{:S(2)}, u32[]{:S(2)}) collective-permute-start(bf16[272,128]{1,0:T(8,128)(2,1)S(1)} %get-tuple-element.60), channel_id=1, source_target_pairs={{0,4},{4,0},{8,12},{12,8},{1,5},{5,1},{9,13},{13,9},{2,6},{6,2},{1... | collective-permute-start | bytes 208904 | tf_op jit(solution)/shard_map/ppermute | solution.py:677
  16.8 8.5 %collective-permute-start.3 = (bf16[272,128]{1,0:T(8,128)(2,1)S(1)}, bf16[272,128]{1,0:T(8,128)(2,1)S(1)}, u32[]{:S(2)}, u32[]{:S(2)}) collective-permute-start(bf16[272,128]{1,0:T(8,128)(2,1)S(1)} %get-tuple-element.61), channel_id=1, source_target_pairs={{0,8},{4,12},{8,0},{12,4},{1,9},{5,13},{9,1},{13,5},{2,10},{6,14},... | collective-permute-start | bytes 208904 | tf_op jit(solution)/shard_map/ppermute | solution.py:677
  16.8 8.5 %collective-permute-start.4 = (bf16[272,128]{1,0:T(8,128)(2,1)S(1)}, bf16[272,128]{1,0:T(8,128)(2,1)S(1)}, u32[]{:S(2)}, u32[]{:S(2)}) collective-permute-start(bf16[272,128]{1,0:T(8,128)(2,1)S(1)} %get-tuple-element.62), channel_id=1, source_target_pairs={{0,12},{4,8},{8,4},{12,0},{1,13},{5,9},{9,5},{13,1},{2,14},{6,10},... | collective-permute-start | bytes 208904 | tf_op jit(solution)/shard_map/ppermute | solution.py:677
  28.7 9.5 %collective-permute-start.5 = (bf16[128,1024]{1,0:T(8,128)(2,1)S(1)}, bf16[128,1024]{1,0:T(8,128)(2,1)S(1)}, u32[]{:S(2)}, u32[]{:S(2)}) collective-permute-start(bf16[128,1024]{1,0:T(8,128)(2,1)S(1)} %attention.1.a), channel_id=1, source_target_pairs={{0,2},{1,3},{2,0},{3,1},{4,6},{5,7},{6,4},{7,5},{8,10},{9,11},{10,... | collective-permute-start | bytes 786440 | tf_op jit(solution)/shard_map/ppermute | solution.py:683
  33.9 4.4 %collective-permute-start.7 = (bf16[128,1024]{1,0:T(8,128)(2,1)S(1)}, bf16[128,1024]{1,0:T(8,128)(2,1)S(1)}, u32[]{:S(2)}, u32[]{:S(2)}) collective-permute-start(bf16[128,1024]{1,0:T(8,128)(2,1)S(1)} %attention.1.a), channel_id=1, source_target_pairs={{0,1},{1,0},{2,3},{3,2},{4,5},{5,4},{6,7},{7,6},{8,9},{9,8},{10,11... | collective-permute-start | bytes 786440 | tf_op jit(solution)/shard_map/ppermute | solution.py:684
  38.3 3.1 %collective-permute-start.6 = (bf16[128,1024]{1,0:T(8,128)(2,1)S(1)}, bf16[128,1024]{1,0:T(8,128)(2,1)S(1)}, u32[]{:S(2)}, u32[]{:S(2)}) collective-permute-start(bf16[128,1024]{1,0:T(8,128)(2,1)S(1)} %collective-permute-done.5.a), channel_id=1, source_target_pairs={{0,1},{1,0},{2,3},{3,2},{4,5},{5,4},{6,7},{7,6},{8,9},{9,8},{10,11... | collective-permute-start | bytes 786440 | tf_op jit(solution)/shard_map/ppermute | solution.py:685
  39.6 8.8 %collective-permute-start.8 = (bf16[128,1024]{1,0:T(8,128)(2,1)S(1)}, bf16[128,1024]{1,0:T(8,128)(2,1)S(1)}, u32[]{:S(2)}, u32[]{:S(2)}) collective-permute-start(bf16[128,1024]{1,0:T(8,128)(2,1)S(1)} %get-tuple-element.75), channel_id=1, source_target_pairs={{0,4},{4,0},{8,12},{12,8},{1,5},{5,1},{9,13},{13,9},{2,6},{6,2},{1... | collective-permute-start | bytes 786440 | tf_op jit(solution)/shard_map/ppermute | solution.py:689
  48.4 14.2 %collective-permute-start.9 = (bf16[128,1024]{1,0:T(8,128)(2,1)S(1)}, bf16[128,1024]{1,0:T(8,128)(2,1)S(1)}, u32[]{:S(2)}, u32[]{:S(2)}) collective-permute-start(bf16[128,1024]{1,0:T(8,128)(2,1)S(1)} %add_convert_fusion.3), channel_id=1, source_target_pairs={{0,12},{1,13},{2,10},{3,11},{4,8},{5,9},{6,14},{7,15},{8,4},{9,5},... | collective-permute-start | bytes 786440 | tf_op jit(solution)/shard_map/ppermute | solution.py:696
  49.7 13.3 %collective-permute-start.10 = (bf16[128,1024]{1,0:T(8,128)(2,1)S(1)}, bf16[128,1024]{1,0:T(8,128)(2,1)S(1)}, u32[]{:S(2)}, u32[]{:S(2)}) collective-permute-start(bf16[128,1024]{1,0:T(8,128)(2,1)S(1)} %get-tuple-element.76), channel_id=1, source_target_pairs={{0,4},{4,0},{8,12},{12,8},{1,5},{5,1},{9,13},{13,9},{2,6},{6,2},{1... | collective-permute-start | bytes 786440 | tf_op jit(solution)/shard_map/ppermute | solution.py:696
  63.1 13.0 %collective-permute-start.11 = (bf16[128,1024]{1,0:T(8,128)(2,1)S(1)}, bf16[128,1024]{1,0:T(8,128)(2,1)S(1)}, u32[]{:S(2)}, u32[]{:S(2)}) collective-permute-start(bf16[128,1024]{1,0:T(8,128)(2,1)S(1)} %residual.1.refs_0_), channel_id=1, source_target_pairs={{0,4},{4,0},{8,12},{12,8},{1,5},{5,1},{9,13},{13,9},{2,6},{6,2},{1... | collective-permute-start | bytes 786440 | tf_op jit(solution)/shard_map/ppermute | solution.py:704
  64.3 11.8 %collective-permute-start.12 = (bf16[128,1024]{1,0:T(8,128)(2,1)S(1)}, bf16[128,1024]{1,0:T(8,128)(2,1)S(1)}, u32[]{:S(2)}, u32[]{:S(2)}) collective-permute-start(bf16[128,1024]{1,0:T(8,128)(2,1)S(1)} %residual.1.refs_0_), channel_id=1, source_target_pairs={{0,8},{4,12},{8,0},{12,4},{1,9},{5,13},{9,1},{13,5},{2,10},{6,14},... | collective-permute-start | bytes 786440 | tf_op jit(solution)/shard_map/ppermute | solution.py:704
  78.5 5.1 %collective-permute-start.13 = (bf16[2,128,2048]{2,1,0:T(8,128)(2,1)S(1)}, bf16[2,128,2048]{2,1,0:T(8,128)(2,1)S(1)}, u32[]{:S(2)}, u32[]{:S(2)}) collective-permute-start(bf16[2,128,2048]{2,1,0:T(8,128)(2,1)S(1)} %gate_up.5), channel_id=1, source_target_pairs={{0,1},{1,0},{2,3},{3,2},{4,5},{5,4},{6,7},{7,6},{8,9},{9,8},{10,11... | collective-permute-start | bytes 3145736 | tf_op jit(solution)/shard_map/ppermute | solution.py:728
  79.3 4.3 %collective-permute-start.14 = (f32[24,256]{1,0:T(8,128)S(1)}, f32[24,256]{1,0:T(8,128)S(1)}, u32[]{:S(2)}, u32[]{:S(2)}) collective-permute-start(f32[24,256]{1,0:T(8,128)S(1)} %stats.2), channel_id=1, source_target_pairs={{0,2},{1,3},{2,0},{3,1},{4,6},{5,7},{6,4},{7,5},{8,10},{9,11},{10,... | collective-permute-start | bytes 73736 | tf_op jit(solution)/shard_map/ppermute | solution.py:730
  83.7 14.1 %collective-permute-start.17 = (bf16[128,2048]{1,0:T(8,128)(2,1)S(1)}, bf16[128,2048]{1,0:T(8,128)(2,1)S(1)}, u32[]{:S(2)}, u32[]{:S(2)}) collective-permute-start(bf16[128,2048]{1,0:T(8,128)(2,1)S(1)} %fusion), channel_id=1, source_target_pairs={{0,2},{1,3},{2,0},{3,1},{4,6},{5,7},{6,4},{7,5},{8,10},{9,11},{10,... | collective-permute-start | bytes 1572872 | tf_op jit(solution)/shard_map/ppermute | solution.py:735
  85.3 7.9 %collective-permute-start.16 = (bf16[128,1024]{1,0:T(8,128)(2,1)S(1)}, bf16[128,1024]{1,0:T(8,128)(2,1)S(1)}, u32[]{:S(2)}, u32[]{:S(2)}) collective-permute-start(bf16[128,1024]{1,0:T(8,128)(2,1)S(1)} %collective-permute-done.12.refs_1_), channel_id=1, source_target_pairs={{0,4},{4,0},{8,12},{12,8},{1,5},{5,1},{9,13},{13,9},{2,6},{6,2},{1... | collective-permute-start | bytes 786440 | tf_op jit(solution)/shard_map/ppermute | solution.py:705
  87.7 6.3 %collective-permute-start.15 = (f32[24,256]{1,0:T(8,128)S(1)}, f32[24,256]{1,0:T(8,128)S(1)}, u32[]{:S(2)}, u32[]{:S(2)}) collective-permute-start(f32[24,256]{1,0:T(8,128)S(1)} %add.46), channel_id=1, source_target_pairs={{0,1},{1,0},{2,3},{3,2},{4,5},{5,4},{6,7},{7,6},{8,9},{9,8},{10,11... | collective-permute-start | bytes 73736 | tf_op jit(solution)/shard_map/ppermute | solution.py:733
  97.9 10.0 %collective-permute-start.18 = (bf16[2,128,2048]{2,1,0:T(8,128)(2,1)S(1)}, bf16[2,128,2048]{2,1,0:T(8,128)(2,1)S(1)}, u32[]{:S(2)}, u32[]{:S(2)}) collective-permute-start(bf16[2,128,2048]{2,1,0:T(8,128)(2,1)S(1)} %gate_up.6), channel_id=1, source_target_pairs={{0,1},{1,0},{2,3},{3,2},{4,5},{5,4},{6,7},{7,6},{8,9},{9,8},{10,11... | collective-permute-start | bytes 3145736 | tf_op jit(solution)/shard_map/ppermute | solution.py:743
  98.8 9.0 %collective-permute-start.20 = (bf16[128,1024]{1,0:T(8,128)(2,1)S(1)}, bf16[128,1024]{1,0:T(8,128)(2,1)S(1)}, u32[]{:S(2)}, u32[]{:S(2)}) collective-permute-start(bf16[128,1024]{1,0:T(8,128)(2,1)S(1)} %activate.2.a), channel_id=1, source_target_pairs={{0,2},{1,3},{2,0},{3,1},{4,6},{5,7},{6,4},{7,5},{8,10},{9,11},{10,... | collective-permute-start | bytes 786440 | tf_op jit(solution)/shard_map/ppermute | solution.py:710
  101.8 6.3 %collective-permute-start.19 = (f32[24,256]{1,0:T(8,128)S(1)}, f32[24,256]{1,0:T(8,128)S(1)}, u32[]{:S(2)}, u32[]{:S(2)}) collective-permute-start(f32[24,256]{1,0:T(8,128)S(1)} %stats.3), channel_id=1, source_target_pairs={{0,2},{1,3},{2,0},{3,1},{4,6},{5,7},{6,4},{7,5},{8,10},{9,11},{10,... | collective-permute-start | bytes 73736 | tf_op jit(solution)/shard_map/ppermute | solution.py:742
  108.1 14.9 %collective-permute-start.22 = (bf16[128,2048]{1,0:T(8,128)(2,1)S(1)}, bf16[128,2048]{1,0:T(8,128)(2,1)S(1)}, u32[]{:S(2)}, u32[]{:S(2)}) collective-permute-start(bf16[128,2048]{1,0:T(8,128)(2,1)S(1)} %fusion.1), channel_id=1, source_target_pairs={{0,2},{1,3},{2,0},{3,1},{4,6},{5,7},{6,4},{7,5},{8,10},{9,11},{10,... | collective-permute-start | bytes 1572872 | tf_op jit(solution)/shard_map/ppermute | solution.py:751
  108.7 1.5 %collective-permute-start.23 = (bf16[128,1024]{1,0:T(8,128)(2,1)S(1)}, bf16[128,1024]{1,0:T(8,128)(2,1)S(1)}, u32[]{:S(2)}, u32[]{:S(2)}) collective-permute-start(bf16[128,1024]{1,0:T(8,128)(2,1)S(1)} %activate.2.a), channel_id=1, source_target_pairs={{0,1},{1,0},{2,3},{3,2},{4,5},{5,4},{6,7},{7,6},{8,9},{9,8},{10,11... | collective-permute-start | bytes 786440 | tf_op jit(solution)/shard_map/ppermute | solution.py:712
  108.7 1.9 %collective-permute-start.24 = (bf16[128,1024]{1,0:T(8,128)(2,1)S(1)}, bf16[128,1024]{1,0:T(8,128)(2,1)S(1)}, u32[]{:S(2)}, u32[]{:S(2)}) collective-permute-start(bf16[128,1024]{1,0:T(8,128)(2,1)S(1)} %collective-permute-done.20.b), channel_id=1, source_target_pairs={{0,1},{1,0},{2,3},{3,2},{4,5},{5,4},{6,7},{7,6},{8,9},{9,8},{10,11... | collective-permute-start | bytes 786440 | tf_op jit(solution)/shard_map/ppermute | solution.py:750
  113.5 9.4 %collective-permute-start.25 = (bf16[64,1024]{1,0:T(8,128)(2,1)S(1)}, bf16[64,1024]{1,0:T(8,128)(2,1)S(1)}, u32[]{:S(2)}, u32[]{:S(2)}) collective-permute-start(bf16[64,1024]{1,0:T(8,128)(2,1)S(1)} %get-tuple-element.93), channel_id=1, source_target_pairs={{0,8},{4,12},{8,0},{12,4},{1,9},{5,13},{9,1},{13,5},{2,10},{6,14},... | collective-permute-start | bytes 393224 | tf_op jit(solution)/shard_map/ppermute | solution.py:753
  115.6 7.3 %collective-permute-start.26 = (bf16[64,1024]{1,0:T(8,128)(2,1)S(1)}, bf16[64,1024]{1,0:T(8,128)(2,1)S(1)}, u32[]{:S(2)}, u32[]{:S(2)}) collective-permute-start(bf16[64,1024]{1,0:T(8,128)(2,1)S(1)} %get-tuple-element.94), channel_id=1, source_target_pairs={{0,4},{4,0},{8,12},{12,8},{1,5},{5,1},{9,13},{13,9},{2,6},{6,2},{1... | collective-permute-start | bytes 393224 | tf_op jit(solution)/shard_map/ppermute | solution.py:754
  123.9 9.7 %collective-permute-start.27 = (bf16[128,1024]{1,0:T(8,128)(2,1)S(1)}, bf16[128,1024]{1,0:T(8,128)(2,1)S(1)}, u32[]{:S(2)}, u32[]{:S(2)}) collective-permute-start(bf16[128,1024]{1,0:T(8,128)(2,1)S(1)} %activate.3.a), channel_id=1, source_target_pairs={{0,2},{1,3},{2,0},{3,1},{4,6},{5,7},{6,4},{7,5},{8,10},{9,11},{10,... | collective-permute-start | bytes 786440 | tf_op jit(solution)/shard_map/ppermute | solution.py:710
  125.4 7.9 %collective-permute-start.28 = (bf16[64,1024]{1,0:T(8,128)(2,1)S(1)}, bf16[64,1024]{1,0:T(8,128)(2,1)S(1)}, u32[]{:S(2)}, u32[]{:S(2)}) collective-permute-start(bf16[64,1024]{1,0:T(8,128)(2,1)S(1)} %get-tuple-element.96), channel_id=1, source_target_pairs={{0,8},{4,12},{8,0},{12,4},{1,9},{5,13},{9,1},{13,5},{2,10},{6,14},... | collective-permute-start | bytes 393224 | tf_op jit(solution)/shard_map/ppermute | solution.py:753
  127.7 5.9 %collective-permute-start.29 = (bf16[64,1024]{1,0:T(8,128)(2,1)S(1)}, bf16[64,1024]{1,0:T(8,128)(2,1)S(1)}, u32[]{:S(2)}, u32[]{:S(2)}) collective-permute-start(bf16[64,1024]{1,0:T(8,128)(2,1)S(1)} %get-tuple-element.97), channel_id=1, source_target_pairs={{0,4},{4,0},{8,12},{12,8},{1,5},{5,1},{9,13},{13,9},{2,6},{6,2},{1... | collective-permute-start | bytes 393224 | tf_op jit(solution)/shard_map/ppermute | solution.py:754
  129.4 4.2 %collective-permute-start.30 = (bf16[128,1024]{1,0:T(8,128)(2,1)S(1)}, bf16[128,1024]{1,0:T(8,128)(2,1)S(1)}, u32[]{:S(2)}, u32[]{:S(2)}) collective-permute-start(bf16[128,1024]{1,0:T(8,128)(2,1)S(1)} %activate.3.a), channel_id=1, source_target_pairs={{0,1},{1,0},{2,3},{3,2},{4,5},{5,4},{6,7},{7,6},{8,9},{9,8},{10,11... | collective-permute-start | bytes 786440 | tf_op jit(solution)/shard_map/ppermute | solution.py:712
  133.6 1.5 %collective-permute-start.31 = (bf16[128,1024]{1,0:T(8,128)(2,1)S(1)}, bf16[128,1024]{1,0:T(8,128)(2,1)S(1)}, u32[]{:S(2)}, u32[]{:S(2)}) collective-permute-start(bf16[128,1024]{1,0:T(8,128)(2,1)S(1)} %collective-permute-done.27.b), channel_id=1, source_target_pairs={{0,1},{1,0},{2,3},{3,2},{4,5},{5,4},{6,7},{7,6},{8,9},{9,8},{10,11... | collective-permute-start | bytes 786440 | tf_op jit(solution)/shard_map/ppermute | solution.py:713
  138.0 10.3 %collective-permute-start.32 = (bf16[128,1024]{1,0:T(8,128)(2,1)S(1)}, bf16[128,1024]{1,0:T(8,128)(2,1)S(1)}, u32[]{:S(2)}, u32[]{:S(2)}) collective-permute-start(bf16[128,1024]{1,0:T(8,128)(2,1)S(1)} %get-tuple-element.102), channel_id=1, source_target_pairs={{0,12},{4,8},{8,4},{12,0},{1,13},{5,9},{9,5},{13,1},{2,14},{6,10},... | collective-permute-start | bytes 786440 | tf_op jit(solution)/shard_map/ppermute | solution.py:763
  (15 other events, 157.5 us)

commit v14 on v13

--- a/solution.py
+++ b/solution.py
@@ -536,7 +536,7 @@
     )(order, *tokens, gain, pick, weight)
 
 
-def activate_body(groups, features, here, pick, stats, *refs):
+def activate_body(groups, features, offset, here, pick, stats, *refs):
     out = refs[-1]
     _, local, capacity, length = pick.shape
     hid = out.shape[1]
@@ -553,7 +553,7 @@
             chosen = jnp.zeros((experts, length), jnp.float32)
             for c in range(8):
                 chosen = jnp.where(ids[c : c + 1, :] == expert, 1.0, chosen)
-            block = slice((base // capacity + k) * length, (base // capacity + k + 1) * length)
+            block = slice((offset + k) * length, (offset + k + 1) * length)
             inv_rms = lax.rsqrt(stats[experts : experts + 1, block] / features + norm_eps)
             logits = jnp.where(chosen > 0.0, stats[:experts, block] * inv_rms, -jnp.inf)
             grown = jnp.exp(logits - jnp.max(logits, axis=0, keepdims=True))
@@ -570,15 +570,16 @@
             act = gate / (1.0 + jnp.exp(-gate)) * summed[:, hid:] * mix_row
             out[base + k * capacity : base + (k + 1) * capacity, :] = act.astype(jnp.bfloat16)
         base += len(ds) * capacity
-
-
-def activate(groups, features, here, sums, pick, stats, pieces, flops=1 << 20):
+        offset += len(ds)
+
+
+def activate(groups, features, here, sums, pick, stats, pieces, flops=1 << 20, offset=0):
     operands = []
     for ds, terms in zip(groups, sums):
         operands += list(terms) + [pieces[d] for d in ds]
     rows = sum(terms[2].shape[0] for terms in sums)
     return call(
-        functools.partial(activate_body, groups, features),
+        functools.partial(activate_body, groups, features, offset),
         jax.ShapeDtypeStruct((rows, sums[0][2].shape[1] // 2), jnp.bfloat16),
         [],
         in_specs=[SMEM] + [VMEM] * (2 + len(operands)),
@@ -723,7 +724,9 @@
     def stats_of(ds):
         return squares_and_logits([tokens[d] for d in ds], gain, router, experts)
 
-    one_chunk, two_chunk = ((1, 2), (0, 3))
+    one_chunk = (1, 2)
+    kept_0, given_0 = terms_of((0,), order)
+    order, kept_0, given_0 = lax.optimization_barrier((order, kept_0, given_0))
     kept, given = terms_of(one_chunk, order)
     taken = lax.ppermute(given, "tp", pairs(n, 1))
     _, stats = lax.optimization_barrier((given, stats_of(one_chunk)))
@@ -736,31 +739,37 @@
 
     order, _, stats_near = lax.optimization_barrier((order, far_sum, stats_near))
     stats = stats + stats_near
-    kept_2, given = terms_of(two_chunk, order)
-    stats_2 = stats_of(two_chunk)
-    given, across, stats_2 = lax.optimization_barrier((given, across, stats_2))
+    kept_3, given_3 = terms_of((3,), order)
+    stats_2 = stats_of((3, 0))
+    given_3, given_0, across, stats_2 = lax.optimization_barrier((given_3, given_0, across, stats_2))
     stats_far = lax.ppermute(stats_2, "tp", pairs(n, 2))
-    taken_2 = lax.ppermute(given, "tp", pairs(n, 1))
+    taken_3 = lax.ppermute(given_3, "tp", pairs(n, 1))
+    taken_0 = lax.ppermute(given_0, "tp", pairs(n, 1))
     sums = [(kept, taken, across)]
     acts = spread_act(activate((one_chunk,), features, here, sums, pick, stats, pieces))
-    far_sum = chip_sum(kept_2, taken_2)
-    far_sum, stats_far, acts[1] = lax.optimization_barrier((far_sum, stats_far, acts[1]))
+    sum_3, sum_0 = (chip_sum(kept_3, taken_3), chip_sum(kept_0, taken_0))
+    sum_3, sum_0, stats_far, acts[1] = lax.optimization_barrier((sum_3, sum_0, stats_far, acts[1]))
     stats_2 = stats_2 + stats_far
     stats_near = lax.ppermute(stats_2, "tp", pairs(n, 1))
     acts[3] = lax.ppermute(acts[1], "tp", pairs(n, 1))
-    across = lax.ppermute(far_sum, "tp", pairs(n, 2))
+    across_3 = lax.ppermute(sum_3, "tp", pairs(n, 2))
+    across_0 = lax.ppermute(sum_0, "tp", pairs(n, 2))
     parts = down(one_chunk, order, acts, spread, w_down, halved=True)
+    across_3, *parts = lax.optimization_barrier((across_3, *parts))
     far = [lax.ppermute(part, "ep", pairs(n, 2)) for part in parts[2:]]
     near = [lax.ppermute(part, "ep", pairs(n, 1)) for part in parts[:2]]
-    across, far[0], near[0] = lax.optimization_barrier((across, far[0], near[0]))
-    sums = [(kept_2, taken_2, across)]
     stats_2 = stats_2 + stats_near
-    acts = spread_act(
-        activate((two_chunk,), features, here, sums, pick, stats_2, pieces, 1 << 32),
-        (far[1], near[1]),
-    )
-    mine, last = down(two_chunk, order, acts, spread, w_down)
+    sums = [(kept_3, taken_3, across_3)]
+    act_3 = activate(((3,),), features, here, sums, pick, stats_2, pieces)
+    across_0, far[0], near[0] = lax.optimization_barrier((across_0, far[0], near[0]))
+    acts = spread_act(act_3)
+    sums = [(kept_0, taken_0, across_0)]
+    act_0 = activate(((0,),), features, here, sums, pick, stats_2, pieces, 1 << 20, 1)
+    acts_0 = spread_act(act_0, (far[1], near[1]))
+    (last,) = down((3,), order, acts, spread, w_down)
+    last, *acts_0 = lax.optimization_barrier((last, *acts_0))
     last = lax.ppermute(last, "ep", pairs(n, 3))
+    (mine,) = down((0,), order, acts_0, spread, w_down)
     returned = [mine, jnp.concatenate(near, axis=0), jnp.concatenate(far, axis=0), last]
     total = residual.astype(jnp.float32)
     for part in returned:

time: 152 us -> 149 us (0.980); the launches traced: 149 us -> 149 us
  starting transfers between devices: 50 us -> 40.1 us
  Pallas kernels: 26.7 us -> 35.6 us
    pallas_call x4 -> x6, Pallas kernels: 9.27 us -> 14.6 us  [gate_up(): call(functools.partial(gate_up_body, ds), jax.ShapeDtypeStruct((count, ro...]
    ppermute x1 -> x4, waiting for transfers between devices: 0.01 us -> 4.24 us  [the longest x1 4.23 us: per_device_square(): across_3 = lax.ppermute(sum_3, 'tp', pairs(n, 2))]
    ppermute x3, starting transfers between devices: 13.2 us -> 9.44 us  [per_device_square(): lax.ppermute(pieces[d], 'ep', pairs(n, d))]
    pallas_call x2 -> x3, Pallas kernels: 5.61 us -> 8.66 us  [down(): call(functools.partial(down_body, ds), shapes, None, grid_spec=pltpu.Pref...]
    ppermute x2, waiting for transfers between devices: 9.79 us -> 6.9 us  [per_device_square(): tokens[d] = lax.ppermute(residual, 'ep', pairs(n, d))]
    ppermute x2, starting transfers between devices: 4.46 us -> 1.69 us  [per_device_square(): far = [lax.ppermute(part, 'ep', pairs(n, 2)) for part in parts[2:]]]
    ppermute x3, waiting for transfers between devices: 3.42 us -> 5.95 us  [per_device_square(): lax.ppermute(pieces[d], 'ep', pairs(n, d))]
    ppermute x2, waiting for transfers between devices: 6.89 us -> 4.56 us  [per_device_square(): far = [lax.ppermute(part, 'ep', pairs(n, 2)) for part in parts[2:]]]
  transfers between devices with their start and end apart: 33 -> 38, of which waited for: 18 -> 17; matrix products, arithmetic and copies ran while one was open for 10% -> 10% of each run, Pallas kernels for 11% -> 20%
where the time goes in v14:
time: 149 us
  waiting for transfers between devices  53.9 us (36%)
  starting transfers between devices  40.1 us (27%)
  Pallas kernels  35.6 us (24%)
  local copies, waits for them, and re-layouts  13.8 us (9%)
  other arithmetic  4.77 us (3%)
    pallas_call x6, Pallas kernels, gate_up(): call(functools.partial(gate_up_body, ds), jax.ShapeDtypeStruct((count, ro...  14.6 us
    optimization_barrier x1, local copies, waits for them, and re-layouts, per_device_square(): kept, w_gate_up = lax.optimization_barrier((kept, w_gate_up))  11.2 us
    ppermute x3, starting transfers between devices, per_device_square(): lax.ppermute(pieces[d], 'ep', pairs(n, d))  9.44 us
    pallas_call x3, Pallas kernels, down(): call(functools.partial(down_body, ds), shapes, None, grid_spec=pltpu.Pref...  8.66 us
    ppermute x2, waiting for transfers between devices, per_device_square(): tokens[d] = lax.ppermute(residual, 'ep', pairs(n, d))  6.9 us
    ppermute x1, waiting for transfers between devices, per_device_square(): tokens[3] = lax.ppermute(tokens[2], 'ep', pairs(n, 1))  6.5 us
    ppermute x1, waiting for transfers between devices, per_device_square(): far = lax.ppermute(attended, 'tp', pairs(n, 2))  5.99 us
    ppermute x3, waiting for transfers between devices, per_device_square(): lax.ppermute(pieces[d], 'ep', pairs(n, d))  5.95 us
  transfers between devices with their start and end apart: 38, of which 17 were waited for; matrix products, arithmetic and copies ran while one was open for 10% of the time, Pallas kernels for 20%

profile of v14, /device:TPU:0, one launch (start us, length us, event | category | flops | bytes accessed | tf_op | source)
XLA Modules:
  0.0 148.7 jit_solution(1480248958915095892)
XLA Ops:
  5.3 6.8 %collective-permute-start.2 = (bf16[272,128]{1,0:T(8,128)(2,1)S(1)}, bf16[272,128]{1,0:T(8,128)(2,1)S(1)}, u32[]{:S(2)}, u32[]{:S(2)}) collective-permute-start(bf16[272,128]{1,0:T(8,128)(2,1)S(1)} %get-tuple-element.73), channel_id=1, source_target_pairs={{0,4},{4,0},{8,12},{12,8},{1,5},{5,1},{9,13},{13,9},{2,6},{6,2},{1... | collective-permute-start | bytes 208904 | tf_op jit(solution)/shard_map/ppermute | solution.py:678
  12.1 2.6 %collective-permute-start.3 = (bf16[272,128]{1,0:T(8,128)(2,1)S(1)}, bf16[272,128]{1,0:T(8,128)(2,1)S(1)}, u32[]{:S(2)}, u32[]{:S(2)}) collective-permute-start(bf16[272,128]{1,0:T(8,128)(2,1)S(1)} %get-tuple-element.74), channel_id=1, source_target_pairs={{0,8},{4,12},{8,0},{12,4},{1,9},{5,13},{9,1},{13,5},{2,10},{6,14},... | collective-permute-start | bytes 208904 | tf_op jit(solution)/shard_map/ppermute | solution.py:678
  15.6 1.7 %broadcast_multiply_fusion.weight = bf16[1024,1024]{1,0:T(8,128)(2,1)S(1)} fusion(bf16[1024,1024]{1,0:T(8,128)(2,1)} %param.21, bf16[]{:T(256)} %constant.23.clone.1), kind=kLoop, calls=%fused_computation.2 | loop fusion | flops 1048576 | bytes 4194306 | tf_op jit(solution)/shard_map/mul | solution.py:682
  18.2 5.9 %collective-permute-done.3.c2.refs_4_ = bf16[272,128]{1,0:T(8,128)(2,1)S(1)} collective-permute-done((bf16[272,128]{1,0:T(8,128)(2,1)S(1)}, bf16[272,128]{1,0:T(8,128)(2,1)S(1)}, u32[]{:S(2)}, u32[]{:S(2)}) %collective-permute-start.3) | collective-permute-done | bytes 69664 | tf_op jit(solution)/shard_map/ppermute | solution.py:678
  24.2 3.4 %attention.1.a = bf16[128,1024]{1,0:T(8,128)(2,1)S(1)} custom-call(s32[2]{0:T(128)S(1)} %pad_add_fusion.here, s32[4,4]{1,0:T(4,128)S(1)} %copy-done.4, s32[8]{0:T(128)S(1)} %copy-done.6, bf16[1280,128]{1,0:T(8,128)(2,1)S(1)} %collective-permute-done.1.q, bf16[272,128]{1,0:T(8,128)(2,1)S(1)} %get-tuple-element.72.c0.refs_3_, ...), custom_call_target="tpu_custom_call" | custom-call | flops 1048576 | bytes 262144 | tf_op jit(solution)/shard_map/attention/pallas_call | solution.py:364
  27.6 4.1 %collective-permute-start.5 = (bf16[128,1024]{1,0:T(8,128)(2,1)S(1)}, bf16[128,1024]{1,0:T(8,128)(2,1)S(1)}, u32[]{:S(2)}, u32[]{:S(2)}) collective-permute-start(bf16[128,1024]{1,0:T(8,128)(2,1)S(1)} %attention.1.a), channel_id=1, source_target_pairs={{0,2},{1,3},{2,0},{3,1},{4,6},{5,7},{6,4},{7,5},{8,10},{9,11},{10,... | collective-permute-start | bytes 786440 | tf_op jit(solution)/shard_map/ppermute | solution.py:684
  31.8 6.0 %collective-permute-done.5.a = bf16[128,1024]{1,0:T(8,128)(2,1)S(1)} collective-permute-done((bf16[128,1024]{1,0:T(8,128)(2,1)S(1)}, bf16[128,1024]{1,0:T(8,128)(2,1)S(1)}, u32[]{:S(2)}, u32[]{:S(2)}) %collective-permute-start.5) | collective-permute-done | bytes 262176 | tf_op jit(solution)/shard_map/ppermute | solution.py:684
  42.6 5.7 %collective-permute-done.8 = bf16[128,1024]{1,0:T(8,128)(2,1)S(1)} collective-permute-done((bf16[128,1024]{1,0:T(8,128)(2,1)S(1)}, bf16[128,1024]{1,0:T(8,128)(2,1)S(1)}, u32[]{:S(2)}, u32[]{:S(2)}) %collective-permute-start.8) | collective-permute-done | bytes 262176 | tf_op jit(solution)/shard_map/ppermute | solution.py:690
  48.3 2.3 %collective-permute-start.9 = (bf16[128,1024]{1,0:T(8,128)(2,1)S(1)}, bf16[128,1024]{1,0:T(8,128)(2,1)S(1)}, u32[]{:S(2)}, u32[]{:S(2)}) collective-permute-start(bf16[128,1024]{1,0:T(8,128)(2,1)S(1)} %add_convert_fusion.4), channel_id=1, source_target_pairs={{0,12},{1,13},{2,10},{3,11},{4,8},{5,9},{6,14},{7,15},{8,4},{9,5},... | collective-permute-start | bytes 786440 | tf_op jit(solution)/shard_map/ppermute | solution.py:697
  51.8 11.2 %copy.25 = bf16[4,1024,2,1024]{3,1,2,0:T(8,128)(2,1)S(1)} copy(bf16[4,1024,2,1024]{3,2,1,0:T(2,128)(2,1)} %param.24) | data formatting | bytes 33554432 | tf_op jit(solution)/shard_map/optimization_barrier | solution.py:692
  63.4 2.0 %collective-permute-start.12 = (bf16[128,1024]{1,0:T(8,128)(2,1)S(1)}, bf16[128,1024]{1,0:T(8,128)(2,1)S(1)}, u32[]{:S(2)}, u32[]{:S(2)}) collective-permute-start(bf16[128,1024]{1,0:T(8,128)(2,1)S(1)} %residual.1.refs_0_.refs_1_), channel_id=1, source_target_pairs={{0,8},{4,12},{8,0},{12,4},{1,9},{5,13},{9,1},{13,5},{2,10},{6,14},... | collective-permute-start | bytes 786440 | tf_op jit(solution)/shard_map/ppermute | solution.py:705
  66.3 2.5 %gate_up.7 = bf16[2,64,2048]{2,1,0:T(8,128)(2,1)S(1)} custom-call(s32[2]{0:T(128)S(1)} %get-tuple-element.133.order, bf16[128,1024]{1,0:T(8,128)(2,1)S(1)} %residual.1.refs_0_.refs_1_, f32[1,1024]{1,0:T(1,128)S(1)} %bitcast.36, bf16[4,4,64,128]{3,2,1,0:T(8,128)(2,1)S(1)} %get-tuple-element.92.refs_2_.refs_3_.pick, bf16[4,2,1024,1024]{3,2,1,0:T(8,128)(2,1)S(1)} %bitcast.25), custom_call_target="tpu_custom_call" | custom-call | flops 1048576 | bytes 262144 | tf_op jit(solution)/shard_map/gate_up/pallas_call | solution.py:519
  68.8 2.5 %gate_up.6.refs_0_ = bf16[2,64,2048]{2,1,0:T(8,128)(2,1)S(1)} custom-call(s32[2]{0:T(128)S(1)} %get-tuple-element.134.order, bf16[128,1024]{1,0:T(8,128)(2,1)S(1)} %residual.1.refs_0_.refs_1_, f32[1,1024]{1,0:T(1,128)S(1)} %bitcast.37, bf16[4,4,64,128]{3,2,1,0:T(8,128)(2,1)S(1)} %get-tuple-element.92.refs_2_.refs_3_.pick, bf16[4,2,1024,1024]{3,2,1,0:T(8,128)(2,1)S(1)} %bitcast.26), custom_call_target="tpu_custom_call" | custom-call | flops 1048576 | bytes 262144 | tf_op jit(solution)/shard_map/gate_up/pallas_call | solution.py:519
  71.3 6.9 %collective-permute-done.12.refs_1_ = bf16[128,1024]{1,0:T(8,128)(2,1)S(1)} collective-permute-done((bf16[128,1024]{1,0:T(8,128)(2,1)S(1)}, bf16[128,1024]{1,0:T(8,128)(2,1)S(1)}, u32[]{:S(2)}, u32[]{:S(2)}) %collective-permute-start.12) | collective-permute-done | bytes 262176 | tf_op jit(solution)/shard_map/ppermute | solution.py:705
  78.2 2.3 %gate_up.9 = bf16[2,128,2048]{2,1,0:T(8,128)(2,1)S(1)} custom-call(s32[2]{0:T(128)S(1)} %get-tuple-element.131.order, bf16[128,1024]{1,0:T(8,128)(2,1)S(1)} %collective-permute-done.11.refs_0_, bf16[128,1024]{1,0:T(8,128)(2,1)S(1)} %collective-permute-done.12.refs_1_, f32[1,1024]{1,0:T(1,128)S(1)} %bitcast.38, ...), custom_call_target="tpu_custom_call" | custom-call | flops 1048576 | bytes 262144 | tf_op jit(solution)/shard_map/gate_up/pallas_call | solution.py:519
  81.4 1.4 collective-permute-start.14
  82.8 2.3 %gate_up.8.refs_0_ = bf16[2,128,2048]{2,1,0:T(8,128)(2,1)S(1)} custom-call(s32[2]{0:T(128)S(1)} %get-tuple-element.132.order, bf16[128,1024]{1,0:T(8,128)(2,1)S(1)} %collective-permute-done.11.refs_0_, bf16[128,1024]{1,0:T(8,128)(2,1)S(1)} %collective-permute-done.12.refs_1_, f32[1,1024]{1,0:T(1,128)S(1)} %bitcast.40, ...), custom_call_target="tpu_custom_call" | custom-call | flops 1048576 | bytes 262144 | tf_op jit(solution)/shard_map/gate_up/pallas_call | solution.py:519
  85.4 1.4 collective-permute-start.17
  87.6 6.5 %collective-permute-done.16.refs_0_ = bf16[128,1024]{1,0:T(8,128)(2,1)S(1)} collective-permute-done((bf16[128,1024]{1,0:T(8,128)(2,1)S(1)}, bf16[128,1024]{1,0:T(8,128)(2,1)S(1)}, u32[]{:S(2)}, u32[]{:S(2)}) %collective-permute-start.16) | collective-permute-done | bytes 262176 | tf_op jit(solution)/shard_map/ppermute | solution.py:706
  94.9 2.5 %gate_up.10 = bf16[2,64,2048]{2,1,0:T(8,128)(2,1)S(1)} custom-call(s32[2]{0:T(128)S(1)} %get-tuple-element.130.order, bf16[128,1024]{1,0:T(8,128)(2,1)S(1)} %collective-permute-done.16.refs_0_, f32[1,1024]{1,0:T(1,128)S(1)} %bitcast.42, bf16[4,4,64,128]{3,2,1,0:T(8,128)(2,1)S(1)} %get-tuple-element.92.refs_2_.refs_3_.pick, ...), custom_call_target="tpu_custom_call" | custom-call | flops 1048576 | bytes 262144 | tf_op jit(solution)/shard_map/gate_up/pallas_call | solution.py:519
  97.4 1.9 %collective-permute-done.17.refs_2_ = bf16[128,2048]{1,0:T(8,128)(2,1)S(1)} collective-permute-done((bf16[128,2048]{1,0:T(8,128)(2,1)S(1)}, bf16[128,2048]{1,0:T(8,128)(2,1)S(1)}, u32[]{:S(2)}, u32[]{:S(2)}) %collective-permute-start.17) | collective-permute-done | bytes 524320 | tf_op jit(solution)/shard_map/ppermute | solution.py:738
  101.3 2.5 %gate_up.11.refs_0_ = bf16[2,64,2048]{2,1,0:T(8,128)(2,1)S(1)} custom-call(s32[2]{0:T(128)S(1)} %get-tuple-element.129.order, bf16[128,1024]{1,0:T(8,128)(2,1)S(1)} %collective-permute-done.16.refs_0_, f32[1,1024]{1,0:T(1,128)S(1)} %bitcast.43, bf16[4,4,64,128]{3,2,1,0:T(8,128)(2,1)S(1)} %get-tuple-element.92.refs_2_.refs_3_.pick, ...), custom_call_target="tpu_custom_call" | custom-call | flops 1048576 | bytes 262144 | tf_op jit(solution)/shard_map/gate_up/pallas_call | solution.py:519
  104.1 1.4 collective-permute-start.20
  105.5 3.9 %collective-permute-done.21.b = bf16[128,1024]{1,0:T(8,128)(2,1)S(1)} collective-permute-done((bf16[128,1024]{1,0:T(8,128)(2,1)S(1)}, bf16[128,1024]{1,0:T(8,128)(2,1)S(1)}, u32[]{:S(2)}, u32[]{:S(2)}) %collective-permute-start.21) | collective-permute-done | bytes 262176 | tf_op jit(solution)/shard_map/ppermute | solution.py:711
  111.7 2.8 %down.3 = (bf16[64,1024]{1,0:T(8,128)(2,1)S(1)}, bf16[64,1024]{1,0:T(8,128)(2,1)S(1)}, bf16[64,1024]{1,0:T(8,128)(2,1)S(1)}, bf16[64,1024]{1,0:T(8,128)(2,1)S(1)}) custom-call(s32[4]{0:T(128)S(1)} %broadcast_xor_fusion.order, bf16[128,1024]{1,0:T(8,128)(2,1)S(1)} %activate.3.a, bf16[128,1024]{1,0:T(8,128)(2,1)S(1)} %collective-permute-done.21.b, ...), custom_call_target="tpu_custom_call" | custom-call | flops 1048576 | bytes 262144 | tf_op jit(solution)/shard_map/down/pallas_call | solution.py:626
  114.5 4.2 %collective-permute-done.23.refs_2_ = bf16[64,2048]{1,0:T(8,128)(2,1)S(1)} collective-permute-done((bf16[64,2048]{1,0:T(8,128)(2,1)S(1)}, bf16[64,2048]{1,0:T(8,128)(2,1)S(1)}, u32[]{:S(2)}, u32[]{:S(2)}) %collective-permute-start.23) | collective-permute-done | bytes 262176 | tf_op jit(solution)/shard_map/ppermute | solution.py:755
  119.3 1.8 %collective-permute-start.31 = (bf16[64,1024]{1,0:T(8,128)(2,1)S(1)}, bf16[64,1024]{1,0:T(8,128)(2,1)S(1)}, u32[]{:S(2)}, u32[]{:S(2)}) collective-permute-start(bf16[64,1024]{1,0:T(8,128)(2,1)S(1)} %get-tuple-element.117), channel_id=1, source_target_pairs={{0,4},{4,0},{8,12},{12,8},{1,5},{5,1},{9,13},{13,9},{2,6},{6,2},{1... | collective-permute-start | bytes 393224 | tf_op jit(solution)/shard_map/ppermute | solution.py:760
  129.1 3.9 %collective-permute-done.33 = bf16[64,1024]{1,0:T(8,128)(2,1)S(1)} collective-permute-done((bf16[64,1024]{1,0:T(8,128)(2,1)S(1)}, bf16[64,1024]{1,0:T(8,128)(2,1)S(1)}, u32[]{:S(2)}, u32[]{:S(2)}) %collective-permute-start.33) | collective-permute-done | bytes 131104 | tf_op jit(solution)/shard_map/ppermute | solution.py:759
  134.3 3.0 %down.4 = bf16[128,1024]{1,0:T(8,128)(2,1)S(1)} custom-call(s32[4]{0:T(128)S(1)} %broadcast_xor_fusion.order, bf16[64,1024]{1,0:T(8,128)(2,1)S(1)} %activate.4.a, bf16[64,1024]{1,0:T(8,128)(2,1)S(1)} %collective-permute-done.26.b, bf16[64,1024]{1,0:T(8,128)(2,1)S(1)} %collective-permute-done.27.c, bf16[64,1024]{1,0:T(8,128)(2,1)S(1)} %collective-permute-done.28.d, ...), custom_call_target="tpu_custom_call" | custom-call | flops 1048576 | bytes 262144 | tf_op jit(solution)/shard_map/down/pallas_call | solution.py:626
  137.4 1.9 %collective-permute-start.37 = (bf16[128,1024]{1,0:T(8,128)(2,1)S(1)}, bf16[128,1024]{1,0:T(8,128)(2,1)S(1)}, u32[]{:S(2)}, u32[]{:S(2)}) collective-permute-start(bf16[128,1024]{1,0:T(8,128)(2,1)S(1)} %down.4), channel_id=1, source_target_pairs={{0,12},{4,8},{8,4},{12,0},{1,13},{5,9},{9,5},{13,1},{2,14},{6,10},... | collective-permute-start | bytes 786440 | tf_op jit(solution)/shard_map/ppermute | solution.py:771
  139.3 2.8 %down.5 = bf16[128,1024]{1,0:T(8,128)(2,1)S(1)} custom-call(s32[4]{0:T(128)S(1)} %broadcast_xor_fusion.order, bf16[64,1024]{1,0:T(8,128)(2,1)S(1)} %activate.5.a, bf16[64,1024]{1,0:T(8,128)(2,1)S(1)} %collective-permute-done.32.b, bf16[64,1024]{1,0:T(8,128)(2,1)S(1)} %collective-permute-done.35.c, bf16[64,1024]{1,0:T(8,128)(2,1)S(1)} %collective-permute-done.36.d, ...), custom_call_target="tpu_custom_call" | custom-call | flops 1048576 | bytes 262144 | tf_op jit(solution)/shard_map/down/pallas_call | solution.py:626
  142.2 5.6 %collective-permute-done.37 = bf16[128,1024]{1,0:T(8,128)(2,1)S(1)} collective-permute-done((bf16[128,1024]{1,0:T(8,128)(2,1)S(1)}, bf16[128,1024]{1,0:T(8,128)(2,1)S(1)}, u32[]{:S(2)}, u32[]{:S(2)}) %collective-permute-start.37) | collective-permute-done | bytes 262176 | tf_op jit(solution)/shard_map/ppermute | solution.py:771
  (121 shorter events, 32.3 us)
Async XLA Ops:
  5.3 13.0 %collective-permute-start.2 = (bf16[272,128]{1,0:T(8,128)(2,1)S(1)}, bf16[272,128]{1,0:T(8,128)(2,1)S(1)}, u32[]{:S(2)}, u32[]{:S(2)}) collective-permute-start(bf16[272,128]{1,0:T(8,128)(2,1)S(1)} %get-tuple-element.73), channel_id=1, source_target_pairs={{0,4},{4,0},{8,12},{12,8},{1,5},{5,1},{9,13},{13,9},{2,6},{6,2},{1... | collective-permute-start | bytes 208904 | tf_op jit(solution)/shard_map/ppermute | solution.py:678
  12.1 12.1 %collective-permute-start.3 = (bf16[272,128]{1,0:T(8,128)(2,1)S(1)}, bf16[272,128]{1,0:T(8,128)(2,1)S(1)}, u32[]{:S(2)}, u32[]{:S(2)}) collective-permute-start(bf16[272,128]{1,0:T(8,128)(2,1)S(1)} %get-tuple-element.74), channel_id=1, source_target_pairs={{0,8},{4,12},{8,0},{12,4},{1,9},{5,13},{9,1},{13,5},{2,10},{6,14},... | collective-permute-start | bytes 208904 | tf_op jit(solution)/shard_map/ppermute | solution.py:678
  14.7 9.5 %collective-permute-start.4 = (bf16[272,128]{1,0:T(8,128)(2,1)S(1)}, bf16[272,128]{1,0:T(8,128)(2,1)S(1)}, u32[]{:S(2)}, u32[]{:S(2)}) collective-permute-start(bf16[272,128]{1,0:T(8,128)(2,1)S(1)} %get-tuple-element.75), channel_id=1, source_target_pairs={{0,12},{4,8},{8,4},{12,0},{1,13},{5,9},{9,5},{13,1},{2,14},{6,10},... | collective-permute-start | bytes 208904 | tf_op jit(solution)/shard_map/ppermute | solution.py:678
  14.8 9.4 %collective-permute-start.1 = (bf16[1280,128]{1,0:T(8,128)(2,1)S(1)}, bf16[1280,128]{1,0:T(8,128)(2,1)S(1)}, u32[]{:S(2)}, u32[]{:S(2)}) collective-permute-start(bf16[1280,128]{1,0:T(8,128)(2,1)S(1)} %pad_maximum_fusion), channel_id=1, source_target_pairs={{0,0},{1,8},{2,6},{3,14},{4,12},{5,4},{6,10},{7,2},{8,1},{9,9},{10... | collective-permute-start | bytes 983048 | tf_op jit(solution)/shard_map/ppermute | solution.py:212
  27.6 10.2 %collective-permute-start.5 = (bf16[128,1024]{1,0:T(8,128)(2,1)S(1)}, bf16[128,1024]{1,0:T(8,128)(2,1)S(1)}, u32[]{:S(2)}, u32[]{:S(2)}) collective-permute-start(bf16[128,1024]{1,0:T(8,128)(2,1)S(1)} %attention.1.a), channel_id=1, source_target_pairs={{0,2},{1,3},{2,0},{3,1},{4,6},{5,7},{6,4},{7,5},{8,10},{9,11},{10,... | collective-permute-start | bytes 786440 | tf_op jit(solution)/shard_map/ppermute | solution.py:684
  31.7 7.0 %collective-permute-start.7 = (bf16[128,1024]{1,0:T(8,128)(2,1)S(1)}, bf16[128,1024]{1,0:T(8,128)(2,1)S(1)}, u32[]{:S(2)}, u32[]{:S(2)}) collective-permute-start(bf16[128,1024]{1,0:T(8,128)(2,1)S(1)} %attention.1.a), channel_id=1, source_target_pairs={{0,1},{1,0},{2,3},{3,2},{4,5},{5,4},{6,7},{7,6},{8,9},{9,8},{10,11... | collective-permute-start | bytes 786440 | tf_op jit(solution)/shard_map/ppermute | solution.py:685
  40.0 8.3 %collective-permute-start.8 = (bf16[128,1024]{1,0:T(8,128)(2,1)S(1)}, bf16[128,1024]{1,0:T(8,128)(2,1)S(1)}, u32[]{:S(2)}, u32[]{:S(2)}) collective-permute-start(bf16[128,1024]{1,0:T(8,128)(2,1)S(1)} %get-tuple-element.88), channel_id=1, source_target_pairs={{0,4},{4,0},{8,12},{12,8},{1,5},{5,1},{9,13},{13,9},{2,6},{6,2},{1... | collective-permute-start | bytes 786440 | tf_op jit(solution)/shard_map/ppermute | solution.py:690
  48.3 14.7 %collective-permute-start.9 = (bf16[128,1024]{1,0:T(8,128)(2,1)S(1)}, bf16[128,1024]{1,0:T(8,128)(2,1)S(1)}, u32[]{:S(2)}, u32[]{:S(2)}) collective-permute-start(bf16[128,1024]{1,0:T(8,128)(2,1)S(1)} %add_convert_fusion.4), channel_id=1, source_target_pairs={{0,12},{1,13},{2,10},{3,11},{4,8},{5,9},{6,14},{7,15},{8,4},{9,5},... | collective-permute-start | bytes 786440 | tf_op jit(solution)/shard_map/ppermute | solution.py:697
  50.7 12.6 %collective-permute-start.10 = (bf16[128,1024]{1,0:T(8,128)(2,1)S(1)}, bf16[128,1024]{1,0:T(8,128)(2,1)S(1)}, u32[]{:S(2)}, u32[]{:S(2)}) collective-permute-start(bf16[128,1024]{1,0:T(8,128)(2,1)S(1)} %get-tuple-element.89), channel_id=1, source_target_pairs={{0,4},{4,0},{8,12},{12,8},{1,5},{5,1},{9,13},{13,9},{2,6},{6,2},{1... | collective-permute-start | bytes 786440 | tf_op jit(solution)/shard_map/ppermute | solution.py:697
  63.4 14.8 %collective-permute-start.12 = (bf16[128,1024]{1,0:T(8,128)(2,1)S(1)}, bf16[128,1024]{1,0:T(8,128)(2,1)S(1)}, u32[]{:S(2)}, u32[]{:S(2)}) collective-permute-start(bf16[128,1024]{1,0:T(8,128)(2,1)S(1)} %residual.1.refs_0_.refs_1_), channel_id=1, source_target_pairs={{0,8},{4,12},{8,0},{12,4},{1,9},{5,13},{9,1},{13,5},{2,10},{6,14},... | collective-permute-start | bytes 786440 | tf_op jit(solution)/shard_map/ppermute | solution.py:705
  65.4 12.8 %collective-permute-start.11 = (bf16[128,1024]{1,0:T(8,128)(2,1)S(1)}, bf16[128,1024]{1,0:T(8,128)(2,1)S(1)}, u32[]{:S(2)}, u32[]{:S(2)}) collective-permute-start(bf16[128,1024]{1,0:T(8,128)(2,1)S(1)} %residual.1.refs_0_.refs_1_), channel_id=1, source_target_pairs={{0,4},{4,0},{8,12},{12,8},{1,5},{5,1},{9,13},{13,9},{2,6},{6,2},{1... | collective-permute-start | bytes 786440 | tf_op jit(solution)/shard_map/ppermute | solution.py:705
  80.6 4.7 %collective-permute-start.13 = (bf16[2,128,2048]{2,1,0:T(8,128)(2,1)S(1)}, bf16[2,128,2048]{2,1,0:T(8,128)(2,1)S(1)}, u32[]{:S(2)}, u32[]{:S(2)}) collective-permute-start(bf16[2,128,2048]{2,1,0:T(8,128)(2,1)S(1)} %gate_up.9), channel_id=1, source_target_pairs={{0,1},{1,0},{2,3},{3,2},{4,5},{5,4},{6,7},{7,6},{8,9},{9,8},{10,11... | collective-permute-start | bytes 3145736 | tf_op jit(solution)/shard_map/ppermute | solution.py:731
  85.4 14.0 %collective-permute-start.17 = (bf16[128,2048]{1,0:T(8,128)(2,1)S(1)}, bf16[128,2048]{1,0:T(8,128)(2,1)S(1)}, u32[]{:S(2)}, u32[]{:S(2)}) collective-permute-start(bf16[128,2048]{1,0:T(8,128)(2,1)S(1)} %fusion), channel_id=1, source_target_pairs={{0,2},{1,3},{2,0},{3,1},{4,6},{5,7},{6,4},{7,5},{8,10},{9,11},{10,... | collective-permute-start | bytes 1572872 | tf_op jit(solution)/shard_map/ppermute | solution.py:738
  86.8 7.3 %collective-permute-start.16 = (bf16[128,1024]{1,0:T(8,128)(2,1)S(1)}, bf16[128,1024]{1,0:T(8,128)(2,1)S(1)}, u32[]{:S(2)}, u32[]{:S(2)}) collective-permute-start(bf16[128,1024]{1,0:T(8,128)(2,1)S(1)} %collective-permute-done.12.refs_1_), channel_id=1, source_target_pairs={{0,4},{4,0},{8,12},{12,8},{1,5},{5,1},{9,13},{13,9},{2,6},{6,2},{1... | collective-permute-start | bytes 786440 | tf_op jit(solution)/shard_map/ppermute | solution.py:706
  87.6 7.3 %collective-permute-start.15 = (f32[24,256]{1,0:T(8,128)S(1)}, f32[24,256]{1,0:T(8,128)S(1)}, u32[]{:S(2)}, u32[]{:S(2)}) collective-permute-start(f32[24,256]{1,0:T(8,128)S(1)} %add.50), channel_id=1, source_target_pairs={{0,1},{1,0},{2,3},{3,2},{4,5},{5,4},{6,7},{7,6},{8,9},{9,8},{10,11... | collective-permute-start | bytes 73736 | tf_op jit(solution)/shard_map/ppermute | solution.py:736
  99.4 10.0 %collective-permute-start.18 = (bf16[2,64,2048]{2,1,0:T(8,128)(2,1)S(1)}, bf16[2,64,2048]{2,1,0:T(8,128)(2,1)S(1)}, u32[]{:S(2)}, u32[]{:S(2)}) collective-permute-start(bf16[2,64,2048]{2,1,0:T(8,128)(2,1)S(1)} %gate_up.10), channel_id=1, source_target_pairs={{0,1},{1,0},{2,3},{3,2},{4,5},{5,4},{6,7},{7,6},{8,9},{9,8},{10,11... | collective-permute-start | bytes 1572872 | tf_op jit(solution)/shard_map/ppermute | solution.py:746
  100.3 9.0 %collective-permute-start.21 = (bf16[128,1024]{1,0:T(8,128)(2,1)S(1)}, bf16[128,1024]{1,0:T(8,128)(2,1)S(1)}, u32[]{:S(2)}, u32[]{:S(2)}) collective-permute-start(bf16[128,1024]{1,0:T(8,128)(2,1)S(1)} %activate.3.a), channel_id=1, source_target_pairs={{0,2},{1,3},{2,0},{3,1},{4,6},{5,7},{6,4},{7,5},{8,10},{9,11},{10,... | collective-permute-start | bytes 786440 | tf_op jit(solution)/shard_map/ppermute | solution.py:711
  101.0 8.4 %collective-permute-start.19 = (bf16[2,64,2048]{2,1,0:T(8,128)(2,1)S(1)}, bf16[2,64,2048]{2,1,0:T(8,128)(2,1)S(1)}, u32[]{:S(2)}, u32[]{:S(2)}) collective-permute-start(bf16[2,64,2048]{2,1,0:T(8,128)(2,1)S(1)} %gate_up.7), channel_id=1, source_target_pairs={{0,1},{1,0},{2,3},{3,2},{4,5},{5,4},{6,7},{7,6},{8,9},{9,8},{10,11... | collective-permute-start | bytes 1572872 | tf_op jit(solution)/shard_map/ppermute | solution.py:747
  103.8 7.9 %collective-permute-start.24 = (bf16[128,1024]{1,0:T(8,128)(2,1)S(1)}, bf16[128,1024]{1,0:T(8,128)(2,1)S(1)}, u32[]{:S(2)}, u32[]{:S(2)}) collective-permute-start(bf16[128,1024]{1,0:T(8,128)(2,1)S(1)} %activate.3.a), channel_id=1, source_target_pairs={{0,1},{1,0},{2,3},{3,2},{4,5},{5,4},{6,7},{7,6},{8,9},{9,8},{10,11... | collective-permute-start | bytes 786440 | tf_op jit(solution)/shard_map/ppermute | solution.py:713
  104.1 5.5 %collective-permute-start.20 = (f32[24,256]{1,0:T(8,128)S(1)}, f32[24,256]{1,0:T(8,128)S(1)}, u32[]{:S(2)}, u32[]{:S(2)}) collective-permute-start(f32[24,256]{1,0:T(8,128)S(1)} %stats.3), channel_id=1, source_target_pairs={{0,2},{1,3},{2,0},{3,1},{4,6},{5,7},{6,4},{7,5},{8,10},{9,11},{10,... | collective-permute-start | bytes 73736 | tf_op jit(solution)/shard_map/ppermute | solution.py:745
  109.6 9.2 %collective-permute-start.23 = (bf16[64,2048]{1,0:T(8,128)(2,1)S(1)}, bf16[64,2048]{1,0:T(8,128)(2,1)S(1)}, u32[]{:S(2)}, u32[]{:S(2)}) collective-permute-start(bf16[64,2048]{1,0:T(8,128)(2,1)S(1)} %fusion.1), channel_id=1, source_target_pairs={{0,2},{1,3},{2,0},{3,1},{4,6},{5,7},{6,4},{7,5},{8,10},{9,11},{10,... | collective-permute-start | bytes 786440 | tf_op jit(solution)/shard_map/ppermute | solution.py:755
  110.3 14.8 %collective-permute-start.29 = (bf16[64,2048]{1,0:T(8,128)(2,1)S(1)}, bf16[64,2048]{1,0:T(8,128)(2,1)S(1)}, u32[]{:S(2)}, u32[]{:S(2)}) collective-permute-start(bf16[64,2048]{1,0:T(8,128)(2,1)S(1)} %fusion.2), channel_id=1, source_target_pairs={{0,2},{1,3},{2,0},{3,1},{4,6},{5,7},{6,4},{7,5},{8,10},{9,11},{10,... | collective-permute-start | bytes 786440 | tf_op jit(solution)/shard_map/ppermute | solution.py:756
  118.8 8.4 %collective-permute-start.30 = (bf16[64,1024]{1,0:T(8,128)(2,1)S(1)}, bf16[64,1024]{1,0:T(8,128)(2,1)S(1)}, u32[]{:S(2)}, u32[]{:S(2)}) collective-permute-start(bf16[64,1024]{1,0:T(8,128)(2,1)S(1)} %get-tuple-element.116), channel_id=1, source_target_pairs={{0,8},{4,12},{8,0},{12,4},{1,9},{5,13},{9,1},{13,5},{2,10},{6,14},... | collective-permute-start | bytes 393224 | tf_op jit(solution)/shard_map/ppermute | solution.py:759
  119.3 7.8 %collective-permute-start.31 = (bf16[64,1024]{1,0:T(8,128)(2,1)S(1)}, bf16[64,1024]{1,0:T(8,128)(2,1)S(1)}, u32[]{:S(2)}, u32[]{:S(2)}) collective-permute-start(bf16[64,1024]{1,0:T(8,128)(2,1)S(1)} %get-tuple-element.117), channel_id=1, source_target_pairs={{0,4},{4,0},{8,12},{12,8},{1,5},{5,1},{9,13},{13,9},{2,6},{6,2},{1... | collective-permute-start | bytes 393224 | tf_op jit(solution)/shard_map/ppermute | solution.py:760
  123.1 5.6 %collective-permute-start.26 = (bf16[64,1024]{1,0:T(8,128)(2,1)S(1)}, bf16[64,1024]{1,0:T(8,128)(2,1)S(1)}, u32[]{:S(2)}, u32[]{:S(2)}) collective-permute-start(bf16[64,1024]{1,0:T(8,128)(2,1)S(1)} %activate.4.a), channel_id=1, source_target_pairs={{0,2},{1,3},{2,0},{3,1},{4,6},{5,7},{6,4},{7,5},{8,10},{9,11},{10,... | collective-permute-start | bytes 393224 | tf_op jit(solution)/shard_map/ppermute | solution.py:711
  124.0 9.0 %collective-permute-start.33 = (bf16[64,1024]{1,0:T(8,128)(2,1)S(1)}, bf16[64,1024]{1,0:T(8,128)(2,1)S(1)}, u32[]{:S(2)}, u32[]{:S(2)}) collective-permute-start(bf16[64,1024]{1,0:T(8,128)(2,1)S(1)} %get-tuple-element.119), channel_id=1, source_target_pairs={{0,8},{4,12},{8,0},{12,4},{1,9},{5,13},{9,1},{13,5},{2,10},{6,14},... | collective-permute-start | bytes 393224 | tf_op jit(solution)/shard_map/ppermute | solution.py:759
  125.2 7.8 %collective-permute-start.34 = (bf16[64,1024]{1,0:T(8,128)(2,1)S(1)}, bf16[64,1024]{1,0:T(8,128)(2,1)S(1)}, u32[]{:S(2)}, u32[]{:S(2)}) collective-permute-start(bf16[64,1024]{1,0:T(8,128)(2,1)S(1)} %get-tuple-element.120), channel_id=1, source_target_pairs={{0,4},{4,0},{8,12},{12,8},{1,5},{5,1},{9,13},{13,9},{2,6},{6,2},{1... | collective-permute-start | bytes 393224 | tf_op jit(solution)/shard_map/ppermute | solution.py:760
  127.9 5.2 %collective-permute-start.32 = (bf16[64,1024]{1,0:T(8,128)(2,1)S(1)}, bf16[64,1024]{1,0:T(8,128)(2,1)S(1)}, u32[]{:S(2)}, u32[]{:S(2)}) collective-permute-start(bf16[64,1024]{1,0:T(8,128)(2,1)S(1)} %activate.5.a), channel_id=1, source_target_pairs={{0,2},{1,3},{2,0},{3,1},{4,6},{5,7},{6,4},{7,5},{8,10},{9,11},{10,... | collective-permute-start | bytes 393224 | tf_op jit(solution)/shard_map/ppermute | solution.py:711
  128.6 4.9 %collective-permute-start.27 = (bf16[64,1024]{1,0:T(8,128)(2,1)S(1)}, bf16[64,1024]{1,0:T(8,128)(2,1)S(1)}, u32[]{:S(2)}, u32[]{:S(2)}) collective-permute-start(bf16[64,1024]{1,0:T(8,128)(2,1)S(1)} %activate.4.a), channel_id=1, source_target_pairs={{0,1},{1,0},{2,3},{3,2},{4,5},{5,4},{6,7},{7,6},{8,9},{9,8},{10,11... | collective-permute-start | bytes 393224 | tf_op jit(solution)/shard_map/ppermute | solution.py:713
  128.7 8.6 %collective-permute-start.35 = (bf16[64,1024]{1,0:T(8,128)(2,1)S(1)}, bf16[64,1024]{1,0:T(8,128)(2,1)S(1)}, u32[]{:S(2)}, u32[]{:S(2)}) collective-permute-start(bf16[64,1024]{1,0:T(8,128)(2,1)S(1)} %activate.5.a), channel_id=1, source_target_pairs={{0,1},{1,0},{2,3},{3,2},{4,5},{5,4},{6,7},{7,6},{8,9},{9,8},{10,11... | collective-permute-start | bytes 393224 | tf_op jit(solution)/shard_map/ppermute | solution.py:713
  133.0 4.4 %collective-permute-start.36 = (bf16[64,1024]{1,0:T(8,128)(2,1)S(1)}, bf16[64,1024]{1,0:T(8,128)(2,1)S(1)}, u32[]{:S(2)}, u32[]{:S(2)}) collective-permute-start(bf16[64,1024]{1,0:T(8,128)(2,1)S(1)} %collective-permute-done.32.b), channel_id=1, source_target_pairs={{0,1},{1,0},{2,3},{3,2},{4,5},{5,4},{6,7},{7,6},{8,9},{9,8},{10,11... | collective-permute-start | bytes 393224 | tf_op jit(solution)/shard_map/ppermute | solution.py:714
  137.4 10.3 %collective-permute-start.37 = (bf16[128,1024]{1,0:T(8,128)(2,1)S(1)}, bf16[128,1024]{1,0:T(8,128)(2,1)S(1)}, u32[]{:S(2)}, u32[]{:S(2)}) collective-permute-start(bf16[128,1024]{1,0:T(8,128)(2,1)S(1)} %down.4), channel_id=1, source_target_pairs={{0,12},{4,8},{8,4},{12,0},{1,13},{5,9},{9,5},{13,1},{2,14},{6,10},... | collective-permute-start | bytes 786440 | tf_op jit(solution)/shard_map/ppermute | solution.py:771
  (20 other events, 149.8 us)

commit v15 on v14

--- a/solution.py
+++ b/solution.py
@@ -752,6 +752,7 @@
     stats_2 = stats_2 + stats_far
     stats_near = lax.ppermute(stats_2, "tp", pairs(n, 1))
     acts[3] = lax.ppermute(acts[1], "tp", pairs(n, 1))
+    acts[3], stats_near = lax.optimization_barrier((acts[3], stats_near))
     across_3 = lax.ppermute(sum_3, "tp", pairs(n, 2))
     across_0 = lax.ppermute(sum_0, "tp", pairs(n, 2))
     parts = down(one_chunk, order, acts, spread, w_down, halved=True)

time: 149 us -> 151 us (1.013)
    ppermute x3, waiting for transfers between devices: 4.05 us -> 6.83 us  [spread_act(): far = lax.ppermute(act, 'tp', pairs(n, 2))]
where the time goes in v15:
time: 151 us; the launch traced here: 150 us
  waiting for transfers between devices  55.4 us (37%)
  starting transfers between devices  39.8 us (26%)
  Pallas kernels  35.6 us (24%)
  local copies, waits for them, and re-layouts  13.8 us (9%)
  other arithmetic  4.77 us (3%)
    pallas_call x6, Pallas kernels, gate_up(): call(functools.partial(gate_up_body, ds), jax.ShapeDtypeStruct((count, ro...  14.6 us
    optimization_barrier x1, local copies, waits for them, and re-layouts, per_device_square(): kept, w_gate_up = lax.optimization_barrier((kept, w_gate_up))  11.2 us
    ppermute x3, starting transfers between devices, per_device_square(): lax.ppermute(pieces[d], 'ep', pairs(n, d))  9.44 us
    pallas_call x3, Pallas kernels, down(): call(functools.partial(down_body, ds), shapes, None, grid_spec=pltpu.Pref...  8.64 us
    ppermute x2, waiting for transfers between devices, per_device_square(): tokens[d] = lax.ppermute(residual, 'ep', pairs(n, d))  6.9 us
    ppermute x3, waiting for transfers between devices, spread_act(): far = lax.ppermute(act, 'tp', pairs(n, 2))  6.83 us
    ppermute x1, waiting for transfers between devices, per_device_square(): tokens[3] = lax.ppermute(tokens[2], 'ep', pairs(n, 1))  6.5 us
    ppermute x1, waiting for transfers between devices, per_device_square(): far = lax.ppermute(attended, 'tp', pairs(n, 2))  5.99 us
  transfers between devices with their start and end apart: 38, of which 17 were waited for; matrix products, arithmetic and copies ran while one was open for 10% of the time, Pallas kernels for 20%

profile of v15, /device:TPU:0, one launch (start us, length us, event | category | flops | bytes accessed | tf_op | source)
XLA Modules:
  0.0 149.8 jit_solution(6717063310351428255)
XLA Ops:
  5.3 6.8 %collective-permute-start.2 = (bf16[272,128]{1,0:T(8,128)(2,1)S(1)}, bf16[272,128]{1,0:T(8,128)(2,1)S(1)}, u32[]{:S(2)}, u32[]{:S(2)}) collective-permute-start(bf16[272,128]{1,0:T(8,128)(2,1)S(1)} %get-tuple-element.75), channel_id=1, source_target_pairs={{0,4},{4,0},{8,12},{12,8},{1,5},{5,1},{9,13},{13,9},{2,6},{6,2},{1... | collective-permute-start | bytes 208904 | tf_op jit(solution)/shard_map/ppermute | solution.py:678
  12.1 2.6 %collective-permute-start.3 = (bf16[272,128]{1,0:T(8,128)(2,1)S(1)}, bf16[272,128]{1,0:T(8,128)(2,1)S(1)}, u32[]{:S(2)}, u32[]{:S(2)}) collective-permute-start(bf16[272,128]{1,0:T(8,128)(2,1)S(1)} %get-tuple-element.76), channel_id=1, source_target_pairs={{0,8},{4,12},{8,0},{12,4},{1,9},{5,13},{9,1},{13,5},{2,10},{6,14},... | collective-permute-start | bytes 208904 | tf_op jit(solution)/shard_map/ppermute | solution.py:678
  15.6 1.7 %broadcast_multiply_fusion.weight = bf16[1024,1024]{1,0:T(8,128)(2,1)S(1)} fusion(bf16[1024,1024]{1,0:T(8,128)(2,1)} %param.21, bf16[]{:T(256)} %constant.23.clone.1), kind=kLoop, calls=%fused_computation.2 | loop fusion | flops 1048576 | bytes 4194306 | tf_op jit(solution)/shard_map/mul | solution.py:682
  18.2 5.9 %collective-permute-done.3.c2.refs_4_ = bf16[272,128]{1,0:T(8,128)(2,1)S(1)} collective-permute-done((bf16[272,128]{1,0:T(8,128)(2,1)S(1)}, bf16[272,128]{1,0:T(8,128)(2,1)S(1)}, u32[]{:S(2)}, u32[]{:S(2)}) %collective-permute-start.3) | collective-permute-done | bytes 69664 | tf_op jit(solution)/shard_map/ppermute | solution.py:678
  24.2 3.4 %attention.1.a = bf16[128,1024]{1,0:T(8,128)(2,1)S(1)} custom-call(s32[2]{0:T(128)S(1)} %pad_add_fusion.here, s32[4,4]{1,0:T(4,128)S(1)} %copy-done.4, s32[8]{0:T(128)S(1)} %copy-done.6, bf16[1280,128]{1,0:T(8,128)(2,1)S(1)} %collective-permute-done.1.q, bf16[272,128]{1,0:T(8,128)(2,1)S(1)} %get-tuple-element.74.c0.refs_3_, ...), custom_call_target="tpu_custom_call" | custom-call | flops 1048576 | bytes 262144 | tf_op jit(solution)/shard_map/attention/pallas_call | solution.py:364
  27.6 4.1 %collective-permute-start.5 = (bf16[128,1024]{1,0:T(8,128)(2,1)S(1)}, bf16[128,1024]{1,0:T(8,128)(2,1)S(1)}, u32[]{:S(2)}, u32[]{:S(2)}) collective-permute-start(bf16[128,1024]{1,0:T(8,128)(2,1)S(1)} %attention.1.a), channel_id=1, source_target_pairs={{0,2},{1,3},{2,0},{3,1},{4,6},{5,7},{6,4},{7,5},{8,10},{9,11},{10,... | collective-permute-start | bytes 786440 | tf_op jit(solution)/shard_map/ppermute | solution.py:684
  31.8 6.0 %collective-permute-done.5.a = bf16[128,1024]{1,0:T(8,128)(2,1)S(1)} collective-permute-done((bf16[128,1024]{1,0:T(8,128)(2,1)S(1)}, bf16[128,1024]{1,0:T(8,128)(2,1)S(1)}, u32[]{:S(2)}, u32[]{:S(2)}) %collective-permute-start.5) | collective-permute-done | bytes 262176 | tf_op jit(solution)/shard_map/ppermute | solution.py:684
  42.6 5.7 %collective-permute-done.8 = bf16[128,1024]{1,0:T(8,128)(2,1)S(1)} collective-permute-done((bf16[128,1024]{1,0:T(8,128)(2,1)S(1)}, bf16[128,1024]{1,0:T(8,128)(2,1)S(1)}, u32[]{:S(2)}, u32[]{:S(2)}) %collective-permute-start.8) | collective-permute-done | bytes 262176 | tf_op jit(solution)/shard_map/ppermute | solution.py:690
  48.3 2.3 %collective-permute-start.9 = (bf16[128,1024]{1,0:T(8,128)(2,1)S(1)}, bf16[128,1024]{1,0:T(8,128)(2,1)S(1)}, u32[]{:S(2)}, u32[]{:S(2)}) collective-permute-start(bf16[128,1024]{1,0:T(8,128)(2,1)S(1)} %add_convert_fusion.4), channel_id=1, source_target_pairs={{0,12},{1,13},{2,10},{3,11},{4,8},{5,9},{6,14},{7,15},{8,4},{9,5},... | collective-permute-start | bytes 786440 | tf_op jit(solution)/shard_map/ppermute | solution.py:697
  51.8 11.2 %copy.25 = bf16[4,1024,2,1024]{3,1,2,0:T(8,128)(2,1)S(1)} copy(bf16[4,1024,2,1024]{3,2,1,0:T(2,128)(2,1)} %param.24) | data formatting | bytes 33554432 | tf_op jit(solution)/shard_map/optimization_barrier | solution.py:692
  63.4 2.0 %collective-permute-start.12 = (bf16[128,1024]{1,0:T(8,128)(2,1)S(1)}, bf16[128,1024]{1,0:T(8,128)(2,1)S(1)}, u32[]{:S(2)}, u32[]{:S(2)}) collective-permute-start(bf16[128,1024]{1,0:T(8,128)(2,1)S(1)} %residual.1.refs_0_.refs_1_), channel_id=1, source_target_pairs={{0,8},{4,12},{8,0},{12,4},{1,9},{5,13},{9,1},{13,5},{2,10},{6,14},... | collective-permute-start | bytes 786440 | tf_op jit(solution)/shard_map/ppermute | solution.py:705
  66.3 2.5 %gate_up.7 = bf16[2,64,2048]{2,1,0:T(8,128)(2,1)S(1)} custom-call(s32[2]{0:T(128)S(1)} %get-tuple-element.137.order, bf16[128,1024]{1,0:T(8,128)(2,1)S(1)} %residual.1.refs_0_.refs_1_, f32[1,1024]{1,0:T(1,128)S(1)} %bitcast.36, bf16[4,4,64,128]{3,2,1,0:T(8,128)(2,1)S(1)} %get-tuple-element.94.refs_2_.refs_3_.pick, bf16[4,2,1024,1024]{3,2,1,0:T(8,128)(2,1)S(1)} %bitcast.25), custom_call_target="tpu_custom_call" | custom-call | flops 1048576 | bytes 262144 | tf_op jit(solution)/shard_map/gate_up/pallas_call | solution.py:519
  68.8 2.5 %gate_up.6.refs_0_ = bf16[2,64,2048]{2,1,0:T(8,128)(2,1)S(1)} custom-call(s32[2]{0:T(128)S(1)} %get-tuple-element.138.order, bf16[128,1024]{1,0:T(8,128)(2,1)S(1)} %residual.1.refs_0_.refs_1_, f32[1,1024]{1,0:T(1,128)S(1)} %bitcast.37, bf16[4,4,64,128]{3,2,1,0:T(8,128)(2,1)S(1)} %get-tuple-element.94.refs_2_.refs_3_.pick, bf16[4,2,1024,1024]{3,2,1,0:T(8,128)(2,1)S(1)} %bitcast.26), custom_call_target="tpu_custom_call" | custom-call | flops 1048576 | bytes 262144 | tf_op jit(solution)/shard_map/gate_up/pallas_call | solution.py:519
  71.3 6.9 %collective-permute-done.12.refs_1_ = bf16[128,1024]{1,0:T(8,128)(2,1)S(1)} collective-permute-done((bf16[128,1024]{1,0:T(8,128)(2,1)S(1)}, bf16[128,1024]{1,0:T(8,128)(2,1)S(1)}, u32[]{:S(2)}, u32[]{:S(2)}) %collective-permute-start.12) | collective-permute-done | bytes 262176 | tf_op jit(solution)/shard_map/ppermute | solution.py:705
  78.2 2.3 %gate_up.9 = bf16[2,128,2048]{2,1,0:T(8,128)(2,1)S(1)} custom-call(s32[2]{0:T(128)S(1)} %get-tuple-element.135.order, bf16[128,1024]{1,0:T(8,128)(2,1)S(1)} %collective-permute-done.11.refs_0_, bf16[128,1024]{1,0:T(8,128)(2,1)S(1)} %collective-permute-done.12.refs_1_, f32[1,1024]{1,0:T(1,128)S(1)} %bitcast.38, ...), custom_call_target="tpu_custom_call" | custom-call | flops 1048576 | bytes 262144 | tf_op jit(solution)/shard_map/gate_up/pallas_call | solution.py:519
  82.8 2.3 %gate_up.8.refs_0_ = bf16[2,128,2048]{2,1,0:T(8,128)(2,1)S(1)} custom-call(s32[2]{0:T(128)S(1)} %get-tuple-element.136.order, bf16[128,1024]{1,0:T(8,128)(2,1)S(1)} %collective-permute-done.11.refs_0_, bf16[128,1024]{1,0:T(8,128)(2,1)S(1)} %collective-permute-done.12.refs_1_, f32[1,1024]{1,0:T(1,128)S(1)} %bitcast.40, ...), custom_call_target="tpu_custom_call" | custom-call | flops 1048576 | bytes 262144 | tf_op jit(solution)/shard_map/gate_up/pallas_call | solution.py:519
  85.4 1.4 collective-permute-start.17
  87.6 6.5 %collective-permute-done.16.refs_0_ = bf16[128,1024]{1,0:T(8,128)(2,1)S(1)} collective-permute-done((bf16[128,1024]{1,0:T(8,128)(2,1)S(1)}, bf16[128,1024]{1,0:T(8,128)(2,1)S(1)}, u32[]{:S(2)}, u32[]{:S(2)}) %collective-permute-start.16) | collective-permute-done | bytes 262176 | tf_op jit(solution)/shard_map/ppermute | solution.py:706
  94.9 2.5 %gate_up.10 = bf16[2,64,2048]{2,1,0:T(8,128)(2,1)S(1)} custom-call(s32[2]{0:T(128)S(1)} %get-tuple-element.134.order, bf16[128,1024]{1,0:T(8,128)(2,1)S(1)} %collective-permute-done.16.refs_0_, f32[1,1024]{1,0:T(1,128)S(1)} %bitcast.42, bf16[4,4,64,128]{3,2,1,0:T(8,128)(2,1)S(1)} %get-tuple-element.94.refs_2_.refs_3_.pick, ...), custom_call_target="tpu_custom_call" | custom-call | flops 1048576 | bytes 262144 | tf_op jit(solution)/shard_map/gate_up/pallas_call | solution.py:519
  97.4 1.9 %collective-permute-done.17.refs_2_ = bf16[128,2048]{1,0:T(8,128)(2,1)S(1)} collective-permute-done((bf16[128,2048]{1,0:T(8,128)(2,1)S(1)}, bf16[128,2048]{1,0:T(8,128)(2,1)S(1)}, u32[]{:S(2)}, u32[]{:S(2)}) %collective-permute-start.17) | collective-permute-done | bytes 524320 | tf_op jit(solution)/shard_map/ppermute | solution.py:738
  101.3 2.5 %gate_up.11.refs_0_ = bf16[2,64,2048]{2,1,0:T(8,128)(2,1)S(1)} custom-call(s32[2]{0:T(128)S(1)} %get-tuple-element.133.order, bf16[128,1024]{1,0:T(8,128)(2,1)S(1)} %collective-permute-done.16.refs_0_, f32[1,1024]{1,0:T(1,128)S(1)} %bitcast.43, bf16[4,4,64,128]{3,2,1,0:T(8,128)(2,1)S(1)} %get-tuple-element.94.refs_2_.refs_3_.pick, ...), custom_call_target="tpu_custom_call" | custom-call | flops 1048576 | bytes 262144 | tf_op jit(solution)/shard_map/gate_up/pallas_call | solution.py:519
  103.8 1.4 collective-permute-start.20
  105.2 4.2 %collective-permute-done.21.b = bf16[128,1024]{1,0:T(8,128)(2,1)S(1)} collective-permute-done((bf16[128,1024]{1,0:T(8,128)(2,1)S(1)}, bf16[128,1024]{1,0:T(8,128)(2,1)S(1)}, u32[]{:S(2)}, u32[]{:S(2)}) %collective-permute-start.21) | collective-permute-done | bytes 262176 | tf_op jit(solution)/shard_map/ppermute | solution.py:711
  113.4 2.8 %down.3 = (bf16[64,1024]{1,0:T(8,128)(2,1)S(1)}, bf16[64,1024]{1,0:T(8,128)(2,1)S(1)}, bf16[64,1024]{1,0:T(8,128)(2,1)S(1)}, bf16[64,1024]{1,0:T(8,128)(2,1)S(1)}) custom-call(s32[4]{0:T(128)S(1)} %broadcast_xor_fusion.order, bf16[128,1024]{1,0:T(8,128)(2,1)S(1)} %activate.3.a, bf16[128,1024]{1,0:T(8,128)(2,1)S(1)} %collective-permute-done.21.b, ...), custom_call_target="tpu_custom_call" | custom-call | flops 1048576 | bytes 262144 | tf_op jit(solution)/shard_map/down/pallas_call | solution.py:626
  116.2 3.1 %collective-permute-done.24.refs_2_ = bf16[64,2048]{1,0:T(8,128)(2,1)S(1)} collective-permute-done((bf16[64,2048]{1,0:T(8,128)(2,1)S(1)}, bf16[64,2048]{1,0:T(8,128)(2,1)S(1)}, u32[]{:S(2)}, u32[]{:S(2)}) %collective-permute-start.24) | collective-permute-done | bytes 262176 | tf_op jit(solution)/shard_map/ppermute | solution.py:756
  119.8 1.8 %collective-permute-start.31 = (bf16[64,1024]{1,0:T(8,128)(2,1)S(1)}, bf16[64,1024]{1,0:T(8,128)(2,1)S(1)}, u32[]{:S(2)}, u32[]{:S(2)}) collective-permute-start(bf16[64,1024]{1,0:T(8,128)(2,1)S(1)} %get-tuple-element.121), channel_id=1, source_target_pairs={{0,4},{4,0},{8,12},{12,8},{1,5},{5,1},{9,13},{13,9},{2,6},{6,2},{1... | collective-permute-start | bytes 393224 | tf_op jit(solution)/shard_map/ppermute | solution.py:761
  125.8 3.6 %collective-permute-done.30 = bf16[64,1024]{1,0:T(8,128)(2,1)S(1)} collective-permute-done((bf16[64,1024]{1,0:T(8,128)(2,1)S(1)}, bf16[64,1024]{1,0:T(8,128)(2,1)S(1)}, u32[]{:S(2)}, u32[]{:S(2)}) %collective-permute-start.30) | collective-permute-done | bytes 131104 | tf_op jit(solution)/shard_map/ppermute | solution.py:760
  132.4 2.7 %collective-permute-done.32.b = bf16[64,1024]{1,0:T(8,128)(2,1)S(1)} collective-permute-done((bf16[64,1024]{1,0:T(8,128)(2,1)S(1)}, bf16[64,1024]{1,0:T(8,128)(2,1)S(1)}, u32[]{:S(2)}, u32[]{:S(2)}) %collective-permute-start.32) | collective-permute-done | bytes 131104 | tf_op jit(solution)/shard_map/ppermute | solution.py:711
  135.1 3.0 %down.4 = bf16[128,1024]{1,0:T(8,128)(2,1)S(1)} custom-call(s32[4]{0:T(128)S(1)} %broadcast_xor_fusion.order, bf16[64,1024]{1,0:T(8,128)(2,1)S(1)} %activate.4.a, bf16[64,1024]{1,0:T(8,128)(2,1)S(1)} %collective-permute-done.26.b, bf16[64,1024]{1,0:T(8,128)(2,1)S(1)} %collective-permute-done.27.c, bf16[64,1024]{1,0:T(8,128)(2,1)S(1)} %collective-permute-done.28.d, ...), custom_call_target="tpu_custom_call" | custom-call | flops 1048576 | bytes 262144 | tf_op jit(solution)/shard_map/down/pallas_call | solution.py:626
  138.2 2.2 %collective-permute-start.37 = (bf16[128,1024]{1,0:T(8,128)(2,1)S(1)}, bf16[128,1024]{1,0:T(8,128)(2,1)S(1)}, u32[]{:S(2)}, u32[]{:S(2)}) collective-permute-start(bf16[128,1024]{1,0:T(8,128)(2,1)S(1)} %down.4), channel_id=1, source_target_pairs={{0,12},{4,8},{8,4},{12,0},{1,13},{5,9},{9,5},{13,1},{2,14},{6,10},... | collective-permute-start | bytes 786440 | tf_op jit(solution)/shard_map/ppermute | solution.py:772
  140.4 2.8 %down.5 = bf16[128,1024]{1,0:T(8,128)(2,1)S(1)} custom-call(s32[4]{0:T(128)S(1)} %broadcast_xor_fusion.order, bf16[64,1024]{1,0:T(8,128)(2,1)S(1)} %activate.5.a, bf16[64,1024]{1,0:T(8,128)(2,1)S(1)} %collective-permute-done.32.b, bf16[64,1024]{1,0:T(8,128)(2,1)S(1)} %collective-permute-done.35.c, bf16[64,1024]{1,0:T(8,128)(2,1)S(1)} %collective-permute-done.36.d, ...), custom_call_target="tpu_custom_call" | custom-call | flops 1048576 | bytes 262144 | tf_op jit(solution)/shard_map/down/pallas_call | solution.py:626
  143.2 5.6 %collective-permute-done.37 = bf16[128,1024]{1,0:T(8,128)(2,1)S(1)} collective-permute-done((bf16[128,1024]{1,0:T(8,128)(2,1)S(1)}, bf16[128,1024]{1,0:T(8,128)(2,1)S(1)}, u32[]{:S(2)}, u32[]{:S(2)}) %collective-permute-start.37) | collective-permute-done | bytes 262176 | tf_op jit(solution)/shard_map/ppermute | solution.py:772
  (121 shorter events, 32.9 us)
Async XLA Ops:
  0.0 4.3 %collective-permute-start = (bf16[1024,128]{1,0:T(8,128)(2,1)}, bf16[1024,128]{1,0:T(8,128)(2,1)S(1)}, u32[]{:S(2)}, u32[]{:S(2)}) collective-permute-start(bf16[1024,128]{1,0:T(8,128)(2,1)} %bitcast.45), channel_id=1, source_target_pairs={{1,2},{2,1},{4,7},{7,4},{9,10},{10,9},{12,15},{15,12},{17,18},{18,... | collective-permute-start | bytes 786440 | tf_op jit(solution)/shard_map/ppermute | solution.py:202
  5.3 13.0 %collective-permute-start.2 = (bf16[272,128]{1,0:T(8,128)(2,1)S(1)}, bf16[272,128]{1,0:T(8,128)(2,1)S(1)}, u32[]{:S(2)}, u32[]{:S(2)}) collective-permute-start(bf16[272,128]{1,0:T(8,128)(2,1)S(1)} %get-tuple-element.75), channel_id=1, source_target_pairs={{0,4},{4,0},{8,12},{12,8},{1,5},{5,1},{9,13},{13,9},{2,6},{6,2},{1... | collective-permute-start | bytes 208904 | tf_op jit(solution)/shard_map/ppermute | solution.py:678
  12.1 12.1 %collective-permute-start.3 = (bf16[272,128]{1,0:T(8,128)(2,1)S(1)}, bf16[272,128]{1,0:T(8,128)(2,1)S(1)}, u32[]{:S(2)}, u32[]{:S(2)}) collective-permute-start(bf16[272,128]{1,0:T(8,128)(2,1)S(1)} %get-tuple-element.76), channel_id=1, source_target_pairs={{0,8},{4,12},{8,0},{12,4},{1,9},{5,13},{9,1},{13,5},{2,10},{6,14},... | collective-permute-start | bytes 208904 | tf_op jit(solution)/shard_map/ppermute | solution.py:678
  14.7 9.5 %collective-permute-start.4 = (bf16[272,128]{1,0:T(8,128)(2,1)S(1)}, bf16[272,128]{1,0:T(8,128)(2,1)S(1)}, u32[]{:S(2)}, u32[]{:S(2)}) collective-permute-start(bf16[272,128]{1,0:T(8,128)(2,1)S(1)} %get-tuple-element.77), channel_id=1, source_target_pairs={{0,12},{4,8},{8,4},{12,0},{1,13},{5,9},{9,5},{13,1},{2,14},{6,10},... | collective-permute-start | bytes 208904 | tf_op jit(solution)/shard_map/ppermute | solution.py:678
  14.8 9.4 %collective-permute-start.1 = (bf16[1280,128]{1,0:T(8,128)(2,1)S(1)}, bf16[1280,128]{1,0:T(8,128)(2,1)S(1)}, u32[]{:S(2)}, u32[]{:S(2)}) collective-permute-start(bf16[1280,128]{1,0:T(8,128)(2,1)S(1)} %pad_maximum_fusion), channel_id=1, source_target_pairs={{0,0},{1,8},{2,6},{3,14},{4,12},{5,4},{6,10},{7,2},{8,1},{9,9},{10... | collective-permute-start | bytes 983048 | tf_op jit(solution)/shard_map/ppermute | solution.py:212
  27.6 10.2 %collective-permute-start.5 = (bf16[128,1024]{1,0:T(8,128)(2,1)S(1)}, bf16[128,1024]{1,0:T(8,128)(2,1)S(1)}, u32[]{:S(2)}, u32[]{:S(2)}) collective-permute-start(bf16[128,1024]{1,0:T(8,128)(2,1)S(1)} %attention.1.a), channel_id=1, source_target_pairs={{0,2},{1,3},{2,0},{3,1},{4,6},{5,7},{6,4},{7,5},{8,10},{9,11},{10,... | collective-permute-start | bytes 786440 | tf_op jit(solution)/shard_map/ppermute | solution.py:684
  31.7 7.0 %collective-permute-start.7 = (bf16[128,1024]{1,0:T(8,128)(2,1)S(1)}, bf16[128,1024]{1,0:T(8,128)(2,1)S(1)}, u32[]{:S(2)}, u32[]{:S(2)}) collective-permute-start(bf16[128,1024]{1,0:T(8,128)(2,1)S(1)} %attention.1.a), channel_id=1, source_target_pairs={{0,1},{1,0},{2,3},{3,2},{4,5},{5,4},{6,7},{7,6},{8,9},{9,8},{10,11... | collective-permute-start | bytes 786440 | tf_op jit(solution)/shard_map/ppermute | solution.py:685
  40.0 8.3 %collective-permute-start.8 = (bf16[128,1024]{1,0:T(8,128)(2,1)S(1)}, bf16[128,1024]{1,0:T(8,128)(2,1)S(1)}, u32[]{:S(2)}, u32[]{:S(2)}) collective-permute-start(bf16[128,1024]{1,0:T(8,128)(2,1)S(1)} %get-tuple-element.90), channel_id=1, source_target_pairs={{0,4},{4,0},{8,12},{12,8},{1,5},{5,1},{9,13},{13,9},{2,6},{6,2},{1... | collective-permute-start | bytes 786440 | tf_op jit(solution)/shard_map/ppermute | solution.py:690
  48.3 14.7 %collective-permute-start.9 = (bf16[128,1024]{1,0:T(8,128)(2,1)S(1)}, bf16[128,1024]{1,0:T(8,128)(2,1)S(1)}, u32[]{:S(2)}, u32[]{:S(2)}) collective-permute-start(bf16[128,1024]{1,0:T(8,128)(2,1)S(1)} %add_convert_fusion.4), channel_id=1, source_target_pairs={{0,12},{1,13},{2,10},{3,11},{4,8},{5,9},{6,14},{7,15},{8,4},{9,5},... | collective-permute-start | bytes 786440 | tf_op jit(solution)/shard_map/ppermute | solution.py:697
  50.7 12.6 %collective-permute-start.10 = (bf16[128,1024]{1,0:T(8,128)(2,1)S(1)}, bf16[128,1024]{1,0:T(8,128)(2,1)S(1)}, u32[]{:S(2)}, u32[]{:S(2)}) collective-permute-start(bf16[128,1024]{1,0:T(8,128)(2,1)S(1)} %get-tuple-element.91), channel_id=1, source_target_pairs={{0,4},{4,0},{8,12},{12,8},{1,5},{5,1},{9,13},{13,9},{2,6},{6,2},{1... | collective-permute-start | bytes 786440 | tf_op jit(solution)/shard_map/ppermute | solution.py:697
  63.4 14.8 %collective-permute-start.12 = (bf16[128,1024]{1,0:T(8,128)(2,1)S(1)}, bf16[128,1024]{1,0:T(8,128)(2,1)S(1)}, u32[]{:S(2)}, u32[]{:S(2)}) collective-permute-start(bf16[128,1024]{1,0:T(8,128)(2,1)S(1)} %residual.1.refs_0_.refs_1_), channel_id=1, source_target_pairs={{0,8},{4,12},{8,0},{12,4},{1,9},{5,13},{9,1},{13,5},{2,10},{6,14},... | collective-permute-start | bytes 786440 | tf_op jit(solution)/shard_map/ppermute | solution.py:705
  65.4 12.8 %collective-permute-start.11 = (bf16[128,1024]{1,0:T(8,128)(2,1)S(1)}, bf16[128,1024]{1,0:T(8,128)(2,1)S(1)}, u32[]{:S(2)}, u32[]{:S(2)}) collective-permute-start(bf16[128,1024]{1,0:T(8,128)(2,1)S(1)} %residual.1.refs_0_.refs_1_), channel_id=1, source_target_pairs={{0,4},{4,0},{8,12},{12,8},{1,5},{5,1},{9,13},{13,9},{2,6},{6,2},{1... | collective-permute-start | bytes 786440 | tf_op jit(solution)/shard_map/ppermute | solution.py:705
  80.6 4.7 %collective-permute-start.13 = (bf16[2,128,2048]{2,1,0:T(8,128)(2,1)S(1)}, bf16[2,128,2048]{2,1,0:T(8,128)(2,1)S(1)}, u32[]{:S(2)}, u32[]{:S(2)}) collective-permute-start(bf16[2,128,2048]{2,1,0:T(8,128)(2,1)S(1)} %gate_up.9), channel_id=1, source_target_pairs={{0,1},{1,0},{2,3},{3,2},{4,5},{5,4},{6,7},{7,6},{8,9},{9,8},{10,11... | collective-permute-start | bytes 3145736 | tf_op jit(solution)/shard_map/ppermute | solution.py:731
  81.4 3.9 %collective-permute-start.14 = (f32[24,256]{1,0:T(8,128)S(1)}, f32[24,256]{1,0:T(8,128)S(1)}, u32[]{:S(2)}, u32[]{:S(2)}) collective-permute-start(f32[24,256]{1,0:T(8,128)S(1)} %stats.2), channel_id=1, source_target_pairs={{0,2},{1,3},{2,0},{3,1},{4,6},{5,7},{6,4},{7,5},{8,10},{9,11},{10,... | collective-permute-start | bytes 73736 | tf_op jit(solution)/shard_map/ppermute | solution.py:733
  85.4 14.0 %collective-permute-start.17 = (bf16[128,2048]{1,0:T(8,128)(2,1)S(1)}, bf16[128,2048]{1,0:T(8,128)(2,1)S(1)}, u32[]{:S(2)}, u32[]{:S(2)}) collective-permute-start(bf16[128,2048]{1,0:T(8,128)(2,1)S(1)} %fusion), channel_id=1, source_target_pairs={{0,2},{1,3},{2,0},{3,1},{4,6},{5,7},{6,4},{7,5},{8,10},{9,11},{10,... | collective-permute-start | bytes 1572872 | tf_op jit(solution)/shard_map/ppermute | solution.py:738
  86.8 7.3 %collective-permute-start.16 = (bf16[128,1024]{1,0:T(8,128)(2,1)S(1)}, bf16[128,1024]{1,0:T(8,128)(2,1)S(1)}, u32[]{:S(2)}, u32[]{:S(2)}) collective-permute-start(bf16[128,1024]{1,0:T(8,128)(2,1)S(1)} %collective-permute-done.12.refs_1_), channel_id=1, source_target_pairs={{0,4},{4,0},{8,12},{12,8},{1,5},{5,1},{9,13},{13,9},{2,6},{6,2},{1... | collective-permute-start | bytes 786440 | tf_op jit(solution)/shard_map/ppermute | solution.py:706
  87.6 7.3 %collective-permute-start.15 = (f32[24,256]{1,0:T(8,128)S(1)}, f32[24,256]{1,0:T(8,128)S(1)}, u32[]{:S(2)}, u32[]{:S(2)}) collective-permute-start(f32[24,256]{1,0:T(8,128)S(1)} %add.50), channel_id=1, source_target_pairs={{0,1},{1,0},{2,3},{3,2},{4,5},{5,4},{6,7},{7,6},{8,9},{9,8},{10,11... | collective-permute-start | bytes 73736 | tf_op jit(solution)/shard_map/ppermute | solution.py:736
  99.4 10.0 %collective-permute-start.18 = (bf16[2,64,2048]{2,1,0:T(8,128)(2,1)S(1)}, bf16[2,64,2048]{2,1,0:T(8,128)(2,1)S(1)}, u32[]{:S(2)}, u32[]{:S(2)}) collective-permute-start(bf16[2,64,2048]{2,1,0:T(8,128)(2,1)S(1)} %gate_up.10), channel_id=1, source_target_pairs={{0,1},{1,0},{2,3},{3,2},{4,5},{5,4},{6,7},{7,6},{8,9},{9,8},{10,11... | collective-permute-start | bytes 1572872 | tf_op jit(solution)/shard_map/ppermute | solution.py:746
  100.3 9.0 %collective-permute-start.21 = (bf16[128,1024]{1,0:T(8,128)(2,1)S(1)}, bf16[128,1024]{1,0:T(8,128)(2,1)S(1)}, u32[]{:S(2)}, u32[]{:S(2)}) collective-permute-start(bf16[128,1024]{1,0:T(8,128)(2,1)S(1)} %activate.3.a), channel_id=1, source_target_pairs={{0,2},{1,3},{2,0},{3,1},{4,6},{5,7},{6,4},{7,5},{8,10},{9,11},{10,... | collective-permute-start | bytes 786440 | tf_op jit(solution)/shard_map/ppermute | solution.py:711
  101.0 8.4 %collective-permute-start.19 = (bf16[2,64,2048]{2,1,0:T(8,128)(2,1)S(1)}, bf16[2,64,2048]{2,1,0:T(8,128)(2,1)S(1)}, u32[]{:S(2)}, u32[]{:S(2)}) collective-permute-start(bf16[2,64,2048]{2,1,0:T(8,128)(2,1)S(1)} %gate_up.7), channel_id=1, source_target_pairs={{0,1},{1,0},{2,3},{3,2},{4,5},{5,4},{6,7},{7,6},{8,9},{9,8},{10,11... | collective-permute-start | bytes 1572872 | tf_op jit(solution)/shard_map/ppermute | solution.py:747
  103.8 5.9 %collective-permute-start.20 = (f32[24,256]{1,0:T(8,128)S(1)}, f32[24,256]{1,0:T(8,128)S(1)}, u32[]{:S(2)}, u32[]{:S(2)}) collective-permute-start(f32[24,256]{1,0:T(8,128)S(1)} %stats.3), channel_id=1, source_target_pairs={{0,2},{1,3},{2,0},{3,1},{4,6},{5,7},{6,4},{7,5},{8,10},{9,11},{10,... | collective-permute-start | bytes 73736 | tf_op jit(solution)/shard_map/ppermute | solution.py:745
  110.1 9.2 %collective-permute-start.24 = (bf16[64,2048]{1,0:T(8,128)(2,1)S(1)}, bf16[64,2048]{1,0:T(8,128)(2,1)S(1)}, u32[]{:S(2)}, u32[]{:S(2)}) collective-permute-start(bf16[64,2048]{1,0:T(8,128)(2,1)S(1)} %fusion.1), channel_id=1, source_target_pairs={{0,2},{1,3},{2,0},{3,1},{4,6},{5,7},{6,4},{7,5},{8,10},{9,11},{10,... | collective-permute-start | bytes 786440 | tf_op jit(solution)/shard_map/ppermute | solution.py:756
  110.8 14.1 %collective-permute-start.29 = (bf16[64,2048]{1,0:T(8,128)(2,1)S(1)}, bf16[64,2048]{1,0:T(8,128)(2,1)S(1)}, u32[]{:S(2)}, u32[]{:S(2)}) collective-permute-start(bf16[64,2048]{1,0:T(8,128)(2,1)S(1)} %fusion.2), channel_id=1, source_target_pairs={{0,2},{1,3},{2,0},{3,1},{4,6},{5,7},{6,4},{7,5},{8,10},{9,11},{10,... | collective-permute-start | bytes 786440 | tf_op jit(solution)/shard_map/ppermute | solution.py:757
  119.3 10.0 %collective-permute-start.30 = (bf16[64,1024]{1,0:T(8,128)(2,1)S(1)}, bf16[64,1024]{1,0:T(8,128)(2,1)S(1)}, u32[]{:S(2)}, u32[]{:S(2)}) collective-permute-start(bf16[64,1024]{1,0:T(8,128)(2,1)S(1)} %get-tuple-element.120), channel_id=1, source_target_pairs={{0,8},{4,12},{8,0},{12,4},{1,9},{5,13},{9,1},{13,5},{2,10},{6,14},... | collective-permute-start | bytes 393224 | tf_op jit(solution)/shard_map/ppermute | solution.py:760
  119.8 9.5 %collective-permute-start.31 = (bf16[64,1024]{1,0:T(8,128)(2,1)S(1)}, bf16[64,1024]{1,0:T(8,128)(2,1)S(1)}, u32[]{:S(2)}, u32[]{:S(2)}) collective-permute-start(bf16[64,1024]{1,0:T(8,128)(2,1)S(1)} %get-tuple-element.121), channel_id=1, source_target_pairs={{0,4},{4,0},{8,12},{12,8},{1,5},{5,1},{9,13},{13,9},{2,6},{6,2},{1... | collective-permute-start | bytes 393224 | tf_op jit(solution)/shard_map/ppermute | solution.py:761
  122.4 8.3 %collective-permute-start.26 = (bf16[64,1024]{1,0:T(8,128)(2,1)S(1)}, bf16[64,1024]{1,0:T(8,128)(2,1)S(1)}, u32[]{:S(2)}, u32[]{:S(2)}) collective-permute-start(bf16[64,1024]{1,0:T(8,128)(2,1)S(1)} %activate.4.a), channel_id=1, source_target_pairs={{0,2},{1,3},{2,0},{3,1},{4,6},{5,7},{6,4},{7,5},{8,10},{9,11},{10,... | collective-permute-start | bytes 393224 | tf_op jit(solution)/shard_map/ppermute | solution.py:711
  123.3 9.1 %collective-permute-start.33 = (bf16[64,1024]{1,0:T(8,128)(2,1)S(1)}, bf16[64,1024]{1,0:T(8,128)(2,1)S(1)}, u32[]{:S(2)}, u32[]{:S(2)}) collective-permute-start(bf16[64,1024]{1,0:T(8,128)(2,1)S(1)} %get-tuple-element.123), channel_id=1, source_target_pairs={{0,8},{4,12},{8,0},{12,4},{1,9},{5,13},{9,1},{13,5},{2,10},{6,14},... | collective-permute-start | bytes 393224 | tf_op jit(solution)/shard_map/ppermute | solution.py:760
  124.9 7.5 %collective-permute-start.34 = (bf16[64,1024]{1,0:T(8,128)(2,1)S(1)}, bf16[64,1024]{1,0:T(8,128)(2,1)S(1)}, u32[]{:S(2)}, u32[]{:S(2)}) collective-permute-start(bf16[64,1024]{1,0:T(8,128)(2,1)S(1)} %get-tuple-element.124), channel_id=1, source_target_pairs={{0,4},{4,0},{8,12},{12,8},{1,5},{5,1},{9,13},{13,9},{2,6},{6,2},{1... | collective-permute-start | bytes 393224 | tf_op jit(solution)/shard_map/ppermute | solution.py:761
  130.1 5.0 %collective-permute-start.32 = (bf16[64,1024]{1,0:T(8,128)(2,1)S(1)}, bf16[64,1024]{1,0:T(8,128)(2,1)S(1)}, u32[]{:S(2)}, u32[]{:S(2)}) collective-permute-start(bf16[64,1024]{1,0:T(8,128)(2,1)S(1)} %activate.5.a), channel_id=1, source_target_pairs={{0,2},{1,3},{2,0},{3,1},{4,6},{5,7},{6,4},{7,5},{8,10},{9,11},{10,... | collective-permute-start | bytes 393224 | tf_op jit(solution)/shard_map/ppermute | solution.py:711
  130.8 4.4 %collective-permute-start.27 = (bf16[64,1024]{1,0:T(8,128)(2,1)S(1)}, bf16[64,1024]{1,0:T(8,128)(2,1)S(1)}, u32[]{:S(2)}, u32[]{:S(2)}) collective-permute-start(bf16[64,1024]{1,0:T(8,128)(2,1)S(1)} %activate.4.a), channel_id=1, source_target_pairs={{0,1},{1,0},{2,3},{3,2},{4,5},{5,4},{6,7},{7,6},{8,9},{9,8},{10,11... | collective-permute-start | bytes 393224 | tf_op jit(solution)/shard_map/ppermute | solution.py:713
  130.8 7.4 %collective-permute-start.35 = (bf16[64,1024]{1,0:T(8,128)(2,1)S(1)}, bf16[64,1024]{1,0:T(8,128)(2,1)S(1)}, u32[]{:S(2)}, u32[]{:S(2)}) collective-permute-start(bf16[64,1024]{1,0:T(8,128)(2,1)S(1)} %activate.5.a), channel_id=1, source_target_pairs={{0,1},{1,0},{2,3},{3,2},{4,5},{5,4},{6,7},{7,6},{8,9},{9,8},{10,11... | collective-permute-start | bytes 393224 | tf_op jit(solution)/shard_map/ppermute | solution.py:713
  138.2 10.7 %collective-permute-start.37 = (bf16[128,1024]{1,0:T(8,128)(2,1)S(1)}, bf16[128,1024]{1,0:T(8,128)(2,1)S(1)}, u32[]{:S(2)}, u32[]{:S(2)}) collective-permute-start(bf16[128,1024]{1,0:T(8,128)(2,1)S(1)} %down.4), channel_id=1, source_target_pairs={{0,12},{4,8},{8,4},{12,0},{1,13},{5,9},{9,5},{13,1},{2,14},{6,10},... | collective-permute-start | bytes 786440 | tf_op jit(solution)/shard_map/ppermute | solution.py:772
  (20 other events, 156.1 us)
